TPU v7x, 32 devices: a whole 2x2x4 slice. The times are simulated.
32 devices in a mesh: blk: 8 (over y, x, core), layer: 4 (over z).
Axes of the slice: x: 2, y: 2, z: 4, core: 2. Of those that a mesh axis runs over, the one named last changes fastest.
Arguments:
- flow_t: bfloat16 [8, 8192, 1536], P('blk', 'layer'), may hold values from 0.1 to 100, as said below
- graph: bfloat16 [8, 8192, 1536], P('blk', 'layer'), may hold values from 0.1 to 100, as said below
- a_pattern: int32 [8, 32, 6], P('blk'), may hold values 0 or 1
- b_pattern: int32 [8, 32, 6], P('blk'), may hold values 0 or 1
- c_pattern: int32 [8, 6, 2], P('blk'), may hold values 0 or 1
Outputs:
- next_flow: float32 [8, 1536, 512], P('blk', 'layer')
Inputs may be any that keep to these rules, and one draw needn't show every extreme that they name: `flow_t`: positive entries. `graph`: positive entries.
All inputs are finite; a program needn't handle non-finite values. No bound on the sum of `a_pattern` or of `b_pattern` or of `c_pattern` on one device may be relied on, other than what follows from the above.
Results may differ from a plain program's by a relative error of at most 0.0003.
Values may be sent and summed in bfloat16 or wider, within the bound.
No kernel may reach another device: no remote copies, remote signals or barrier semaphores. Data moves between devices by JAX's collectives and lax.ppermute only.
A program may use at most 64 MiB of HBM per device.

v0:
```python
import jax
import jax.numpy as jnp
from jax import lax
from jax.sharding import PartitionSpec as P

BS = 256


def from_behind(block, axis, distance):
    devices = range(lax.axis_size(axis))
    route = [((i - distance) % len(devices), i) for i in devices]
    return lax.ppermute(block, axis, route)


def block_rows(pattern, start_row, row_count):
    block_index = (start_row + jnp.arange(row_count, dtype=jnp.int32)) // BS
    chosen = (
        block_index[:, None] == jnp.arange(pattern.shape[0], dtype=jnp.int32)[None, :]
    ).astype(jnp.float32)
    row_values = jnp.dot(chosen, pattern.astype(jnp.float32), preferred_element_type=jnp.float32)
    return jnp.repeat(row_values, BS, axis=1)


def contract(left_side, right_side):
    return lax.dot_general(
        left_side, right_side, (((0,), (0,)), ((), ())), preferred_element_type=jnp.float32
    )


def shards(flow_t, graph, a_pattern, b_pattern, c_pattern):
    layers = lax.axis_size("layer")
    layer_id = lax.axis_index("layer")
    flow_local = flow_t[0]
    graph_local = graph[0]
    inner_count = flow_local.shape[0]
    panel_cols = flow_local.shape[1] // 3
    flow_masked = (
        flow_local * block_rows(a_pattern[0], layer_id * inner_count, inner_count)
    ).astype(jnp.bfloat16)
    graph_masked = (
        graph_local * block_rows(b_pattern[0], layer_id * inner_count, inner_count)
    ).astype(jnp.bfloat16)
    own_part = contract(flow_masked, graph_masked[:, panel_cols : 2 * panel_cols])
    to_left = contract(flow_masked[:, : 2 * panel_cols], graph_masked[:, :panel_cols])
    to_right = contract(flow_masked[:, panel_cols:], graph_masked[:, 2 * panel_cols :])
    from_below = from_behind(to_right, "blk", 1)
    from_above = from_behind(to_left, "blk", -1)
    panel_sum = own_part + jnp.pad(from_above, ((panel_cols, 0), (0, 0)))
    panel_sum = panel_sum + jnp.pad(from_below, ((0, panel_cols), (0, 0)))
    row_count = 3 * panel_cols // layers
    owned_rows = lax.psum_scatter(panel_sum, "layer", scatter_dimension=0, tiled=True)
    kept_blocks = owned_rows * block_rows(c_pattern[0], layer_id * row_count, row_count)
    squared = kept_blocks * kept_blocks
    column_total = lax.psum(jnp.sum(squared, axis=0), "layer")
    col_mean = column_total / (3.0 * panel_cols)
    result = squared / (col_mean[None, :] + 1e-06)
    return result[None]


def solution(mesh):
    placed = (
        P("blk", "layer", None),
        P("blk", "layer", None),
        P("blk", None, None),
        P("blk", None, None),
        P("blk", None, None),
    )
    return jax.shard_map(
        shards, mesh=mesh, in_specs=placed, out_specs=P("blk", "layer", None), check_vma=False
    )
```

profile of v0, /device:TPU:0, one launch (start us, length us, event | category | flops | bytes accessed | tf_op | source)
XLA Modules:
  0.0 173.0 jit_solution(18397199987769214008)
XLA Ops:
  6.5 0.0 reduce-scatter.2.cloned.1.call-start
  6.6 0.7 convert_element_type.50
  7.2 0.7 convert_element_type.45
  7.9 0.6 fusion.12
  8.6 0.6 fusion.13
  9.2 8.7 %copy.10 = bf16[1,2048,1536]{1,2,0:T(8,128)(2,1)} copy(bf16[1,2048,1536]{2,1,0:T(8,128)(2,1)} %param.6) | data formatting | bytes 12582912 | tf_op args[1]
  17.9 8.7 %copy.9 = bf16[1,2048,1536]{1,2,0:T(8,128)(2,1)} copy(bf16[1,2048,1536]{2,1,0:T(8,128)(2,1)} %param.5) | data formatting | bytes 12582912 | tf_op args[0]
  26.6 6.7 %fusion = (bf16[2048,1536]{0,1:T(8,128)(2,1)S(1)}, bf16[2048,1536]{0,1:T(8,128)(2,1)S(1)}) fusion(bf16[1,2048,1536]{1,2,0:T(8,128)(2,1)} %copy.10, f32[2048,6]{0,1:T(8,128)S(1)} %fusion.12, f32[2048,6]{0,1:T(8,128)S(1)} %fusion.13, bf16[1,2048,1536]{1,2,0:T(8,128)(2,1)} %copy.9), kind=kLoop, calls=%fused_computation.1 | loop fusion | flops 18874368 | bytes 25264128 | tf_op jit(solution)/shard_map/convert_element_type | solution.py:42
  33.3 2.4 %fusion.4 = f32[1024,512]{1,0:T(8,128)S(1)} fusion(bf16[2048,1536]{0,1:T(8,128)(2,1)S(1)} %get-tuple-element.6, bf16[2048,1536]{0,1:T(8,128)(2,1)S(1)} %get-tuple-element.5), kind=kOutput, calls=%fused_computation.6 | convolution fusion | flops 2147483648 | bytes 8388608 | tf_op jit(solution)/shard_map/dot_general | solution.py:25
  35.7 3.4 %collective-permute-start = (f32[1024,512]{1,0:T(8,128)S(1)}, f32[1024,512]{1,0:T(8,128)S(1)}, u32[]{:S(2)}, u32[]{:S(2)}) collective-permute-start(f32[1024,512]{1,0:T(8,128)S(1)} %fusion.4), channel_id=1, source_target_pairs={{4,0},{8,4},{12,8},{16,12},{20,16},{24,20},{28,24},{0,28},{5,1},{9... | collective-permute-start | bytes 6291464 | tf_op jit(solution)/shard_map/ppermute | solution.py:12
  39.0 2.4 %fusion.2 = f32[1024,512]{1,0:T(8,128)S(1)} fusion(bf16[2048,1536]{0,1:T(8,128)(2,1)S(1)} %get-tuple-element.6, bf16[2048,1536]{0,1:T(8,128)(2,1)S(1)} %get-tuple-element.5), kind=kOutput, calls=%fused_computation.4 | convolution fusion | flops 2147483648 | bytes 8388608 | tf_op jit(solution)/shard_map/dot_general | solution.py:25
  41.4 0.0 copy-start
  41.4 0.1 collective-permute-start.1
  41.5 42.0 %collective-permute-done = f32[1024,512]{1,0:T(8,128)S(1)} collective-permute-done((f32[1024,512]{1,0:T(8,128)S(1)}, f32[1024,512]{1,0:T(8,128)S(1)}, u32[]{:S(2)}, u32[]{:S(2)}) %collective-permute-start) | collective-permute-done | bytes 2097184 | tf_op jit(solution)/shard_map/ppermute | solution.py:12
  83.5 2.6 %collective-permute-done.1 = f32[1024,512]{1,0:T(8,128)S(1)} collective-permute-done((f32[1024,512]{1,0:T(8,128)S(1)}, f32[1024,512]{1,0:T(8,128)S(1)}, u32[]{:S(2)}, u32[]{:S(2)}) %collective-permute-start.1) | collective-permute-done | bytes 2097184 | tf_op jit(solution)/shard_map/ppermute | solution.py:12
  86.1 5.4 %pad_add_fusion = f32[1536,512]{1,0:T(8,128)} fusion(f32[1024,512]{1,0:T(8,128)S(1)} %collective-permute-done.1, f32[1024,512]{1,0:T(8,128)S(1)} %collective-permute-done, bf16[2048,1536]{0,1:T(8,128)(2,1)S(1)} %get-tuple-element.6, bf16[2048,1536]{0,1:T(8,128)(2,1)S(1)} %get-tuple-element.5), kind=kOutput, calls=%fused_computation.8 | convolution fusion | flops 3222798336 | bytes 15728640 | tf_op jit(solution)/shard_map/dot_general | solution.py:25
  91.5 0.0 reduce-scatter.2.cloned.1.call-update
  91.5 0.0 copy-done
  91.6 0.2 fusion.17
  91.8 0.5 broadcast_in_dim.10
  92.3 0.1 copy.15
  92.3 59.9 %reduce-scatter.2.cloned.1.call-done = f32[384,512]{1,0:T(8,128)} async-done(((f32[1536,512]{1,0:T(8,128)}), f32[384,512]{1,0:T(8,128)}) %reduce-scatter.2.cloned.1.call-update) | async-done | bytes 786448 | tf_op jit(solution)/shard_map/reduce_scatter | solution.py:51
  152.2 1.3 fusion.16
  153.5 10.4 %psum.7 = f32[512]{0:T(512)S(1)} all-reduce(f32[512]{0:T(512)S(1)} %fusion.16), channel_id=1, replica_groups=mesh['blk'=8,'layer'=4] {'layer'}, use_global_device_ids=true, to_apply=%region_2.3 | all-reduce | flops 512 | bytes 4096 | tf_op jit(solution)/shard_map/psum | solution.py:54
  163.9 2.2 %divide_bitcast_fusion = f32[1,384,512]{2,1,0:T(8,128)} fusion(f32[512]{0:T(512)S(1)} %multiply_add_fusion, f32[384,512]{1,0:T(8,128)} %reduce-scatter.2.cloned.1.call-done, f32[384,512]{1,0:T(8,128)S(1)} %bitcast.25), kind=kLoop, calls=%fused_computation.16 | loop fusion | flops 589824 | bytes 2361344 | tf_op jit(solution)/shard_map/broadcast_in_dim | solution.py:57
  (3 shorter events, 0.0 us)
Async XLA Ops:
  6.5 145.7 %reduce-scatter.2.cloned.1.call-start = ((), (), s32[]{:S(2)}) async-start(), calls=%async_computation.1 | async-start | bytes 3932160 | tf_op jit(solution)/shard_map/reduce_scatter | solution.py:51
  35.7 47.9 %collective-permute-start = (f32[1024,512]{1,0:T(8,128)S(1)}, f32[1024,512]{1,0:T(8,128)S(1)}, u32[]{:S(2)}, u32[]{:S(2)}) collective-permute-start(f32[1024,512]{1,0:T(8,128)S(1)} %fusion.4), channel_id=1, source_target_pairs={{4,0},{8,4},{12,8},{16,12},{20,16},{24,20},{28,24},{0,28},{5,1},{9... | collective-permute-start | bytes 6291464 | tf_op jit(solution)/shard_map/ppermute | solution.py:12
  41.4 50.1 %copy-start = (s32[1,6,2]{1,2,0:T(2,128)S(1)}, s32[1,6,2]{1,2,0:T(2,128)}, u32[]{:S(2)}) copy-start(s32[1,6,2]{1,2,0:T(2,128)} %param.9) | copy-start | bytes 148
  41.4 44.7 %collective-permute-start.1 = (f32[1024,512]{1,0:T(8,128)S(1)}, f32[1024,512]{1,0:T(8,128)S(1)}, u32[]{:S(2)}, u32[]{:S(2)}) collective-permute-start(f32[1024,512]{1,0:T(8,128)S(1)} %fusion.2), channel_id=1, source_target_pairs={{28,0},{0,4},{4,8},{8,12},{12,16},{16,20},{20,24},{24,28},{29,1},{... | collective-permute-start | bytes 6291464 | tf_op jit(solution)/shard_map/ppermute | solution.py:12
Sparse Core Ops, SparseCore 0:
  91.6 60.5 reduce-scatter.1
where the time goes:
time: 174 us; the launch traced here: 173 us
  waiting for transfers between devices  105 us (60%)
  local copies, waits for them, and re-layouts  17.9 us (10%)
  between operations  13.5 us (8%)
  other arithmetic  11.6 us (7%)
  matrix products  11.6 us (7%)
  blocking collectives  10.4 us (6%)
  starting transfers between devices  3.45 us (2%)
    reduce_scatter x1, waiting for transfers between devices, shards(): lax.psum_scatter(panel_sum, 'layer', scatter_dimension=0, tiled=True)  59.9 us
    ppermute x2, waiting for transfers between devices, from_behind(): return lax.ppermute(block, axis, route)  44.6 us
    unnamed x5, local copies, waits for them, and re-layouts  17.4 us
    psum x1, blocking collectives, shards(): column_total = lax.psum(jnp.sum(squared, axis=0), 'layer')  10.4 us
    dot_general x3, matrix products, contract(): lax.dot_general(left_side, right_side, (((0,), (0,)), ((), ())), preferre...  10.1 us
    convert_element_type x1, other arithmetic, shards(): graph_masked = (graph_local * block_rows(b_pattern[0], layer_id * inner_c...  6.72 us
  transfers between devices with their start and end apart: 3, of which 3 were waited for; matrix products, arithmetic and copies ran while one was open for 2% of the time, Pallas kernels for 0%

commit v1 on v0

v1 whole, which is shorter than its diff:
```python
import functools

import jax
import jax.numpy as jnp
from jax import lax
from jax.experimental import pallas as pl
from jax.experimental.pallas import tpu as pltpu
from jax.sharding import PartitionSpec as P

BS = 256
LANES = 128
HEAD = 16
STEPS = 256.0
TOP = 65534.0
LN2 = 0.6931471805599453
VMEM_LIMIT = 57500000
SMALL_LIMIT = 8 * 1024 * 1024
IN_SMEM = pl.BlockSpec(memory_space=pltpu.SMEM)
IN_VMEM = pl.BlockSpec(memory_space=pltpu.VMEM)
IN_HBM = pl.BlockSpec(memory_space=pltpu.HBM)


def swap(block, axis, partner):
    return lax.ppermute(block, axis, [(partner(i), i) for i in range(lax.axis_size(axis))])


def after(value, *others):
    return lax.optimization_barrier((value, *others))[0]


def call(kernel, name, operands, in_specs, out_shape, scratch_shapes=(), flops=0, moved=0, limit=SMALL_LIMIT):
    return pl.pallas_call(
        kernel,
        out_shape=out_shape,
        in_specs=in_specs,
        out_specs=jax.tree.map(lambda _: IN_VMEM, out_shape),
        scratch_shapes=list(scratch_shapes),
        compiler_params=pltpu.CompilerParams(vmem_limit_bytes=limit),
        cost_estimate=pl.CostEstimate(flops=flops, bytes_accessed=moved, transcendentals=0),
        name=name,
    )(*operands)


def powers(values):
    largest = jnp.maximum(jnp.max(values, axis=0, keepdims=True), 1e-3)
    return jnp.floor(jnp.log(largest) * (STEPS / LN2)) + 2.0


def code(values, power):
    scaled = values * (TOP * jnp.exp(power * (-LN2 / STEPS)))
    return ((scaled + 0.5).astype(jnp.int32) - 32767).astype(jnp.int16)


def scales(head):
    return jnp.exp(head.astype(jnp.int32).astype(jnp.float32) * (LN2 / STEPS)) * (1.0 / TOP)


def decode(codes, scale):
    return (codes.astype(jnp.int32) + 32767).astype(jnp.float32) * scale


def masked(values, pattern, column, first):
    parts = []
    for u in range(values.shape[0] // BS):
        factor = jnp.full((1, values.shape[1]), pattern[column, 0, first + u].astype(jnp.float32))
        parts.append(values[u * BS : (u + 1) * BS] * factor.astype(values.dtype))
    return jnp.concatenate(parts, axis=0) if len(parts) > 1 else parts[0]


def contract(left_side, right_side):
    return lax.dot_general(
        left_side, right_side, (((0,), (0,)), ((), ())), preferred_element_type=jnp.float32
    )


def column_block(ref, block):
    return ref.at[0, :, pl.ds(pl.multiple_of(block * BS, BS), BS)]


def product_kernel(half, wanted, a_ref, b_ref, flow_ref, graph_ref, *rest):
    outs, (flow_buf, graph_buf, sems) = rest[:-3], rest[-3:]
    outs = iter(outs)
    count, inner = flow_buf.shape[:2]
    panel = flow_ref.shape[2] // BS // 3
    odd = lax.rem(lax.axis_index("blk"), 2)
    first = lax.axis_index("layer") * (inner // BS)
    ext_side, int_side = odd * (2 * panel), (1 - odd) * (2 * panel)
    columns = {"ext": ext_side + half, "own": panel + half, "int": int_side + half}
    starts = {"ext": odd * panel, "own": 0, "int": (1 - odd) * panel}
    users = [(panel, ("ext", "own", "int")), (ext_side, ("ext", "own")), (int_side, ("own", "int"))]
    parts = [part for part in ("ext", "own", "int") if part in wanted]
    refs = {part: [next(outs) for _ in wanted[part]] for part in parts}
    blocks = []
    for side, names in users:
        used = [part for part in parts if part in names]
        blocks += [(side + i, used) for i in range(panel) if used]

    graph_copies = [
        pltpu.make_async_copy(column_block(graph_ref, columns[part]), graph_buf.at[j], sems.at[count + j])
        for j, part in enumerate(parts)
    ]
    flow_copies = [
        pltpu.make_async_copy(column_block(flow_ref, block), flow_buf.at[i], sems.at[i])
        for i, (block, _) in enumerate(blocks)
    ]
    for copy in graph_copies + flow_copies:
        copy.start()
    sides = []
    for j, part in enumerate(parts):
        graph_copies[j].wait()
        sides.append(masked(graph_buf[j], b_ref, columns[part], first))
    sides = jnp.concatenate(sides, axis=1) if len(sides) > 1 else sides[0]

    heads = {part: [jnp.zeros((HEAD, ref.shape[1]), jnp.float32) for ref in refs[part]] for part in parts}
    for i, (block, used) in enumerate(blocks):
        flow_copies[i].wait()
        low = parts.index(used[0]) * BS
        product = contract(masked(flow_buf[i], a_ref, block, first), sides[:, low : low + len(used) * BS])
        for j, part in enumerate(used):
            place = block - starts[part]
            column = j * BS
            for c, ref in enumerate(refs[part]):
                chunk = product[:, column : column + ref.shape[1]]
                column += ref.shape[1]
                if part == "own":
                    ref[pl.ds(pl.multiple_of(place * BS, BS), BS), :] = chunk
                else:
                    power = powers(chunk)
                    ref[pl.ds(pl.multiple_of(HEAD + place * BS, HEAD), BS), :] = code(chunk, power)
                    line = lax.broadcasted_iota(jnp.int32, heads[part][c].shape, 0)
                    heads[part][c] = jnp.where(line == place, power, heads[part][c])
    for part in parts:
        for ref, head in zip(refs[part], heads[part]):
            if part != "own":
                ref[0:HEAD, :] = head.astype(jnp.int32).astype(jnp.int16)


def products(flow_t, graph, a_lines, b_lines, half, wanted):
    inner, width = flow_t.shape[1:]
    panel = width // 3
    rows = width if "own" in wanted or len(wanted) > 1 else 2 * panel
    count = rows // BS
    outs = []
    for part in ("ext", "own", "int"):
        for w in wanted.get(part, ()):
            if part == "own":
                outs.append(jax.ShapeDtypeStruct((width, w), jnp.float32))
            else:
                outs.append(jax.ShapeDtypeStruct((HEAD + 2 * panel, w), jnp.int16))
    return call(
        functools.partial(product_kernel, half, wanted),
        "_".join(wanted) + f"_products_{half}",
        (a_lines, b_lines, flow_t, graph),
        [IN_SMEM, IN_SMEM, IN_HBM, IN_HBM],
        outs,
        [
            pltpu.VMEM((count, inner, BS), flow_t.dtype),
            pltpu.VMEM((len(wanted), inner, BS), graph.dtype),
            pltpu.SemaphoreType.DMA((count + len(wanted),)),
        ],
        flops=2 * inner * BS * sum(width if part == "own" else 2 * panel for part in wanted),
        moved=2 * inner * (rows + len(wanted) * BS),
        limit=VMEM_LIMIT,
    )


def split_strips(total, rows, position, keep_ref, send_ref):
    bit = lax.rem(lax.axis_index("layer") // position, 2)
    pairs = keep_ref.shape[0]
    for j in range(pairs):
        keep_ref[j] = total[pl.ds((2 * j + bit) * rows, rows), :]
    away = [total[pl.ds((2 * j + 1 - bit) * rows, rows), :] for j in range(pairs)]
    power = functools.reduce(jnp.maximum, [powers(strip) for strip in away])
    for j, strip in enumerate(away):
        send_ref[HEAD + j * rows : HEAD + (j + 1) * rows, :] = code(strip, power)
    send_ref[0:HEAD, :] = jnp.broadcast_to(power, (HEAD, power.shape[1])).astype(jnp.int32).astype(jnp.int16)


def join_kernel(rows, half, lane, c_ref, own_ref, ext_ref, int_ref, keep_ref, send_ref, total):
    odd = lax.rem(lax.axis_index("blk"), 2)
    blocks = own_ref.shape[0] // BS
    panel = blocks // 3
    lanes = slice(lane, lane + ext_ref.shape[1])
    for v in range(blocks):
        kept = c_ref[0, half, v].astype(jnp.float32)
        total[v * BS : (v + 1) * BS, :] = own_ref[v * BS : (v + 1) * BS, lanes] * kept
    for ref, part, start in ((ext_ref, slice(None), odd * panel), (int_ref, lanes, (1 - odd) * panel)):
        scale = scales(ref[0:HEAD, part])
        for i in range(2 * panel):
            kept = c_ref[0, half, start + i].astype(jnp.float32)
            place = pl.ds(pl.multiple_of((start + i) * BS, BS), BS)
            codes = ref[HEAD + i * BS : HEAD + (i + 1) * BS, part]
            total[place, :] += decode(codes, scale[i : i + 1] * kept)
    split_strips(total, rows, 1, keep_ref, send_ref)


def strips_shapes(pairs, rows, width):
    return [
        jax.ShapeDtypeStruct((pairs, rows, width), jnp.float32),
        jax.ShapeDtypeStruct((HEAD + pairs * rows, width), jnp.int16),
    ]


def join(own, ext_part, int_part, c_lines, half, lane, layers):
    height = own.shape[0]
    width = ext_part.shape[1]
    rows = height // layers
    return call(
        functools.partial(join_kernel, rows, half, lane),
        f"join_{half}_{lane}",
        (c_lines, own, ext_part, int_part),
        [IN_SMEM] + [IN_VMEM] * 3,
        strips_shapes(layers // 2, rows, width),
        [pltpu.VMEM((height, width), jnp.float32)],
        moved=8 * height * width,
    )


def halve_kernel(rows, position, kept_ref, got_ref, keep_ref, send_ref, total):
    scale = scales(got_ref[0:HEAD, :])[0:1]
    for j in range(kept_ref.shape[0]):
        codes = got_ref[HEAD + j * rows : HEAD + (j + 1) * rows, :]
        total[j * rows : (j + 1) * rows, :] = kept_ref[j] + decode(codes, scale)
    split_strips(total, rows, position, keep_ref, send_ref)


def halve(kept, got, position, chunk):
    strips, rows, width = kept.shape
    return call(
        functools.partial(halve_kernel, rows, position),
        f"halve_{position}_{chunk}",
        (kept, got),
        [IN_VMEM] * 2,
        strips_shapes(strips // 2, rows, width),
        [pltpu.VMEM((strips * rows, width), jnp.float32)],
        moved=8 * kept.size,
    )


def square_kernel(kept_ref, got_ref, *rest):
    earlier, (square_ref, sums_ref) = rest[:-2], rest[-2:]
    value = kept_ref[0] + decode(got_ref[HEAD:, :], scales(got_ref[0:HEAD, :])[0:1])
    square = value * value
    square_ref[...] = square
    sums = jnp.broadcast_to(jnp.sum(square, axis=0, keepdims=True), (8, square.shape[1]))
    sums_ref[...] = jnp.concatenate([ref[...] for ref in earlier] + [sums], axis=1)


def square(kept, got, earlier, chunk):
    _, rows, width = kept.shape
    return call(
        square_kernel,
        f"square_{chunk}",
        (kept, got, *earlier),
        [IN_VMEM] * (2 + len(earlier)),
        [
            jax.ShapeDtypeStruct((rows, width), jnp.float32),
            jax.ShapeDtypeStruct((8, width + sum(sums.shape[1] for sums in earlier)), jnp.float32),
        ],
        moved=8 * kept.size,
    )


def rescale_kernel(height, *refs):
    squares, (mine_ref, other_ref, out_ref) = refs[:-3], refs[-3:]
    divisor = (mine_ref[0:1, :] + other_ref[0:1, :]) / height + 1e-6
    column = 0
    for ref in squares:
        columns = slice(column, column + ref.shape[1])
        column += ref.shape[1]
        out_ref[0, :, columns] = ref[...] / divisor[:, columns]


def rescale(squares, mine, other, height):
    rows = squares[0].shape[0]
    width = mine.shape[1]
    return call(
        functools.partial(rescale_kernel, float(height)),
        "rescale",
        (*squares, mine, other),
        [IN_VMEM] * (len(squares) + 2),
        jax.ShapeDtypeStruct((1, rows, width), jnp.float32),
        moved=8 * rows * width,
    )


def shards(flow_t, graph, a_pattern, b_pattern, c_pattern):
    layers = lax.axis_size("layer")
    blks = lax.axis_size("blk")
    width = flow_t.shape[2]
    panel = width // 3
    a_lines = a_pattern.transpose(2, 0, 1)
    b_lines = b_pattern.transpose(2, 0, 1)
    c_lines = c_pattern.transpose(0, 2, 1)

    def other_chip(i):
        return (i + 1 if i % 2 else i - 1) % blks

    def same_chip(i):
        return i ^ 1

    halved = []

    def scatter(kept, send):
        position = 1
        while kept.shape[0] > 1:
            got = swap(send, "layer", lambda i: i ^ position)
            position *= 2
            kept, send = halve(kept, got, position, len(halved))
        halved.append((kept, send))

    def join_all(own, ext_parts, int_part, half):
        lane = 0
        sent = []
        for part in ext_parts:
            kept, send = join(own, part, int_part, c_lines, half, lane, layers)
            scatter(kept, send)
            sent.append(send)
            lane += part.shape[1]
        return sent

    halves = panel // BS
    fine = (LANES,) * (BS // LANES)
    (ext_part,) = products(flow_t, graph, a_lines, b_lines, 0, {"ext": (BS,)})
    got_ext = swap(ext_part, "blk", other_chip)
    own, int_part = products(flow_t, graph, after(a_lines, ext_part), b_lines, 0, {"own": (BS,), "int": (BS,)})
    got_int = swap(int_part, "blk", same_chip)
    a_next = after(a_lines, int_part)
    for half in range(1, halves):
        widths = fine if half == halves - 1 else (BS,)
        *ext_parts, int_part = products(flow_t, graph, a_next, b_lines, half, {"ext": widths, "int": (BS,)})
        next_ext = [swap(part, "blk", other_chip) for part in ext_parts]
        next_int = swap(int_part, "blk", same_chip)
        got_ext = got_ext if half > 1 else [got_ext]
        sent = join_all(own, got_ext, got_int, half - 1)
        (own,) = products(flow_t, graph, after(a_lines, sent[-1]), b_lines, half, {"own": (BS,)})
        a_next = after(a_lines, own)
        got_ext, got_int = next_ext, next_int
    join_all(own, got_ext, got_int, halves - 1)

    squares, sums = [], []
    for chunk, (kept, send) in enumerate(halved):
        got = swap(send, "layer", lambda i: i ^ (layers // 2))
        squared, summed = square(kept, got, sums if chunk == len(halved) - 1 else [], chunk)
        squares.append(squared)
        sums.append(summed)

    total = sums[-1]
    position = 1
    while 2 * position < layers:
        total = total + swap(total, "layer", lambda i: i ^ position)
        position *= 2
    return rescale(squares, total, swap(total, "layer", lambda i: i ^ position), width)


def solution(mesh):
    placed = (
        P("blk", "layer", None),
        P("blk", "layer", None),
        P("blk", None, None),
        P("blk", None, None),
        P("blk", None, None),
    )
    return jax.shard_map(
        shards, mesh=mesh, in_specs=placed, out_specs=P("blk", "layer", None), check_vma=False
    )
```

time: 174 us -> 78.4 us (0.45)
  waiting for transfers between devices: 105 us -> 24.3 us
  Pallas kernels: 0 us -> 37.3 us
  local copies, waits for them, and re-layouts: 17.9 us -> 1.41 us
  between operations: 13.5 us -> 0.17 us
  matrix products: 11.6 us -> 0 us
  other arithmetic: 11.6 us -> 0.01 us
  starting transfers between devices: 3.45 us -> 14.7 us
  blocking collectives: 10.4 us -> 0 us
    reduce_scatter x1 -> x0, waiting for transfers between devices: 59.9 us -> none  [shards(): lax.psum_scatter(panel_sum, 'layer', scatter_dimension=0, tiled=True)]
    pallas_call x0 -> x14, Pallas kernels: none -> 37.3 us  [call(): pl.pallas_call(kernel, out_shape=out_shape, in_specs=in_specs, out_specs=...]
    ppermute x2 -> x13, waiting for transfers between devices: 44.6 us -> 24.3 us  [swap(): lax.ppermute(block, axis, [(partner(i), i) for i in range(lax.axis_size(a...]
    unnamed x5 -> x6, local copies, waits for them, and re-layouts: 17.4 us -> 1.41 us
    dot_general x6 -> x0, matrix products: 11.6 us -> none  [the longest x3 10.1 us: contract(): lax.dot_general(left_side, right_side, (((0,), (0,)), ((), ())), preferre...]
    ppermute x2 -> x13, starting transfers between devices: 3.44 us -> 14.7 us  [swap(): lax.ppermute(block, axis, [(partner(i), i) for i in range(lax.axis_size(a...]
    psum x1 -> x0, blocking collectives: 10.4 us -> none  [shards(): column_total = lax.psum(jnp.sum(squared, axis=0), 'layer')]
    convert_element_type x3 -> x0, other arithmetic: 8.1 us -> none  [the longest x1 6.72 us: shards(): graph_masked = (graph_local * block_rows(b_pattern[0], layer_id * inner_c...]
  transfers between devices with their start and end apart: 3 -> 13, of which waited for: 3 -> 7; matrix products, arithmetic and copies ran while one was open for 2% -> 0% of each run, Pallas kernels for 0% -> 38%
where the time goes in v1:
time: 78.4 us; the launch traced here: 77.9 us
  Pallas kernels  37.3 us (48%)
  waiting for transfers between devices  24.3 us (31%)
  starting transfers between devices  14.7 us (19%)
  local copies, waits for them, and re-layouts  1.41 us (2%)
    pallas_call x14, Pallas kernels, call(): pl.pallas_call(kernel, out_shape=out_shape, in_specs=in_specs, out_specs=...  37.3 us
    ppermute x13, waiting for transfers between devices, swap(): lax.ppermute(block, axis, [(partner(i), i) for i in range(lax.axis_size(a...  24.3 us
    ppermute x13, starting transfers between devices, swap(): lax.ppermute(block, axis, [(partner(i), i) for i in range(lax.axis_size(a...  14.7 us
  transfers between devices with their start and end apart: 13, of which 7 were waited for; matrix products, arithmetic and copies ran while one was open for 0% of the time, Pallas kernels for 38%

profile of v1, /device:TPU:0, one launch (start us, length us, event | category | flops | bytes accessed | tf_op | source)
XLA Modules:
  0.0 77.9 jit_solution(8723927804715896605)
XLA Ops:
  0.0 6.4 %ext_products_0.1 = s16[1040,256]{1,0:T(8,128)(2,1)} custom-call(s32[6,1,32]{2,1,0:T(1,128)} %bitcast.6, s32[6,1,32]{2,1,0:T(1,128)} %bitcast.10, bf16[1,2048,1536]{2,1,0:T(8,128)(2,1)} %flow_ref.7, bf16[1,2048,1536]{2,1,0:T(8,128)(2,1)} %graph_ref.7), custom_call_target="tpu_custom_call" | custom-call | flops 1073741824 | bytes 5242880 | tf_op jit(solution)/shard_map/ext_products_0/pallas_call | solution.py:32
  6.4 3.4 %collective-permute-start = (s16[1040,256]{1,0:T(8,128)(2,1)}, s16[1040,256]{1,0:T(8,128)(2,1)S(1)}, u32[]{:S(2)}, u32[]{:S(2)}) collective-permute-start(s16[1040,256]{1,0:T(8,128)(2,1)} %ext_products_0.1), channel_id=1, source_target_pairs={{28,0},{8,4},{4,8},{16,12},{12,16},{24,20},{20,24},{0,28},{29,1},{... | collective-permute-start | bytes 1597448 | tf_op jit(solution)/shard_map/ppermute | solution.py:24
  9.8 8.7 %own_int_products_0.1 = (f32[1536,256]{1,0:T(8,128)}, s16[1040,256]{1,0:T(8,128)(2,1)}) custom-call(s32[6,1,32]{2,1,0:T(1,128)} %bitcast.7, s32[6,1,32]{2,1,0:T(1,128)} %bitcast.11, bf16[1,2048,1536]{2,1,0:T(8,128)(2,1)} %flow_ref.7, bf16[1,2048,1536]{2,1,0:T(8,128)(2,1)} %graph_ref.7), custom_call_target="tpu_custom_call" | custom-call | flops 2684354560 | bytes 8388608 | tf_op jit(solution)/shard_map/own_int_products_0/pallas_call | solution.py:32
  18.6 8.7 %ext_int_products_1.1 = (s16[1040,128]{1,0:T(8,128)(2,1)}, s16[1040,128]{1,0:T(8,128)(2,1)}, s16[1040,256]{1,0:T(8,128)(2,1)}) custom-call(s32[6,1,32]{2,1,0:T(1,128)} %bitcast.8, s32[6,1,32]{2,1,0:T(1,128)} %bitcast.12, bf16[1,2048,1536]{2,1,0:T(8,128)(2,1)} %flow_ref.7, bf16[1,2048,1536]{2,1,0:T(8,128)(2,1)} %graph_ref.7), custom_call_target="tpu_custom_call" | custom-call | flops 2147483648 | bytes 8388608 | tf_op jit(solution)/shard_map/ext_int_products_1/pallas_call | solution.py:32
  27.4 0.4 collective-permute-start.5
  27.8 1.5 %join_0_0.1 = (f32[2,384,256]{2,1,0:T(8,128)S(1)}, s16[784,256]{1,0:T(8,128)(2,1)S(1)}) custom-call(s32[1,2,6]{2,1,0:T(2,128)S(1)} %bitcast.3, f32[1536,256]{1,0:T(8,128)S(1)} %copy-done.1, s16[1040,256]{1,0:T(8,128)(2,1)S(1)} %collective-permute-done.ext_ref, s16[1040,256]{1,0:T(8,128)(2,1)S(1)} %collective-permute-done.1.int_ref), custom_call_target="tpu_custom_call" | custom-call | bytes 3145728 | tf_op jit(solution)/shard_map/join_0_0/pallas_call | solution.py:32
  29.3 1.6 %collective-permute-start.2 = (s16[784,256]{1,0:T(8,128)(2,1)S(1)}, s16[784,256]{1,0:T(8,128)(2,1)S(1)}, u32[]{:S(2)}, u32[]{:S(2)}) collective-permute-start(s16[784,256]{1,0:T(8,128)(2,1)S(1)} %get-tuple-element.35), channel_id=1, source_target_pairs={{1,0},{0,1},{3,2},{2,3},{5,4},{4,5},{7,6},{6,7},{9,8},{8,9},{11,10... | collective-permute-start | bytes 1204232 | tf_op jit(solution)/shard_map/ppermute | solution.py:24
  30.9 0.5 collective-permute-start.4
  31.4 2.2 %collective-permute-start.8 = (s16[1040,128]{1,0:T(8,128)(2,1)}, s16[1040,128]{1,0:T(8,128)(2,1)S(1)}, u32[]{:S(2)}, u32[]{:S(2)}) collective-permute-start(s16[1040,128]{1,0:T(8,128)(2,1)} %get-tuple-element.48), channel_id=1, source_target_pairs={{28,0},{8,4},{4,8},{16,12},{12,16},{24,20},{20,24},{0,28},{29,1},{... | collective-permute-start | bytes 798728 | tf_op jit(solution)/shard_map/ppermute | solution.py:24
  33.6 8.1 %own_products_1.1.own_ref = f32[1536,256]{1,0:T(8,128)} custom-call(s32[6,1,32]{2,1,0:T(1,128)} %bitcast.9, s32[6,1,32]{2,1,0:T(1,128)} %bitcast.13, bf16[1,2048,1536]{2,1,0:T(8,128)(2,1)} %flow_ref.7, bf16[1,2048,1536]{2,1,0:T(8,128)(2,1)} %graph_ref.7), custom_call_target="tpu_custom_call" | custom-call | flops 1610612736 | bytes 7340032 | tf_op jit(solution)/shard_map/own_products_1/pallas_call | solution.py:32
  41.7 1.4 %copy-done = f32[1536,256]{1,0:T(8,128)S(1)} copy-done((f32[1536,256]{1,0:T(8,128)S(1)}, f32[1536,256]{1,0:T(8,128)}, u32[]{:S(2)}) %copy-start) | copy-done | bytes 1572888
  43.1 1.0 %join_1_0.1 = (f32[2,384,128]{2,1,0:T(8,128)S(1)}, s16[784,128]{1,0:T(8,128)(2,1)S(1)}) custom-call(s32[1,2,6]{2,1,0:T(2,128)S(1)} %bitcast.4, f32[1536,256]{1,0:T(8,128)S(1)} %copy-done, s16[1040,128]{1,0:T(8,128)(2,1)S(1)} %collective-permute-done.4.ext_ref, s16[1040,256]{1,0:T(8,128)(2,1)S(1)} %collective-permute-done.5.int_ref), custom_call_target="tpu_custom_call" | custom-call | bytes 1572864 | tf_op jit(solution)/shard_map/join_1_0/pallas_call | solution.py:32
  44.1 0.5 collective-permute-start.6
  44.6 1.5 %collective-permute-done.8.ext_ref = s16[1040,128]{1,0:T(8,128)(2,1)S(1)} collective-permute-done((s16[1040,128]{1,0:T(8,128)(2,1)}, s16[1040,128]{1,0:T(8,128)(2,1)S(1)}, u32[]{:S(2)}, u32[]{:S(2)}) %collective-permute-start.8) | collective-permute-done | bytes 266272 | tf_op jit(solution)/shard_map/ppermute | solution.py:24
  46.1 1.0 %join_1_128.1 = (f32[2,384,128]{2,1,0:T(8,128)S(1)}, s16[784,128]{1,0:T(8,128)(2,1)S(1)}) custom-call(s32[1,2,6]{2,1,0:T(2,128)S(1)} %bitcast.5, f32[1536,256]{1,0:T(8,128)S(1)} %copy-done, s16[1040,128]{1,0:T(8,128)(2,1)S(1)} %collective-permute-done.8.ext_ref, s16[1040,256]{1,0:T(8,128)(2,1)S(1)} %collective-permute-done.5.int_ref), custom_call_target="tpu_custom_call" | custom-call | bytes 1572864 | tf_op jit(solution)/shard_map/join_1_128/pallas_call | solution.py:32
  47.1 0.5 collective-permute-start.9
  47.6 0.4 halve_2_0.1
  48.0 2.7 %collective-permute-start.3 = (s16[400,256]{1,0:T(8,128)(2,1)S(1)}, s16[400,256]{1,0:T(8,128)(2,1)S(1)}, u32[]{:S(2)}, u32[]{:S(2)}) collective-permute-start(s16[400,256]{1,0:T(8,128)(2,1)S(1)} %get-tuple-element.37), channel_id=1, source_target_pairs={{2,0},{3,1},{0,2},{1,3},{6,4},{7,5},{4,6},{5,7},{10,8},{11,9},{8,1... | collective-permute-start | bytes 614408 | tf_op jit(solution)/shard_map/ppermute | solution.py:24
  50.7 5.1 %collective-permute-done.6.got_ref = s16[784,128]{1,0:T(8,128)(2,1)S(1)} collective-permute-done((s16[784,128]{1,0:T(8,128)(2,1)S(1)}, s16[784,128]{1,0:T(8,128)(2,1)S(1)}, u32[]{:S(2)}, u32[]{:S(2)}) %collective-permute-start.6) | collective-permute-done | bytes 200736 | tf_op jit(solution)/shard_map/ppermute | solution.py:24
  55.8 0.2 halve_2_1.1
  56.1 3.7 %collective-permute-done.9.got_ref = s16[784,128]{1,0:T(8,128)(2,1)S(1)} collective-permute-done((s16[784,128]{1,0:T(8,128)(2,1)S(1)}, s16[784,128]{1,0:T(8,128)(2,1)S(1)}, u32[]{:S(2)}, u32[]{:S(2)}) %collective-permute-start.9) | collective-permute-done | bytes 200736 | tf_op jit(solution)/shard_map/ppermute | solution.py:24
  59.8 0.2 halve_2_2.1
  60.0 7.1 %collective-permute-done.7.got_ref = s16[400,128]{1,0:T(8,128)(2,1)S(1)} collective-permute-done((s16[400,128]{1,0:T(8,128)(2,1)S(1)}, s16[400,128]{1,0:T(8,128)(2,1)S(1)}, u32[]{:S(2)}, u32[]{:S(2)}) %collective-permute-start.7) | collective-permute-done | bytes 102432 | tf_op jit(solution)/shard_map/ppermute | solution.py:24
  67.2 0.1 square_1.1
  67.3 0.1 square_0.1
  67.4 1.0 %collective-permute-done.10.got_ref = s16[400,128]{1,0:T(8,128)(2,1)S(1)} collective-permute-done((s16[400,128]{1,0:T(8,128)(2,1)S(1)}, s16[400,128]{1,0:T(8,128)(2,1)S(1)}, u32[]{:S(2)}, u32[]{:S(2)}) %collective-permute-start.10) | collective-permute-done | bytes 102432 | tf_op jit(solution)/shard_map/ppermute | solution.py:24
  68.4 0.1 square_2.1
  68.5 0.7 collective-permute-start.11
  69.1 3.1 %collective-permute-done.11 = f32[8,512]{1,0:T(8,128)S(1)} collective-permute-done((f32[8,512]{1,0:T(8,128)S(1)}, f32[8,512]{1,0:T(8,128)S(1)}, u32[]{:S(2)}, u32[]{:S(2)}) %collective-permute-start.11) | collective-permute-done | bytes 16416 | tf_op jit(solution)/shard_map/ppermute | solution.py:24
  72.3 2.0 %collective-permute-start.12 = (f32[8,512]{1,0:T(8,128)S(1)}, f32[8,512]{1,0:T(8,128)S(1)}, u32[]{:S(2)}, u32[]{:S(2)}) collective-permute-start(f32[8,512]{1,0:T(8,128)S(1)} %add.3.refs_3_), channel_id=1, source_target_pairs={{2,0},{3,1},{0,2},{1,3},{6,4},{7,5},{4,6},{5,7},{10,8},{11,9},{8,1... | collective-permute-start | bytes 49160 | tf_op jit(solution)/shard_map/ppermute | solution.py:24
  74.2 2.7 %collective-permute-done.12.refs_4_ = f32[8,512]{1,0:T(8,128)S(1)} collective-permute-done((f32[8,512]{1,0:T(8,128)S(1)}, f32[8,512]{1,0:T(8,128)S(1)}, u32[]{:S(2)}, u32[]{:S(2)}) %collective-permute-start.12) | collective-permute-done | bytes 16416 | tf_op jit(solution)/shard_map/ppermute | solution.py:24
  76.9 1.0 %rescale.1 = f32[1,384,512]{2,1,0:T(8,128)} custom-call(f32[384,256]{1,0:T(8,128)S(1)} %get-tuple-element.38.refs_0_, f32[384,128]{1,0:T(8,128)S(1)} %get-tuple-element.47.refs_1_, f32[384,128]{1,0:T(8,128)S(1)} %get-tuple-element.55.refs_2_, f32[8,512]{1,0:T(8,128)S(1)} %add.3.refs_3_, f32[8,512]{1,0:T(8,128)S(1)} %collective-permute-done.12.refs_4_), custom_call_target="tpu_custom_call" | custom-call | bytes 1572864 | tf_op jit(solution)/shard_map/rescale/pallas_call | solution.py:32
  (15 shorter events, 0.2 us)
Async XLA Ops:
  6.4 21.4 %collective-permute-start = (s16[1040,256]{1,0:T(8,128)(2,1)}, s16[1040,256]{1,0:T(8,128)(2,1)S(1)}, u32[]{:S(2)}, u32[]{:S(2)}) collective-permute-start(s16[1040,256]{1,0:T(8,128)(2,1)} %ext_products_0.1), channel_id=1, source_target_pairs={{28,0},{8,4},{4,8},{16,12},{12,16},{24,20},{20,24},{0,28},{29,1},{... | collective-permute-start | bytes 1597448 | tf_op jit(solution)/shard_map/ppermute | solution.py:24
  18.5 9.3 %copy-start.1 = (f32[1536,256]{1,0:T(8,128)S(1)}, f32[1536,256]{1,0:T(8,128)}, u32[]{:S(2)}) copy-start(f32[1536,256]{1,0:T(8,128)} %get-tuple-element.32.own_ref) | copy-start | bytes 4718596
  18.5 9.3 %copy-start.2 = (s32[1,6,2]{1,2,0:T(2,128)S(1)}, s32[1,6,2]{1,2,0:T(2,128)}, u32[]{:S(2)}) copy-start(s32[1,6,2]{1,2,0:T(2,128)} %param.9) | copy-start | bytes 148
  18.5 9.3 %collective-permute-start.1 = (s16[1040,256]{1,0:T(8,128)(2,1)}, s16[1040,256]{1,0:T(8,128)(2,1)S(1)}, u32[]{:S(2)}, u32[]{:S(2)}) collective-permute-start(s16[1040,256]{1,0:T(8,128)(2,1)} %get-tuple-element.33), channel_id=1, source_target_pairs={{4,0},{0,4},{12,8},{8,12},{20,16},{16,20},{28,24},{24,28},{5,1},{1... | collective-permute-start | bytes 1597448 | tf_op jit(solution)/shard_map/ppermute | solution.py:24
  27.4 14.3 %collective-permute-start.5 = (s16[1040,256]{1,0:T(8,128)(2,1)}, s16[1040,256]{1,0:T(8,128)(2,1)S(1)}, u32[]{:S(2)}, u32[]{:S(2)}) collective-permute-start(s16[1040,256]{1,0:T(8,128)(2,1)} %get-tuple-element.42), channel_id=1, source_target_pairs={{4,0},{0,4},{12,8},{8,12},{20,16},{16,20},{28,24},{24,28},{5,1},{1... | collective-permute-start | bytes 1597448 | tf_op jit(solution)/shard_map/ppermute | solution.py:24
  29.3 18.3 %collective-permute-start.2 = (s16[784,256]{1,0:T(8,128)(2,1)S(1)}, s16[784,256]{1,0:T(8,128)(2,1)S(1)}, u32[]{:S(2)}, u32[]{:S(2)}) collective-permute-start(s16[784,256]{1,0:T(8,128)(2,1)S(1)} %get-tuple-element.35), channel_id=1, source_target_pairs={{1,0},{0,1},{3,2},{2,3},{5,4},{4,5},{7,6},{6,7},{9,8},{8,9},{11,10... | collective-permute-start | bytes 1204232 | tf_op jit(solution)/shard_map/ppermute | solution.py:24
  30.9 10.7 %collective-permute-start.4 = (s16[1040,128]{1,0:T(8,128)(2,1)}, s16[1040,128]{1,0:T(8,128)(2,1)S(1)}, u32[]{:S(2)}, u32[]{:S(2)}) collective-permute-start(s16[1040,128]{1,0:T(8,128)(2,1)} %get-tuple-element.41), channel_id=1, source_target_pairs={{28,0},{8,4},{4,8},{16,12},{12,16},{24,20},{20,24},{0,28},{29,1},{... | collective-permute-start | bytes 798728 | tf_op jit(solution)/shard_map/ppermute | solution.py:24
  31.4 14.7 %collective-permute-start.8 = (s16[1040,128]{1,0:T(8,128)(2,1)}, s16[1040,128]{1,0:T(8,128)(2,1)S(1)}, u32[]{:S(2)}, u32[]{:S(2)}) collective-permute-start(s16[1040,128]{1,0:T(8,128)(2,1)} %get-tuple-element.48), channel_id=1, source_target_pairs={{28,0},{8,4},{4,8},{16,12},{12,16},{24,20},{20,24},{0,28},{29,1},{... | collective-permute-start | bytes 798728 | tf_op jit(solution)/shard_map/ppermute | solution.py:24
  41.7 1.4 %copy-start = (f32[1536,256]{1,0:T(8,128)S(1)}, f32[1536,256]{1,0:T(8,128)}, u32[]{:S(2)}) copy-start(f32[1536,256]{1,0:T(8,128)} %own_products_1.1.own_ref) | copy-start | bytes 4718596
  44.1 11.7 %collective-permute-start.6 = (s16[784,128]{1,0:T(8,128)(2,1)S(1)}, s16[784,128]{1,0:T(8,128)(2,1)S(1)}, u32[]{:S(2)}, u32[]{:S(2)}) collective-permute-start(s16[784,128]{1,0:T(8,128)(2,1)S(1)} %get-tuple-element.44), channel_id=1, source_target_pairs={{1,0},{0,1},{3,2},{2,3},{5,4},{4,5},{7,6},{6,7},{9,8},{8,9},{11,10... | collective-permute-start | bytes 602120 | tf_op jit(solution)/shard_map/ppermute | solution.py:24
  47.1 12.7 %collective-permute-start.9 = (s16[784,128]{1,0:T(8,128)(2,1)S(1)}, s16[784,128]{1,0:T(8,128)(2,1)S(1)}, u32[]{:S(2)}, u32[]{:S(2)}) collective-permute-start(s16[784,128]{1,0:T(8,128)(2,1)S(1)} %get-tuple-element.50), channel_id=1, source_target_pairs={{1,0},{0,1},{3,2},{2,3},{5,4},{4,5},{7,6},{6,7},{9,8},{8,9},{11,10... | collective-permute-start | bytes 602120 | tf_op jit(solution)/shard_map/ppermute | solution.py:24
  48.0 19.2 %collective-permute-start.3 = (s16[400,256]{1,0:T(8,128)(2,1)S(1)}, s16[400,256]{1,0:T(8,128)(2,1)S(1)}, u32[]{:S(2)}, u32[]{:S(2)}) collective-permute-start(s16[400,256]{1,0:T(8,128)(2,1)S(1)} %get-tuple-element.37), channel_id=1, source_target_pairs={{2,0},{3,1},{0,2},{1,3},{6,4},{7,5},{4,6},{5,7},{10,8},{11,9},{8,1... | collective-permute-start | bytes 614408 | tf_op jit(solution)/shard_map/ppermute | solution.py:24
  56.0 11.2 %collective-permute-start.7 = (s16[400,128]{1,0:T(8,128)(2,1)S(1)}, s16[400,128]{1,0:T(8,128)(2,1)S(1)}, u32[]{:S(2)}, u32[]{:S(2)}) collective-permute-start(s16[400,128]{1,0:T(8,128)(2,1)S(1)} %get-tuple-element.46), channel_id=1, source_target_pairs={{2,0},{3,1},{0,2},{1,3},{6,4},{7,5},{4,6},{5,7},{10,8},{11,9},{8,1... | collective-permute-start | bytes 307208 | tf_op jit(solution)/shard_map/ppermute | solution.py:24
  60.0 8.4 %collective-permute-start.10 = (s16[400,128]{1,0:T(8,128)(2,1)S(1)}, s16[400,128]{1,0:T(8,128)(2,1)S(1)}, u32[]{:S(2)}, u32[]{:S(2)}) collective-permute-start(s16[400,128]{1,0:T(8,128)(2,1)S(1)} %get-tuple-element.52), channel_id=1, source_target_pairs={{2,0},{3,1},{0,2},{1,3},{6,4},{7,5},{4,6},{5,7},{10,8},{11,9},{8,1... | collective-permute-start | bytes 307208 | tf_op jit(solution)/shard_map/ppermute | solution.py:24
  68.5 3.8 %collective-permute-start.11 = (f32[8,512]{1,0:T(8,128)S(1)}, f32[8,512]{1,0:T(8,128)S(1)}, u32[]{:S(2)}, u32[]{:S(2)}) collective-permute-start(f32[8,512]{1,0:T(8,128)S(1)} %get-tuple-element.56), channel_id=1, source_target_pairs={{1,0},{0,1},{3,2},{2,3},{5,4},{4,5},{7,6},{6,7},{9,8},{8,9},{11,10... | collective-permute-start | bytes 49160 | tf_op jit(solution)/shard_map/ppermute | solution.py:24
  72.3 4.6 %collective-permute-start.12 = (f32[8,512]{1,0:T(8,128)S(1)}, f32[8,512]{1,0:T(8,128)S(1)}, u32[]{:S(2)}, u32[]{:S(2)}) collective-permute-start(f32[8,512]{1,0:T(8,128)S(1)} %add.3.refs_3_), channel_id=1, source_target_pairs={{2,0},{3,1},{0,2},{1,3},{6,4},{7,5},{4,6},{5,7},{10,8},{11,9},{8,1... | collective-permute-start | bytes 49160 | tf_op jit(solution)/shard_map/ppermute | solution.py:24

commit v2 on v1

--- a/solution.py
+++ b/solution.py
@@ -13,7 +13,8 @@
 STEPS = 256.0
 TOP = 65534.0
 LN2 = 0.6931471805599453
-VMEM_LIMIT = 57500000
+FIRST_LIMIT = 48000000
+PRODUCT_LIMIT = 48000000
 SMALL_LIMIT = 8 * 1024 * 1024
 IN_SMEM = pl.BlockSpec(memory_space=pltpu.SMEM)
 IN_VMEM = pl.BlockSpec(memory_space=pltpu.VMEM)
@@ -60,86 +61,119 @@
 
 
 def masked(values, pattern, column, first):
+    depth, width = values.shape
+    place = lax.broadcasted_iota(jnp.int32, (1, width), 1) // BS
     parts = []
-    for u in range(values.shape[0] // BS):
-        factor = jnp.full((1, values.shape[1]), pattern[column, 0, first + u].astype(jnp.float32))
+    for u in range(depth // BS):
+        factor = jnp.zeros((1, width), jnp.float32)
+        for v in range(width // BS):
+            factor = jnp.where(place == v, pattern[column + v, 0, first + u].astype(jnp.float32), factor)
         parts.append(values[u * BS : (u + 1) * BS] * factor.astype(values.dtype))
     return jnp.concatenate(parts, axis=0) if len(parts) > 1 else parts[0]
 
 
-def contract(left_side, right_side):
+def dot(left_side, right_side):
     return lax.dot_general(
-        left_side, right_side, (((0,), (0,)), ((), ())), preferred_element_type=jnp.float32
-    )
-
-
-def column_block(ref, block):
-    return ref.at[0, :, pl.ds(pl.multiple_of(block * BS, BS), BS)]
-
-
-def product_kernel(half, wanted, a_ref, b_ref, flow_ref, graph_ref, *rest):
-    outs, (flow_buf, graph_buf, sems) = rest[:-3], rest[-3:]
-    outs = iter(outs)
-    count, inner = flow_buf.shape[:2]
+        left_side, right_side, (((1,), (0,)), ((), ())), preferred_element_type=jnp.float32
+    )
+
+
+def blocks(ref, start, count):
+    return ref.at[0, :, pl.ds(pl.multiple_of(start * BS, BS), count * BS)]
+
+
+def product_kernel(half, wanted, depth, known, a_ref, b_ref, flow_ref, graph_ref, *rest):
+    refs = list(rest)
+    held = {name: refs.pop(0) for name in known}
+    inner = flow_ref.shape[1]
     panel = flow_ref.shape[2] // BS // 3
     odd = lax.rem(lax.axis_index("blk"), 2)
     first = lax.axis_index("layer") * (inner // BS)
     ext_side, int_side = odd * (2 * panel), (1 - odd) * (2 * panel)
     columns = {"ext": ext_side + half, "own": panel + half, "int": int_side + half}
     starts = {"ext": odd * panel, "own": 0, "int": (1 - odd) * panel}
-    users = [(panel, ("ext", "own", "int")), (ext_side, ("ext", "own")), (int_side, ("own", "int"))]
     parts = [part for part in ("ext", "own", "int") if part in wanted]
-    refs = {part: [next(outs) for _ in wanted[part]] for part in parts}
-    blocks = []
-    for side, names in users:
-        used = [part for part in parts if part in names]
-        blocks += [(side + i, used) for i in range(panel) if used]
+    outs = {part: [refs.pop(0) for _ in wanted[part]] for part in parts}
+    makes = None
+    if len(known) < 2:
+        makes = ("ext", "int")[len(known)]
+        held[makes] = refs.pop(0)
+        flow_buf = refs.pop(0)
+    graph_buf, sems = refs
+    turned_start = {"ext": odd * panel, "int": int_side}
 
     graph_copies = [
-        pltpu.make_async_copy(column_block(graph_ref, columns[part]), graph_buf.at[j], sems.at[count + j])
+        pltpu.make_async_copy(blocks(graph_ref, columns[part], 1), graph_buf.at[j], sems.at[j])
         for j, part in enumerate(parts)
     ]
-    flow_copies = [
-        pltpu.make_async_copy(column_block(flow_ref, block), flow_buf.at[i], sems.at[i])
-        for i, (block, _) in enumerate(blocks)
-    ]
+    flow_copies = []
+    if makes:
+        source = blocks(flow_ref, turned_start[makes], held[makes].shape[0] // BS)
+        for t in range(inner // depth):
+            rows = slice(t * depth, (t + 1) * depth)
+            flow_copies.append(
+                pltpu.make_async_copy(source.at[rows], flow_buf.at[rows], sems.at[len(parts) + t])
+            )
     for copy in graph_copies + flow_copies:
         copy.start()
+
     sides = []
     for j, part in enumerate(parts):
         graph_copies[j].wait()
         sides.append(masked(graph_buf[j], b_ref, columns[part], first))
     sides = jnp.concatenate(sides, axis=1) if len(sides) > 1 else sides[0]
 
-    heads = {part: [jnp.zeros((HEAD, ref.shape[1]), jnp.float32) for ref in refs[part]] for part in parts}
-    for i, (block, used) in enumerate(blocks):
-        flow_copies[i].wait()
+    def turn():
+        for t, copy in enumerate(flow_copies):
+            rows = slice(t * depth, (t + 1) * depth)
+            copy.wait()
+            chunk = masked(flow_buf[rows, :], a_ref, turned_start[makes], first + t * (depth // BS))
+            held[makes][:, rows] = chunk.T
+
+    heads = {part: [jnp.zeros((HEAD, ref.shape[1]), jnp.float32) for ref in outs[part]] for part in parts}
+
+    def multiply(side, names):
+        used = [part for part in parts if part in names]
+        if not used:
+            return
         low = parts.index(used[0]) * BS
-        product = contract(masked(flow_buf[i], a_ref, block, first), sides[:, low : low + len(used) * BS])
-        for j, part in enumerate(used):
-            place = block - starts[part]
-            column = j * BS
-            for c, ref in enumerate(refs[part]):
-                chunk = product[:, column : column + ref.shape[1]]
-                column += ref.shape[1]
-                if part == "own":
-                    ref[pl.ds(pl.multiple_of(place * BS, BS), BS), :] = chunk
-                else:
-                    power = powers(chunk)
-                    ref[pl.ds(pl.multiple_of(HEAD + place * BS, HEAD), BS), :] = code(chunk, power)
-                    line = lax.broadcasted_iota(jnp.int32, heads[part][c].shape, 0)
-                    heads[part][c] = jnp.where(line == place, power, heads[part][c])
+        for i in range(panel):
+            block = side + i
+            source = "int" if side is int_side else "ext"
+            at = pl.ds(pl.multiple_of((block - turned_start[source]) * BS, BS), BS)
+            product = dot(held[source][at, :], sides[:, low : low + len(used) * BS])
+            for j, part in enumerate(used):
+                place = block - starts[part]
+                column = j * BS
+                for c, ref in enumerate(outs[part]):
+                    chunk = product[:, column : column + ref.shape[1]]
+                    column += ref.shape[1]
+                    if part == "own":
+                        ref[pl.ds(pl.multiple_of(place * BS, BS), BS), :] = chunk
+                    else:
+                        power = powers(chunk)
+                        ref[pl.ds(pl.multiple_of(HEAD + place * BS, HEAD), BS), :] = code(chunk, power)
+                        line = lax.broadcasted_iota(jnp.int32, heads[part][c].shape, 0)
+                        heads[part][c] = jnp.where(line == place, power, heads[part][c])
+
+    if makes == "ext":
+        turn()
+    multiply(panel, ("ext", "own", "int"))
+    multiply(ext_side, ("ext", "own"))
+    if makes == "int":
+        turn()
+    multiply(int_side, ("own", "int"))
     for part in parts:
-        for ref, head in zip(refs[part], heads[part]):
+        for ref, head in zip(outs[part], heads[part]):
             if part != "own":
                 ref[0:HEAD, :] = head.astype(jnp.int32).astype(jnp.int16)
 
 
-def products(flow_t, graph, a_lines, b_lines, half, wanted):
+def products(flow_t, graph, a_lines, b_lines, half, wanted, turned, limit):
     inner, width = flow_t.shape[1:]
     panel = width // 3
-    rows = width if "own" in wanted or len(wanted) > 1 else 2 * panel
-    count = rows // BS
+    depth = min(512, inner)
+    known = tuple(turned)
     outs = []
     for part in ("ext", "own", "int"):
         for w in wanted.get(part, ()):
@@ -147,21 +181,29 @@
                 outs.append(jax.ShapeDtypeStruct((width, w), jnp.float32))
             else:
                 outs.append(jax.ShapeDtypeStruct((HEAD + 2 * panel, w), jnp.int16))
-    return call(
-        functools.partial(product_kernel, half, wanted),
+    scratch = []
+    if len(known) < 2:
+        rows = (2 * panel, panel)[len(known)]
+        outs.append(jax.ShapeDtypeStruct((rows, inner), flow_t.dtype))
+        scratch.append(pltpu.VMEM((inner, rows), flow_t.dtype))
+    results = list(call(
+        functools.partial(product_kernel, half, wanted, depth, known),
         "_".join(wanted) + f"_products_{half}",
-        (a_lines, b_lines, flow_t, graph),
-        [IN_SMEM, IN_SMEM, IN_HBM, IN_HBM],
+        (a_lines, b_lines, flow_t, graph, *turned.values()),
+        [IN_SMEM, IN_SMEM, IN_HBM, IN_HBM] + [IN_VMEM] * len(known),
         outs,
-        [
-            pltpu.VMEM((count, inner, BS), flow_t.dtype),
+        scratch
+        + [
             pltpu.VMEM((len(wanted), inner, BS), graph.dtype),
-            pltpu.SemaphoreType.DMA((count + len(wanted),)),
+            pltpu.SemaphoreType.DMA((len(wanted) + inner // depth,)),
         ],
         flops=2 * inner * BS * sum(width if part == "own" else 2 * panel for part in wanted),
-        moved=2 * inner * (rows + len(wanted) * BS),
-        limit=VMEM_LIMIT,
-    )
+        moved=2 * inner * (width + len(wanted) * BS),
+        limit=limit,
+    ))
+    if len(known) < 2:
+        turned[("ext", "int")[len(known)]] = results.pop()
+    return results
 
 
 def split_strips(total, rows, position, keep_ref, send_ref):
@@ -261,9 +303,10 @@
     )
 
 
-def rescale_kernel(height, *refs):
-    squares, (mine_ref, other_ref, out_ref) = refs[:-3], refs[-3:]
-    divisor = (mine_ref[0:1, :] + other_ref[0:1, :]) / height + 1e-6
+def rescale_kernel(height, count, *refs):
+    squares, sums, out_ref = refs[:count], refs[count:-1], refs[-1]
+    total = functools.reduce(jnp.add, [ref[0:1, :] for ref in sums])
+    divisor = total / height + 1e-6
     column = 0
     for ref in squares:
         columns = slice(column, column + ref.shape[1])
@@ -271,14 +314,14 @@
         out_ref[0, :, columns] = ref[...] / divisor[:, columns]
 
 
-def rescale(squares, mine, other, height):
+def rescale(squares, sums, height):
     rows = squares[0].shape[0]
-    width = mine.shape[1]
+    width = sums[0].shape[1]
     return call(
-        functools.partial(rescale_kernel, float(height)),
+        functools.partial(rescale_kernel, float(height), len(squares)),
         "rescale",
-        (*squares, mine, other),
-        [IN_VMEM] * (len(squares) + 2),
+        (*squares, *sums),
+        [IN_VMEM] * (len(squares) + len(sums)),
         jax.ShapeDtypeStruct((1, rows, width), jnp.float32),
         moved=8 * rows * width,
     )
@@ -321,19 +364,23 @@
 
     halves = panel // BS
     fine = (LANES,) * (BS // LANES)
-    (ext_part,) = products(flow_t, graph, a_lines, b_lines, 0, {"ext": (BS,)})
+    turned = {}
+    (ext_part,) = products(flow_t, graph, a_lines, b_lines, 0, {"ext": (BS,)}, turned, FIRST_LIMIT)
     got_ext = swap(ext_part, "blk", other_chip)
-    own, int_part = products(flow_t, graph, after(a_lines, ext_part), b_lines, 0, {"own": (BS,), "int": (BS,)})
+    wanted = {"own": (BS,), "int": (BS,)}
+    own, int_part = products(flow_t, graph, a_lines, b_lines, 0, wanted, turned, PRODUCT_LIMIT)
     got_int = swap(int_part, "blk", same_chip)
     a_next = after(a_lines, int_part)
     for half in range(1, halves):
         widths = fine if half == halves - 1 else (BS,)
-        *ext_parts, int_part = products(flow_t, graph, a_next, b_lines, half, {"ext": widths, "int": (BS,)})
+        wanted = {"ext": widths, "int": (BS,)}
+        *ext_parts, int_part = products(flow_t, graph, a_next, b_lines, half, wanted, turned, PRODUCT_LIMIT)
         next_ext = [swap(part, "blk", other_chip) for part in ext_parts]
         next_int = swap(int_part, "blk", same_chip)
         got_ext = got_ext if half > 1 else [got_ext]
         sent = join_all(own, got_ext, got_int, half - 1)
-        (own,) = products(flow_t, graph, after(a_lines, sent[-1]), b_lines, half, {"own": (BS,)})
+        wanted = {"own": (BS,)}
+        (own,) = products(flow_t, graph, after(a_lines, sent[-1]), b_lines, half, wanted, turned, PRODUCT_LIMIT)
         a_next = after(a_lines, own)
         got_ext, got_int = next_ext, next_int
     join_all(own, got_ext, got_int, halves - 1)
@@ -345,12 +392,9 @@
         squares.append(squared)
         sums.append(summed)
 
-    total = sums[-1]
-    position = 1
-    while 2 * position < layers:
-        total = total + swap(total, "layer", lambda i: i ^ position)
-        position *= 2
-    return rescale(squares, total, swap(total, "layer", lambda i: i ^ position), width)
+    mine = sums[-1]
+    others = [swap(mine, "layer", lambda i: i ^ other) for other in range(1, layers)]
+    return rescale(squares, [mine, *others], width)
 
 
 def solution(mesh):

time: 78.4 us -> 70.3 us (0.90)
  Pallas kernels: 37.3 us -> 25.4 us
  starting transfers between devices: 14.7 us -> 17.6 us
  waiting for transfers between devices: 24.3 us -> 25.4 us
    pallas_call x14, Pallas kernels: 37.3 us -> 25.4 us  [call(): pl.pallas_call(kernel, out_shape=out_shape, in_specs=in_specs, out_specs=...]
    ppermute x13 -> x14, starting transfers between devices: 14.7 us -> 17.6 us  [swap(): lax.ppermute(block, axis, [(partner(i), i) for i in range(lax.axis_size(a...]
    ppermute x13 -> x14, waiting for transfers between devices: 24.3 us -> 25.4 us  [swap(): lax.ppermute(block, axis, [(partner(i), i) for i in range(lax.axis_size(a...]
  transfers between devices with their start and end apart: 13 -> 14, of which waited for: 7 -> 8; matrix products, arithmetic and copies ran while one was open for 0% -> 0% of each run, Pallas kernels for 38% -> 28%
where the time goes in v2:
time: 70.3 us; the launch traced here: 69.9 us
  Pallas kernels  25.4 us (36%)
  waiting for transfers between devices  25.4 us (36%)
  starting transfers between devices  17.6 us (25%)
  local copies, waits for them, and re-layouts  1.37 us (2%)
    pallas_call x14, Pallas kernels, call(): pl.pallas_call(kernel, out_shape=out_shape, in_specs=in_specs, out_specs=...  25.4 us
    ppermute x14, waiting for transfers between devices, swap(): lax.ppermute(block, axis, [(partner(i), i) for i in range(lax.axis_size(a...  25.4 us
    ppermute x14, starting transfers between devices, swap(): lax.ppermute(block, axis, [(partner(i), i) for i in range(lax.axis_size(a...  17.6 us
  transfers between devices with their start and end apart: 14, of which 8 were waited for; matrix products, arithmetic and copies ran while one was open for 0% of the time, Pallas kernels for 28%

profile of v2, /device:TPU:0, one launch (start us, length us, event | category | flops | bytes accessed | tf_op | source)
XLA Modules:
  0.0 69.9 jit_solution(3398121703911848164)
XLA Ops:
  0.0 0.7 copy-done
  0.7 0.7 copy-done.1
  1.4 5.0 %ext_products_0.1 = (s16[1040,256]{1,0:T(8,128)(2,1)S(1)}, bf16[1024,2048]{1,0:T(8,128)(2,1)S(1)}) custom-call(s32[6,1,32]{2,1,0:T(1,128)S(1)} %bitcast.3, s32[6,1,32]{2,1,0:T(1,128)S(1)} %bitcast.7, bf16[1,2048,1536]{2,1,0:T(8,128)(2,1)} %flow_ref.7, bf16[1,2048,1536]{2,1,0:T(8,128)(2,1)} %graph_ref.7), custom_call_target="tpu_custom_call" | custom-call | flops 1073741824 | bytes 7340032 | tf_op jit(solution)/shard_map/ext_products_0/pallas_call | solution.py:33
  6.4 3.4 %collective-permute-start = (s16[1040,256]{1,0:T(8,128)(2,1)S(1)}, s16[1040,256]{1,0:T(8,128)(2,1)S(1)}, u32[]{:S(2)}, u32[]{:S(2)}) collective-permute-start(s16[1040,256]{1,0:T(8,128)(2,1)S(1)} %get-tuple-element.35), channel_id=1, source_target_pairs={{28,0},{8,4},{4,8},{16,12},{12,16},{24,20},{20,24},{0,28},{29,1},{... | collective-permute-start | bytes 1597448 | tf_op jit(solution)/shard_map/ppermute | solution.py:25
  9.8 6.1 %own_int_products_0.1 = (f32[1536,256]{1,0:T(8,128)S(1)}, s16[1040,256]{1,0:T(8,128)(2,1)S(1)}, bf16[512,2048]{1,0:T(8,128)(2,1)S(1)}) custom-call(s32[6,1,32]{2,1,0:T(1,128)S(1)} %bitcast.4, s32[6,1,32]{2,1,0:T(1,128)S(1)} %bitcast.8, bf16[1,2048,1536]{2,1,0:T(8,128)(2,1)} %flow_ref.7, bf16[1,2048,1536]{2,1,0:T(8,128)(2,1)} %graph_ref.7, ...), custom_call_target="tpu_custom_call" | custom-call | flops 2684354560 | bytes 8388608 | tf_op jit(solution)/shard_map/own_int_products_0/pallas_call | solution.py:33
  16.0 5.2 %ext_int_products_1.1 = (s16[1040,128]{1,0:T(8,128)(2,1)S(1)}, s16[1040,128]{1,0:T(8,128)(2,1)S(1)}, s16[1040,256]{1,0:T(8,128)(2,1)S(1)}) custom-call(s32[6,1,32]{2,1,0:T(1,128)S(1)} %bitcast.5, s32[6,1,32]{2,1,0:T(1,128)S(1)} %bitcast.9, bf16[1,2048,1536]{2,1,0:T(8,128)(2,1)} %flow_ref.7, bf16[1,2048,1536]{2,1,0:T(8,128)(2,1)} %graph_ref.7, ...), custom_call_target="tpu_custom_call" | custom-call | flops 2147483648 | bytes 8388608 | tf_op jit(solution)/shard_map/ext_int_products_1/pallas_call | solution.py:33
  21.2 0.5 collective-permute-start.5
  21.7 1.5 %join_0_0.1 = (f32[2,384,256]{2,1,0:T(8,128)S(1)}, s16[784,256]{1,0:T(8,128)(2,1)S(1)}) custom-call(s32[1,2,6]{2,1,0:T(2,128)S(1)} %bitcast.11, f32[1536,256]{1,0:T(8,128)S(1)} %get-tuple-element.34.own_ref, s16[1040,256]{1,0:T(8,128)(2,1)S(1)} %collective-permute-done.ext_ref, s16[1040,256]{1,0:T(8,128)(2,1)S(1)} %collective-permute-done.1.int_ref), custom_call_target="tpu_custom_call" | custom-call | bytes 3145728 | tf_op jit(solution)/shard_map/join_0_0/pallas_call | solution.py:33
  23.2 3.1 %collective-permute-start.2 = (s16[784,256]{1,0:T(8,128)(2,1)S(1)}, s16[784,256]{1,0:T(8,128)(2,1)S(1)}, u32[]{:S(2)}, u32[]{:S(2)}) collective-permute-start(s16[784,256]{1,0:T(8,128)(2,1)S(1)} %get-tuple-element.38), channel_id=1, source_target_pairs={{1,0},{0,1},{3,2},{2,3},{5,4},{4,5},{7,6},{6,7},{9,8},{8,9},{11,10... | collective-permute-start | bytes 1204232 | tf_op jit(solution)/shard_map/ppermute | solution.py:25
  26.2 0.7 %collective-permute-start.4 = (s16[1040,128]{1,0:T(8,128)(2,1)S(1)}, s16[1040,128]{1,0:T(8,128)(2,1)S(1)}, u32[]{:S(2)}, u32[]{:S(2)}) collective-permute-start(s16[1040,128]{1,0:T(8,128)(2,1)S(1)} %get-tuple-element.45), channel_id=1, source_target_pairs={{28,0},{8,4},{4,8},{16,12},{12,16},{24,20},{20,24},{0,28},{29,1},{... | collective-permute-start | bytes 798728 | tf_op jit(solution)/shard_map/ppermute | solution.py:25
  27.0 1.9 %collective-permute-start.8 = (s16[1040,128]{1,0:T(8,128)(2,1)S(1)}, s16[1040,128]{1,0:T(8,128)(2,1)S(1)}, u32[]{:S(2)}, u32[]{:S(2)}) collective-permute-start(s16[1040,128]{1,0:T(8,128)(2,1)S(1)} %get-tuple-element.52), channel_id=1, source_target_pairs={{28,0},{8,4},{4,8},{16,12},{12,16},{24,20},{20,24},{0,28},{29,1},{... | collective-permute-start | bytes 798728 | tf_op jit(solution)/shard_map/ppermute | solution.py:25
  28.9 3.7 %own_products_1.1.own_ref = f32[1536,256]{1,0:T(8,128)S(1)} custom-call(s32[6,1,32]{2,1,0:T(1,128)S(1)} %bitcast.6, s32[6,1,32]{2,1,0:T(1,128)S(1)} %bitcast.10, bf16[1,2048,1536]{2,1,0:T(8,128)(2,1)} %flow_ref.7, bf16[1,2048,1536]{2,1,0:T(8,128)(2,1)} %graph_ref.7, bf16[1024,2048]{1,0:T(8,128)(2,1)S(1)} %get-tuple-element.33.rest_0_, ...), custom_call_target="tpu_custom_call" | custom-call | flops 1610612736 | bytes 7340032 | tf_op jit(solution)/shard_map/own_products_1/pallas_call | solution.py:33
  32.6 3.2 %collective-permute-done.4.ext_ref = s16[1040,128]{1,0:T(8,128)(2,1)S(1)} collective-permute-done((s16[1040,128]{1,0:T(8,128)(2,1)S(1)}, s16[1040,128]{1,0:T(8,128)(2,1)S(1)}, u32[]{:S(2)}, u32[]{:S(2)}) %collective-permute-start.4) | collective-permute-done | bytes 266272 | tf_op jit(solution)/shard_map/ppermute | solution.py:25
  35.8 1.0 %join_1_0.1 = (f32[2,384,128]{2,1,0:T(8,128)S(1)}, s16[784,128]{1,0:T(8,128)(2,1)S(1)}) custom-call(s32[1,2,6]{2,1,0:T(2,128)S(1)} %bitcast.12, f32[1536,256]{1,0:T(8,128)S(1)} %own_products_1.1.own_ref, s16[1040,128]{1,0:T(8,128)(2,1)S(1)} %collective-permute-done.4.ext_ref, s16[1040,256]{1,0:T(8,128)(2,1)S(1)} %collective-permute-done.5.int_ref), custom_call_target="tpu_custom_call" | custom-call | bytes 1572864 | tf_op jit(solution)/shard_map/join_1_0/pallas_call | solution.py:33
  36.9 3.9 %collective-permute-done.8.ext_ref = s16[1040,128]{1,0:T(8,128)(2,1)S(1)} collective-permute-done((s16[1040,128]{1,0:T(8,128)(2,1)S(1)}, s16[1040,128]{1,0:T(8,128)(2,1)S(1)}, u32[]{:S(2)}, u32[]{:S(2)}) %collective-permute-start.8) | collective-permute-done | bytes 266272 | tf_op jit(solution)/shard_map/ppermute | solution.py:25
  40.8 1.0 %join_1_128.1 = (f32[2,384,128]{2,1,0:T(8,128)S(1)}, s16[784,128]{1,0:T(8,128)(2,1)S(1)}) custom-call(s32[1,2,6]{2,1,0:T(2,128)S(1)} %bitcast.13, f32[1536,256]{1,0:T(8,128)S(1)} %own_products_1.1.own_ref, s16[1040,128]{1,0:T(8,128)(2,1)S(1)} %collective-permute-done.8.ext_ref, s16[1040,256]{1,0:T(8,128)(2,1)S(1)} %collective-permute-done.5.int_ref), custom_call_target="tpu_custom_call" | custom-call | bytes 1572864 | tf_op jit(solution)/shard_map/join_1_128/pallas_call | solution.py:33
  41.8 0.5 collective-permute-start.9
  42.3 0.4 halve_2_0.1
  42.7 2.7 %collective-permute-start.3 = (s16[400,256]{1,0:T(8,128)(2,1)S(1)}, s16[400,256]{1,0:T(8,128)(2,1)S(1)}, u32[]{:S(2)}, u32[]{:S(2)}) collective-permute-start(s16[400,256]{1,0:T(8,128)(2,1)S(1)} %get-tuple-element.40), channel_id=1, source_target_pairs={{2,0},{3,1},{0,2},{1,3},{6,4},{7,5},{4,6},{5,7},{10,8},{11,9},{8,1... | collective-permute-start | bytes 614408 | tf_op jit(solution)/shard_map/ppermute | solution.py:25
  45.4 1.8 %collective-permute-done.6.got_ref = s16[784,128]{1,0:T(8,128)(2,1)S(1)} collective-permute-done((s16[784,128]{1,0:T(8,128)(2,1)S(1)}, s16[784,128]{1,0:T(8,128)(2,1)S(1)}, u32[]{:S(2)}, u32[]{:S(2)}) %collective-permute-start.6) | collective-permute-done | bytes 200736 | tf_op jit(solution)/shard_map/ppermute | solution.py:25
  47.2 0.2 halve_2_1.1
  47.5 4.8 %collective-permute-done.9.got_ref = s16[784,128]{1,0:T(8,128)(2,1)S(1)} collective-permute-done((s16[784,128]{1,0:T(8,128)(2,1)S(1)}, s16[784,128]{1,0:T(8,128)(2,1)S(1)}, u32[]{:S(2)}, u32[]{:S(2)}) %collective-permute-start.9) | collective-permute-done | bytes 200736 | tf_op jit(solution)/shard_map/ppermute | solution.py:25
  52.3 0.2 halve_2_2.1
  52.5 0.1 collective-permute-start.10
  52.6 7.3 %collective-permute-done.7.got_ref = s16[400,128]{1,0:T(8,128)(2,1)S(1)} collective-permute-done((s16[400,128]{1,0:T(8,128)(2,1)S(1)}, s16[400,128]{1,0:T(8,128)(2,1)S(1)}, u32[]{:S(2)}, u32[]{:S(2)}) %collective-permute-start.7) | collective-permute-done | bytes 102432 | tf_op jit(solution)/shard_map/ppermute | solution.py:25
  60.0 0.1 square_0.1
  60.1 0.9 %collective-permute-done.10.got_ref = s16[400,128]{1,0:T(8,128)(2,1)S(1)} collective-permute-done((s16[400,128]{1,0:T(8,128)(2,1)S(1)}, s16[400,128]{1,0:T(8,128)(2,1)S(1)}, u32[]{:S(2)}, u32[]{:S(2)}) %collective-permute-start.10) | collective-permute-done | bytes 102432 | tf_op jit(solution)/shard_map/ppermute | solution.py:25
  61.1 3.2 %collective-permute-start.13 = (f32[8,512]{1,0:T(8,128)S(1)}, f32[8,512]{1,0:T(8,128)S(1)}, u32[]{:S(2)}, u32[]{:S(2)}) collective-permute-start(f32[8,512]{1,0:T(8,128)S(1)} %get-tuple-element.60.refs_3_), channel_id=1, source_target_pairs={{3,0},{2,1},{1,2},{0,3},{7,4},{6,5},{5,6},{4,7},{11,8},{10,9},{9,1... | collective-permute-start | bytes 49160 | tf_op jit(solution)/shard_map/ppermute | solution.py:25
  64.3 1.2 %collective-permute-start.11 = (f32[8,512]{1,0:T(8,128)S(1)}, f32[8,512]{1,0:T(8,128)S(1)}, u32[]{:S(2)}, u32[]{:S(2)}) collective-permute-start(f32[8,512]{1,0:T(8,128)S(1)} %get-tuple-element.60.refs_3_), channel_id=1, source_target_pairs={{1,0},{0,1},{3,2},{2,3},{5,4},{4,5},{7,6},{6,7},{9,8},{8,9},{11,10... | collective-permute-start | bytes 49160 | tf_op jit(solution)/shard_map/ppermute | solution.py:25
  65.5 1.1 %collective-permute-done.13.refs_6_ = f32[8,512]{1,0:T(8,128)S(1)} collective-permute-done((f32[8,512]{1,0:T(8,128)S(1)}, f32[8,512]{1,0:T(8,128)S(1)}, u32[]{:S(2)}, u32[]{:S(2)}) %collective-permute-start.13) | collective-permute-done | bytes 16416 | tf_op jit(solution)/shard_map/ppermute | solution.py:25
  66.7 2.2 %collective-permute-done.12.refs_5_ = f32[8,512]{1,0:T(8,128)S(1)} collective-permute-done((f32[8,512]{1,0:T(8,128)S(1)}, f32[8,512]{1,0:T(8,128)S(1)}, u32[]{:S(2)}, u32[]{:S(2)}) %collective-permute-start.12) | collective-permute-done | bytes 16416 | tf_op jit(solution)/shard_map/ppermute | solution.py:25
  68.9 1.0 %rescale.1 = f32[1,384,512]{2,1,0:T(8,128)} custom-call(f32[384,256]{1,0:T(8,128)S(1)} %get-tuple-element.41.refs_0_, f32[384,128]{1,0:T(8,128)S(1)} %get-tuple-element.51.refs_1_, f32[384,128]{1,0:T(8,128)S(1)} %get-tuple-element.59.refs_2_, f32[8,512]{1,0:T(8,128)S(1)} %get-tuple-element.60.refs_3_, f32[8,512]{1,0:T(8,128)S(1)} %collective-permute-done.11.refs_4_, ...), custom_call_target="tpu_custom_call" | custom-call | bytes 1572864 | tf_op jit(solution)/shard_map/rescale/pallas_call | solution.py:33
  (16 shorter events, 0.4 us)
Async XLA Ops:
  0.0 0.7 copy-start
  0.7 0.7 copy-start.1
  6.4 15.3 %collective-permute-start = (s16[1040,256]{1,0:T(8,128)(2,1)S(1)}, s16[1040,256]{1,0:T(8,128)(2,1)S(1)}, u32[]{:S(2)}, u32[]{:S(2)}) collective-permute-start(s16[1040,256]{1,0:T(8,128)(2,1)S(1)} %get-tuple-element.35), channel_id=1, source_target_pairs={{28,0},{8,4},{4,8},{16,12},{12,16},{24,20},{20,24},{0,28},{29,1},{... | collective-permute-start | bytes 1597448 | tf_op jit(solution)/shard_map/ppermute | solution.py:25
  15.9 5.8 %collective-permute-start.1 = (s16[1040,256]{1,0:T(8,128)(2,1)S(1)}, s16[1040,256]{1,0:T(8,128)(2,1)S(1)}, u32[]{:S(2)}, u32[]{:S(2)}) collective-permute-start(s16[1040,256]{1,0:T(8,128)(2,1)S(1)} %get-tuple-element.36), channel_id=1, source_target_pairs={{4,0},{0,4},{12,8},{8,12},{20,16},{16,20},{28,24},{24,28},{5,1},{1... | collective-permute-start | bytes 1597448 | tf_op jit(solution)/shard_map/ppermute | solution.py:25
  16.0 5.7 %copy-start.2 = (s32[1,6,2]{1,2,0:T(2,128)S(1)}, s32[1,6,2]{1,2,0:T(2,128)}, u32[]{:S(2)}) copy-start(s32[1,6,2]{1,2,0:T(2,128)} %param.9) | copy-start | bytes 148
  21.2 14.6 %collective-permute-start.5 = (s16[1040,256]{1,0:T(8,128)(2,1)S(1)}, s16[1040,256]{1,0:T(8,128)(2,1)S(1)}, u32[]{:S(2)}, u32[]{:S(2)}) collective-permute-start(s16[1040,256]{1,0:T(8,128)(2,1)S(1)} %get-tuple-element.46), channel_id=1, source_target_pairs={{4,0},{0,4},{12,8},{8,12},{20,16},{16,20},{28,24},{24,28},{5,1},{1... | collective-permute-start | bytes 1597448 | tf_op jit(solution)/shard_map/ppermute | solution.py:25
  23.2 19.1 %collective-permute-start.2 = (s16[784,256]{1,0:T(8,128)(2,1)S(1)}, s16[784,256]{1,0:T(8,128)(2,1)S(1)}, u32[]{:S(2)}, u32[]{:S(2)}) collective-permute-start(s16[784,256]{1,0:T(8,128)(2,1)S(1)} %get-tuple-element.38), channel_id=1, source_target_pairs={{1,0},{0,1},{3,2},{2,3},{5,4},{4,5},{7,6},{6,7},{9,8},{8,9},{11,10... | collective-permute-start | bytes 1204232 | tf_op jit(solution)/shard_map/ppermute | solution.py:25
  26.2 9.5 %collective-permute-start.4 = (s16[1040,128]{1,0:T(8,128)(2,1)S(1)}, s16[1040,128]{1,0:T(8,128)(2,1)S(1)}, u32[]{:S(2)}, u32[]{:S(2)}) collective-permute-start(s16[1040,128]{1,0:T(8,128)(2,1)S(1)} %get-tuple-element.45), channel_id=1, source_target_pairs={{28,0},{8,4},{4,8},{16,12},{12,16},{24,20},{20,24},{0,28},{29,1},{... | collective-permute-start | bytes 798728 | tf_op jit(solution)/shard_map/ppermute | solution.py:25
  27.0 13.8 %collective-permute-start.8 = (s16[1040,128]{1,0:T(8,128)(2,1)S(1)}, s16[1040,128]{1,0:T(8,128)(2,1)S(1)}, u32[]{:S(2)}, u32[]{:S(2)}) collective-permute-start(s16[1040,128]{1,0:T(8,128)(2,1)S(1)} %get-tuple-element.52), channel_id=1, source_target_pairs={{28,0},{8,4},{4,8},{16,12},{12,16},{24,20},{20,24},{0,28},{29,1},{... | collective-permute-start | bytes 798728 | tf_op jit(solution)/shard_map/ppermute | solution.py:25
  36.8 10.4 %collective-permute-start.6 = (s16[784,128]{1,0:T(8,128)(2,1)S(1)}, s16[784,128]{1,0:T(8,128)(2,1)S(1)}, u32[]{:S(2)}, u32[]{:S(2)}) collective-permute-start(s16[784,128]{1,0:T(8,128)(2,1)S(1)} %get-tuple-element.48), channel_id=1, source_target_pairs={{1,0},{0,1},{3,2},{2,3},{5,4},{4,5},{7,6},{6,7},{9,8},{8,9},{11,10... | collective-permute-start | bytes 602120 | tf_op jit(solution)/shard_map/ppermute | solution.py:25
  41.8 10.5 %collective-permute-start.9 = (s16[784,128]{1,0:T(8,128)(2,1)S(1)}, s16[784,128]{1,0:T(8,128)(2,1)S(1)}, u32[]{:S(2)}, u32[]{:S(2)}) collective-permute-start(s16[784,128]{1,0:T(8,128)(2,1)S(1)} %get-tuple-element.54), channel_id=1, source_target_pairs={{1,0},{0,1},{3,2},{2,3},{5,4},{4,5},{7,6},{6,7},{9,8},{8,9},{11,10... | collective-permute-start | bytes 602120 | tf_op jit(solution)/shard_map/ppermute | solution.py:25
  42.7 17.2 %collective-permute-start.3 = (s16[400,256]{1,0:T(8,128)(2,1)S(1)}, s16[400,256]{1,0:T(8,128)(2,1)S(1)}, u32[]{:S(2)}, u32[]{:S(2)}) collective-permute-start(s16[400,256]{1,0:T(8,128)(2,1)S(1)} %get-tuple-element.40), channel_id=1, source_target_pairs={{2,0},{3,1},{0,2},{1,3},{6,4},{7,5},{4,6},{5,7},{10,8},{11,9},{8,1... | collective-permute-start | bytes 614408 | tf_op jit(solution)/shard_map/ppermute | solution.py:25
  47.4 12.5 %collective-permute-start.7 = (s16[400,128]{1,0:T(8,128)(2,1)S(1)}, s16[400,128]{1,0:T(8,128)(2,1)S(1)}, u32[]{:S(2)}, u32[]{:S(2)}) collective-permute-start(s16[400,128]{1,0:T(8,128)(2,1)S(1)} %get-tuple-element.50), channel_id=1, source_target_pairs={{2,0},{3,1},{0,2},{1,3},{6,4},{7,5},{4,6},{5,7},{10,8},{11,9},{8,1... | collective-permute-start | bytes 307208 | tf_op jit(solution)/shard_map/ppermute | solution.py:25
  52.5 8.5 %collective-permute-start.10 = (s16[400,128]{1,0:T(8,128)(2,1)S(1)}, s16[400,128]{1,0:T(8,128)(2,1)S(1)}, u32[]{:S(2)}, u32[]{:S(2)}) collective-permute-start(s16[400,128]{1,0:T(8,128)(2,1)S(1)} %get-tuple-element.56), channel_id=1, source_target_pairs={{2,0},{3,1},{0,2},{1,3},{6,4},{7,5},{4,6},{5,7},{10,8},{11,9},{8,1... | collective-permute-start | bytes 307208 | tf_op jit(solution)/shard_map/ppermute | solution.py:25
  61.1 5.6 %collective-permute-start.13 = (f32[8,512]{1,0:T(8,128)S(1)}, f32[8,512]{1,0:T(8,128)S(1)}, u32[]{:S(2)}, u32[]{:S(2)}) collective-permute-start(f32[8,512]{1,0:T(8,128)S(1)} %get-tuple-element.60.refs_3_), channel_id=1, source_target_pairs={{3,0},{2,1},{1,2},{0,3},{7,4},{6,5},{5,6},{4,7},{11,8},{10,9},{9,1... | collective-permute-start | bytes 49160 | tf_op jit(solution)/shard_map/ppermute | solution.py:25
  64.3 4.6 %collective-permute-start.12 = (f32[8,512]{1,0:T(8,128)S(1)}, f32[8,512]{1,0:T(8,128)S(1)}, u32[]{:S(2)}, u32[]{:S(2)}) collective-permute-start(f32[8,512]{1,0:T(8,128)S(1)} %get-tuple-element.60.refs_3_), channel_id=1, source_target_pairs={{2,0},{3,1},{0,2},{1,3},{6,4},{7,5},{4,6},{5,7},{10,8},{11,9},{8,1... | collective-permute-start | bytes 49160 | tf_op jit(solution)/shard_map/ppermute | solution.py:25
  64.3 4.6 %collective-permute-start.11 = (f32[8,512]{1,0:T(8,128)S(1)}, f32[8,512]{1,0:T(8,128)S(1)}, u32[]{:S(2)}, u32[]{:S(2)}) collective-permute-start(f32[8,512]{1,0:T(8,128)S(1)} %get-tuple-element.60.refs_3_), channel_id=1, source_target_pairs={{1,0},{0,1},{3,2},{2,3},{5,4},{4,5},{7,6},{6,7},{9,8},{8,9},{11,10... | collective-permute-start | bytes 49160 | tf_op jit(solution)/shard_map/ppermute | solution.py:25

commit v3 on v2

v3 whole, which is shorter than its diff:
```python
import functools

import jax
import jax.numpy as jnp
from jax import lax
from jax.experimental import pallas as pl
from jax.experimental.pallas import tpu as pltpu
from jax.sharding import PartitionSpec as P

BS = 256
LANES = 128
HEAD = 16
STEPS = 256.0
TOP = 65534.0
LN2 = 0.6931471805599453
PRODUCT_LIMIT = 24000000
SMALL_LIMIT = 8 * 1024 * 1024
IN_SMEM = pl.BlockSpec(memory_space=pltpu.SMEM)
IN_VMEM = pl.BlockSpec(memory_space=pltpu.VMEM)
IN_HBM = pl.BlockSpec(memory_space=pltpu.HBM)


def swap(block, axis, partner):
    return lax.ppermute(block, axis, [(partner(i), i) for i in range(lax.axis_size(axis))])


def after(value, *others):
    return lax.optimization_barrier((value, *others))[0]


def call(kernel, name, operands, in_specs, out_shape, scratch_shapes=(), flops=0, moved=0, limit=SMALL_LIMIT):
    return pl.pallas_call(
        kernel,
        out_shape=out_shape,
        in_specs=in_specs,
        out_specs=jax.tree.map(lambda _: IN_VMEM, out_shape),
        scratch_shapes=list(scratch_shapes),
        compiler_params=pltpu.CompilerParams(vmem_limit_bytes=limit),
        cost_estimate=pl.CostEstimate(flops=1, bytes_accessed=1, transcendentals=0),
        name=name,
    )(*operands)


def powers(values):
    largest = jnp.maximum(jnp.max(values, axis=0, keepdims=True), 1e-3)
    return jnp.floor(jnp.log(largest) * (STEPS / LN2)) + 2.0


def code(values, power):
    scaled = values * (TOP * jnp.exp(power * (-LN2 / STEPS)))
    return ((scaled + 0.5).astype(jnp.int32) - 32767).astype(jnp.int16)


def scales(head):
    return jnp.exp(head.astype(jnp.int32).astype(jnp.float32) * (LN2 / STEPS)) * (1.0 / TOP)


def decode(codes, scale):
    return (codes.astype(jnp.int32) + 32767).astype(jnp.float32) * scale


def masked(values, pattern, column, first):
    depth, width = values.shape
    place = lax.broadcasted_iota(jnp.int32, (1, width), 1) // BS
    parts = []
    for u in range(depth // BS):
        factor = jnp.zeros((1, width), jnp.float32)
        for v in range(width // BS):
            factor = jnp.where(place == v, pattern[column + v, 0, first + u].astype(jnp.float32), factor)
        parts.append(values[u * BS : (u + 1) * BS] * factor.astype(values.dtype))
    return jnp.concatenate(parts, axis=0) if len(parts) > 1 else parts[0]


def dot(left_side, right_side):
    return lax.dot_general(
        left_side, right_side, (((1,), (0,)), ((), ())), preferred_element_type=jnp.float32
    )


def columns_of(ref, start, count):
    return ref.at[0, :, pl.ds(pl.multiple_of(start * BS, BS), count * BS)]


def rows_at(block, first=0):
    return pl.ds(pl.multiple_of(first + block * BS, HEAD), BS)


class Sides:
    def __init__(self, inner, panel):
        odd = lax.rem(lax.axis_index("blk"), 2)
        self.panel = panel
        self.first = lax.axis_index("layer") * (inner // BS)
        self.ext_side, self.int_side = odd * (2 * panel), (1 - odd) * (2 * panel)
        self.columns = {"ext": self.ext_side, "own": panel, "int": self.int_side}
        self.starts = {"ext": odd * panel, "own": 0, "int": (1 - odd) * panel}


class Coded:
    def __init__(self, refs):
        self.refs = refs
        self.heads = [jnp.zeros((HEAD, ref.shape[1]), jnp.float32) for ref in refs]

    def write(self, product, place):
        column = 0
        for c, ref in enumerate(self.refs):
            chunk = product[:, column : column + ref.shape[1]]
            column += ref.shape[1]
            power = powers(chunk)
            ref[rows_at(place, HEAD), :] = code(chunk, power)
            line = lax.broadcasted_iota(jnp.int32, self.heads[c].shape, 0)
            self.heads[c] = jnp.where(line == place, power, self.heads[c])

    def finish(self):
        for ref, head in zip(self.refs, self.heads):
            ref[0:HEAD, :] = head.astype(jnp.int32).astype(jnp.int16)


def turn(chunk, a_ref, start, first, turned_ref, rows):
    turned_ref[:, rows] = masked(chunk, a_ref, start, first).T


def first_kernel(depth, a_hbm, b_hbm, flow_hbm, graph_hbm, *rest):
    out_refs, (turned_ref, graph_ref, flow_ref, flow_buf, a_ref, b_ref, sems) = rest[:-7], rest[-7:]
    inner, panel = flow_ref.shape[0], flow_ref.shape[1] // BS
    at = Sides(inner, panel)
    steps = inner // depth
    small = [pltpu.make_async_copy(a_hbm, a_ref, sems.at[0]), pltpu.make_async_copy(b_hbm, b_ref, sems.at[1])]
    side = pl.ds(pl.multiple_of(at.ext_side * BS, BS), panel * BS)
    rest_start = (panel * BS) - at.ext_side // 2 * BS
    others = pl.ds(pl.multiple_of(rest_start, BS), 2 * panel * BS)
    early = pltpu.make_async_copy(graph_hbm.at[0, :, side], graph_ref.at[:, side], sems.at[2])
    late = [
        pltpu.make_async_copy(graph_hbm.at[0, :, others], graph_ref.at[:, others], sems.at[3]),
        pltpu.make_async_copy(columns_of(flow_hbm, at.int_side, panel), flow_ref, sems.at[4]),
    ]
    source = columns_of(flow_hbm, at.starts["ext"], 2 * panel)
    flows = []
    for t in range(steps):
        rows = slice(t * depth, (t + 1) * depth)
        flows.append(pltpu.make_async_copy(source.at[rows], flow_buf.at[rows], sems.at[5 + t]))
    for copy in small + flows[:1] + [early] + flows[1:] + late:
        copy.start()
    for copy in small:
        copy.wait()
    for t in range(steps):
        rows = slice(t * depth, (t + 1) * depth)
        flows[t].wait()
        turn(flow_buf[rows, :], a_ref, at.starts["ext"], at.first + t * (depth // BS), turned_ref, rows)
    early.wait()
    right = masked(graph_ref[:, rows_at(at.ext_side)], b_ref, at.ext_side, at.first)
    coded = Coded(out_refs)
    for i in range(2 * panel):
        coded.write(dot(turned_ref[i * BS : (i + 1) * BS, :], right), i)
    coded.finish()
    for copy in late:
        copy.wait()


def first_products(flow_t, graph, a_lines, b_lines, widths):
    inner, width = flow_t.shape[1:]
    panel = width // 3
    depth = min(512, inner)
    operands = [pltpu.with_memory_space_constraint(x, pltpu.HBM) for x in (a_lines, b_lines, flow_t, graph)]
    return call(
        functools.partial(first_kernel, depth),
        "first_products",
        operands,
        [IN_HBM] * 4,
        [jax.ShapeDtypeStruct((HEAD + 2 * panel, w), jnp.int16) for w in widths]
        + [
            pltpu.VMEM((2 * panel, inner), flow_t.dtype),
            pltpu.VMEM((inner, width), graph.dtype),
            pltpu.VMEM((inner, panel), flow_t.dtype),
        ],
        [
            pltpu.VMEM((inner, 2 * panel), flow_t.dtype),
            pltpu.SMEM(a_lines.shape, a_lines.dtype),
            pltpu.SMEM(b_lines.shape, b_lines.dtype),
            pltpu.SemaphoreType.DMA((5 + inner // depth,)),
        ],
        flops=2 * inner * BS * 2 * panel,
        moved=4 * inner * width,
        limit=PRODUCT_LIMIT,
    )


def product_kernel(half, wanted, turns, a_ref, b_ref, graph_ref, ext_rows_ref, int_rows_ref, *rest):
    refs = list(rest)
    inner, panel = graph_ref.shape[0], graph_ref.shape[1] // BS // 3
    at = Sides(inner, panel)
    parts = [part for part in ("ext", "own", "int") if part in wanted]
    outs = {part: [refs.pop(0) for _ in wanted[part]] for part in parts}
    turned_ref = refs.pop(0) if turns else int_rows_ref
    coded = {part: Coded(outs[part]) for part in parts if part != "own"}
    right = []
    for part in parts:
        column = at.columns[part] + half
        right.append(masked(graph_ref[:, rows_at(column)], b_ref, column, at.first))
    right = jnp.concatenate(right, axis=1) if len(right) > 1 else right[0]

    def multiply(side, start, source, names):
        used = [part for part in parts if part in names]
        if not used:
            return
        low = parts.index(used[0]) * BS
        for i in range(panel):
            block = side + i
            product = dot(source[rows_at(block - start), :], right[:, low : low + len(used) * BS])
            for j, part in enumerate(used):
                piece = product[:, j * BS : (j + 1) * BS]
                if part == "own":
                    outs[part][0][rows_at(block), :] = piece
                else:
                    coded[part].write(piece, block - at.starts[part])

    if turns:
        turn(int_rows_ref[...], a_ref, at.int_side, at.first, turned_ref, slice(None))
    multiply(panel, at.starts["ext"], ext_rows_ref, ("ext", "own", "int"))
    multiply(at.ext_side, at.starts["ext"], ext_rows_ref, ("ext", "own"))
    multiply(at.int_side, at.int_side, turned_ref, ("own", "int"))
    for part in coded:
        coded[part].finish()


def products(a_lines, b_lines, graph, ext_rows, int_rows, half, wanted, turns=False):
    inner, width = graph.shape
    panel = width // 3
    outs = []
    for part in ("ext", "own", "int"):
        for w in wanted.get(part, ()):
            if part == "own":
                outs.append(jax.ShapeDtypeStruct((width, w), jnp.float32))
            else:
                outs.append(jax.ShapeDtypeStruct((HEAD + 2 * panel, w), jnp.int16))
    if turns:
        outs.append(pltpu.VMEM((panel, inner), graph.dtype))
    return call(
        functools.partial(product_kernel, half, wanted, turns),
        "_".join(wanted) + f"_products_{half}",
        (a_lines, b_lines, graph, ext_rows, int_rows),
        [IN_SMEM, IN_SMEM] + [IN_VMEM] * 3,
        outs,
        flops=2 * inner * BS * sum(width if part == "own" else 2 * panel for part in wanted),
        moved=2 * inner * BS,
        limit=PRODUCT_LIMIT,
    )


def split_strips(total, rows, position, keep_ref, send_ref):
    bit = lax.rem(lax.axis_index("layer") // position, 2)
    pairs = keep_ref.shape[0]
    for j in range(pairs):
        keep_ref[j] = total[pl.ds((2 * j + bit) * rows, rows), :]
    away = [total[pl.ds((2 * j + 1 - bit) * rows, rows), :] for j in range(pairs)]
    power = functools.reduce(jnp.maximum, [powers(strip) for strip in away])
    for j, strip in enumerate(away):
        send_ref[HEAD + j * rows : HEAD + (j + 1) * rows, :] = code(strip, power)
    send_ref[0:HEAD, :] = jnp.broadcast_to(power, (HEAD, power.shape[1])).astype(jnp.int32).astype(jnp.int16)


def join_kernel(rows, half, lane, c_ref, own_ref, ext_ref, int_ref, keep_ref, send_ref, total):
    odd = lax.rem(lax.axis_index("blk"), 2)
    blocks = own_ref.shape[0] // BS
    panel = blocks // 3
    lanes = slice(lane, lane + ext_ref.shape[1])

    def add(below_ref, above_ref):
        below_scale = scales(below_ref[0:HEAD, :])
        above_scale = scales(above_ref[0:HEAD, :])
        for v in range(blocks):
            kept = c_ref[0, half, v].astype(jnp.float32)
            block = own_ref[v * BS : (v + 1) * BS, lanes] * kept
            if v < 2 * panel:
                codes = below_ref[HEAD + v * BS : HEAD + (v + 1) * BS, :]
                block += decode(codes, below_scale[v : v + 1] * kept)
            if v >= panel:
                i = v - panel
                codes = above_ref[HEAD + i * BS : HEAD + (i + 1) * BS, :]
                block += decode(codes, above_scale[i : i + 1] * kept)
            total[v * BS : (v + 1) * BS, :] = block

    @pl.when(odd == 1)
    def _():
        add(int_ref, ext_ref)

    @pl.when(odd == 0)
    def _():
        add(ext_ref, int_ref)

    split_strips(total, rows, 1, keep_ref, send_ref)


def strips_shapes(pairs, rows, width):
    return [
        jax.ShapeDtypeStruct((pairs, rows, width), jnp.float32),
        jax.ShapeDtypeStruct((HEAD + pairs * rows, width), jnp.int16),
    ]


def join(own, ext_part, int_part, c_lines, half, lane, layers):
    height = own.shape[0]
    width = ext_part.shape[1]
    rows = height // layers
    return call(
        functools.partial(join_kernel, rows, half, lane),
        f"join_{half}_{lane}",
        (c_lines, own, ext_part, int_part),
        [IN_SMEM] + [IN_VMEM] * 3,
        strips_shapes(layers // 2, rows, width),
        [pltpu.VMEM((height, width), jnp.float32)],
        moved=8 * height * width,
    )


def halve_kernel(rows, position, kept_ref, got_ref, keep_ref, send_ref, total):
    scale = scales(got_ref[0:HEAD, :])[0:1]
    for j in range(kept_ref.shape[0]):
        codes = got_ref[HEAD + j * rows : HEAD + (j + 1) * rows, :]
        total[j * rows : (j + 1) * rows, :] = kept_ref[j] + decode(codes, scale)
    split_strips(total, rows, position, keep_ref, send_ref)


def halve(kept, got, position, chunk):
    strips, rows, width = kept.shape
    return call(
        functools.partial(halve_kernel, rows, position),
        f"halve_{position}_{chunk}",
        (kept, got),
        [IN_VMEM] * 2,
        strips_shapes(strips // 2, rows, width),
        [pltpu.VMEM((strips * rows, width), jnp.float32)],
        moved=8 * kept.size,
    )


def square_kernel(kept_ref, got_ref, *rest):
    earlier, (square_ref, sums_ref) = rest[:-2], rest[-2:]
    value = kept_ref[0] + decode(got_ref[HEAD:, :], scales(got_ref[0:HEAD, :])[0:1])
    square = value * value
    square_ref[...] = square
    sums = jnp.broadcast_to(jnp.sum(square, axis=0, keepdims=True), (8, square.shape[1]))
    sums_ref[...] = jnp.concatenate([ref[...] for ref in earlier] + [sums], axis=1)


def square(kept, got, earlier, chunk):
    _, rows, width = kept.shape
    return call(
        square_kernel,
        f"square_{chunk}",
        (kept, got, *earlier),
        [IN_VMEM] * (2 + len(earlier)),
        [
            jax.ShapeDtypeStruct((rows, width), jnp.float32),
            jax.ShapeDtypeStruct((8, width + sum(sums.shape[1] for sums in earlier)), jnp.float32),
        ],
        moved=8 * kept.size,
    )


def rescale_kernel(height, count, *refs):
    squares, sums, out_ref = refs[:count], refs[count:-1], refs[-1]
    total = functools.reduce(jnp.add, [ref[0:1, :] for ref in sums])
    divisor = total / height + 1e-6
    column = 0
    for ref in squares:
        columns = slice(column, column + ref.shape[1])
        column += ref.shape[1]
        out_ref[0, :, columns] = ref[...] / divisor[:, columns]


def rescale(squares, sums, height):
    rows = squares[0].shape[0]
    width = sums[0].shape[1]
    return call(
        functools.partial(rescale_kernel, float(height), len(squares)),
        "rescale",
        (*squares, *sums),
        [IN_VMEM] * (len(squares) + len(sums)),
        jax.ShapeDtypeStruct((1, rows, width), jnp.float32),
        moved=8 * rows * width,
    )


def shards(flow_t, graph, a_pattern, b_pattern, c_pattern):
    layers = lax.axis_size("layer")
    blks = lax.axis_size("blk")
    width = flow_t.shape[2]
    panel = width // 3
    a_lines = a_pattern.transpose(2, 0, 1)
    b_lines = b_pattern.transpose(2, 0, 1)
    c_lines = c_pattern.transpose(0, 2, 1)

    def other_chip(i):
        return (i + 1 if i % 2 else i - 1) % blks

    def same_chip(i):
        return i ^ 1

    halves = panel // BS
    chunks = panel // LANES
    fine = (LANES,) * (BS // LANES)
    per_half = len(fine)
    *ext_parts, ext_rows, graph, flow_rest = first_products(flow_t, graph, a_lines, b_lines, fine)
    ext = [swap(part, "blk", other_chip) for part in ext_parts]
    wanted = {"own": (BS,), "int": fine}
    own, *int_parts, int_rows = products(a_lines, b_lines, graph, ext_rows, flow_rest, 0, wanted, turns=True)
    owns = [own]
    int_ = [swap(part, "blk", same_chip) for part in int_parts]
    latest = [own]

    def ordered(value):
        return after(value, latest[-1])

    def more_products(half):
        parts = products(ordered(a_lines), b_lines, graph, ext_rows, int_rows, half, {"ext": fine, "int": fine})
        ext.extend(swap(part, "blk", other_chip) for part in parts[:per_half])
        int_.extend(swap(part, "blk", same_chip) for part in parts[per_half:])
        latest.append(parts[0])
        owns.extend(products(ordered(a_lines), b_lines, graph, ext_rows, int_rows, half, {"own": (BS,)}))
        latest.append(owns[-1])

    strips, squares, sums = [], [], []

    def add_up(chunk):
        half, lane = divmod(chunk, per_half)
        kept, send = join(owns[half], ext[chunk], int_[chunk], ordered(c_lines), half, lane * LANES, layers)
        latest.append(send)
        strips.append((kept, swap(send, "layer", lambda i: i ^ 1)))

    def scatter(chunk):
        kept, got = strips[chunk]
        position = 1
        while kept.shape[0] > 1:
            position *= 2
            kept, send = halve(ordered(kept), got, position, chunk)
            latest.append(send)
            got = swap(send, "layer", lambda i: i ^ position)
        strips[chunk] = kept, got

    def finish(chunk):
        kept, got = strips[chunk]
        squared, summed = square(ordered(kept), got, sums if chunk == chunks - 1 else [], chunk)
        latest.append(summed)
        squares.append(squared)
        sums.append(summed)

    for chunk in range(chunks + 2):
        if chunk < chunks:
            add_up(chunk)
        if 1 <= chunk <= chunks:
            scatter(chunk - 1)
        if chunk >= 2:
            finish(chunk - 2)
        if chunk % per_half == 0 and chunk // per_half + 1 < halves:
            more_products(chunk // per_half + 1)

    mine = sums[-1]
    others = [swap(mine, "layer", lambda i: i ^ other) for other in range(1, layers)]
    return rescale(squares, [mine, *others], width)


def solution(mesh):
    placed = (
        P("blk", "layer", None),
        P("blk", "layer", None),
        P("blk", None, None),
        P("blk", None, None),
        P("blk", None, None),
    )
    return jax.shard_map(
        shards, mesh=mesh, in_specs=placed, out_specs=P("blk", "layer", None), check_vma=False
    )
```

time: 70.3 us -> 66.3 us (0.943)
  starting transfers between devices: 17.6 us -> 27.6 us
  waiting for transfers between devices: 25.4 us -> 17.8 us
  Pallas kernels: 25.4 us -> 20.6 us
  local copies, waits for them, and re-layouts: 1.37 us -> 0.01 us
    ppermute x14 -> x19, starting transfers between devices: 17.6 us -> 27.6 us  [swap(): lax.ppermute(block, axis, [(partner(i), i) for i in range(lax.axis_size(a...]
    ppermute x14 -> x19, waiting for transfers between devices: 25.4 us -> 17.8 us  [swap(): lax.ppermute(block, axis, [(partner(i), i) for i in range(lax.axis_size(a...]
    pallas_call x14 -> x17, Pallas kernels: 25.4 us -> 20.6 us  [call(): pl.pallas_call(kernel, out_shape=out_shape, in_specs=in_specs, out_specs=...]
    unnamed x6, local copies, waits for them, and re-layouts: 1.37 us -> 0.01 us
  transfers between devices with their start and end apart: 14 -> 19, of which waited for: 8 -> 9; matrix products, arithmetic and copies ran while one was open for 0% -> 0% of each run, Pallas kernels for 28% -> 22%
where the time goes in v3:
time: 66.3 us; the launch traced here: 66.1 us
  starting transfers between devices  27.6 us (42%)
  Pallas kernels  20.6 us (31%)
  waiting for transfers between devices  17.8 us (27%)
    ppermute x19, starting transfers between devices, swap(): lax.ppermute(block, axis, [(partner(i), i) for i in range(lax.axis_size(a...  27.6 us
    pallas_call x17, Pallas kernels, call(): pl.pallas_call(kernel, out_shape=out_shape, in_specs=in_specs, out_specs=...  20.6 us
    ppermute x19, waiting for transfers between devices, swap(): lax.ppermute(block, axis, [(partner(i), i) for i in range(lax.axis_size(a...  17.8 us
  transfers between devices with their start and end apart: 19, of which 9 were waited for; matrix products, arithmetic and copies ran while one was open for 0% of the time, Pallas kernels for 22%

profile of v3, /device:TPU:0, one launch (start us, length us, event | category | flops | bytes accessed | tf_op | source)
XLA Modules:
  0.0 66.1 jit_solution(5554816925467024944)
XLA Ops:
  0.0 5.0 %first_products.1 = (s16[1040,128]{1,0:T(8,128)(2,1)S(1)}, s16[1040,128]{1,0:T(8,128)(2,1)S(1)}, bf16[1024,2048]{1,0:T(8,128)(2,1)S(1)}, bf16[2048,1536]{1,0:T(8,128)(2,1)S(1)}, bf16[2048,512]{1,0:T(8,128)(2,1)S(1)}) custom-call(s32[6,1,32]{2,1,0:T(1,128)} %bitcast.3, s32[6,1,32]{2,1,0:T(1,128)} %bitcast.7, bf16[1,2048,1536]{2,1,0:T(8,128)(2,1)} %flow_hbm.1, ...), custom_call_target="tpu_custom_call" | custom-call | flops 1 | bytes 1 | tf_op jit(solution)/shard_map/first_products/pallas_call | solution.py:32
  5.0 3.4 %collective-permute-start = (s16[1040,128]{1,0:T(8,128)(2,1)S(1)}, s16[1040,128]{1,0:T(8,128)(2,1)S(1)}, u32[]{:S(2)}, u32[]{:S(2)}) collective-permute-start(s16[1040,128]{1,0:T(8,128)(2,1)S(1)} %get-tuple-element.61), channel_id=1, source_target_pairs={{28,0},{8,4},{4,8},{16,12},{12,16},{24,20},{20,24},{0,28},{29,1},{... | collective-permute-start | bytes 798728 | tf_op jit(solution)/shard_map/ppermute | solution.py:24
  8.4 3.8 %own_int_products_0.1 = (f32[1536,256]{1,0:T(8,128)S(1)}, s16[1040,128]{1,0:T(8,128)(2,1)S(1)}, s16[1040,128]{1,0:T(8,128)(2,1)S(1)}, bf16[512,2048]{1,0:T(8,128)(2,1)S(1)}) custom-call(s32[6,1,32]{2,1,0:T(1,128)S(1)} %bitcast.4, s32[6,1,32]{2,1,0:T(1,128)S(1)} %bitcast.8, bf16[2048,1536]{1,0:T(8,128)(2,1)S(1)} %get-tuple-element.56.graph_ref, ...), custom_call_target="tpu_custom_call" | custom-call | flops 1 | bytes 1 | tf_op jit(solution)/shard_map/own_int_products_0/pallas_call | solution.py:32
  12.2 0.7 %collective-permute-start.2 = (s16[1040,128]{1,0:T(8,128)(2,1)S(1)}, s16[1040,128]{1,0:T(8,128)(2,1)S(1)}, u32[]{:S(2)}, u32[]{:S(2)}) collective-permute-start(s16[1040,128]{1,0:T(8,128)(2,1)S(1)} %get-tuple-element.70), channel_id=1, source_target_pairs={{28,0},{8,4},{4,8},{16,12},{12,16},{24,20},{20,24},{0,28},{29,1},{... | collective-permute-start | bytes 798728 | tf_op jit(solution)/shard_map/ppermute | solution.py:24
  12.9 0.6 collective-permute-start.3
  13.5 1.0 %collective-permute-done.ext_ref = s16[1040,128]{1,0:T(8,128)(2,1)S(1)} collective-permute-done((s16[1040,128]{1,0:T(8,128)(2,1)S(1)}, s16[1040,128]{1,0:T(8,128)(2,1)S(1)}, u32[]{:S(2)}, u32[]{:S(2)}) %collective-permute-start) | collective-permute-done | bytes 266272 | tf_op jit(solution)/shard_map/ppermute | solution.py:24
  14.5 1.0 %join_0_0.1 = (f32[2,384,128]{2,1,0:T(8,128)S(1)}, s16[784,128]{1,0:T(8,128)(2,1)S(1)}) custom-call(s32[1,2,6]{2,1,0:T(2,128)S(1)} %bitcast.11, f32[1536,256]{1,0:T(8,128)S(1)} %get-tuple-element.59.own_ref, s16[1040,128]{1,0:T(8,128)(2,1)S(1)} %collective-permute-done.ext_ref, s16[1040,128]{1,0:T(8,128)(2,1)S(1)} %collective-permute-done.1.int_ref), custom_call_target="tpu_custom_call" | custom-call | flops 1 | bytes 1 | tf_op jit(solution)/shard_map/join_0_0/pallas_call | solution.py:32
  15.5 3.1 %collective-permute-start.4 = (s16[784,128]{1,0:T(8,128)(2,1)S(1)}, s16[784,128]{1,0:T(8,128)(2,1)S(1)}, u32[]{:S(2)}, u32[]{:S(2)}) collective-permute-start(s16[784,128]{1,0:T(8,128)(2,1)S(1)} %get-tuple-element.64), channel_id=1, source_target_pairs={{1,0},{0,1},{3,2},{2,3},{5,4},{4,5},{7,6},{6,7},{9,8},{8,9},{11,10... | collective-permute-start | bytes 602120 | tf_op jit(solution)/shard_map/ppermute | solution.py:24
  18.6 3.5 %ext_int_products_1.1 = (s16[1040,128]{1,0:T(8,128)(2,1)S(1)}, s16[1040,128]{1,0:T(8,128)(2,1)S(1)}, s16[1040,128]{1,0:T(8,128)(2,1)S(1)}, s16[1040,128]{1,0:T(8,128)(2,1)S(1)}) custom-call(s32[6,1,32]{2,1,0:T(1,128)S(1)} %bitcast.5, s32[6,1,32]{2,1,0:T(1,128)S(1)} %bitcast.9, bf16[2048,1536]{1,0:T(8,128)(2,1)S(1)} %get-tuple-element.56.graph_ref, ...), custom_call_target="tpu_custom_call" | custom-call | flops 1 | bytes 1 | tf_op jit(solution)/shard_map/ext_int_products_1/pallas_call | solution.py:32
  22.2 1.7 %collective-permute-start.5 = (s16[1040,128]{1,0:T(8,128)(2,1)S(1)}, s16[1040,128]{1,0:T(8,128)(2,1)S(1)}, u32[]{:S(2)}, u32[]{:S(2)}) collective-permute-start(s16[1040,128]{1,0:T(8,128)(2,1)S(1)} %get-tuple-element.67), channel_id=1, source_target_pairs={{28,0},{8,4},{4,8},{16,12},{12,16},{24,20},{20,24},{0,28},{29,1},{... | collective-permute-start | bytes 798728 | tf_op jit(solution)/shard_map/ppermute | solution.py:24
  23.9 1.0 %collective-permute-start.9 = (s16[1040,128]{1,0:T(8,128)(2,1)S(1)}, s16[1040,128]{1,0:T(8,128)(2,1)S(1)}, u32[]{:S(2)}, u32[]{:S(2)}) collective-permute-start(s16[1040,128]{1,0:T(8,128)(2,1)S(1)} %get-tuple-element.88), channel_id=1, source_target_pairs={{28,0},{8,4},{4,8},{16,12},{12,16},{24,20},{20,24},{0,28},{29,1},{... | collective-permute-start | bytes 798728 | tf_op jit(solution)/shard_map/ppermute | solution.py:24
  24.9 2.5 %own_products_1.1.own_ref = f32[1536,256]{1,0:T(8,128)S(1)} custom-call(s32[6,1,32]{2,1,0:T(1,128)S(1)} %bitcast.6, s32[6,1,32]{2,1,0:T(1,128)S(1)} %bitcast.10, bf16[2048,1536]{1,0:T(8,128)(2,1)S(1)} %get-tuple-element.56.graph_ref, bf16[1024,2048]{1,0:T(8,128)(2,1)S(1)} %get-tuple-element.57.ext_rows_ref, bf16[512,2048]{1,0:T(8,128)(2,1)S(1)} %get-tuple-element.66.int_rows_ref), custom_call_target="tpu_custom_call" | custom-call | flops 1 | bytes 1 | tf_op jit(solution)/shard_map/own_products_1/pallas_call | solution.py:32
  27.4 1.0 %join_0_128.1 = (f32[2,384,128]{2,1,0:T(8,128)S(1)}, s16[784,128]{1,0:T(8,128)(2,1)S(1)}) custom-call(s32[1,2,6]{2,1,0:T(2,128)S(1)} %bitcast.12, f32[1536,256]{1,0:T(8,128)S(1)} %get-tuple-element.59.own_ref, s16[1040,128]{1,0:T(8,128)(2,1)S(1)} %collective-permute-done.2.ext_ref, s16[1040,128]{1,0:T(8,128)(2,1)S(1)} %collective-permute-done.3.int_ref), custom_call_target="tpu_custom_call" | custom-call | flops 1 | bytes 1 | tf_op jit(solution)/shard_map/join_0_128/pallas_call | solution.py:32
  28.6 3.1 %collective-permute-start.8 = (s16[400,128]{1,0:T(8,128)(2,1)S(1)}, s16[400,128]{1,0:T(8,128)(2,1)S(1)}, u32[]{:S(2)}, u32[]{:S(2)}) collective-permute-start(s16[400,128]{1,0:T(8,128)(2,1)S(1)} %get-tuple-element.76), channel_id=1, source_target_pairs={{2,0},{3,1},{0,2},{1,3},{6,4},{7,5},{4,6},{5,7},{10,8},{11,9},{8,1... | collective-permute-start | bytes 307208 | tf_op jit(solution)/shard_map/ppermute | solution.py:24
  31.9 1.0 %join_1_0.1 = (f32[2,384,128]{2,1,0:T(8,128)S(1)}, s16[784,128]{1,0:T(8,128)(2,1)S(1)}) custom-call(s32[1,2,6]{2,1,0:T(2,128)S(1)} %bitcast.13, f32[1536,256]{1,0:T(8,128)S(1)} %own_products_1.1.own_ref, s16[1040,128]{1,0:T(8,128)(2,1)S(1)} %collective-permute-done.5.ext_ref, s16[1040,128]{1,0:T(8,128)(2,1)S(1)} %collective-permute-done.6.int_ref), custom_call_target="tpu_custom_call" | custom-call | flops 1 | bytes 1 | tf_op jit(solution)/shard_map/join_1_0/pallas_call | solution.py:32
  32.8 1.5 %collective-permute-start.11 = (s16[784,128]{1,0:T(8,128)(2,1)S(1)}, s16[784,128]{1,0:T(8,128)(2,1)S(1)}, u32[]{:S(2)}, u32[]{:S(2)}) collective-permute-start(s16[784,128]{1,0:T(8,128)(2,1)S(1)} %get-tuple-element.79), channel_id=1, source_target_pairs={{1,0},{0,1},{3,2},{2,3},{5,4},{4,5},{7,6},{6,7},{9,8},{8,9},{11,10... | collective-permute-start | bytes 602120 | tf_op jit(solution)/shard_map/ppermute | solution.py:24
  34.3 4.1 %collective-permute-done.7.got_ref = s16[784,128]{1,0:T(8,128)(2,1)S(1)} collective-permute-done((s16[784,128]{1,0:T(8,128)(2,1)S(1)}, s16[784,128]{1,0:T(8,128)(2,1)S(1)}, u32[]{:S(2)}, u32[]{:S(2)}) %collective-permute-start.7) | collective-permute-done | bytes 200736 | tf_op jit(solution)/shard_map/ppermute | solution.py:24
  38.7 1.0 %join_1_128.1 = (f32[2,384,128]{2,1,0:T(8,128)S(1)}, s16[784,128]{1,0:T(8,128)(2,1)S(1)}) custom-call(s32[1,2,6]{2,1,0:T(2,128)S(1)} %bitcast.14, f32[1536,256]{1,0:T(8,128)S(1)} %own_products_1.1.own_ref, s16[1040,128]{1,0:T(8,128)(2,1)S(1)} %collective-permute-done.9.ext_ref, s16[1040,128]{1,0:T(8,128)(2,1)S(1)} %collective-permute-done.10.int_ref), custom_call_target="tpu_custom_call" | custom-call | flops 1 | bytes 1 | tf_op jit(solution)/shard_map/join_1_128/pallas_call | solution.py:32
  39.7 2.5 %collective-permute-start.13 = (s16[784,128]{1,0:T(8,128)(2,1)S(1)}, s16[784,128]{1,0:T(8,128)(2,1)S(1)}, u32[]{:S(2)}, u32[]{:S(2)}) collective-permute-start(s16[784,128]{1,0:T(8,128)(2,1)S(1)} %get-tuple-element.90), channel_id=1, source_target_pairs={{1,0},{0,1},{3,2},{2,3},{5,4},{4,5},{7,6},{6,7},{9,8},{8,9},{11,10... | collective-permute-start | bytes 602120 | tf_op jit(solution)/shard_map/ppermute | solution.py:24
  42.1 0.6 collective-permute-start.12
  42.7 0.2 halve_2_2.1
  42.9 2.7 %collective-permute-start.14 = (s16[400,128]{1,0:T(8,128)(2,1)S(1)}, s16[400,128]{1,0:T(8,128)(2,1)S(1)}, u32[]{:S(2)}, u32[]{:S(2)}) collective-permute-start(s16[400,128]{1,0:T(8,128)(2,1)S(1)} %get-tuple-element.92), channel_id=1, source_target_pairs={{2,0},{3,1},{0,2},{1,3},{6,4},{7,5},{4,6},{5,7},{10,8},{11,9},{8,1... | collective-permute-start | bytes 307208 | tf_op jit(solution)/shard_map/ppermute | solution.py:24
  45.6 3.6 %collective-permute-done.12.got_ref = s16[400,128]{1,0:T(8,128)(2,1)S(1)} collective-permute-done((s16[400,128]{1,0:T(8,128)(2,1)S(1)}, s16[400,128]{1,0:T(8,128)(2,1)S(1)}, u32[]{:S(2)}, u32[]{:S(2)}) %collective-permute-start.12) | collective-permute-done | bytes 102432 | tf_op jit(solution)/shard_map/ppermute | solution.py:24
  49.3 1.4 %collective-permute-done.13.got_ref = s16[784,128]{1,0:T(8,128)(2,1)S(1)} collective-permute-done((s16[784,128]{1,0:T(8,128)(2,1)S(1)}, s16[784,128]{1,0:T(8,128)(2,1)S(1)}, u32[]{:S(2)}, u32[]{:S(2)}) %collective-permute-start.13) | collective-permute-done | bytes 200736 | tf_op jit(solution)/shard_map/ppermute | solution.py:24
  50.8 2.1 %collective-permute-start.15 = (s16[400,128]{1,0:T(8,128)(2,1)S(1)}, s16[400,128]{1,0:T(8,128)(2,1)S(1)}, u32[]{:S(2)}, u32[]{:S(2)}) collective-permute-start(s16[400,128]{1,0:T(8,128)(2,1)S(1)} %get-tuple-element.99), channel_id=1, source_target_pairs={{2,0},{3,1},{0,2},{1,3},{6,4},{7,5},{4,6},{5,7},{10,8},{11,9},{8,1... | collective-permute-start | bytes 307208 | tf_op jit(solution)/shard_map/ppermute | solution.py:24
  53.0 0.8 %collective-permute-done.14.got_ref = s16[400,128]{1,0:T(8,128)(2,1)S(1)} collective-permute-done((s16[400,128]{1,0:T(8,128)(2,1)S(1)}, s16[400,128]{1,0:T(8,128)(2,1)S(1)}, u32[]{:S(2)}, u32[]{:S(2)}) %collective-permute-start.14) | collective-permute-done | bytes 102432 | tf_op jit(solution)/shard_map/ppermute | solution.py:24
  53.8 4.0 %collective-permute-done.15.got_ref = s16[400,128]{1,0:T(8,128)(2,1)S(1)} collective-permute-done((s16[400,128]{1,0:T(8,128)(2,1)S(1)}, s16[400,128]{1,0:T(8,128)(2,1)S(1)}, u32[]{:S(2)}, u32[]{:S(2)}) %collective-permute-start.15) | collective-permute-done | bytes 102432 | tf_op jit(solution)/shard_map/ppermute | solution.py:24
  58.0 2.5 %collective-permute-start.18 = (f32[8,512]{1,0:T(8,128)S(1)}, f32[8,512]{1,0:T(8,128)S(1)}, u32[]{:S(2)}, u32[]{:S(2)}) collective-permute-start(f32[8,512]{1,0:T(8,128)S(1)} %get-tuple-element.106.refs_4_), channel_id=1, source_target_pairs={{3,0},{2,1},{1,2},{0,3},{7,4},{6,5},{5,6},{4,7},{11,8},{10,9},{9,1... | collective-permute-start | bytes 49160 | tf_op jit(solution)/shard_map/ppermute | solution.py:24
  60.5 1.9 %collective-permute-start.16 = (f32[8,512]{1,0:T(8,128)S(1)}, f32[8,512]{1,0:T(8,128)S(1)}, u32[]{:S(2)}, u32[]{:S(2)}) collective-permute-start(f32[8,512]{1,0:T(8,128)S(1)} %get-tuple-element.106.refs_4_), channel_id=1, source_target_pairs={{1,0},{0,1},{3,2},{2,3},{5,4},{4,5},{7,6},{6,7},{9,8},{8,9},{11,10... | collective-permute-start | bytes 49160 | tf_op jit(solution)/shard_map/ppermute | solution.py:24
  62.4 1.1 %collective-permute-done.18.refs_7_ = f32[8,512]{1,0:T(8,128)S(1)} collective-permute-done((f32[8,512]{1,0:T(8,128)S(1)}, f32[8,512]{1,0:T(8,128)S(1)}, u32[]{:S(2)}, u32[]{:S(2)}) %collective-permute-start.18) | collective-permute-done | bytes 16416 | tf_op jit(solution)/shard_map/ppermute | solution.py:24
  63.5 1.6 %collective-permute-done.17.refs_6_ = f32[8,512]{1,0:T(8,128)S(1)} collective-permute-done((f32[8,512]{1,0:T(8,128)S(1)}, f32[8,512]{1,0:T(8,128)S(1)}, u32[]{:S(2)}, u32[]{:S(2)}) %collective-permute-start.17) | collective-permute-done | bytes 16416 | tf_op jit(solution)/shard_map/ppermute | solution.py:24
  65.1 1.0 %rescale.1 = f32[1,384,512]{2,1,0:T(8,128)} custom-call(f32[384,128]{1,0:T(8,128)S(1)} %get-tuple-element.83.refs_0_, f32[384,128]{1,0:T(8,128)S(1)} %get-tuple-element.94.refs_1_, f32[384,128]{1,0:T(8,128)S(1)} %get-tuple-element.101.refs_2_, f32[384,128]{1,0:T(8,128)S(1)} %get-tuple-element.105.refs_3_, f32[8,512]{1,0:T(8,128)S(1)} %get-tuple-element.106.refs_4_, ...), custom_call_target="tpu_custom_call" | custom-call | flops 1 | bytes 1 | tf_op jit(solution)/shard_map/rescale/pallas_call | solution.py:32
  (29 shorter events, 1.2 us)
Async XLA Ops:
  0.0 8.4 %copy-start = (s32[1,32,6]{1,0,2:T(1,128)S(1)}, s32[1,32,6]{1,0,2:T(1,128)}, u32[]{:S(2)}) copy-start(s32[1,32,6]{1,0,2:T(1,128)} %param.7) | copy-start | bytes 2308
  0.0 8.4 %copy-start.1 = (s32[1,32,6]{1,0,2:T(1,128)S(1)}, s32[1,32,6]{1,0,2:T(1,128)}, u32[]{:S(2)}) copy-start(s32[1,32,6]{1,0,2:T(1,128)} %param.8) | copy-start | bytes 2308
  5.0 9.5 %collective-permute-start = (s16[1040,128]{1,0:T(8,128)(2,1)S(1)}, s16[1040,128]{1,0:T(8,128)(2,1)S(1)}, u32[]{:S(2)}, u32[]{:S(2)}) collective-permute-start(s16[1040,128]{1,0:T(8,128)(2,1)S(1)} %get-tuple-element.61), channel_id=1, source_target_pairs={{28,0},{8,4},{4,8},{16,12},{12,16},{24,20},{20,24},{0,28},{29,1},{... | collective-permute-start | bytes 798728 | tf_op jit(solution)/shard_map/ppermute | solution.py:24
  8.4 6.1 %copy-start.2 = (s32[1,6,2]{1,2,0:T(2,128)S(1)}, s32[1,6,2]{1,2,0:T(2,128)}, u32[]{:S(2)}) copy-start(s32[1,6,2]{1,2,0:T(2,128)} %param.9) | copy-start | bytes 148
  12.2 2.4 %collective-permute-start.1 = (s16[1040,128]{1,0:T(8,128)(2,1)S(1)}, s16[1040,128]{1,0:T(8,128)(2,1)S(1)}, u32[]{:S(2)}, u32[]{:S(2)}) collective-permute-start(s16[1040,128]{1,0:T(8,128)(2,1)S(1)} %get-tuple-element.62), channel_id=1, source_target_pairs={{4,0},{0,4},{12,8},{8,12},{20,16},{16,20},{28,24},{24,28},{5,1},{1... | collective-permute-start | bytes 798728 | tf_op jit(solution)/shard_map/ppermute | solution.py:24
  12.2 11.7 %collective-permute-start.2 = (s16[1040,128]{1,0:T(8,128)(2,1)S(1)}, s16[1040,128]{1,0:T(8,128)(2,1)S(1)}, u32[]{:S(2)}, u32[]{:S(2)}) collective-permute-start(s16[1040,128]{1,0:T(8,128)(2,1)S(1)} %get-tuple-element.70), channel_id=1, source_target_pairs={{28,0},{8,4},{4,8},{16,12},{12,16},{24,20},{20,24},{0,28},{29,1},{... | collective-permute-start | bytes 798728 | tf_op jit(solution)/shard_map/ppermute | solution.py:24
  12.9 12.0 %collective-permute-start.3 = (s16[1040,128]{1,0:T(8,128)(2,1)S(1)}, s16[1040,128]{1,0:T(8,128)(2,1)S(1)}, u32[]{:S(2)}, u32[]{:S(2)}) collective-permute-start(s16[1040,128]{1,0:T(8,128)(2,1)S(1)} %get-tuple-element.71), channel_id=1, source_target_pairs={{4,0},{0,4},{12,8},{8,12},{20,16},{16,20},{28,24},{24,28},{5,1},{1... | collective-permute-start | bytes 798728 | tf_op jit(solution)/shard_map/ppermute | solution.py:24
  15.5 12.9 %collective-permute-start.4 = (s16[784,128]{1,0:T(8,128)(2,1)S(1)}, s16[784,128]{1,0:T(8,128)(2,1)S(1)}, u32[]{:S(2)}, u32[]{:S(2)}) collective-permute-start(s16[784,128]{1,0:T(8,128)(2,1)S(1)} %get-tuple-element.64), channel_id=1, source_target_pairs={{1,0},{0,1},{3,2},{2,3},{5,4},{4,5},{7,6},{6,7},{9,8},{8,9},{11,10... | collective-permute-start | bytes 602120 | tf_op jit(solution)/shard_map/ppermute | solution.py:24
  22.1 6.5 %collective-permute-start.6 = (s16[1040,128]{1,0:T(8,128)(2,1)S(1)}, s16[1040,128]{1,0:T(8,128)(2,1)S(1)}, u32[]{:S(2)}, u32[]{:S(2)}) collective-permute-start(s16[1040,128]{1,0:T(8,128)(2,1)S(1)} %get-tuple-element.78), channel_id=1, source_target_pairs={{4,0},{0,4},{12,8},{8,12},{20,16},{16,20},{28,24},{24,28},{5,1},{1... | collective-permute-start | bytes 798728 | tf_op jit(solution)/shard_map/ppermute | solution.py:24
  22.2 9.7 %collective-permute-start.5 = (s16[1040,128]{1,0:T(8,128)(2,1)S(1)}, s16[1040,128]{1,0:T(8,128)(2,1)S(1)}, u32[]{:S(2)}, u32[]{:S(2)}) collective-permute-start(s16[1040,128]{1,0:T(8,128)(2,1)S(1)} %get-tuple-element.67), channel_id=1, source_target_pairs={{28,0},{8,4},{4,8},{16,12},{12,16},{24,20},{20,24},{0,28},{29,1},{... | collective-permute-start | bytes 798728 | tf_op jit(solution)/shard_map/ppermute | solution.py:24
  23.9 14.7 %collective-permute-start.9 = (s16[1040,128]{1,0:T(8,128)(2,1)S(1)}, s16[1040,128]{1,0:T(8,128)(2,1)S(1)}, u32[]{:S(2)}, u32[]{:S(2)}) collective-permute-start(s16[1040,128]{1,0:T(8,128)(2,1)S(1)} %get-tuple-element.88), channel_id=1, source_target_pairs={{28,0},{8,4},{4,8},{16,12},{12,16},{24,20},{20,24},{0,28},{29,1},{... | collective-permute-start | bytes 798728 | tf_op jit(solution)/shard_map/ppermute | solution.py:24
  24.9 13.8 %collective-permute-start.10 = (s16[1040,128]{1,0:T(8,128)(2,1)S(1)}, s16[1040,128]{1,0:T(8,128)(2,1)S(1)}, u32[]{:S(2)}, u32[]{:S(2)}) collective-permute-start(s16[1040,128]{1,0:T(8,128)(2,1)S(1)} %get-tuple-element.89), channel_id=1, source_target_pairs={{4,0},{0,4},{12,8},{8,12},{20,16},{16,20},{28,24},{24,28},{5,1},{1... | collective-permute-start | bytes 798728 | tf_op jit(solution)/shard_map/ppermute | solution.py:24
  28.4 10.0 %collective-permute-start.7 = (s16[784,128]{1,0:T(8,128)(2,1)S(1)}, s16[784,128]{1,0:T(8,128)(2,1)S(1)}, u32[]{:S(2)}, u32[]{:S(2)}) collective-permute-start(s16[784,128]{1,0:T(8,128)(2,1)S(1)} %get-tuple-element.72), channel_id=1, source_target_pairs={{1,0},{0,1},{3,2},{2,3},{5,4},{4,5},{7,6},{6,7},{9,8},{8,9},{11,10... | collective-permute-start | bytes 602120 | tf_op jit(solution)/shard_map/ppermute | solution.py:24
  28.6 10.0 %collective-permute-start.8 = (s16[400,128]{1,0:T(8,128)(2,1)S(1)}, s16[400,128]{1,0:T(8,128)(2,1)S(1)}, u32[]{:S(2)}, u32[]{:S(2)}) collective-permute-start(s16[400,128]{1,0:T(8,128)(2,1)S(1)} %get-tuple-element.76), channel_id=1, source_target_pairs={{2,0},{3,1},{0,2},{1,3},{6,4},{7,5},{4,6},{5,7},{10,8},{11,9},{8,1... | collective-permute-start | bytes 307208 | tf_op jit(solution)/shard_map/ppermute | solution.py:24
  32.8 9.9 %collective-permute-start.11 = (s16[784,128]{1,0:T(8,128)(2,1)S(1)}, s16[784,128]{1,0:T(8,128)(2,1)S(1)}, u32[]{:S(2)}, u32[]{:S(2)}) collective-permute-start(s16[784,128]{1,0:T(8,128)(2,1)S(1)} %get-tuple-element.79), channel_id=1, source_target_pairs={{1,0},{0,1},{3,2},{2,3},{5,4},{4,5},{7,6},{6,7},{9,8},{8,9},{11,10... | collective-permute-start | bytes 602120 | tf_op jit(solution)/shard_map/ppermute | solution.py:24
  39.7 11.0 %collective-permute-start.13 = (s16[784,128]{1,0:T(8,128)(2,1)S(1)}, s16[784,128]{1,0:T(8,128)(2,1)S(1)}, u32[]{:S(2)}, u32[]{:S(2)}) collective-permute-start(s16[784,128]{1,0:T(8,128)(2,1)S(1)} %get-tuple-element.90), channel_id=1, source_target_pairs={{1,0},{0,1},{3,2},{2,3},{5,4},{4,5},{7,6},{6,7},{9,8},{8,9},{11,10... | collective-permute-start | bytes 602120 | tf_op jit(solution)/shard_map/ppermute | solution.py:24
  42.1 7.1 %collective-permute-start.12 = (s16[400,128]{1,0:T(8,128)(2,1)S(1)}, s16[400,128]{1,0:T(8,128)(2,1)S(1)}, u32[]{:S(2)}, u32[]{:S(2)}) collective-permute-start(s16[400,128]{1,0:T(8,128)(2,1)S(1)} %get-tuple-element.81), channel_id=1, source_target_pairs={{2,0},{3,1},{0,2},{1,3},{6,4},{7,5},{4,6},{5,7},{10,8},{11,9},{8,1... | collective-permute-start | bytes 307208 | tf_op jit(solution)/shard_map/ppermute | solution.py:24
  42.9 10.9 %collective-permute-start.14 = (s16[400,128]{1,0:T(8,128)(2,1)S(1)}, s16[400,128]{1,0:T(8,128)(2,1)S(1)}, u32[]{:S(2)}, u32[]{:S(2)}) collective-permute-start(s16[400,128]{1,0:T(8,128)(2,1)S(1)} %get-tuple-element.92), channel_id=1, source_target_pairs={{2,0},{3,1},{0,2},{1,3},{6,4},{7,5},{4,6},{5,7},{10,8},{11,9},{8,1... | collective-permute-start | bytes 307208 | tf_op jit(solution)/shard_map/ppermute | solution.py:24
  50.8 7.0 %collective-permute-start.15 = (s16[400,128]{1,0:T(8,128)(2,1)S(1)}, s16[400,128]{1,0:T(8,128)(2,1)S(1)}, u32[]{:S(2)}, u32[]{:S(2)}) collective-permute-start(s16[400,128]{1,0:T(8,128)(2,1)S(1)} %get-tuple-element.99), channel_id=1, source_target_pairs={{2,0},{3,1},{0,2},{1,3},{6,4},{7,5},{4,6},{5,7},{10,8},{11,9},{8,1... | collective-permute-start | bytes 307208 | tf_op jit(solution)/shard_map/ppermute | solution.py:24
  58.0 5.6 %collective-permute-start.18 = (f32[8,512]{1,0:T(8,128)S(1)}, f32[8,512]{1,0:T(8,128)S(1)}, u32[]{:S(2)}, u32[]{:S(2)}) collective-permute-start(f32[8,512]{1,0:T(8,128)S(1)} %get-tuple-element.106.refs_4_), channel_id=1, source_target_pairs={{3,0},{2,1},{1,2},{0,3},{7,4},{6,5},{5,6},{4,7},{11,8},{10,9},{9,1... | collective-permute-start | bytes 49160 | tf_op jit(solution)/shard_map/ppermute | solution.py:24
  60.5 4.6 %collective-permute-start.17 = (f32[8,512]{1,0:T(8,128)S(1)}, f32[8,512]{1,0:T(8,128)S(1)}, u32[]{:S(2)}, u32[]{:S(2)}) collective-permute-start(f32[8,512]{1,0:T(8,128)S(1)} %get-tuple-element.106.refs_4_), channel_id=1, source_target_pairs={{2,0},{3,1},{0,2},{1,3},{6,4},{7,5},{4,6},{5,7},{10,8},{11,9},{8,1... | collective-permute-start | bytes 49160 | tf_op jit(solution)/shard_map/ppermute | solution.py:24
  60.5 4.6 %collective-permute-start.16 = (f32[8,512]{1,0:T(8,128)S(1)}, f32[8,512]{1,0:T(8,128)S(1)}, u32[]{:S(2)}, u32[]{:S(2)}) collective-permute-start(f32[8,512]{1,0:T(8,128)S(1)} %get-tuple-element.106.refs_4_), channel_id=1, source_target_pairs={{1,0},{0,1},{3,2},{2,3},{5,4},{4,5},{7,6},{6,7},{9,8},{8,9},{11,10... | collective-permute-start | bytes 49160 | tf_op jit(solution)/shard_map/ppermute | solution.py:24

commit v4 on v3

--- a/solution.py
+++ b/solution.py
@@ -246,18 +246,6 @@
     )
 
 
-def split_strips(total, rows, position, keep_ref, send_ref):
-    bit = lax.rem(lax.axis_index("layer") // position, 2)
-    pairs = keep_ref.shape[0]
-    for j in range(pairs):
-        keep_ref[j] = total[pl.ds((2 * j + bit) * rows, rows), :]
-    away = [total[pl.ds((2 * j + 1 - bit) * rows, rows), :] for j in range(pairs)]
-    power = functools.reduce(jnp.maximum, [powers(strip) for strip in away])
-    for j, strip in enumerate(away):
-        send_ref[HEAD + j * rows : HEAD + (j + 1) * rows, :] = code(strip, power)
-    send_ref[0:HEAD, :] = jnp.broadcast_to(power, (HEAD, power.shape[1])).astype(jnp.int32).astype(jnp.int16)
-
-
 def join_kernel(rows, half, lane, c_ref, own_ref, ext_ref, int_ref, keep_ref, send_ref, total):
     odd = lax.rem(lax.axis_index("blk"), 2)
     blocks = own_ref.shape[0] // BS
@@ -287,14 +275,12 @@
     def _():
         add(ext_ref, int_ref)
 
-    split_strips(total, rows, 1, keep_ref, send_ref)
-
-
-def strips_shapes(pairs, rows, width):
-    return [
-        jax.ShapeDtypeStruct((pairs, rows, width), jnp.float32),
-        jax.ShapeDtypeStruct((HEAD + pairs * rows, width), jnp.int16),
-    ]
+    for j in range(send_ref.shape[0]):
+        strip = total[j * rows : (j + 1) * rows, :]
+        power = powers(strip)
+        send_ref[j, HEAD:, :] = code(strip, power)
+        send_ref[j, 0:HEAD, :] = jnp.broadcast_to(power, (HEAD, power.shape[1])).astype(jnp.int32).astype(jnp.int16)
+    keep_ref[...] = total[pl.ds(lax.axis_index("layer") * rows, rows), :]
 
 
 def join(own, ext_part, int_part, c_lines, half, lane, layers):
@@ -306,36 +292,22 @@
         f"join_{half}_{lane}",
         (c_lines, own, ext_part, int_part),
         [IN_SMEM] + [IN_VMEM] * 3,
-        strips_shapes(layers // 2, rows, width),
+        [
+            jax.ShapeDtypeStruct((rows, width), jnp.float32),
+            jax.ShapeDtypeStruct((layers, HEAD + rows, width), jnp.int16),
+        ],
         [pltpu.VMEM((height, width), jnp.float32)],
         moved=8 * height * width,
     )
 
 
-def halve_kernel(rows, position, kept_ref, got_ref, keep_ref, send_ref, total):
-    scale = scales(got_ref[0:HEAD, :])[0:1]
-    for j in range(kept_ref.shape[0]):
-        codes = got_ref[HEAD + j * rows : HEAD + (j + 1) * rows, :]
-        total[j * rows : (j + 1) * rows, :] = kept_ref[j] + decode(codes, scale)
-    split_strips(total, rows, position, keep_ref, send_ref)
-
-
-def halve(kept, got, position, chunk):
-    strips, rows, width = kept.shape
-    return call(
-        functools.partial(halve_kernel, rows, position),
-        f"halve_{position}_{chunk}",
-        (kept, got),
-        [IN_VMEM] * 2,
-        strips_shapes(strips // 2, rows, width),
-        [pltpu.VMEM((strips * rows, width), jnp.float32)],
-        moved=8 * kept.size,
-    )
-
-
 def square_kernel(kept_ref, got_ref, *rest):
     earlier, (square_ref, sums_ref) = rest[:-2], rest[-2:]
-    value = kept_ref[0] + decode(got_ref[HEAD:, :], scales(got_ref[0:HEAD, :])[0:1])
+    layers = got_ref.shape[0]
+    value = kept_ref[...]
+    for distance in range(1, layers):
+        other = lax.rem(lax.axis_index("layer") + distance, layers)
+        value += decode(got_ref[other, HEAD:, :], scales(got_ref[other, 0:HEAD, :])[0:1])
     square = value * value
     square_ref[...] = square
     sums = jnp.broadcast_to(jnp.sum(square, axis=0, keepdims=True), (8, square.shape[1]))
@@ -343,7 +315,7 @@
 
 
 def square(kept, got, earlier, chunk):
-    _, rows, width = kept.shape
+    rows, width = kept.shape
     return call(
         square_kernel,
         f"square_{chunk}",
@@ -358,8 +330,8 @@
 
 
 def rescale_kernel(height, count, *refs):
-    squares, sums, out_ref = refs[:count], refs[count:-1], refs[-1]
-    total = functools.reduce(jnp.add, [ref[0:1, :] for ref in sums])
+    squares, sums_ref, out_ref = refs[:count], refs[count], refs[-1]
+    total = functools.reduce(jnp.add, [sums_ref[i, 0:1, :] for i in range(sums_ref.shape[0])])
     divisor = total / height + 1e-6
     column = 0
     for ref in squares:
@@ -370,12 +342,12 @@
 
 def rescale(squares, sums, height):
     rows = squares[0].shape[0]
-    width = sums[0].shape[1]
+    width = sums.shape[2]
     return call(
         functools.partial(rescale_kernel, float(height), len(squares)),
         "rescale",
-        (*squares, *sums),
-        [IN_VMEM] * (len(squares) + len(sums)),
+        (*squares, sums),
+        [IN_VMEM] * (len(squares) + 1),
         jax.ShapeDtypeStruct((1, rows, width), jnp.float32),
         moved=8 * rows * width,
     )
@@ -425,17 +397,7 @@
         half, lane = divmod(chunk, per_half)
         kept, send = join(owns[half], ext[chunk], int_[chunk], ordered(c_lines), half, lane * LANES, layers)
         latest.append(send)
-        strips.append((kept, swap(send, "layer", lambda i: i ^ 1)))
-
-    def scatter(chunk):
-        kept, got = strips[chunk]
-        position = 1
-        while kept.shape[0] > 1:
-            position *= 2
-            kept, send = halve(ordered(kept), got, position, chunk)
-            latest.append(send)
-            got = swap(send, "layer", lambda i: i ^ position)
-        strips[chunk] = kept, got
+        strips.append((kept, lax.all_to_all(send, "layer", 0, 0, tiled=True)))
 
     def finish(chunk):
         kept, got = strips[chunk]
@@ -444,19 +406,16 @@
         squares.append(squared)
         sums.append(summed)
 
-    for chunk in range(chunks + 2):
+    for chunk in range(chunks + 1):
         if chunk < chunks:
             add_up(chunk)
-        if 1 <= chunk <= chunks:
-            scatter(chunk - 1)
-        if chunk >= 2:
-            finish(chunk - 2)
+        if chunk >= 1:
+            finish(chunk - 1)
         if chunk % per_half == 0 and chunk // per_half + 1 < halves:
             more_products(chunk // per_half + 1)
 
-    mine = sums[-1]
-    others = [swap(mine, "layer", lambda i: i ^ other) for other in range(1, layers)]
-    return rescale(squares, [mine, *others], width)
+    all_sums = lax.all_to_all(jnp.broadcast_to(sums[-1], (layers, *sums[-1].shape)), "layer", 0, 0, tiled=True)
+    return rescale(squares, all_sums, width)
 
 
 def solution(mesh):

time: 66.3 us -> 100 us (1.51)
  waiting for transfers between devices: 17.8 us -> 28.7 us
  local copies, waits for them, and re-layouts: 0.01 us -> 9.94 us
  blocking collectives: 0 us -> 8.32 us
  Pallas kernels: 20.6 us -> 24.7 us
    ppermute x19 -> x8, starting transfers between devices: 27.6 us -> 8.7 us  [swap(): lax.ppermute(block, axis, [(partner(i), i) for i in range(lax.axis_size(a...]
    all_to_all x0 -> x4, starting transfers between devices: none -> 18.9 us  [add_up(): strips.append((kept, lax.all_to_all(send, 'layer', 0, 0, tiled=True)))]
    all_to_all x0 -> x4, waiting for transfers between devices: none -> 13 us  [add_up(): strips.append((kept, lax.all_to_all(send, 'layer', 0, 0, tiled=True)))]
    unnamed x6 -> x30, local copies, waits for them, and re-layouts: 0.01 us -> 9.93 us
    all_to_all x0 -> x1, blocking collectives: none -> 8.32 us  [shards(): lax.all_to_all(jnp.broadcast_to(sums[-1], (layers, *sums[-1].shape)), 'la...]
    pallas_call x17 -> x13, Pallas kernels: 20.6 us -> 24.7 us  [call(): pl.pallas_call(kernel, out_shape=out_shape, in_specs=in_specs, out_specs=...]
    ppermute x19 -> x8, waiting for transfers between devices: 17.8 us -> 15.7 us  [swap(): lax.ppermute(block, axis, [(partner(i), i) for i in range(lax.axis_size(a...]
  transfers between devices with their start and end apart: 19 -> 12, of which waited for: 9 -> 6; matrix products, arithmetic and copies ran while one was open for 0% -> 0% of each run, Pallas kernels for 22% -> 16%
where the time goes in v4:
time: 100 us; the launch traced here: 99.3 us
  waiting for transfers between devices  28.7 us (29%)
  starting transfers between devices  27.6 us (28%)
  Pallas kernels  24.7 us (25%)
  local copies, waits for them, and re-layouts  9.94 us (10%)
  blocking collectives  8.32 us (8%)
    pallas_call x13, Pallas kernels, call(): pl.pallas_call(kernel, out_shape=out_shape, in_specs=in_specs, out_specs=...  24.7 us
    all_to_all x4, starting transfers between devices, add_up(): strips.append((kept, lax.all_to_all(send, 'layer', 0, 0, tiled=True)))  18.9 us
    ppermute x8, waiting for transfers between devices, swap(): lax.ppermute(block, axis, [(partner(i), i) for i in range(lax.axis_size(a...  15.7 us
    all_to_all x4, waiting for transfers between devices, add_up(): strips.append((kept, lax.all_to_all(send, 'layer', 0, 0, tiled=True)))  13 us
    unnamed x30, local copies, waits for them, and re-layouts  9.93 us
    ppermute x8, starting transfers between devices, swap(): lax.ppermute(block, axis, [(partner(i), i) for i in range(lax.axis_size(a...  8.7 us
    all_to_all x1, blocking collectives, shards(): lax.all_to_all(jnp.broadcast_to(sums[-1], (layers, *sums[-1].shape)), 'la...  8.32 us
  transfers between devices with their start and end apart: 12, of which 6 were waited for; matrix products, arithmetic and copies ran while one was open for 0% of the time, Pallas kernels for 16%

profile of v4, /device:TPU:0, one launch (start us, length us, event | category | flops | bytes accessed | tf_op | source)
XLA Modules:
  0.0 99.3 jit_solution(3439561825937309350)
XLA Ops:
  0.0 5.7 %first_products.1 = (s16[1040,128]{1,0:T(8,128)(2,1)S(1)}, s16[1040,128]{1,0:T(8,128)(2,1)}, bf16[1024,2048]{1,0:T(8,128)(2,1)S(1)}, bf16[2048,1536]{1,0:T(8,128)(2,1)S(1)}, bf16[2048,512]{1,0:T(8,128)(2,1)S(1)}) custom-call(s32[6,1,32]{2,1,0:T(1,128)} %bitcast.3, s32[6,1,32]{2,1,0:T(1,128)} %bitcast.7, bf16[1,2048,1536]{2,1,0:T(8,128)(2,1)} %flow_hbm.1, ...), custom_call_target="tpu_custom_call" | custom-call | flops 1 | bytes 1 | tf_op jit(solution)/shard_map/first_products/pallas_call | solution.py:32
  5.7 3.4 %collective-permute-start = (s16[1040,128]{1,0:T(8,128)(2,1)S(1)}, s16[1040,128]{1,0:T(8,128)(2,1)S(1)}, u32[]{:S(2)}, u32[]{:S(2)}) collective-permute-start(s16[1040,128]{1,0:T(8,128)(2,1)S(1)} %get-tuple-element.49), channel_id=1, source_target_pairs={{28,0},{8,4},{4,8},{16,12},{12,16},{24,20},{20,24},{0,28},{29,1},{... | collective-permute-start | bytes 798728 | tf_op jit(solution)/shard_map/ppermute | solution.py:24
  9.1 4.4 %own_int_products_0.1 = (f32[1536,256]{1,0:T(8,128)S(1)}, s16[1040,128]{1,0:T(8,128)(2,1)S(1)}, s16[1040,128]{1,0:T(8,128)(2,1)}, bf16[512,2048]{1,0:T(8,128)(2,1)S(1)}) custom-call(s32[6,1,32]{2,1,0:T(1,128)S(1)} %bitcast.4, s32[6,1,32]{2,1,0:T(1,128)S(1)} %bitcast.8, bf16[2048,1536]{1,0:T(8,128)(2,1)S(1)} %get-tuple-element.44.graph_ref, ...), custom_call_target="tpu_custom_call" | custom-call | flops 1 | bytes 1 | tf_op jit(solution)/shard_map/own_int_products_0/pallas_call | solution.py:32
  13.6 1.6 %collective-permute-done.ext_ref = s16[1040,128]{1,0:T(8,128)(2,1)S(1)} collective-permute-done((s16[1040,128]{1,0:T(8,128)(2,1)S(1)}, s16[1040,128]{1,0:T(8,128)(2,1)S(1)}, u32[]{:S(2)}, u32[]{:S(2)}) %collective-permute-start) | collective-permute-done | bytes 266272 | tf_op jit(solution)/shard_map/ppermute | solution.py:24
  15.3 1.8 %join_0_0.1 = (f32[384,128]{1,0:T(8,128)S(1)}, s16[4,400,128]{2,1,0:T(8,128)(2,1)}) custom-call(s32[1,2,6]{2,1,0:T(2,128)S(1)} %bitcast.11, f32[1536,256]{1,0:T(8,128)S(1)} %get-tuple-element.47.own_ref, s16[1040,128]{1,0:T(8,128)(2,1)S(1)} %collective-permute-done.ext_ref, s16[1040,128]{1,0:T(8,128)(2,1)S(1)} %collective-permute-done.1.int_ref), custom_call_target="tpu_custom_call" | custom-call | flops 1 | bytes 1 | tf_op jit(solution)/shard_map/join_0_0/pallas_call | solution.py:32
  17.0 1.1 %copy-done.6 = f32[1536,256]{1,0:T(8,128)} copy-done((f32[1536,256]{1,0:T(8,128)}, f32[1536,256]{1,0:T(8,128)S(1)}, u32[]{:S(2)}) %copy-start.6) | copy-done | bytes 1572888
  18.2 6.3 %all-to-all-start = ((s16[4,400,128]{2,1,0:T(8,128)(2,1)}), s16[4,400,128]{2,1,0:T(8,128)(2,1)S(1)}, u32[]{:S(2)}, u32[]{:S(2)}) async-start(s16[4,400,128]{2,1,0:T(8,128)(2,1)} %get-tuple-element.52), calls=%async_computation | async-start | bytes 819200 | tf_op jit(solution)/shard_map/all_to_all | solution.py:400
  24.5 0.7 collective-permute-start.2
  25.2 2.8 %copy-done.1 = bf16[2048,1536]{1,0:T(8,128)(2,1)S(1)} copy-done((bf16[2048,1536]{1,0:T(8,128)(2,1)S(1)}, bf16[2048,1536]{1,0:T(8,128)(2,1)}, u32[]{:S(2)}) %copy-start.1) | copy-done | bytes 6291480
  28.0 2.2 %copy-done.3 = bf16[1024,2048]{1,0:T(8,128)(2,1)S(1)} copy-done((bf16[1024,2048]{1,0:T(8,128)(2,1)S(1)}, bf16[1024,2048]{1,0:T(8,128)(2,1)}, u32[]{:S(2)}) %copy-start.3) | copy-done | bytes 4194328
  30.2 3.5 %ext_int_products_1.1 = (s16[1040,128]{1,0:T(8,128)(2,1)S(1)}, s16[1040,128]{1,0:T(8,128)(2,1)S(1)}, s16[1040,128]{1,0:T(8,128)(2,1)S(1)}, s16[1040,128]{1,0:T(8,128)(2,1)S(1)}) custom-call(s32[6,1,32]{2,1,0:T(1,128)S(1)} %bitcast.5, s32[6,1,32]{2,1,0:T(1,128)S(1)} %bitcast.9, bf16[2048,1536]{1,0:T(8,128)(2,1)S(1)} %copy-done.1, ...), custom_call_target="tpu_custom_call" | custom-call | flops 1 | bytes 1 | tf_op jit(solution)/shard_map/ext_int_products_1/pallas_call | solution.py:32
  33.8 0.7 copy-done.12
  34.5 0.7 copy-done.13
  35.2 0.7 copy-done.14
  35.9 1.7 %copy-done.5 = bf16[512,2048]{1,0:T(8,128)(2,1)S(1)} copy-done((bf16[512,2048]{1,0:T(8,128)(2,1)S(1)}, bf16[512,2048]{1,0:T(8,128)(2,1)}, u32[]{:S(2)}) %copy-start.5) | copy-done | bytes 2097176
  37.6 2.5 %own_products_1.1.own_ref = f32[1536,256]{1,0:T(8,128)S(1)} custom-call(s32[6,1,32]{2,1,0:T(1,128)S(1)} %bitcast.6, s32[6,1,32]{2,1,0:T(1,128)S(1)} %bitcast.10, bf16[2048,1536]{1,0:T(8,128)(2,1)S(1)} %copy-done.1, bf16[1024,2048]{1,0:T(8,128)(2,1)S(1)} %copy-done.3, bf16[512,2048]{1,0:T(8,128)(2,1)S(1)} %copy-done.5), custom_call_target="tpu_custom_call" | custom-call | flops 1 | bytes 1 | tf_op jit(solution)/shard_map/own_products_1/pallas_call | solution.py:32
  40.1 1.8 %join_0_128.1 = (f32[384,128]{1,0:T(8,128)S(1)}, s16[4,400,128]{2,1,0:T(8,128)(2,1)}) custom-call(s32[1,2,6]{2,1,0:T(2,128)S(1)} %bitcast.12, f32[1536,256]{1,0:T(8,128)S(1)} %copy-done.7, s16[1040,128]{1,0:T(8,128)(2,1)S(1)} %collective-permute-done.2.ext_ref, s16[1040,128]{1,0:T(8,128)(2,1)S(1)} %collective-permute-done.3.int_ref), custom_call_target="tpu_custom_call" | custom-call | flops 1 | bytes 1 | tf_op jit(solution)/shard_map/join_0_128/pallas_call | solution.py:32
  41.8 4.8 %all-to-all-start.1 = ((s16[4,400,128]{2,1,0:T(8,128)(2,1)}), s16[4,400,128]{2,1,0:T(8,128)(2,1)S(1)}, u32[]{:S(2)}, u32[]{:S(2)}) async-start(s16[4,400,128]{2,1,0:T(8,128)(2,1)} %get-tuple-element.60), calls=%async_computation.1 | async-start | bytes 819200 | tf_op jit(solution)/shard_map/all_to_all | solution.py:400
  46.7 0.2 collective-permute-start.5
  46.9 2.5 %collective-permute-start.4 = (s16[1040,128]{1,0:T(8,128)(2,1)}, s16[1040,128]{1,0:T(8,128)(2,1)S(1)}, u32[]{:S(2)}, u32[]{:S(2)}) collective-permute-start(s16[1040,128]{1,0:T(8,128)(2,1)} %copy-done.13), channel_id=1, source_target_pairs={{28,0},{8,4},{4,8},{16,12},{12,16},{24,20},{20,24},{0,28},{29,1},{... | collective-permute-start | bytes 798728 | tf_op jit(solution)/shard_map/ppermute | solution.py:24
  49.5 6.4 %collective-permute-done.4.ext_ref = s16[1040,128]{1,0:T(8,128)(2,1)S(1)} collective-permute-done((s16[1040,128]{1,0:T(8,128)(2,1)}, s16[1040,128]{1,0:T(8,128)(2,1)S(1)}, u32[]{:S(2)}, u32[]{:S(2)}) %collective-permute-start.4) | collective-permute-done | bytes 266272 | tf_op jit(solution)/shard_map/ppermute | solution.py:24
  55.9 1.8 %join_1_0.1 = (f32[384,128]{1,0:T(8,128)S(1)}, s16[4,400,128]{2,1,0:T(8,128)(2,1)}) custom-call(s32[1,2,6]{2,1,0:T(2,128)S(1)} %bitcast.13, f32[1536,256]{1,0:T(8,128)S(1)} %own_products_1.1.own_ref, s16[1040,128]{1,0:T(8,128)(2,1)S(1)} %collective-permute-done.4.ext_ref, s16[1040,128]{1,0:T(8,128)(2,1)S(1)} %collective-permute-done.5.int_ref), custom_call_target="tpu_custom_call" | custom-call | flops 1 | bytes 1 | tf_op jit(solution)/shard_map/join_1_0/pallas_call | solution.py:32
  57.7 1.7 %all-to-all-done.1.got_ref = s16[4,400,128]{2,1,0:T(8,128)(2,1)S(1)} async-done(((s16[4,400,128]{2,1,0:T(8,128)(2,1)}), s16[4,400,128]{2,1,0:T(8,128)(2,1)S(1)}, u32[]{:S(2)}, u32[]{:S(2)}) %all-to-all-start.1) | async-done | bytes 409632 | tf_op jit(solution)/shard_map/all_to_all | solution.py:400
  59.4 3.5 %all-to-all-start.2 = ((s16[4,400,128]{2,1,0:T(8,128)(2,1)}), s16[4,400,128]{2,1,0:T(8,128)(2,1)S(1)}, u32[]{:S(2)}, u32[]{:S(2)}) async-start(s16[4,400,128]{2,1,0:T(8,128)(2,1)} %get-tuple-element.67), calls=%async_computation.2 | async-start | bytes 819200 | tf_op jit(solution)/shard_map/all_to_all | solution.py:400
  62.8 1.8 %collective-permute-start.6 = (s16[1040,128]{1,0:T(8,128)(2,1)}, s16[1040,128]{1,0:T(8,128)(2,1)S(1)}, u32[]{:S(2)}, u32[]{:S(2)}) collective-permute-start(s16[1040,128]{1,0:T(8,128)(2,1)} %copy-done.12), channel_id=1, source_target_pairs={{28,0},{8,4},{4,8},{16,12},{12,16},{24,20},{20,24},{0,28},{29,1},{... | collective-permute-start | bytes 798728 | tf_op jit(solution)/shard_map/ppermute | solution.py:24
  64.7 7.7 %collective-permute-done.6.ext_ref = s16[1040,128]{1,0:T(8,128)(2,1)S(1)} collective-permute-done((s16[1040,128]{1,0:T(8,128)(2,1)}, s16[1040,128]{1,0:T(8,128)(2,1)S(1)}, u32[]{:S(2)}, u32[]{:S(2)}) %collective-permute-start.6) | collective-permute-done | bytes 266272 | tf_op jit(solution)/shard_map/ppermute | solution.py:24
  72.4 1.8 %join_1_128.1 = (f32[384,128]{1,0:T(8,128)S(1)}, s16[4,400,128]{2,1,0:T(8,128)(2,1)}) custom-call(s32[1,2,6]{2,1,0:T(2,128)S(1)} %bitcast.14, f32[1536,256]{1,0:T(8,128)S(1)} %own_products_1.1.own_ref, s16[1040,128]{1,0:T(8,128)(2,1)S(1)} %collective-permute-done.6.ext_ref, s16[1040,128]{1,0:T(8,128)(2,1)S(1)} %collective-permute-done.7.int_ref), custom_call_target="tpu_custom_call" | custom-call | flops 1 | bytes 1 | tf_op jit(solution)/shard_map/join_1_128/pallas_call | solution.py:32
  74.2 0.7 all-to-all-done.2.got_ref
  74.9 4.3 %all-to-all-start.3 = ((s16[4,400,128]{2,1,0:T(8,128)(2,1)}), s16[4,400,128]{2,1,0:T(8,128)(2,1)S(1)}, u32[]{:S(2)}, u32[]{:S(2)}) async-start(s16[4,400,128]{2,1,0:T(8,128)(2,1)} %get-tuple-element.75), calls=%async_computation.3 | async-start | bytes 819200 | tf_op jit(solution)/shard_map/all_to_all | solution.py:400
  79.3 10.5 %all-to-all-done.3.got_ref = s16[4,400,128]{2,1,0:T(8,128)(2,1)S(1)} async-done(((s16[4,400,128]{2,1,0:T(8,128)(2,1)}), s16[4,400,128]{2,1,0:T(8,128)(2,1)S(1)}, u32[]{:S(2)}, u32[]{:S(2)}) %all-to-all-start.3) | async-done | bytes 409632 | tf_op jit(solution)/shard_map/all_to_all | solution.py:400
  90.0 8.3 %all_to_all.25.refs_4_ = f32[4,8,512]{2,1,0:T(8,128)S(1)} all-to-all(f32[4,8,512]{2,1,0:T(8,128)S(1)} %broadcast_in_dim.3), channel_id=1, replica_groups=mesh['blk'=8,'layer'=4] {'layer'}, dimensions={0} | all-to-all | bytes 131072 | tf_op jit(solution)/shard_map/all_to_all | solution.py:417
  98.3 1.0 %rescale.1 = f32[1,384,512]{2,1,0:T(8,128)} custom-call(f32[384,128]{1,0:T(8,128)S(1)} %get-tuple-element.62.refs_0_, f32[384,128]{1,0:T(8,128)S(1)} %get-tuple-element.69.refs_1_, f32[384,128]{1,0:T(8,128)S(1)} %get-tuple-element.77.refs_2_, f32[384,128]{1,0:T(8,128)S(1)} %get-tuple-element.81.refs_3_, f32[4,8,512]{2,1,0:T(8,128)S(1)} %all_to_all.25.refs_4_), custom_call_target="tpu_custom_call" | custom-call | flops 1 | bytes 1 | tf_op jit(solution)/shard_map/rescale/pallas_call | solution.py:32
  (37 shorter events, 0.6 us)
Async XLA Ops:
  0.0 9.1 %copy-start.8 = (s32[1,32,6]{1,0,2:T(1,128)S(1)}, s32[1,32,6]{1,0,2:T(1,128)}, u32[]{:S(2)}) copy-start(s32[1,32,6]{1,0,2:T(1,128)} %param.7) | copy-start | bytes 2308
  0.0 9.1 %copy-start.9 = (s32[1,32,6]{1,0,2:T(1,128)S(1)}, s32[1,32,6]{1,0,2:T(1,128)}, u32[]{:S(2)}) copy-start(s32[1,32,6]{1,0,2:T(1,128)} %param.8) | copy-start | bytes 2308
  5.7 7.9 %copy-start = (bf16[2048,1536]{1,0:T(8,128)(2,1)}, bf16[2048,1536]{1,0:T(8,128)(2,1)S(1)}, u32[]{:S(2)}) copy-start(bf16[2048,1536]{1,0:T(8,128)(2,1)S(1)} %get-tuple-element.44.graph_ref) | copy-start | bytes 18874372
  5.7 7.8 %copy-start.2 = (bf16[1024,2048]{1,0:T(8,128)(2,1)}, bf16[1024,2048]{1,0:T(8,128)(2,1)S(1)}, u32[]{:S(2)}) copy-start(bf16[1024,2048]{1,0:T(8,128)(2,1)S(1)} %get-tuple-element.45.ext_rows_ref) | copy-start | bytes 12582916
  5.7 9.5 %collective-permute-start = (s16[1040,128]{1,0:T(8,128)(2,1)S(1)}, s16[1040,128]{1,0:T(8,128)(2,1)S(1)}, u32[]{:S(2)}, u32[]{:S(2)}) collective-permute-start(s16[1040,128]{1,0:T(8,128)(2,1)S(1)} %get-tuple-element.49), channel_id=1, source_target_pairs={{28,0},{8,4},{4,8},{16,12},{12,16},{24,20},{20,24},{0,28},{29,1},{... | collective-permute-start | bytes 798728 | tf_op jit(solution)/shard_map/ppermute | solution.py:24
  9.1 6.1 %copy-start.10 = (s32[1,6,2]{1,2,0:T(2,128)S(1)}, s32[1,6,2]{1,2,0:T(2,128)}, u32[]{:S(2)}) copy-start(s32[1,6,2]{1,2,0:T(2,128)} %param.9) | copy-start | bytes 148
  13.6 20.2 %copy-start.4 = (bf16[512,2048]{1,0:T(8,128)(2,1)}, bf16[512,2048]{1,0:T(8,128)(2,1)S(1)}, u32[]{:S(2)}) copy-start(bf16[512,2048]{1,0:T(8,128)(2,1)S(1)} %get-tuple-element.54.int_rows_ref) | copy-start | bytes 6291460
  13.6 1.7 %collective-permute-start.1 = (s16[1040,128]{1,0:T(8,128)(2,1)S(1)}, s16[1040,128]{1,0:T(8,128)(2,1)S(1)}, u32[]{:S(2)}, u32[]{:S(2)}) collective-permute-start(s16[1040,128]{1,0:T(8,128)(2,1)S(1)} %get-tuple-element.50), channel_id=1, source_target_pairs={{4,0},{0,4},{12,8},{8,12},{20,16},{16,20},{28,24},{24,28},{5,1},{1... | collective-permute-start | bytes 798728 | tf_op jit(solution)/shard_map/ppermute | solution.py:24
  17.0 1.1 %copy-start.6 = (f32[1536,256]{1,0:T(8,128)}, f32[1536,256]{1,0:T(8,128)S(1)}, u32[]{:S(2)}) copy-start(f32[1536,256]{1,0:T(8,128)S(1)} %get-tuple-element.47.own_ref) | copy-start | bytes 4718596
  18.2 23.7 %all-to-all-start = ((s16[4,400,128]{2,1,0:T(8,128)(2,1)}), s16[4,400,128]{2,1,0:T(8,128)(2,1)S(1)}, u32[]{:S(2)}, u32[]{:S(2)}) async-start(s16[4,400,128]{2,1,0:T(8,128)(2,1)} %get-tuple-element.52), calls=%async_computation | async-start | bytes 819200 | tf_op jit(solution)/shard_map/all_to_all | solution.py:400
  24.5 15.5 %collective-permute-start.2 = (s16[1040,128]{1,0:T(8,128)(2,1)}, s16[1040,128]{1,0:T(8,128)(2,1)S(1)}, u32[]{:S(2)}, u32[]{:S(2)}) collective-permute-start(s16[1040,128]{1,0:T(8,128)(2,1)} %get-tuple-element.58), channel_id=1, source_target_pairs={{28,0},{8,4},{4,8},{16,12},{12,16},{24,20},{20,24},{0,28},{29,1},{... | collective-permute-start | bytes 798728 | tf_op jit(solution)/shard_map/ppermute | solution.py:24
  25.2 14.8 %collective-permute-start.3 = (s16[1040,128]{1,0:T(8,128)(2,1)}, s16[1040,128]{1,0:T(8,128)(2,1)S(1)}, u32[]{:S(2)}, u32[]{:S(2)}) collective-permute-start(s16[1040,128]{1,0:T(8,128)(2,1)} %get-tuple-element.59), channel_id=1, source_target_pairs={{4,0},{0,4},{12,8},{8,12},{20,16},{16,20},{28,24},{24,28},{5,1},{1... | collective-permute-start | bytes 798728 | tf_op jit(solution)/shard_map/ppermute | solution.py:24
  25.2 2.8 %copy-start.1 = (bf16[2048,1536]{1,0:T(8,128)(2,1)S(1)}, bf16[2048,1536]{1,0:T(8,128)(2,1)}, u32[]{:S(2)}) copy-start(bf16[2048,1536]{1,0:T(8,128)(2,1)} %copy-done) | copy-start | bytes 18874372
  28.0 2.2 %copy-start.3 = (bf16[1024,2048]{1,0:T(8,128)(2,1)S(1)}, bf16[1024,2048]{1,0:T(8,128)(2,1)}, u32[]{:S(2)}) copy-start(bf16[1024,2048]{1,0:T(8,128)(2,1)} %copy-done.2) | copy-start | bytes 12582916
  33.8 0.7 copy-start.12
  34.5 0.7 copy-start.13
  35.2 0.7 copy-start.14
  35.9 4.2 %copy-start.11 = (s16[1040,128]{1,0:T(8,128)(2,1)}, s16[1040,128]{1,0:T(8,128)(2,1)S(1)}, u32[]{:S(2)}) copy-start(s16[1040,128]{1,0:T(8,128)(2,1)S(1)} %get-tuple-element.74) | copy-start | bytes 798724
  35.9 1.7 %copy-start.5 = (bf16[512,2048]{1,0:T(8,128)(2,1)S(1)}, bf16[512,2048]{1,0:T(8,128)(2,1)}, u32[]{:S(2)}) copy-start(bf16[512,2048]{1,0:T(8,128)(2,1)} %copy-done.4) | copy-start | bytes 6291460
  37.6 2.5 %copy-start.7 = (f32[1536,256]{1,0:T(8,128)S(1)}, f32[1536,256]{1,0:T(8,128)}, u32[]{:S(2)}) copy-start(f32[1536,256]{1,0:T(8,128)} %copy-done.6) | copy-start | bytes 4718596
  41.8 17.5 %all-to-all-start.1 = ((s16[4,400,128]{2,1,0:T(8,128)(2,1)}), s16[4,400,128]{2,1,0:T(8,128)(2,1)S(1)}, u32[]{:S(2)}, u32[]{:S(2)}) async-start(s16[4,400,128]{2,1,0:T(8,128)(2,1)} %get-tuple-element.60), calls=%async_computation.1 | async-start | bytes 819200 | tf_op jit(solution)/shard_map/all_to_all | solution.py:400
  46.7 2.8 %collective-permute-start.5 = (s16[1040,128]{1,0:T(8,128)(2,1)}, s16[1040,128]{1,0:T(8,128)(2,1)S(1)}, u32[]{:S(2)}, u32[]{:S(2)}) collective-permute-start(s16[1040,128]{1,0:T(8,128)(2,1)} %copy-done.14), channel_id=1, source_target_pairs={{4,0},{0,4},{12,8},{8,12},{20,16},{16,20},{28,24},{24,28},{5,1},{1... | collective-permute-start | bytes 798728 | tf_op jit(solution)/shard_map/ppermute | solution.py:24
  46.9 9.0 %collective-permute-start.4 = (s16[1040,128]{1,0:T(8,128)(2,1)}, s16[1040,128]{1,0:T(8,128)(2,1)S(1)}, u32[]{:S(2)}, u32[]{:S(2)}) collective-permute-start(s16[1040,128]{1,0:T(8,128)(2,1)} %copy-done.13), channel_id=1, source_target_pairs={{28,0},{8,4},{4,8},{16,12},{12,16},{24,20},{20,24},{0,28},{29,1},{... | collective-permute-start | bytes 798728 | tf_op jit(solution)/shard_map/ppermute | solution.py:24
  59.4 15.5 %all-to-all-start.2 = ((s16[4,400,128]{2,1,0:T(8,128)(2,1)}), s16[4,400,128]{2,1,0:T(8,128)(2,1)S(1)}, u32[]{:S(2)}, u32[]{:S(2)}) async-start(s16[4,400,128]{2,1,0:T(8,128)(2,1)} %get-tuple-element.67), calls=%async_computation.2 | async-start | bytes 819200 | tf_op jit(solution)/shard_map/all_to_all | solution.py:400
  62.8 9.6 %collective-permute-start.6 = (s16[1040,128]{1,0:T(8,128)(2,1)}, s16[1040,128]{1,0:T(8,128)(2,1)S(1)}, u32[]{:S(2)}, u32[]{:S(2)}) collective-permute-start(s16[1040,128]{1,0:T(8,128)(2,1)} %copy-done.12), channel_id=1, source_target_pairs={{28,0},{8,4},{4,8},{16,12},{12,16},{24,20},{20,24},{0,28},{29,1},{... | collective-permute-start | bytes 798728 | tf_op jit(solution)/shard_map/ppermute | solution.py:24
  64.6 7.8 %collective-permute-start.7 = (s16[1040,128]{1,0:T(8,128)(2,1)}, s16[1040,128]{1,0:T(8,128)(2,1)S(1)}, u32[]{:S(2)}, u32[]{:S(2)}) collective-permute-start(s16[1040,128]{1,0:T(8,128)(2,1)} %copy-done.11), channel_id=1, source_target_pairs={{4,0},{0,4},{12,8},{8,12},{20,16},{16,20},{28,24},{24,28},{5,1},{1... | collective-permute-start | bytes 798728 | tf_op jit(solution)/shard_map/ppermute | solution.py:24
  74.9 15.0 %all-to-all-start.3 = ((s16[4,400,128]{2,1,0:T(8,128)(2,1)}), s16[4,400,128]{2,1,0:T(8,128)(2,1)S(1)}, u32[]{:S(2)}, u32[]{:S(2)}) async-start(s16[4,400,128]{2,1,0:T(8,128)(2,1)} %get-tuple-element.75), calls=%async_computation.3 | async-start | bytes 819200 | tf_op jit(solution)/shard_map/all_to_all | solution.py:400

commit v5 on v3

--- a/solution.py
+++ b/solution.py
@@ -28,7 +28,7 @@
     return lax.optimization_barrier((value, *others))[0]
 
 
-def call(kernel, name, operands, in_specs, out_shape, scratch_shapes=(), flops=0, moved=0, limit=SMALL_LIMIT):
+def call(kernel, name, operands, in_specs, out_shape, scratch_shapes=(), limit=SMALL_LIMIT):
     return pl.pallas_call(
         kernel,
         out_shape=out_shape,
@@ -115,95 +115,26 @@
             ref[0:HEAD, :] = head.astype(jnp.int32).astype(jnp.int16)
 
 
-def turn(chunk, a_ref, start, first, turned_ref, rows):
-    turned_ref[:, rows] = masked(chunk, a_ref, start, first).T
-
-
-def first_kernel(depth, a_hbm, b_hbm, flow_hbm, graph_hbm, *rest):
-    out_refs, (turned_ref, graph_ref, flow_ref, flow_buf, a_ref, b_ref, sems) = rest[:-7], rest[-7:]
-    inner, panel = flow_ref.shape[0], flow_ref.shape[1] // BS
-    at = Sides(inner, panel)
-    steps = inner // depth
-    small = [pltpu.make_async_copy(a_hbm, a_ref, sems.at[0]), pltpu.make_async_copy(b_hbm, b_ref, sems.at[1])]
-    side = pl.ds(pl.multiple_of(at.ext_side * BS, BS), panel * BS)
-    rest_start = (panel * BS) - at.ext_side // 2 * BS
-    others = pl.ds(pl.multiple_of(rest_start, BS), 2 * panel * BS)
-    early = pltpu.make_async_copy(graph_hbm.at[0, :, side], graph_ref.at[:, side], sems.at[2])
-    late = [
-        pltpu.make_async_copy(graph_hbm.at[0, :, others], graph_ref.at[:, others], sems.at[3]),
-        pltpu.make_async_copy(columns_of(flow_hbm, at.int_side, panel), flow_ref, sems.at[4]),
-    ]
-    source = columns_of(flow_hbm, at.starts["ext"], 2 * panel)
-    flows = []
-    for t in range(steps):
-        rows = slice(t * depth, (t + 1) * depth)
-        flows.append(pltpu.make_async_copy(source.at[rows], flow_buf.at[rows], sems.at[5 + t]))
-    for copy in small + flows[:1] + [early] + flows[1:] + late:
-        copy.start()
-    for copy in small:
-        copy.wait()
-    for t in range(steps):
-        rows = slice(t * depth, (t + 1) * depth)
-        flows[t].wait()
-        turn(flow_buf[rows, :], a_ref, at.starts["ext"], at.first + t * (depth // BS), turned_ref, rows)
-    early.wait()
-    right = masked(graph_ref[:, rows_at(at.ext_side)], b_ref, at.ext_side, at.first)
-    coded = Coded(out_refs)
-    for i in range(2 * panel):
-        coded.write(dot(turned_ref[i * BS : (i + 1) * BS, :], right), i)
-    coded.finish()
-    for copy in late:
-        copy.wait()
-
-
-def first_products(flow_t, graph, a_lines, b_lines, widths):
-    inner, width = flow_t.shape[1:]
-    panel = width // 3
-    depth = min(512, inner)
-    operands = [pltpu.with_memory_space_constraint(x, pltpu.HBM) for x in (a_lines, b_lines, flow_t, graph)]
-    return call(
-        functools.partial(first_kernel, depth),
-        "first_products",
-        operands,
-        [IN_HBM] * 4,
-        [jax.ShapeDtypeStruct((HEAD + 2 * panel, w), jnp.int16) for w in widths]
-        + [
-            pltpu.VMEM((2 * panel, inner), flow_t.dtype),
-            pltpu.VMEM((inner, width), graph.dtype),
-            pltpu.VMEM((inner, panel), flow_t.dtype),
-        ],
-        [
-            pltpu.VMEM((inner, 2 * panel), flow_t.dtype),
-            pltpu.SMEM(a_lines.shape, a_lines.dtype),
-            pltpu.SMEM(b_lines.shape, b_lines.dtype),
-            pltpu.SemaphoreType.DMA((5 + inner // depth,)),
-        ],
-        flops=2 * inner * BS * 2 * panel,
-        moved=4 * inner * width,
-        limit=PRODUCT_LIMIT,
-    )
-
-
-def product_kernel(half, wanted, turns, a_ref, b_ref, graph_ref, ext_rows_ref, int_rows_ref, *rest):
-    refs = list(rest)
-    inner, panel = graph_ref.shape[0], graph_ref.shape[1] // BS // 3
-    at = Sides(inner, panel)
-    parts = [part for part in ("ext", "own", "int") if part in wanted]
-    outs = {part: [refs.pop(0) for _ in wanted[part]] for part in parts}
-    turned_ref = refs.pop(0) if turns else int_rows_ref
+def multiply(at, parts, half, b_ref, graph_ref, ext_rows_ref, int_rows_ref, outs, ahead=None):
     coded = {part: Coded(outs[part]) for part in parts if part != "own"}
     right = []
     for part in parts:
         column = at.columns[part] + half
         right.append(masked(graph_ref[:, rows_at(column)], b_ref, column, at.first))
     right = jnp.concatenate(right, axis=1) if len(right) > 1 else right[0]
-
-    def multiply(side, start, source, names):
+    sides = (
+        (at.panel, at.starts["ext"], ext_rows_ref, ("ext", "own", "int")),
+        (at.ext_side, at.starts["ext"], ext_rows_ref, ("ext", "own")),
+        (at.int_side, at.int_side, int_rows_ref, ("own", "int")),
+    )
+    for side, start, source, names in sides:
         used = [part for part in parts if part in names]
         if not used:
-            return
+            continue
+        if ahead and source is int_rows_ref:
+            ahead()
         low = parts.index(used[0]) * BS
-        for i in range(panel):
+        for i in range(at.panel):
             block = side + i
             product = dot(source[rows_at(block - start), :], right[:, low : low + len(used) * BS])
             for j, part in enumerate(used):
@@ -212,36 +143,107 @@
                     outs[part][0][rows_at(block), :] = piece
                 else:
                     coded[part].write(piece, block - at.starts[part])
-
-    if turns:
-        turn(int_rows_ref[...], a_ref, at.int_side, at.first, turned_ref, slice(None))
-    multiply(panel, at.starts["ext"], ext_rows_ref, ("ext", "own", "int"))
-    multiply(at.ext_side, at.starts["ext"], ext_rows_ref, ("ext", "own"))
-    multiply(at.int_side, at.int_side, turned_ref, ("own", "int"))
     for part in coded:
         coded[part].finish()
 
 
-def products(a_lines, b_lines, graph, ext_rows, int_rows, half, wanted, turns=False):
-    inner, width = graph.shape
-    panel = width // 3
-    outs = []
+def take(refs, wanted):
+    parts = [part for part in ("ext", "own", "int") if part in wanted]
+    return parts, {part: [refs.pop(0) for _ in wanted[part]] for part in parts}
+
+
+def product_shapes(wanted, width):
+    shapes = []
     for part in ("ext", "own", "int"):
         for w in wanted.get(part, ()):
             if part == "own":
-                outs.append(jax.ShapeDtypeStruct((width, w), jnp.float32))
+                shapes.append(jax.ShapeDtypeStruct((width, w), jnp.float32))
             else:
-                outs.append(jax.ShapeDtypeStruct((HEAD + 2 * panel, w), jnp.int16))
-    if turns:
-        outs.append(pltpu.VMEM((panel, inner), graph.dtype))
-    return call(
-        functools.partial(product_kernel, half, wanted, turns),
+                shapes.append(jax.ShapeDtypeStruct((HEAD + 2 * (width // 3), w), jnp.int16))
+    return shapes
+
+
+def first_kernel(depth, wanted, a_hbm, b_hbm, flow_hbm, graph_hbm, *rest):
+    refs = list(rest)
+    parts, outs = take(refs, wanted)
+    ext_rows_ref, int_rows_ref, graph_ref, ext_buf, int_buf, a_ref, b_ref, sems = refs
+    inner, panel = int_buf.shape[0], int_buf.shape[1] // BS
+    at = Sides(inner, panel)
+    steps = inner // depth
+    small = [pltpu.make_async_copy(a_hbm, a_ref, sems.at[0]), pltpu.make_async_copy(b_hbm, b_ref, sems.at[1])]
+    side = pl.ds(pl.multiple_of(at.ext_side * BS, BS), panel * BS)
+    others = pl.ds(pl.multiple_of((panel * BS) - at.ext_side // 2 * BS, BS), 2 * panel * BS)
+    graphs = [
+        pltpu.make_async_copy(graph_hbm.at[0, :, side], graph_ref.at[:, side], sems.at[2]),
+        pltpu.make_async_copy(graph_hbm.at[0, :, others], graph_ref.at[:, others], sems.at[3]),
+    ]
+
+    def row_copies(start, buf, sem):
+        source = columns_of(flow_hbm, start, buf.shape[1] // BS)
+        for t in range(steps):
+            rows = slice(t * depth, (t + 1) * depth)
+            yield pltpu.make_async_copy(source.at[rows], buf.at[rows], sems.at[sem + t])
+
+    ext_copies = list(row_copies(at.starts["ext"], ext_buf, 4))
+    int_copies = list(row_copies(at.int_side, int_buf, 4 + steps))
+    for copy in small + ext_copies[:1] + graphs[:1] + ext_copies[1:] + int_copies + graphs[1:]:
+        copy.start()
+    for copy in small:
+        copy.wait()
+
+    def turn(copies, buf, start, turned_ref):
+        for t, copy in enumerate(copies):
+            copy.wait()
+            rows = slice(t * depth, (t + 1) * depth)
+            turned_ref[:, rows] = masked(buf[rows, :], a_ref, start, at.first + t * (depth // BS)).T
+
+    turn(ext_copies, ext_buf, at.starts["ext"], ext_rows_ref)
+    for copy in graphs:
+        copy.wait()
+    turn_int = functools.partial(turn, int_copies, int_buf, at.int_side, int_rows_ref)
+    multiply(at, parts, 0, b_ref, graph_ref, ext_rows_ref, int_rows_ref, outs, turn_int)
+
+
+def first_products(flow_t, graph, a_lines, b_lines, wanted):
+    inner, width = flow_t.shape[1:]
+    panel = width // 3
+    depth = min(512, inner)
+    operands = [pltpu.with_memory_space_constraint(x, pltpu.HBM) for x in (a_lines, b_lines, flow_t, graph)]
+    return call(
+        functools.partial(first_kernel, depth, wanted),
+        "first_products",
+        operands,
+        [IN_HBM] * 4,
+        product_shapes(wanted, width)
+        + [
+            pltpu.VMEM((2 * panel, inner), flow_t.dtype),
+            pltpu.VMEM((panel, inner), flow_t.dtype),
+            pltpu.VMEM((inner, width), graph.dtype),
+        ],
+        [
+            pltpu.VMEM((inner, 2 * panel), flow_t.dtype),
+            pltpu.VMEM((inner, panel), flow_t.dtype),
+            pltpu.SMEM(a_lines.shape, a_lines.dtype),
+            pltpu.SMEM(b_lines.shape, b_lines.dtype),
+            pltpu.SemaphoreType.DMA((4 + 2 * (inner // depth),)),
+        ],
+        limit=PRODUCT_LIMIT,
+    )
+
+
+def product_kernel(half, wanted, b_ref, graph_ref, ext_rows_ref, int_rows_ref, *rest):
+    parts, outs = take(list(rest), wanted)
+    inner, panel = graph_ref.shape[0], graph_ref.shape[1] // BS // 3
+    multiply(Sides(inner, panel), parts, half, b_ref, graph_ref, ext_rows_ref, int_rows_ref, outs)
+
+
+def products(b_lines, graph, ext_rows, int_rows, half, wanted):
+    return call(
+        functools.partial(product_kernel, half, wanted),
         "_".join(wanted) + f"_products_{half}",
-        (a_lines, b_lines, graph, ext_rows, int_rows),
-        [IN_SMEM, IN_SMEM] + [IN_VMEM] * 3,
-        outs,
-        flops=2 * inner * BS * sum(width if part == "own" else 2 * panel for part in wanted),
-        moved=2 * inner * BS,
+        (b_lines, graph, ext_rows, int_rows),
+        [IN_SMEM] + [IN_VMEM] * 3,
+        product_shapes(wanted, graph.shape[1]),
         limit=PRODUCT_LIMIT,
     )
 
@@ -308,7 +310,6 @@
         [IN_SMEM] + [IN_VMEM] * 3,
         strips_shapes(layers // 2, rows, width),
         [pltpu.VMEM((height, width), jnp.float32)],
-        moved=8 * height * width,
     )
 
 
@@ -329,7 +330,6 @@
         [IN_VMEM] * 2,
         strips_shapes(strips // 2, rows, width),
         [pltpu.VMEM((strips * rows, width), jnp.float32)],
-        moved=8 * kept.size,
     )
 
 
@@ -353,7 +353,6 @@
             jax.ShapeDtypeStruct((rows, width), jnp.float32),
             jax.ShapeDtypeStruct((8, width + sum(sums.shape[1] for sums in earlier)), jnp.float32),
         ],
-        moved=8 * kept.size,
     )
 
 
@@ -377,7 +376,6 @@
         (*squares, *sums),
         [IN_VMEM] * (len(squares) + len(sums)),
         jax.ShapeDtypeStruct((1, rows, width), jnp.float32),
-        moved=8 * rows * width,
     )
 
 
@@ -400,23 +398,27 @@
     chunks = panel // LANES
     fine = (LANES,) * (BS // LANES)
     per_half = len(fine)
-    *ext_parts, ext_rows, graph, flow_rest = first_products(flow_t, graph, a_lines, b_lines, fine)
-    ext = [swap(part, "blk", other_chip) for part in ext_parts]
-    wanted = {"own": (BS,), "int": fine}
-    own, *int_parts, int_rows = products(a_lines, b_lines, graph, ext_rows, flow_rest, 0, wanted, turns=True)
-    owns = [own]
-    int_ = [swap(part, "blk", same_chip) for part in int_parts]
-    latest = [own]
+    ext, int_, owns, latest = [], [], [], []
 
     def ordered(value):
         return after(value, latest[-1])
 
-    def more_products(half):
-        parts = products(ordered(a_lines), b_lines, graph, ext_rows, int_rows, half, {"ext": fine, "int": fine})
+    def send_sides(parts):
         ext.extend(swap(part, "blk", other_chip) for part in parts[:per_half])
         int_.extend(swap(part, "blk", same_chip) for part in parts[per_half:])
+
+    both = {"ext": fine, "int": fine}
+    *parts, ext_rows, int_rows, graph = first_products(flow_t, graph, a_lines, b_lines, both)
+    send_sides(parts)
+    latest.append(parts[0])
+
+    def side_products(half):
+        parts = products(ordered(b_lines), graph, ext_rows, int_rows, half, both)
+        send_sides(parts)
         latest.append(parts[0])
-        owns.extend(products(ordered(a_lines), b_lines, graph, ext_rows, int_rows, half, {"own": (BS,)}))
+
+    def own_products(half):
+        owns.extend(products(ordered(b_lines), graph, ext_rows, int_rows, half, {"own": (BS,)}))
         latest.append(owns[-1])
 
     strips, squares, sums = [], [], []
@@ -444,15 +446,18 @@
         squares.append(squared)
         sums.append(summed)
 
+    own_products(0)
+    for half in range(1, halves):
+        side_products(half)
     for chunk in range(chunks + 2):
         if chunk < chunks:
             add_up(chunk)
+        if (chunk + 1) % per_half == 0 and len(owns) < halves:
+            own_products(len(owns))
         if 1 <= chunk <= chunks:
             scatter(chunk - 1)
         if chunk >= 2:
             finish(chunk - 2)
-        if chunk % per_half == 0 and chunk // per_half + 1 < halves:
-            more_products(chunk // per_half + 1)
 
     mine = sums[-1]
     others = [swap(mine, "layer", lambda i: i ^ other) for other in range(1, layers)]

time: 66.3 us -> 66.8 us (level)
  starting transfers between devices: 27.6 us -> 24.3 us
  Pallas kernels: 20.6 us -> 22.8 us
  waiting for transfers between devices: 17.8 us -> 19 us
    ppermute x19, starting transfers between devices: 27.6 us -> 24.3 us  [swap(): lax.ppermute(block, axis, [(partner(i), i) for i in range(lax.axis_size(a...]
    pallas_call x17, Pallas kernels: 20.6 us -> 22.8 us  [call(): pl.pallas_call(kernel, out_shape=out_shape, in_specs=in_specs, out_specs=...]
    ppermute x19, waiting for transfers between devices: 17.8 us -> 19 us  [swap(): lax.ppermute(block, axis, [(partner(i), i) for i in range(lax.axis_size(a...]
  transfers between devices with their start and end apart: 19 -> 19, of which waited for: 9 -> 8; matrix products, arithmetic and copies ran while one was open for 0% -> 0% of each run, Pallas kernels for 22% -> 20%
where the time goes in v5:
time: 66.8 us; the launch traced here: 66.3 us
  starting transfers between devices  24.3 us (36%)
  Pallas kernels  22.8 us (34%)
  waiting for transfers between devices  19 us (28%)
    ppermute x19, starting transfers between devices, swap(): lax.ppermute(block, axis, [(partner(i), i) for i in range(lax.axis_size(a...  24.3 us
    pallas_call x17, Pallas kernels, call(): pl.pallas_call(kernel, out_shape=out_shape, in_specs=in_specs, out_specs=...  22.8 us
    ppermute x19, waiting for transfers between devices, swap(): lax.ppermute(block, axis, [(partner(i), i) for i in range(lax.axis_size(a...  19 us
  transfers between devices with their start and end apart: 19, of which 8 were waited for; matrix products, arithmetic and copies ran while one was open for 0% of the time, Pallas kernels for 20%

profile of v5, /device:TPU:0, one launch (start us, length us, event | category | flops | bytes accessed | tf_op | source)
XLA Modules:
  0.0 66.3 jit_solution(3700067674196671053)
XLA Ops:
  0.0 8.6 %first_products.1 = (s16[1040,128]{1,0:T(8,128)(2,1)S(1)}, s16[1040,128]{1,0:T(8,128)(2,1)S(1)}, s16[1040,128]{1,0:T(8,128)(2,1)S(1)}, s16[1040,128]{1,0:T(8,128...) custom-call(s32[6,1,32]{2,1,0:T(1,128)} %bitcast.11, ...), custom_call_target="tpu_custom_call" | custom-call | flops 1 | bytes 1 | tf_op jit(solution)/shard_map/first_products/pallas_call | solution.py:32
  8.6 0.5 collective-permute-start.1
  9.1 3.5 %collective-permute-start = (s16[1040,128]{1,0:T(8,128)(2,1)S(1)}, s16[1040,128]{1,0:T(8,128)(2,1)S(1)}, u32[]{:S(2)}, u32[]{:S(2)}) collective-permute-start(s16[1040,128]{1,0:T(8,128)(2,1)S(1)} %get-tuple-element.55), channel_id=1, source_target_pairs={{28,0},{8,4},{4,8},{16,12},{12,16},{24,20},{20,24},{0,28},{29,1},{... | collective-permute-start | bytes 798728 | tf_op jit(solution)/shard_map/ppermute | solution.py:24
  12.7 2.4 %own_products_0.1.own_ref = f32[1536,256]{1,0:T(8,128)S(1)} custom-call(s32[6,1,32]{2,1,0:T(1,128)S(1)} %bitcast.4, bf16[2048,1536]{1,0:T(8,128)(2,1)S(1)} %get-tuple-element.57.graph_ref, bf16[1024,2048]{1,0:T(8,128)(2,1)S(1)} %get-tuple-element.58.ext_rows_ref, bf16[512,2048]{1,0:T(8,128)(2,1)S(1)} %get-tuple-element.59.int_rows_ref), custom_call_target="tpu_custom_call" | custom-call | flops 1 | bytes 1 | tf_op jit(solution)/shard_map/own_products_0/pallas_call | solution.py:32
  15.1 3.5 %ext_int_products_1.1 = (s16[1040,128]{1,0:T(8,128)(2,1)S(1)}, s16[1040,128]{1,0:T(8,128)(2,1)S(1)}, s16[1040,128]{1,0:T(8,128)(2,1)S(1)}, s16[1040,128]{1,0:T(8,128)(2,1)S(1)}) custom-call(s32[6,1,32]{2,1,0:T(1,128)S(1)} %bitcast.5, bf16[2048,1536]{1,0:T(8,128)(2,1)S(1)} %get-tuple-element.57.graph_ref, ...), custom_call_target="tpu_custom_call" | custom-call | flops 1 | bytes 1 | tf_op jit(solution)/shard_map/ext_int_products_1/pallas_call | solution.py:32
  18.6 0.9 %collective-permute-done.ext_ref = s16[1040,128]{1,0:T(8,128)(2,1)S(1)} collective-permute-done((s16[1040,128]{1,0:T(8,128)(2,1)S(1)}, s16[1040,128]{1,0:T(8,128)(2,1)S(1)}, u32[]{:S(2)}, u32[]{:S(2)}) %collective-permute-start) | collective-permute-done | bytes 266272 | tf_op jit(solution)/shard_map/ppermute | solution.py:24
  19.5 1.0 %join_0_0.1 = (f32[2,384,128]{2,1,0:T(8,128)S(1)}, s16[784,128]{1,0:T(8,128)(2,1)S(1)}) custom-call(s32[1,2,6]{2,1,0:T(2,128)S(1)} %bitcast.7, f32[1536,256]{1,0:T(8,128)S(1)} %own_products_0.1.own_ref, s16[1040,128]{1,0:T(8,128)(2,1)S(1)} %collective-permute-done.ext_ref, s16[1040,128]{1,0:T(8,128)(2,1)S(1)} %collective-permute-done.1.int_ref), custom_call_target="tpu_custom_call" | custom-call | flops 1 | bytes 1 | tf_op jit(solution)/shard_map/join_0_0/pallas_call | solution.py:32
  20.5 1.6 %collective-permute-start.4 = (s16[784,128]{1,0:T(8,128)(2,1)S(1)}, s16[784,128]{1,0:T(8,128)(2,1)S(1)}, u32[]{:S(2)}, u32[]{:S(2)}) collective-permute-start(s16[784,128]{1,0:T(8,128)(2,1)S(1)} %get-tuple-element.65), channel_id=1, source_target_pairs={{1,0},{0,1},{3,2},{2,3},{5,4},{4,5},{7,6},{6,7},{9,8},{8,9},{11,10... | collective-permute-start | bytes 602120 | tf_op jit(solution)/shard_map/ppermute | solution.py:24
  22.2 2.5 %collective-permute-start.5 = (s16[1040,128]{1,0:T(8,128)(2,1)S(1)}, s16[1040,128]{1,0:T(8,128)(2,1)S(1)}, u32[]{:S(2)}, u32[]{:S(2)}) collective-permute-start(s16[1040,128]{1,0:T(8,128)(2,1)S(1)} %get-tuple-element.61), channel_id=1, source_target_pairs={{28,0},{8,4},{4,8},{16,12},{12,16},{24,20},{20,24},{0,28},{29,1},{... | collective-permute-start | bytes 798728 | tf_op jit(solution)/shard_map/ppermute | solution.py:24
  24.7 1.7 %collective-permute-start.9 = (s16[1040,128]{1,0:T(8,128)(2,1)S(1)}, s16[1040,128]{1,0:T(8,128)(2,1)S(1)}, u32[]{:S(2)}, u32[]{:S(2)}) collective-permute-start(s16[1040,128]{1,0:T(8,128)(2,1)S(1)} %get-tuple-element.86), channel_id=1, source_target_pairs={{28,0},{8,4},{4,8},{16,12},{12,16},{24,20},{20,24},{0,28},{29,1},{... | collective-permute-start | bytes 798728 | tf_op jit(solution)/shard_map/ppermute | solution.py:24
  26.4 1.0 %join_0_128.1 = (f32[2,384,128]{2,1,0:T(8,128)S(1)}, s16[784,128]{1,0:T(8,128)(2,1)S(1)}) custom-call(s32[1,2,6]{2,1,0:T(2,128)S(1)} %bitcast.8, f32[1536,256]{1,0:T(8,128)S(1)} %own_products_0.1.own_ref, s16[1040,128]{1,0:T(8,128)(2,1)S(1)} %collective-permute-done.2.ext_ref, s16[1040,128]{1,0:T(8,128)(2,1)S(1)} %collective-permute-done.3.int_ref), custom_call_target="tpu_custom_call" | custom-call | flops 1 | bytes 1 | tf_op jit(solution)/shard_map/join_0_128/pallas_call | solution.py:32
  27.4 1.8 %collective-permute-start.7 = (s16[784,128]{1,0:T(8,128)(2,1)S(1)}, s16[784,128]{1,0:T(8,128)(2,1)S(1)}, u32[]{:S(2)}, u32[]{:S(2)}) collective-permute-start(s16[784,128]{1,0:T(8,128)(2,1)S(1)} %get-tuple-element.69), channel_id=1, source_target_pairs={{1,0},{0,1},{3,2},{2,3},{5,4},{4,5},{7,6},{6,7},{9,8},{8,9},{11,10... | collective-permute-start | bytes 602120 | tf_op jit(solution)/shard_map/ppermute | solution.py:24
  29.2 2.4 %own_products_1.1.own_ref = f32[1536,256]{1,0:T(8,128)S(1)} custom-call(s32[6,1,32]{2,1,0:T(1,128)S(1)} %bitcast.6, bf16[2048,1536]{1,0:T(8,128)(2,1)S(1)} %get-tuple-element.57.graph_ref, bf16[1024,2048]{1,0:T(8,128)(2,1)S(1)} %get-tuple-element.58.ext_rows_ref, bf16[512,2048]{1,0:T(8,128)(2,1)S(1)} %get-tuple-element.59.int_rows_ref), custom_call_target="tpu_custom_call" | custom-call | flops 1 | bytes 1 | tf_op jit(solution)/shard_map/own_products_1/pallas_call | solution.py:32
  31.7 0.2 halve_2_0.1
  31.9 2.6 %collective-permute-start.8 = (s16[400,128]{1,0:T(8,128)(2,1)S(1)}, s16[400,128]{1,0:T(8,128)(2,1)S(1)}, u32[]{:S(2)}, u32[]{:S(2)}) collective-permute-start(s16[400,128]{1,0:T(8,128)(2,1)S(1)} %get-tuple-element.74), channel_id=1, source_target_pairs={{2,0},{3,1},{0,2},{1,3},{6,4},{7,5},{4,6},{5,7},{10,8},{11,9},{8,1... | collective-permute-start | bytes 307208 | tf_op jit(solution)/shard_map/ppermute | solution.py:24
  34.5 1.0 %join_1_0.1 = (f32[2,384,128]{2,1,0:T(8,128)S(1)}, s16[784,128]{1,0:T(8,128)(2,1)S(1)}) custom-call(s32[1,2,6]{2,1,0:T(2,128)S(1)} %bitcast.9, f32[1536,256]{1,0:T(8,128)S(1)} %own_products_1.1.own_ref, s16[1040,128]{1,0:T(8,128)(2,1)S(1)} %collective-permute-done.5.ext_ref, s16[1040,128]{1,0:T(8,128)(2,1)S(1)} %collective-permute-done.6.int_ref), custom_call_target="tpu_custom_call" | custom-call | flops 1 | bytes 1 | tf_op jit(solution)/shard_map/join_1_0/pallas_call | solution.py:32
  35.5 0.4 collective-permute-start.11
  35.8 0.2 halve_2_1.1
  36.0 4.1 %collective-permute-done.8.got_ref = s16[400,128]{1,0:T(8,128)(2,1)S(1)} collective-permute-done((s16[400,128]{1,0:T(8,128)(2,1)S(1)}, s16[400,128]{1,0:T(8,128)(2,1)S(1)}, u32[]{:S(2)}, u32[]{:S(2)}) %collective-permute-start.8) | collective-permute-done | bytes 102432 | tf_op jit(solution)/shard_map/ppermute | solution.py:24
  40.2 1.0 %join_1_128.1 = (f32[2,384,128]{2,1,0:T(8,128)S(1)}, s16[784,128]{1,0:T(8,128)(2,1)S(1)}) custom-call(s32[1,2,6]{2,1,0:T(2,128)S(1)} %bitcast.10, f32[1536,256]{1,0:T(8,128)S(1)} %own_products_1.1.own_ref, s16[1040,128]{1,0:T(8,128)(2,1)S(1)} %collective-permute-done.9.ext_ref, s16[1040,128]{1,0:T(8,128)(2,1)S(1)} %collective-permute-done.10.int_ref), custom_call_target="tpu_custom_call" | custom-call | flops 1 | bytes 1 | tf_op jit(solution)/shard_map/join_1_128/pallas_call | solution.py:32
  41.3 2.9 %collective-permute-start.12 = (s16[400,128]{1,0:T(8,128)(2,1)S(1)}, s16[400,128]{1,0:T(8,128)(2,1)S(1)}, u32[]{:S(2)}, u32[]{:S(2)}) collective-permute-start(s16[400,128]{1,0:T(8,128)(2,1)S(1)} %get-tuple-element.79), channel_id=1, source_target_pairs={{2,0},{3,1},{0,2},{1,3},{6,4},{7,5},{4,6},{5,7},{10,8},{11,9},{8,1... | collective-permute-start | bytes 307208 | tf_op jit(solution)/shard_map/ppermute | solution.py:24
  44.2 0.2 halve_2_2.1
  44.5 5.1 %collective-permute-done.12.got_ref = s16[400,128]{1,0:T(8,128)(2,1)S(1)} collective-permute-done((s16[400,128]{1,0:T(8,128)(2,1)S(1)}, s16[400,128]{1,0:T(8,128)(2,1)S(1)}, u32[]{:S(2)}, u32[]{:S(2)}) %collective-permute-start.12) | collective-permute-done | bytes 102432 | tf_op jit(solution)/shard_map/ppermute | solution.py:24
  49.7 0.9 %collective-permute-done.13.got_ref = s16[784,128]{1,0:T(8,128)(2,1)S(1)} collective-permute-done((s16[784,128]{1,0:T(8,128)(2,1)S(1)}, s16[784,128]{1,0:T(8,128)(2,1)S(1)}, u32[]{:S(2)}, u32[]{:S(2)}) %collective-permute-start.13) | collective-permute-done | bytes 200736 | tf_op jit(solution)/shard_map/ppermute | solution.py:24
  50.8 1.9 %collective-permute-start.15 = (s16[400,128]{1,0:T(8,128)(2,1)S(1)}, s16[400,128]{1,0:T(8,128)(2,1)S(1)}, u32[]{:S(2)}, u32[]{:S(2)}) collective-permute-start(s16[400,128]{1,0:T(8,128)(2,1)S(1)} %get-tuple-element.97), channel_id=1, source_target_pairs={{2,0},{3,1},{0,2},{1,3},{6,4},{7,5},{4,6},{5,7},{10,8},{11,9},{8,1... | collective-permute-start | bytes 307208 | tf_op jit(solution)/shard_map/ppermute | solution.py:24
  52.7 2.7 %collective-permute-done.14.got_ref = s16[400,128]{1,0:T(8,128)(2,1)S(1)} collective-permute-done((s16[400,128]{1,0:T(8,128)(2,1)S(1)}, s16[400,128]{1,0:T(8,128)(2,1)S(1)}, u32[]{:S(2)}, u32[]{:S(2)}) %collective-permute-start.14) | collective-permute-done | bytes 102432 | tf_op jit(solution)/shard_map/ppermute | solution.py:24
  55.5 2.5 %collective-permute-done.15.got_ref = s16[400,128]{1,0:T(8,128)(2,1)S(1)} collective-permute-done((s16[400,128]{1,0:T(8,128)(2,1)S(1)}, s16[400,128]{1,0:T(8,128)(2,1)S(1)}, u32[]{:S(2)}, u32[]{:S(2)}) %collective-permute-start.15) | collective-permute-done | bytes 102432 | tf_op jit(solution)/shard_map/ppermute | solution.py:24
  58.1 2.5 %collective-permute-start.18 = (f32[8,512]{1,0:T(8,128)S(1)}, f32[8,512]{1,0:T(8,128)S(1)}, u32[]{:S(2)}, u32[]{:S(2)}) collective-permute-start(f32[8,512]{1,0:T(8,128)S(1)} %get-tuple-element.104.refs_4_), channel_id=1, source_target_pairs={{3,0},{2,1},{1,2},{0,3},{7,4},{6,5},{5,6},{4,7},{11,8},{10,9},{9,1... | collective-permute-start | bytes 49160 | tf_op jit(solution)/shard_map/ppermute | solution.py:24
  60.6 1.9 %collective-permute-start.16 = (f32[8,512]{1,0:T(8,128)S(1)}, f32[8,512]{1,0:T(8,128)S(1)}, u32[]{:S(2)}, u32[]{:S(2)}) collective-permute-start(f32[8,512]{1,0:T(8,128)S(1)} %get-tuple-element.104.refs_4_), channel_id=1, source_target_pairs={{1,0},{0,1},{3,2},{2,3},{5,4},{4,5},{7,6},{6,7},{9,8},{8,9},{11,10... | collective-permute-start | bytes 49160 | tf_op jit(solution)/shard_map/ppermute | solution.py:24
  62.6 1.1 %collective-permute-done.18.refs_7_ = f32[8,512]{1,0:T(8,128)S(1)} collective-permute-done((f32[8,512]{1,0:T(8,128)S(1)}, f32[8,512]{1,0:T(8,128)S(1)}, u32[]{:S(2)}, u32[]{:S(2)}) %collective-permute-start.18) | collective-permute-done | bytes 16416 | tf_op jit(solution)/shard_map/ppermute | solution.py:24
  63.7 1.5 %collective-permute-done.17.refs_6_ = f32[8,512]{1,0:T(8,128)S(1)} collective-permute-done((f32[8,512]{1,0:T(8,128)S(1)}, f32[8,512]{1,0:T(8,128)S(1)}, u32[]{:S(2)}, u32[]{:S(2)}) %collective-permute-start.17) | collective-permute-done | bytes 16416 | tf_op jit(solution)/shard_map/ppermute | solution.py:24
  65.3 1.0 %rescale.1 = f32[1,384,512]{2,1,0:T(8,128)} custom-call(f32[384,128]{1,0:T(8,128)S(1)} %get-tuple-element.81.refs_0_, f32[384,128]{1,0:T(8,128)S(1)} %get-tuple-element.92.refs_1_, f32[384,128]{1,0:T(8,128)S(1)} %get-tuple-element.99.refs_2_, f32[384,128]{1,0:T(8,128)S(1)} %get-tuple-element.103.refs_3_, f32[8,512]{1,0:T(8,128)S(1)} %get-tuple-element.104.refs_4_, ...), custom_call_target="tpu_custom_call" | custom-call | flops 1 | bytes 1 | tf_op jit(solution)/shard_map/rescale/pallas_call | solution.py:32
  (27 shorter events, 0.8 us)
Async XLA Ops:
  0.0 12.7 %copy-start = (s32[1,32,6]{1,0,2:T(1,128)S(1)}, s32[1,32,6]{1,0,2:T(1,128)}, u32[]{:S(2)}) copy-start(s32[1,32,6]{1,0,2:T(1,128)} %param.8) | copy-start | bytes 2308
  8.6 10.0 %collective-permute-start.1 = (s16[1040,128]{1,0:T(8,128)(2,1)S(1)}, s16[1040,128]{1,0:T(8,128)(2,1)S(1)}, u32[]{:S(2)}, u32[]{:S(2)}) collective-permute-start(s16[1040,128]{1,0:T(8,128)(2,1)S(1)} %get-tuple-element.63), channel_id=1, source_target_pairs={{4,0},{0,4},{12,8},{8,12},{20,16},{16,20},{28,24},{24,28},{5,1},{1... | collective-permute-start | bytes 798728 | tf_op jit(solution)/shard_map/ppermute | solution.py:24
  9.1 10.4 %collective-permute-start = (s16[1040,128]{1,0:T(8,128)(2,1)S(1)}, s16[1040,128]{1,0:T(8,128)(2,1)S(1)}, u32[]{:S(2)}, u32[]{:S(2)}) collective-permute-start(s16[1040,128]{1,0:T(8,128)(2,1)S(1)} %get-tuple-element.55), channel_id=1, source_target_pairs={{28,0},{8,4},{4,8},{16,12},{12,16},{24,20},{20,24},{0,28},{29,1},{... | collective-permute-start | bytes 798728 | tf_op jit(solution)/shard_map/ppermute | solution.py:24
  12.7 12.0 %collective-permute-start.2 = (s16[1040,128]{1,0:T(8,128)(2,1)S(1)}, s16[1040,128]{1,0:T(8,128)(2,1)S(1)}, u32[]{:S(2)}, u32[]{:S(2)}) collective-permute-start(s16[1040,128]{1,0:T(8,128)(2,1)S(1)} %get-tuple-element.67), channel_id=1, source_target_pairs={{28,0},{8,4},{4,8},{16,12},{12,16},{24,20},{20,24},{0,28},{29,1},{... | collective-permute-start | bytes 798728 | tf_op jit(solution)/shard_map/ppermute | solution.py:24
  12.7 13.7 %collective-permute-start.3 = (s16[1040,128]{1,0:T(8,128)(2,1)S(1)}, s16[1040,128]{1,0:T(8,128)(2,1)S(1)}, u32[]{:S(2)}, u32[]{:S(2)}) collective-permute-start(s16[1040,128]{1,0:T(8,128)(2,1)S(1)} %get-tuple-element.68), channel_id=1, source_target_pairs={{4,0},{0,4},{12,8},{8,12},{20,16},{16,20},{28,24},{24,28},{5,1},{1... | collective-permute-start | bytes 798728 | tf_op jit(solution)/shard_map/ppermute | solution.py:24
  15.1 4.4 %copy-start.1 = (s32[1,6,2]{1,2,0:T(2,128)S(1)}, s32[1,6,2]{1,2,0:T(2,128)}, u32[]{:S(2)}) copy-start(s32[1,6,2]{1,2,0:T(2,128)} %param.9) | copy-start | bytes 148
  20.5 6.9 %collective-permute-start.4 = (s16[784,128]{1,0:T(8,128)(2,1)S(1)}, s16[784,128]{1,0:T(8,128)(2,1)S(1)}, u32[]{:S(2)}, u32[]{:S(2)}) collective-permute-start(s16[784,128]{1,0:T(8,128)(2,1)S(1)} %get-tuple-element.65), channel_id=1, source_target_pairs={{1,0},{0,1},{3,2},{2,3},{5,4},{4,5},{7,6},{6,7},{9,8},{8,9},{11,10... | collective-permute-start | bytes 602120 | tf_op jit(solution)/shard_map/ppermute | solution.py:24
  22.2 9.7 %collective-permute-start.6 = (s16[1040,128]{1,0:T(8,128)(2,1)S(1)}, s16[1040,128]{1,0:T(8,128)(2,1)S(1)}, u32[]{:S(2)}, u32[]{:S(2)}) collective-permute-start(s16[1040,128]{1,0:T(8,128)(2,1)S(1)} %get-tuple-element.76), channel_id=1, source_target_pairs={{4,0},{0,4},{12,8},{8,12},{20,16},{16,20},{28,24},{24,28},{5,1},{1... | collective-permute-start | bytes 798728 | tf_op jit(solution)/shard_map/ppermute | solution.py:24
  22.2 12.3 %collective-permute-start.5 = (s16[1040,128]{1,0:T(8,128)(2,1)S(1)}, s16[1040,128]{1,0:T(8,128)(2,1)S(1)}, u32[]{:S(2)}, u32[]{:S(2)}) collective-permute-start(s16[1040,128]{1,0:T(8,128)(2,1)S(1)} %get-tuple-element.61), channel_id=1, source_target_pairs={{28,0},{8,4},{4,8},{16,12},{12,16},{24,20},{20,24},{0,28},{29,1},{... | collective-permute-start | bytes 798728 | tf_op jit(solution)/shard_map/ppermute | solution.py:24
  24.7 15.5 %collective-permute-start.9 = (s16[1040,128]{1,0:T(8,128)(2,1)S(1)}, s16[1040,128]{1,0:T(8,128)(2,1)S(1)}, u32[]{:S(2)}, u32[]{:S(2)}) collective-permute-start(s16[1040,128]{1,0:T(8,128)(2,1)S(1)} %get-tuple-element.86), channel_id=1, source_target_pairs={{28,0},{8,4},{4,8},{16,12},{12,16},{24,20},{20,24},{0,28},{29,1},{... | collective-permute-start | bytes 798728 | tf_op jit(solution)/shard_map/ppermute | solution.py:24
  26.4 13.8 %collective-permute-start.10 = (s16[1040,128]{1,0:T(8,128)(2,1)S(1)}, s16[1040,128]{1,0:T(8,128)(2,1)S(1)}, u32[]{:S(2)}, u32[]{:S(2)}) collective-permute-start(s16[1040,128]{1,0:T(8,128)(2,1)S(1)} %get-tuple-element.87), channel_id=1, source_target_pairs={{4,0},{0,4},{12,8},{8,12},{20,16},{16,20},{28,24},{24,28},{5,1},{1... | collective-permute-start | bytes 798728 | tf_op jit(solution)/shard_map/ppermute | solution.py:24
  27.4 8.4 %collective-permute-start.7 = (s16[784,128]{1,0:T(8,128)(2,1)S(1)}, s16[784,128]{1,0:T(8,128)(2,1)S(1)}, u32[]{:S(2)}, u32[]{:S(2)}) collective-permute-start(s16[784,128]{1,0:T(8,128)(2,1)S(1)} %get-tuple-element.69), channel_id=1, source_target_pairs={{1,0},{0,1},{3,2},{2,3},{5,4},{4,5},{7,6},{6,7},{9,8},{8,9},{11,10... | collective-permute-start | bytes 602120 | tf_op jit(solution)/shard_map/ppermute | solution.py:24
  31.9 8.3 %collective-permute-start.8 = (s16[400,128]{1,0:T(8,128)(2,1)S(1)}, s16[400,128]{1,0:T(8,128)(2,1)S(1)}, u32[]{:S(2)}, u32[]{:S(2)}) collective-permute-start(s16[400,128]{1,0:T(8,128)(2,1)S(1)} %get-tuple-element.74), channel_id=1, source_target_pairs={{2,0},{3,1},{0,2},{1,3},{6,4},{7,5},{4,6},{5,7},{10,8},{11,9},{8,1... | collective-permute-start | bytes 307208 | tf_op jit(solution)/shard_map/ppermute | solution.py:24
  35.5 8.7 %collective-permute-start.11 = (s16[784,128]{1,0:T(8,128)(2,1)S(1)}, s16[784,128]{1,0:T(8,128)(2,1)S(1)}, u32[]{:S(2)}, u32[]{:S(2)}) collective-permute-start(s16[784,128]{1,0:T(8,128)(2,1)S(1)} %get-tuple-element.77), channel_id=1, source_target_pairs={{1,0},{0,1},{3,2},{2,3},{5,4},{4,5},{7,6},{6,7},{9,8},{8,9},{11,10... | collective-permute-start | bytes 602120 | tf_op jit(solution)/shard_map/ppermute | solution.py:24
  41.2 9.4 %collective-permute-start.13 = (s16[784,128]{1,0:T(8,128)(2,1)S(1)}, s16[784,128]{1,0:T(8,128)(2,1)S(1)}, u32[]{:S(2)}, u32[]{:S(2)}) collective-permute-start(s16[784,128]{1,0:T(8,128)(2,1)S(1)} %get-tuple-element.88), channel_id=1, source_target_pairs={{1,0},{0,1},{3,2},{2,3},{5,4},{4,5},{7,6},{6,7},{9,8},{8,9},{11,10... | collective-permute-start | bytes 602120 | tf_op jit(solution)/shard_map/ppermute | solution.py:24
  41.3 8.4 %collective-permute-start.12 = (s16[400,128]{1,0:T(8,128)(2,1)S(1)}, s16[400,128]{1,0:T(8,128)(2,1)S(1)}, u32[]{:S(2)}, u32[]{:S(2)}) collective-permute-start(s16[400,128]{1,0:T(8,128)(2,1)S(1)} %get-tuple-element.79), channel_id=1, source_target_pairs={{2,0},{3,1},{0,2},{1,3},{6,4},{7,5},{4,6},{5,7},{10,8},{11,9},{8,1... | collective-permute-start | bytes 307208 | tf_op jit(solution)/shard_map/ppermute | solution.py:24
  44.4 11.1 %collective-permute-start.14 = (s16[400,128]{1,0:T(8,128)(2,1)S(1)}, s16[400,128]{1,0:T(8,128)(2,1)S(1)}, u32[]{:S(2)}, u32[]{:S(2)}) collective-permute-start(s16[400,128]{1,0:T(8,128)(2,1)S(1)} %get-tuple-element.90), channel_id=1, source_target_pairs={{2,0},{3,1},{0,2},{1,3},{6,4},{7,5},{4,6},{5,7},{10,8},{11,9},{8,1... | collective-permute-start | bytes 307208 | tf_op jit(solution)/shard_map/ppermute | solution.py:24
  50.8 7.2 %collective-permute-start.15 = (s16[400,128]{1,0:T(8,128)(2,1)S(1)}, s16[400,128]{1,0:T(8,128)(2,1)S(1)}, u32[]{:S(2)}, u32[]{:S(2)}) collective-permute-start(s16[400,128]{1,0:T(8,128)(2,1)S(1)} %get-tuple-element.97), channel_id=1, source_target_pairs={{2,0},{3,1},{0,2},{1,3},{6,4},{7,5},{4,6},{5,7},{10,8},{11,9},{8,1... | collective-permute-start | bytes 307208 | tf_op jit(solution)/shard_map/ppermute | solution.py:24
  58.1 5.6 %collective-permute-start.18 = (f32[8,512]{1,0:T(8,128)S(1)}, f32[8,512]{1,0:T(8,128)S(1)}, u32[]{:S(2)}, u32[]{:S(2)}) collective-permute-start(f32[8,512]{1,0:T(8,128)S(1)} %get-tuple-element.104.refs_4_), channel_id=1, source_target_pairs={{3,0},{2,1},{1,2},{0,3},{7,4},{6,5},{5,6},{4,7},{11,8},{10,9},{9,1... | collective-permute-start | bytes 49160 | tf_op jit(solution)/shard_map/ppermute | solution.py:24
  60.6 4.6 %collective-permute-start.17 = (f32[8,512]{1,0:T(8,128)S(1)}, f32[8,512]{1,0:T(8,128)S(1)}, u32[]{:S(2)}, u32[]{:S(2)}) collective-permute-start(f32[8,512]{1,0:T(8,128)S(1)} %get-tuple-element.104.refs_4_), channel_id=1, source_target_pairs={{2,0},{3,1},{0,2},{1,3},{6,4},{7,5},{4,6},{5,7},{10,8},{11,9},{8,1... | collective-permute-start | bytes 49160 | tf_op jit(solution)/shard_map/ppermute | solution.py:24
  60.6 4.6 %collective-permute-start.16 = (f32[8,512]{1,0:T(8,128)S(1)}, f32[8,512]{1,0:T(8,128)S(1)}, u32[]{:S(2)}, u32[]{:S(2)}) collective-permute-start(f32[8,512]{1,0:T(8,128)S(1)} %get-tuple-element.104.refs_4_), channel_id=1, source_target_pairs={{1,0},{0,1},{3,2},{2,3},{5,4},{4,5},{7,6},{6,7},{9,8},{8,9},{11,10... | collective-permute-start | bytes 49160 | tf_op jit(solution)/shard_map/ppermute | solution.py:24

commit v6 on v3

--- a/solution.py
+++ b/solution.py
@@ -28,7 +28,7 @@
     return lax.optimization_barrier((value, *others))[0]
 
 
-def call(kernel, name, operands, in_specs, out_shape, scratch_shapes=(), flops=0, moved=0, limit=SMALL_LIMIT):
+def call(kernel, name, operands, in_specs, out_shape, scratch_shapes=(), limit=SMALL_LIMIT):
     return pl.pallas_call(
         kernel,
         out_shape=out_shape,
@@ -115,48 +115,50 @@
             ref[0:HEAD, :] = head.astype(jnp.int32).astype(jnp.int16)
 
 
-def turn(chunk, a_ref, start, first, turned_ref, rows):
-    turned_ref[:, rows] = masked(chunk, a_ref, start, first).T
-
-
 def first_kernel(depth, a_hbm, b_hbm, flow_hbm, graph_hbm, *rest):
-    out_refs, (turned_ref, graph_ref, flow_ref, flow_buf, a_ref, b_ref, sems) = rest[:-7], rest[-7:]
+    out_ref, rows_ref, graph_ref, flow_ref, flow_buf, total, a_ref, b_ref, sems = rest
     inner, panel = flow_ref.shape[0], flow_ref.shape[1] // BS
     at = Sides(inner, panel)
     steps = inner // depth
     small = [pltpu.make_async_copy(a_hbm, a_ref, sems.at[0]), pltpu.make_async_copy(b_hbm, b_ref, sems.at[1])]
     side = pl.ds(pl.multiple_of(at.ext_side * BS, BS), panel * BS)
-    rest_start = (panel * BS) - at.ext_side // 2 * BS
-    others = pl.ds(pl.multiple_of(rest_start, BS), 2 * panel * BS)
+    others = pl.ds(pl.multiple_of((panel * BS) - at.ext_side // 2 * BS, BS), 2 * panel * BS)
     early = pltpu.make_async_copy(graph_hbm.at[0, :, side], graph_ref.at[:, side], sems.at[2])
     late = [
-        pltpu.make_async_copy(graph_hbm.at[0, :, others], graph_ref.at[:, others], sems.at[3]),
-        pltpu.make_async_copy(columns_of(flow_hbm, at.int_side, panel), flow_ref, sems.at[4]),
+        pltpu.make_async_copy(columns_of(flow_hbm, at.int_side, panel), flow_ref, sems.at[3]),
+        pltpu.make_async_copy(graph_hbm.at[0, :, others], graph_ref.at[:, others], sems.at[4]),
     ]
     source = columns_of(flow_hbm, at.starts["ext"], 2 * panel)
     flows = []
     for t in range(steps):
         rows = slice(t * depth, (t + 1) * depth)
         flows.append(pltpu.make_async_copy(source.at[rows], flow_buf.at[rows], sems.at[5 + t]))
-    for copy in small + flows[:1] + [early] + flows[1:] + late:
+    for copy in small + [early] + flows + late:
         copy.start()
     for copy in small:
         copy.wait()
     for t in range(steps):
         rows = slice(t * depth, (t + 1) * depth)
+        first = at.first + t * (depth // BS)
         flows[t].wait()
-        turn(flow_buf[rows, :], a_ref, at.starts["ext"], at.first + t * (depth // BS), turned_ref, rows)
-    early.wait()
-    right = masked(graph_ref[:, rows_at(at.ext_side)], b_ref, at.ext_side, at.first)
-    coded = Coded(out_refs)
+        turned = masked(flow_buf[rows, :], a_ref, at.starts["ext"], first).T
+        rows_ref[:, rows] = turned
+        if t == 0:
+            early.wait()
+        right = masked(graph_ref[rows, rows_at(at.ext_side)], b_ref, at.ext_side, first)
+        product = dot(turned, right[:, : out_ref.shape[1]])
+        if t < steps - 1:
+            total[...] = product if t == 0 else total[...] + product
+    coded = Coded([out_ref])
     for i in range(2 * panel):
-        coded.write(dot(turned_ref[i * BS : (i + 1) * BS, :], right), i)
+        rows = slice(i * BS, (i + 1) * BS)
+        coded.write(product[rows] if steps == 1 else total[rows, :] + product[rows], i)
     coded.finish()
     for copy in late:
         copy.wait()
 
 
-def first_products(flow_t, graph, a_lines, b_lines, widths):
+def first_products(flow_t, graph, a_lines, b_lines):
     inner, width = flow_t.shape[1:]
     panel = width // 3
     depth = min(512, inner)
@@ -166,82 +168,91 @@
         "first_products",
         operands,
         [IN_HBM] * 4,
-        [jax.ShapeDtypeStruct((HEAD + 2 * panel, w), jnp.int16) for w in widths]
-        + [
+        [
+            jax.ShapeDtypeStruct((HEAD + 2 * panel, LANES), jnp.int16),
             pltpu.VMEM((2 * panel, inner), flow_t.dtype),
             pltpu.VMEM((inner, width), graph.dtype),
             pltpu.VMEM((inner, panel), flow_t.dtype),
         ],
         [
             pltpu.VMEM((inner, 2 * panel), flow_t.dtype),
+            pltpu.VMEM((2 * panel, LANES), jnp.float32),
             pltpu.SMEM(a_lines.shape, a_lines.dtype),
             pltpu.SMEM(b_lines.shape, b_lines.dtype),
             pltpu.SemaphoreType.DMA((5 + inner // depth,)),
         ],
-        flops=2 * inner * BS * 2 * panel,
-        moved=4 * inner * width,
         limit=PRODUCT_LIMIT,
     )
 
 
-def product_kernel(half, wanted, turns, a_ref, b_ref, graph_ref, ext_rows_ref, int_rows_ref, *rest):
-    refs = list(rest)
-    inner, panel = graph_ref.shape[0], graph_ref.shape[1] // BS // 3
-    at = Sides(inner, panel)
-    parts = [part for part in ("ext", "own", "int") if part in wanted]
-    outs = {part: [refs.pop(0) for _ in wanted[part]] for part in parts}
-    turned_ref = refs.pop(0) if turns else int_rows_ref
-    coded = {part: Coded(outs[part]) for part in parts if part != "own"}
+def right_side(at, parts, half, b_ref, graph_ref):
     right = []
     for part in parts:
         column = at.columns[part] + half
         right.append(masked(graph_ref[:, rows_at(column)], b_ref, column, at.first))
-    right = jnp.concatenate(right, axis=1) if len(right) > 1 else right[0]
-
-    def multiply(side, start, source, names):
-        used = [part for part in parts if part in names]
-        if not used:
-            return
-        low = parts.index(used[0]) * BS
-        for i in range(panel):
-            block = side + i
-            product = dot(source[rows_at(block - start), :], right[:, low : low + len(used) * BS])
-            for j, part in enumerate(used):
-                piece = product[:, j * BS : (j + 1) * BS]
-                if part == "own":
-                    outs[part][0][rows_at(block), :] = piece
-                else:
-                    coded[part].write(piece, block - at.starts[part])
-
+    return jnp.concatenate(right, axis=1) if len(right) > 1 else right[0]
+
+
+def ext_kernel(b_ref, graph_ref, ext_rows_ref, *out_refs):
+    inner, panel = graph_ref.shape[0], graph_ref.shape[1] // BS // 3
+    at = Sides(inner, panel)
+    side = pl.ds(pl.multiple_of(at.ext_side * BS, BS), panel * BS)
+    right = masked(graph_ref[:, side], b_ref, at.ext_side, at.first)[:, LANES:]
+    coded = Coded(out_refs)
+    for i in range(2 * panel):
+        coded.write(dot(ext_rows_ref[i * BS : (i + 1) * BS, :], right), i)
+    coded.finish()
+
+
+def ext_products(b_lines, graph, ext_rows, widths):
+    rows = HEAD + 2 * (graph.shape[1] // 3)
+    return call(
+        ext_kernel,
+        "ext_products",
+        (b_lines, graph, ext_rows),
+        [IN_SMEM] + [IN_VMEM] * 2,
+        [jax.ShapeDtypeStruct((rows, w), jnp.int16) for w in widths],
+        limit=PRODUCT_LIMIT,
+    )
+
+
+def own_kernel(half, turns, a_ref, b_ref, graph_ref, ext_rows_ref, side_ref, own_ref, *rest):
+    refs = list(rest)
+    inner, panel = graph_ref.shape[0], graph_ref.shape[1] // BS // 3
+    at = Sides(inner, panel)
+    int_rows_ref = refs.pop() if turns else side_ref
+    coded = Coded(refs)
     if turns:
-        turn(int_rows_ref[...], a_ref, at.int_side, at.first, turned_ref, slice(None))
-    multiply(panel, at.starts["ext"], ext_rows_ref, ("ext", "own", "int"))
-    multiply(at.ext_side, at.starts["ext"], ext_rows_ref, ("ext", "own"))
-    multiply(at.int_side, at.int_side, turned_ref, ("own", "int"))
-    for part in coded:
-        coded[part].finish()
-
-
-def products(a_lines, b_lines, graph, ext_rows, int_rows, half, wanted, turns=False):
+        int_rows_ref[...] = masked(side_ref[...], a_ref, at.int_side, at.first).T
+    right = right_side(at, ("own", "int"), half, b_ref, graph_ref)
+    for i in range(panel):
+        block = panel + i
+        product = dot(ext_rows_ref[rows_at(block - at.starts["ext"]), :], right)
+        own_ref[rows_at(block), :] = product[:, :BS]
+        coded.write(product[:, BS:], i)
+    for i in range(panel):
+        block = at.ext_side + i
+        own_ref[rows_at(block), :] = dot(ext_rows_ref[rows_at(block - at.starts["ext"]), :], right[:, :BS])
+    for i in range(panel):
+        product = dot(int_rows_ref[i * BS : (i + 1) * BS, :], right)
+        own_ref[rows_at(at.int_side + i), :] = product[:, :BS]
+        coded.write(product[:, BS:], panel + i)
+    coded.finish()
+
+
+def own_products(a_lines, b_lines, graph, ext_rows, side_rows, half, widths, turns=False):
     inner, width = graph.shape
     panel = width // 3
-    outs = []
-    for part in ("ext", "own", "int"):
-        for w in wanted.get(part, ()):
-            if part == "own":
-                outs.append(jax.ShapeDtypeStruct((width, w), jnp.float32))
-            else:
-                outs.append(jax.ShapeDtypeStruct((HEAD + 2 * panel, w), jnp.int16))
+    outs = [jax.ShapeDtypeStruct((width, BS), jnp.float32)]
+    outs += [jax.ShapeDtypeStruct((HEAD + 2 * panel, w), jnp.int16) for w in widths]
     if turns:
         outs.append(pltpu.VMEM((panel, inner), graph.dtype))
     return call(
-        functools.partial(product_kernel, half, wanted, turns),
-        "_".join(wanted) + f"_products_{half}",
-        (a_lines, b_lines, graph, ext_rows, int_rows),
+        functools.partial(own_kernel, half, turns),
+        f"own_products_{half}",
+        (a_lines, b_lines, graph, ext_rows, side_rows),
         [IN_SMEM, IN_SMEM] + [IN_VMEM] * 3,
         outs,
-        flops=2 * inner * BS * sum(width if part == "own" else 2 * panel for part in wanted),
-        moved=2 * inner * BS,
         limit=PRODUCT_LIMIT,
     )
 
@@ -258,34 +269,36 @@
     send_ref[0:HEAD, :] = jnp.broadcast_to(power, (HEAD, power.shape[1])).astype(jnp.int32).astype(jnp.int16)
 
 
-def join_kernel(rows, half, lane, c_ref, own_ref, ext_ref, int_ref, keep_ref, send_ref, total):
+def join_kernel(rows, half, lane, ext_lane, c_ref, own_ref, ext_ref, int_ref, keep_ref, send_ref, total):
     odd = lax.rem(lax.axis_index("blk"), 2)
-    blocks = own_ref.shape[0] // BS
-    panel = blocks // 3
-    lanes = slice(lane, lane + ext_ref.shape[1])
-
-    def add(below_ref, above_ref):
-        below_scale = scales(below_ref[0:HEAD, :])
-        above_scale = scales(above_ref[0:HEAD, :])
-        for v in range(blocks):
+    panel = own_ref.shape[0] // BS // 3
+    width = send_ref.shape[1]
+    lanes = slice(lane, lane + width)
+    refs = (ext_ref.at[:, ext_lane : ext_lane + width], int_ref)
+    ext, int_ = ([(r, i) for i in range(2 * panel)] for r in range(2))
+    odd_parts = [[part] for part in int_] + [[] for _ in range(panel)]
+    even_parts = [[] for _ in range(panel)] + [[part] for part in int_[panel:] + int_[:panel]]
+    for i, part in enumerate(ext):
+        odd_parts[panel + i].append(part)
+        even_parts[i].append(part)
+
+    def add(parts):
+        scale = [scales(ref[0:HEAD, :]) for ref in refs]
+        for v in range(3 * panel):
             kept = c_ref[0, half, v].astype(jnp.float32)
             block = own_ref[v * BS : (v + 1) * BS, lanes] * kept
-            if v < 2 * panel:
-                codes = below_ref[HEAD + v * BS : HEAD + (v + 1) * BS, :]
-                block += decode(codes, below_scale[v : v + 1] * kept)
-            if v >= panel:
-                i = v - panel
-                codes = above_ref[HEAD + i * BS : HEAD + (i + 1) * BS, :]
-                block += decode(codes, above_scale[i : i + 1] * kept)
+            for r, i in parts[v]:
+                codes = refs[r][HEAD + i * BS : HEAD + (i + 1) * BS, :]
+                block += decode(codes, scale[r][i : i + 1] * kept)
             total[v * BS : (v + 1) * BS, :] = block
 
     @pl.when(odd == 1)
     def _():
-        add(int_ref, ext_ref)
+        add(odd_parts)
 
     @pl.when(odd == 0)
     def _():
-        add(ext_ref, int_ref)
+        add(even_parts)
 
     split_strips(total, rows, 1, keep_ref, send_ref)
 
@@ -297,18 +310,17 @@
     ]
 
 
-def join(own, ext_part, int_part, c_lines, half, lane, layers):
+def join(own, ext_part, ext_lane, int_part, c_lines, half, lane, layers):
     height = own.shape[0]
-    width = ext_part.shape[1]
+    width = int_part.shape[1]
     rows = height // layers
     return call(
-        functools.partial(join_kernel, rows, half, lane),
+        functools.partial(join_kernel, rows, half, lane, ext_lane),
         f"join_{half}_{lane}",
         (c_lines, own, ext_part, int_part),
         [IN_SMEM] + [IN_VMEM] * 3,
         strips_shapes(layers // 2, rows, width),
         [pltpu.VMEM((height, width), jnp.float32)],
-        moved=8 * height * width,
     )
 
 
@@ -329,7 +341,6 @@
         [IN_VMEM] * 2,
         strips_shapes(strips // 2, rows, width),
         [pltpu.VMEM((strips * rows, width), jnp.float32)],
-        moved=8 * kept.size,
     )
 
 
@@ -353,7 +364,6 @@
             jax.ShapeDtypeStruct((rows, width), jnp.float32),
             jax.ShapeDtypeStruct((8, width + sum(sums.shape[1] for sums in earlier)), jnp.float32),
         ],
-        moved=8 * kept.size,
     )
 
 
@@ -377,7 +387,6 @@
         (*squares, *sums),
         [IN_VMEM] * (len(squares) + len(sums)),
         jax.ShapeDtypeStruct((1, rows, width), jnp.float32),
-        moved=8 * rows * width,
     )
 
 
@@ -400,30 +409,36 @@
     chunks = panel // LANES
     fine = (LANES,) * (BS // LANES)
     per_half = len(fine)
-    *ext_parts, ext_rows, graph, flow_rest = first_products(flow_t, graph, a_lines, b_lines, fine)
-    ext = [swap(part, "blk", other_chip) for part in ext_parts]
-    wanted = {"own": (BS,), "int": fine}
-    own, *int_parts, int_rows = products(a_lines, b_lines, graph, ext_rows, flow_rest, 0, wanted, turns=True)
-    owns = [own]
-    int_ = [swap(part, "blk", same_chip) for part in int_parts]
-    latest = [own]
+    ext, ints, owns, latest = [], [], [], []
 
     def ordered(value):
         return after(value, latest[-1])
 
-    def more_products(half):
-        parts = products(ordered(a_lines), b_lines, graph, ext_rows, int_rows, half, {"ext": fine, "int": fine})
-        ext.extend(swap(part, "blk", other_chip) for part in parts[:per_half])
-        int_.extend(swap(part, "blk", same_chip) for part in parts[per_half:])
+    def send_ext(parts):
+        for part in parts:
+            got = swap(part, "blk", other_chip)
+            ext.extend((got, lane) for lane in range(0, part.shape[1], LANES))
         latest.append(parts[0])
-        owns.extend(products(ordered(a_lines), b_lines, graph, ext_rows, int_rows, half, {"own": (BS,)}))
-        latest.append(owns[-1])
-
+
+    first_part, ext_rows, graph, side_rows = first_products(flow_t, graph, a_lines, b_lines)
+    send_ext([first_part])
+
+    def own_half(half, side_rows, turns):
+        own, *parts = own_products(a_lines, ordered(b_lines), graph, ext_rows, side_rows, half, fine, turns)
+        if turns:
+            side_rows = parts.pop()
+        ints.extend(swap(part, "blk", same_chip) for part in parts)
+        owns.append(own)
+        latest.append(own)
+        return side_rows
+
+    side_rows = own_half(0, side_rows, True)
+    send_ext(ext_products(ordered(b_lines), graph, ext_rows, (panel - 2 * LANES, LANES)))
     strips, squares, sums = [], [], []
 
     def add_up(chunk):
         half, lane = divmod(chunk, per_half)
-        kept, send = join(owns[half], ext[chunk], int_[chunk], ordered(c_lines), half, lane * LANES, layers)
+        kept, send = join(owns[half], *ext[chunk], ints[chunk], ordered(c_lines), half, lane * LANES, layers)
         latest.append(send)
         strips.append((kept, swap(send, "layer", lambda i: i ^ 1)))
 
@@ -444,15 +459,18 @@
         squares.append(squared)
         sums.append(summed)
 
-    for chunk in range(chunks + 2):
-        if chunk < chunks:
-            add_up(chunk)
-        if 1 <= chunk <= chunks:
-            scatter(chunk - 1)
-        if chunk >= 2:
-            finish(chunk - 2)
-        if chunk % per_half == 0 and chunk // per_half + 1 < halves:
-            more_products(chunk // per_half + 1)
+    add_up(0)
+    for half in range(1, halves):
+        own_half(half, side_rows, False)
+    scatter(0)
+    for chunk in range(1, chunks):
+        if chunk == chunks - 1:
+            finish(0)
+        add_up(chunk)
+    for chunk in range(1, chunks):
+        scatter(chunk)
+    for chunk in range(1, chunks):
+        finish(chunk)
 
     mine = sums[-1]
     others = [swap(mine, "layer", lambda i: i ^ other) for other in range(1, layers)]

time: 66.3 us -> 67.2 us (1.014)
  starting transfers between devices: 27.6 us -> 23.6 us
  waiting for transfers between devices: 17.8 us -> 21.4 us
  Pallas kernels: 20.6 us -> 21.9 us
    ppermute x19 -> x18, starting transfers between devices: 27.6 us -> 23.6 us  [swap(): lax.ppermute(block, axis, [(partner(i), i) for i in range(lax.axis_size(a...]
    ppermute x19 -> x18, waiting for transfers between devices: 17.8 us -> 21.4 us  [swap(): lax.ppermute(block, axis, [(partner(i), i) for i in range(lax.axis_size(a...]
    pallas_call x17, Pallas kernels: 20.6 us -> 21.9 us  [call(): pl.pallas_call(kernel, out_shape=out_shape, in_specs=in_specs, out_specs=...]
  transfers between devices with their start and end apart: 19 -> 18, of which waited for: 9 -> 9; matrix products, arithmetic and copies ran while one was open for 0% -> 0% of each run, Pallas kernels for 22% -> 23%
where the time goes in v6:
time: 67.2 us; the launch traced here: 67.1 us
  starting transfers between devices  23.6 us (35%)
  Pallas kernels  21.9 us (33%)
  waiting for transfers between devices  21.4 us (32%)
    ppermute x18, starting transfers between devices, swap(): lax.ppermute(block, axis, [(partner(i), i) for i in range(lax.axis_size(a...  23.6 us
    pallas_call x17, Pallas kernels, call(): pl.pallas_call(kernel, out_shape=out_shape, in_specs=in_specs, out_specs=...  21.9 us
    ppermute x18, waiting for transfers between devices, swap(): lax.ppermute(block, axis, [(partner(i), i) for i in range(lax.axis_size(a...  21.4 us
  transfers between devices with their start and end apart: 18, of which 9 were waited for; matrix products, arithmetic and copies ran while one was open for 0% of the time, Pallas kernels for 23%

profile of v6, /device:TPU:0, one launch (start us, length us, event | category | flops | bytes accessed | tf_op | source)
XLA Modules:
  0.0 67.1 jit_solution(11146917402673664784)
XLA Ops:
  0.0 5.1 %first_products.1 = (s16[1040,128]{1,0:T(8,128)(2,1)S(1)}, bf16[1024,2048]{1,0:T(8,128)(2,1)S(1)}, bf16[2048,1536]{1,0:T(8,128)(2,1)S(1)}, bf16[2048,512]{1,0:T(8,128)(2,1)S(1)}) custom-call(s32[6,1,32]{2,1,0:T(1,128)} %bitcast.7, s32[6,1,32]{2,1,0:T(1,128)} %bitcast.3, bf16[1,2048,1536]{2,1,0:T(8,128)(2,1)} %flow_hbm.1, bf16[1,2048,1536]{2,1,0:T(8,128)(2,1)} %graph_hbm.1), custom_call_target="tpu_custom_call" | custom-call | flops 1 | bytes 1 | tf_op jit(solution)/shard_map/first_products/pallas_call | solution.py:32
  5.1 3.4 %collective-permute-start = (s16[1040,128]{1,0:T(8,128)(2,1)S(1)}, s16[1040,128]{1,0:T(8,128)(2,1)S(1)}, u32[]{:S(2)}, u32[]{:S(2)}) collective-permute-start(s16[1040,128]{1,0:T(8,128)(2,1)S(1)} %get-tuple-element.57), channel_id=1, source_target_pairs={{28,0},{8,4},{4,8},{16,12},{12,16},{24,20},{20,24},{0,28},{29,1},{... | collective-permute-start | bytes 798728 | tf_op jit(solution)/shard_map/ppermute | solution.py:24
  8.5 3.7 %own_products_0.1 = (f32[1536,256]{1,0:T(8,128)S(1)}, s16[1040,128]{1,0:T(8,128)(2,1)S(1)}, s16[1040,128]{1,0:T(8,128)(2,1)S(1)}, bf16[512,2048]{1,0:T(8,128)(2,1)S(1)}) custom-call(s32[6,1,32]{2,1,0:T(1,128)S(1)} %bitcast.8, s32[6,1,32]{2,1,0:T(1,128)S(1)} %bitcast.4, bf16[2048,1536]{1,0:T(8,128)(2,1)S(1)} %get-tuple-element.59.graph_ref, ...), custom_call_target="tpu_custom_call" | custom-call | flops 1 | bytes 1 | tf_op jit(solution)/shard_map/own_products_0/pallas_call | solution.py:32
  12.3 3.3 %ext_products.1 = (s16[1040,256]{1,0:T(8,128)(2,1)S(1)}, s16[1040,128]{1,0:T(8,128)(2,1)S(1)}) custom-call(s32[6,1,32]{2,1,0:T(1,128)S(1)} %bitcast.5, bf16[2048,1536]{1,0:T(8,128)(2,1)S(1)} %get-tuple-element.59.graph_ref, bf16[1024,2048]{1,0:T(8,128)(2,1)S(1)} %get-tuple-element.60.ext_rows_ref), custom_call_target="tpu_custom_call" | custom-call | flops 1 | bytes 1 | tf_op jit(solution)/shard_map/ext_products/pallas_call | solution.py:32
  15.6 0.7 %collective-permute-start.3 = (s16[1040,256]{1,0:T(8,128)(2,1)S(1)}, s16[1040,256]{1,0:T(8,128)(2,1)S(1)}, u32[]{:S(2)}, u32[]{:S(2)}) collective-permute-start(s16[1040,256]{1,0:T(8,128)(2,1)S(1)} %get-tuple-element.64), channel_id=1, source_target_pairs={{28,0},{8,4},{4,8},{16,12},{12,16},{24,20},{20,24},{0,28},{29,1},{... | collective-permute-start | bytes 1597448 | tf_op jit(solution)/shard_map/ppermute | solution.py:24
  16.4 1.0 %join_0_0.1 = (f32[2,384,128]{2,1,0:T(8,128)S(1)}, s16[784,128]{1,0:T(8,128)(2,1)S(1)}) custom-call(s32[1,2,6]{2,1,0:T(2,128)S(1)} %bitcast.10, f32[1536,256]{1,0:T(8,128)S(1)} %get-tuple-element.62.own_ref, s16[1040,128]{1,0:T(8,128)(2,1)S(1)} %collective-permute-done.ext_ref, s16[1040,128]{1,0:T(8,128)(2,1)S(1)} %collective-permute-done.1.int_ref), custom_call_target="tpu_custom_call" | custom-call | flops 1 | bytes 1 | tf_op jit(solution)/shard_map/join_0_0/pallas_call | solution.py:32
  17.4 1.7 %collective-permute-start.2 = (s16[784,128]{1,0:T(8,128)(2,1)S(1)}, s16[784,128]{1,0:T(8,128)(2,1)S(1)}, u32[]{:S(2)}, u32[]{:S(2)}) collective-permute-start(s16[784,128]{1,0:T(8,128)(2,1)S(1)} %get-tuple-element.68), channel_id=1, source_target_pairs={{1,0},{0,1},{3,2},{2,3},{5,4},{4,5},{7,6},{6,7},{9,8},{8,9},{11,10... | collective-permute-start | bytes 602120 | tf_op jit(solution)/shard_map/ppermute | solution.py:24
  19.3 3.7 %own_products_1.1 = (f32[1536,256]{1,0:T(8,128)S(1)}, s16[1040,128]{1,0:T(8,128)(2,1)S(1)}, s16[1040,128]{1,0:T(8,128)(2,1)S(1)}) custom-call(s32[6,1,32]{2,1,0:T(1,128)S(1)} %bitcast.9, s32[6,1,32]{2,1,0:T(1,128)S(1)} %bitcast.6, bf16[2048,1536]{1,0:T(8,128)(2,1)S(1)} %get-tuple-element.59.graph_ref, bf16[1024,2048]{1,0:T(8,128)(2,1)S(1)} %get-tuple-element.60.ext_rows_ref, ...), custom_call_target="tpu_custom_call" | custom-call | flops 1 | bytes 1 | tf_op jit(solution)/shard_map/own_products_1/pallas_call | solution.py:32
  23.1 0.3 collective-permute-start.5
  23.4 1.6 %collective-permute-start.7 = (s16[1040,128]{1,0:T(8,128)(2,1)S(1)}, s16[1040,128]{1,0:T(8,128)(2,1)S(1)}, u32[]{:S(2)}, u32[]{:S(2)}) collective-permute-start(s16[1040,128]{1,0:T(8,128)(2,1)S(1)} %get-tuple-element.86), channel_id=1, source_target_pairs={{28,0},{8,4},{4,8},{16,12},{12,16},{24,20},{20,24},{0,28},{29,1},{... | collective-permute-start | bytes 798728 | tf_op jit(solution)/shard_map/ppermute | solution.py:24
  25.2 2.7 %collective-permute-start.6 = (s16[400,128]{1,0:T(8,128)(2,1)S(1)}, s16[400,128]{1,0:T(8,128)(2,1)S(1)}, u32[]{:S(2)}, u32[]{:S(2)}) collective-permute-start(s16[400,128]{1,0:T(8,128)(2,1)S(1)} %get-tuple-element.74), channel_id=1, source_target_pairs={{2,0},{3,1},{0,2},{1,3},{6,4},{7,5},{4,6},{5,7},{10,8},{11,9},{8,1... | collective-permute-start | bytes 307208 | tf_op jit(solution)/shard_map/ppermute | solution.py:24
  27.9 3.1 %collective-permute-done.3.ext_ref = s16[1040,256]{1,0:T(8,128)(2,1)S(1)} collective-permute-done((s16[1040,256]{1,0:T(8,128)(2,1)S(1)}, s16[1040,256]{1,0:T(8,128)(2,1)S(1)}, u32[]{:S(2)}, u32[]{:S(2)}) %collective-permute-start.3) | collective-permute-done | bytes 532512 | tf_op jit(solution)/shard_map/ppermute | solution.py:24
  31.0 1.1 %join_0_128.1 = (f32[2,384,128]{2,1,0:T(8,128)S(1)}, s16[784,128]{1,0:T(8,128)(2,1)S(1)}) custom-call(s32[1,2,6]{2,1,0:T(2,128)S(1)} %bitcast.11, f32[1536,256]{1,0:T(8,128)S(1)} %get-tuple-element.62.own_ref, s16[1040,256]{1,0:T(8,128)(2,1)S(1)} %collective-permute-done.3.ext_ref, s16[1040,128]{1,0:T(8,128)(2,1)S(1)} %collective-permute-done.4.int_ref), custom_call_target="tpu_custom_call" | custom-call | flops 1 | bytes 1 | tf_op jit(solution)/shard_map/join_0_128/pallas_call | solution.py:32
  32.2 1.6 %collective-permute-start.9 = (s16[784,128]{1,0:T(8,128)(2,1)S(1)}, s16[784,128]{1,0:T(8,128)(2,1)S(1)}, u32[]{:S(2)}, u32[]{:S(2)}) collective-permute-start(s16[784,128]{1,0:T(8,128)(2,1)S(1)} %get-tuple-element.77), channel_id=1, source_target_pairs={{1,0},{0,1},{3,2},{2,3},{5,4},{4,5},{7,6},{6,7},{9,8},{8,9},{11,10... | collective-permute-start | bytes 602120 | tf_op jit(solution)/shard_map/ppermute | solution.py:24
  33.8 1.0 %join_1_0.1 = (f32[2,384,128]{2,1,0:T(8,128)S(1)}, s16[784,128]{1,0:T(8,128)(2,1)S(1)}) custom-call(s32[1,2,6]{2,1,0:T(2,128)S(1)} %bitcast.12, f32[1536,256]{1,0:T(8,128)S(1)} %get-tuple-element.71.own_ref, s16[1040,256]{1,0:T(8,128)(2,1)S(1)} %collective-permute-done.3.ext_ref, s16[1040,128]{1,0:T(8,128)(2,1)S(1)} %collective-permute-done.5.int_ref), custom_call_target="tpu_custom_call" | custom-call | flops 1 | bytes 1 | tf_op jit(solution)/shard_map/join_1_0/pallas_call | solution.py:32
  34.8 0.5 collective-permute-start.10
  35.4 1.3 %collective-permute-done.7.ext_ref = s16[1040,128]{1,0:T(8,128)(2,1)S(1)} collective-permute-done((s16[1040,128]{1,0:T(8,128)(2,1)S(1)}, s16[1040,128]{1,0:T(8,128)(2,1)S(1)}, u32[]{:S(2)}, u32[]{:S(2)}) %collective-permute-start.7) | collective-permute-done | bytes 266272 | tf_op jit(solution)/shard_map/ppermute | solution.py:24
  36.7 1.0 %join_1_128.1 = (f32[2,384,128]{2,1,0:T(8,128)S(1)}, s16[784,128]{1,0:T(8,128)(2,1)S(1)}) custom-call(s32[1,2,6]{2,1,0:T(2,128)S(1)} %bitcast.13, f32[1536,256]{1,0:T(8,128)S(1)} %get-tuple-element.71.own_ref, s16[1040,128]{1,0:T(8,128)(2,1)S(1)} %collective-permute-done.7.ext_ref, s16[1040,128]{1,0:T(8,128)(2,1)S(1)} %collective-permute-done.8.int_ref), custom_call_target="tpu_custom_call" | custom-call | flops 1 | bytes 1 | tf_op jit(solution)/shard_map/join_1_128/pallas_call | solution.py:32
  37.6 1.6 %collective-permute-start.11 = (s16[784,128]{1,0:T(8,128)(2,1)S(1)}, s16[784,128]{1,0:T(8,128)(2,1)S(1)}, u32[]{:S(2)}, u32[]{:S(2)}) collective-permute-start(s16[784,128]{1,0:T(8,128)(2,1)S(1)} %get-tuple-element.88), channel_id=1, source_target_pairs={{1,0},{0,1},{3,2},{2,3},{5,4},{4,5},{7,6},{6,7},{9,8},{8,9},{11,10... | collective-permute-start | bytes 602120 | tf_op jit(solution)/shard_map/ppermute | solution.py:24
  39.3 0.8 %collective-permute-done.9.got_ref = s16[784,128]{1,0:T(8,128)(2,1)S(1)} collective-permute-done((s16[784,128]{1,0:T(8,128)(2,1)S(1)}, s16[784,128]{1,0:T(8,128)(2,1)S(1)}, u32[]{:S(2)}, u32[]{:S(2)}) %collective-permute-start.9) | collective-permute-done | bytes 200736 | tf_op jit(solution)/shard_map/ppermute | solution.py:24
  40.3 2.7 %collective-permute-start.12 = (s16[400,128]{1,0:T(8,128)(2,1)S(1)}, s16[400,128]{1,0:T(8,128)(2,1)S(1)}, u32[]{:S(2)}, u32[]{:S(2)}) collective-permute-start(s16[400,128]{1,0:T(8,128)(2,1)S(1)} %get-tuple-element.93), channel_id=1, source_target_pairs={{2,0},{3,1},{0,2},{1,3},{6,4},{7,5},{4,6},{5,7},{10,8},{11,9},{8,1... | collective-permute-start | bytes 307208 | tf_op jit(solution)/shard_map/ppermute | solution.py:24
  42.9 4.8 %collective-permute-done.10.got_ref = s16[784,128]{1,0:T(8,128)(2,1)S(1)} collective-permute-done((s16[784,128]{1,0:T(8,128)(2,1)S(1)}, s16[784,128]{1,0:T(8,128)(2,1)S(1)}, u32[]{:S(2)}, u32[]{:S(2)}) %collective-permute-start.10) | collective-permute-done | bytes 200736 | tf_op jit(solution)/shard_map/ppermute | solution.py:24
  47.9 0.5 collective-permute-start.13
  48.4 2.5 %collective-permute-done.11.got_ref = s16[784,128]{1,0:T(8,128)(2,1)S(1)} collective-permute-done((s16[784,128]{1,0:T(8,128)(2,1)S(1)}, s16[784,128]{1,0:T(8,128)(2,1)S(1)}, u32[]{:S(2)}, u32[]{:S(2)}) %collective-permute-start.11) | collective-permute-done | bytes 200736 | tf_op jit(solution)/shard_map/ppermute | solution.py:24
  51.1 1.4 %collective-permute-start.14 = (s16[400,128]{1,0:T(8,128)(2,1)S(1)}, s16[400,128]{1,0:T(8,128)(2,1)S(1)}, u32[]{:S(2)}, u32[]{:S(2)}) collective-permute-start(s16[400,128]{1,0:T(8,128)(2,1)S(1)} %get-tuple-element.97), channel_id=1, source_target_pairs={{2,0},{3,1},{0,2},{1,3},{6,4},{7,5},{4,6},{5,7},{10,8},{11,9},{8,1... | collective-permute-start | bytes 307208 | tf_op jit(solution)/shard_map/ppermute | solution.py:24
  52.6 5.7 %collective-permute-done.13.got_ref = s16[400,128]{1,0:T(8,128)(2,1)S(1)} collective-permute-done((s16[400,128]{1,0:T(8,128)(2,1)S(1)}, s16[400,128]{1,0:T(8,128)(2,1)S(1)}, u32[]{:S(2)}, u32[]{:S(2)}) %collective-permute-start.13) | collective-permute-done | bytes 102432 | tf_op jit(solution)/shard_map/ppermute | solution.py:24
  58.4 1.1 %collective-permute-done.14.got_ref = s16[400,128]{1,0:T(8,128)(2,1)S(1)} collective-permute-done((s16[400,128]{1,0:T(8,128)(2,1)S(1)}, s16[400,128]{1,0:T(8,128)(2,1)S(1)}, u32[]{:S(2)}, u32[]{:S(2)}) %collective-permute-start.14) | collective-permute-done | bytes 102432 | tf_op jit(solution)/shard_map/ppermute | solution.py:24
  59.6 1.8 %collective-permute-start.17 = (f32[8,512]{1,0:T(8,128)S(1)}, f32[8,512]{1,0:T(8,128)S(1)}, u32[]{:S(2)}, u32[]{:S(2)}) collective-permute-start(f32[8,512]{1,0:T(8,128)S(1)} %get-tuple-element.108.refs_4_), channel_id=1, source_target_pairs={{3,0},{2,1},{1,2},{0,3},{7,4},{6,5},{5,6},{4,7},{11,8},{10,9},{9,1... | collective-permute-start | bytes 49160 | tf_op jit(solution)/shard_map/ppermute | solution.py:24
  61.4 2.6 %collective-permute-start.15 = (f32[8,512]{1,0:T(8,128)S(1)}, f32[8,512]{1,0:T(8,128)S(1)}, u32[]{:S(2)}, u32[]{:S(2)}) collective-permute-start(f32[8,512]{1,0:T(8,128)S(1)} %get-tuple-element.108.refs_4_), channel_id=1, source_target_pairs={{1,0},{0,1},{3,2},{2,3},{5,4},{4,5},{7,6},{6,7},{9,8},{8,9},{11,10... | collective-permute-start | bytes 49160 | tf_op jit(solution)/shard_map/ppermute | solution.py:24
  64.0 1.2 %collective-permute-done.17.refs_7_ = f32[8,512]{1,0:T(8,128)S(1)} collective-permute-done((f32[8,512]{1,0:T(8,128)S(1)}, f32[8,512]{1,0:T(8,128)S(1)}, u32[]{:S(2)}, u32[]{:S(2)}) %collective-permute-start.17) | collective-permute-done | bytes 16416 | tf_op jit(solution)/shard_map/ppermute | solution.py:24
  65.2 0.8 %collective-permute-done.16.refs_6_ = f32[8,512]{1,0:T(8,128)S(1)} collective-permute-done((f32[8,512]{1,0:T(8,128)S(1)}, f32[8,512]{1,0:T(8,128)S(1)}, u32[]{:S(2)}, u32[]{:S(2)}) %collective-permute-start.16) | collective-permute-done | bytes 16416 | tf_op jit(solution)/shard_map/ppermute | solution.py:24
  66.1 1.0 %rescale.1 = f32[1,384,512]{2,1,0:T(8,128)} custom-call(f32[384,128]{1,0:T(8,128)S(1)} %get-tuple-element.82.refs_0_, f32[384,128]{1,0:T(8,128)S(1)} %get-tuple-element.99.refs_1_, f32[384,128]{1,0:T(8,128)S(1)} %get-tuple-element.103.refs_2_, f32[384,128]{1,0:T(8,128)S(1)} %get-tuple-element.107.refs_3_, f32[8,512]{1,0:T(8,128)S(1)} %get-tuple-element.108.refs_4_, ...), custom_call_target="tpu_custom_call" | custom-call | flops 1 | bytes 1 | tf_op jit(solution)/shard_map/rescale/pallas_call | solution.py:32
  (27 shorter events, 1.4 us)
Async XLA Ops:
  0.0 8.5 %copy-start = (s32[1,32,6]{1,0,2:T(1,128)S(1)}, s32[1,32,6]{1,0,2:T(1,128)}, u32[]{:S(2)}) copy-start(s32[1,32,6]{1,0,2:T(1,128)} %param.8) | copy-start | bytes 2308
  0.0 8.5 %copy-start.1 = (s32[1,32,6]{1,0,2:T(1,128)S(1)}, s32[1,32,6]{1,0,2:T(1,128)}, u32[]{:S(2)}) copy-start(s32[1,32,6]{1,0,2:T(1,128)} %param.7) | copy-start | bytes 2308
  5.1 11.3 %collective-permute-start = (s16[1040,128]{1,0:T(8,128)(2,1)S(1)}, s16[1040,128]{1,0:T(8,128)(2,1)S(1)}, u32[]{:S(2)}, u32[]{:S(2)}) collective-permute-start(s16[1040,128]{1,0:T(8,128)(2,1)S(1)} %get-tuple-element.57), channel_id=1, source_target_pairs={{28,0},{8,4},{4,8},{16,12},{12,16},{24,20},{20,24},{0,28},{29,1},{... | collective-permute-start | bytes 798728 | tf_op jit(solution)/shard_map/ppermute | solution.py:24
  12.2 4.2 %collective-permute-start.1 = (s16[1040,128]{1,0:T(8,128)(2,1)S(1)}, s16[1040,128]{1,0:T(8,128)(2,1)S(1)}, u32[]{:S(2)}, u32[]{:S(2)}) collective-permute-start(s16[1040,128]{1,0:T(8,128)(2,1)S(1)} %get-tuple-element.66), channel_id=1, source_target_pairs={{4,0},{0,4},{12,8},{8,12},{20,16},{16,20},{28,24},{24,28},{5,1},{1... | collective-permute-start | bytes 798728 | tf_op jit(solution)/shard_map/ppermute | solution.py:24
  12.3 4.1 %copy-start.2 = (s32[1,6,2]{1,2,0:T(2,128)S(1)}, s32[1,6,2]{1,2,0:T(2,128)}, u32[]{:S(2)}) copy-start(s32[1,6,2]{1,2,0:T(2,128)} %param.9) | copy-start | bytes 148
  15.6 15.4 %collective-permute-start.3 = (s16[1040,256]{1,0:T(8,128)(2,1)S(1)}, s16[1040,256]{1,0:T(8,128)(2,1)S(1)}, u32[]{:S(2)}, u32[]{:S(2)}) collective-permute-start(s16[1040,256]{1,0:T(8,128)(2,1)S(1)} %get-tuple-element.64), channel_id=1, source_target_pairs={{28,0},{8,4},{4,8},{16,12},{12,16},{24,20},{20,24},{0,28},{29,1},{... | collective-permute-start | bytes 1597448 | tf_op jit(solution)/shard_map/ppermute | solution.py:24
  17.4 7.6 %collective-permute-start.2 = (s16[784,128]{1,0:T(8,128)(2,1)S(1)}, s16[784,128]{1,0:T(8,128)(2,1)S(1)}, u32[]{:S(2)}, u32[]{:S(2)}) collective-permute-start(s16[784,128]{1,0:T(8,128)(2,1)S(1)} %get-tuple-element.68), channel_id=1, source_target_pairs={{1,0},{0,1},{3,2},{2,3},{5,4},{4,5},{7,6},{6,7},{9,8},{8,9},{11,10... | collective-permute-start | bytes 602120 | tf_op jit(solution)/shard_map/ppermute | solution.py:24
  19.1 6.1 %collective-permute-start.4 = (s16[1040,128]{1,0:T(8,128)(2,1)S(1)}, s16[1040,128]{1,0:T(8,128)(2,1)S(1)}, u32[]{:S(2)}, u32[]{:S(2)}) collective-permute-start(s16[1040,128]{1,0:T(8,128)(2,1)S(1)} %get-tuple-element.76), channel_id=1, source_target_pairs={{4,0},{0,4},{12,8},{8,12},{20,16},{16,20},{28,24},{24,28},{5,1},{1... | collective-permute-start | bytes 798728 | tf_op jit(solution)/shard_map/ppermute | solution.py:24
  23.1 10.7 %collective-permute-start.5 = (s16[1040,128]{1,0:T(8,128)(2,1)S(1)}, s16[1040,128]{1,0:T(8,128)(2,1)S(1)}, u32[]{:S(2)}, u32[]{:S(2)}) collective-permute-start(s16[1040,128]{1,0:T(8,128)(2,1)S(1)} %get-tuple-element.79), channel_id=1, source_target_pairs={{4,0},{0,4},{12,8},{8,12},{20,16},{16,20},{28,24},{24,28},{5,1},{1... | collective-permute-start | bytes 798728 | tf_op jit(solution)/shard_map/ppermute | solution.py:24
  23.4 13.3 %collective-permute-start.7 = (s16[1040,128]{1,0:T(8,128)(2,1)S(1)}, s16[1040,128]{1,0:T(8,128)(2,1)S(1)}, u32[]{:S(2)}, u32[]{:S(2)}) collective-permute-start(s16[1040,128]{1,0:T(8,128)(2,1)S(1)} %get-tuple-element.86), channel_id=1, source_target_pairs={{28,0},{8,4},{4,8},{16,12},{12,16},{24,20},{20,24},{0,28},{29,1},{... | collective-permute-start | bytes 798728 | tf_op jit(solution)/shard_map/ppermute | solution.py:24
  25.0 11.7 %collective-permute-start.8 = (s16[1040,128]{1,0:T(8,128)(2,1)S(1)}, s16[1040,128]{1,0:T(8,128)(2,1)S(1)}, u32[]{:S(2)}, u32[]{:S(2)}) collective-permute-start(s16[1040,128]{1,0:T(8,128)(2,1)S(1)} %get-tuple-element.87), channel_id=1, source_target_pairs={{4,0},{0,4},{12,8},{8,12},{20,16},{16,20},{28,24},{24,28},{5,1},{1... | collective-permute-start | bytes 798728 | tf_op jit(solution)/shard_map/ppermute | solution.py:24
  25.2 10.1 %collective-permute-start.6 = (s16[400,128]{1,0:T(8,128)(2,1)S(1)}, s16[400,128]{1,0:T(8,128)(2,1)S(1)}, u32[]{:S(2)}, u32[]{:S(2)}) collective-permute-start(s16[400,128]{1,0:T(8,128)(2,1)S(1)} %get-tuple-element.74), channel_id=1, source_target_pairs={{2,0},{3,1},{0,2},{1,3},{6,4},{7,5},{4,6},{5,7},{10,8},{11,9},{8,1... | collective-permute-start | bytes 307208 | tf_op jit(solution)/shard_map/ppermute | solution.py:24
  32.2 7.9 %collective-permute-start.9 = (s16[784,128]{1,0:T(8,128)(2,1)S(1)}, s16[784,128]{1,0:T(8,128)(2,1)S(1)}, u32[]{:S(2)}, u32[]{:S(2)}) collective-permute-start(s16[784,128]{1,0:T(8,128)(2,1)S(1)} %get-tuple-element.77), channel_id=1, source_target_pairs={{1,0},{0,1},{3,2},{2,3},{5,4},{4,5},{7,6},{6,7},{9,8},{8,9},{11,10... | collective-permute-start | bytes 602120 | tf_op jit(solution)/shard_map/ppermute | solution.py:24
  34.8 12.9 %collective-permute-start.10 = (s16[784,128]{1,0:T(8,128)(2,1)S(1)}, s16[784,128]{1,0:T(8,128)(2,1)S(1)}, u32[]{:S(2)}, u32[]{:S(2)}) collective-permute-start(s16[784,128]{1,0:T(8,128)(2,1)S(1)} %get-tuple-element.80), channel_id=1, source_target_pairs={{1,0},{0,1},{3,2},{2,3},{5,4},{4,5},{7,6},{6,7},{9,8},{8,9},{11,10... | collective-permute-start | bytes 602120 | tf_op jit(solution)/shard_map/ppermute | solution.py:24
  37.6 13.2 %collective-permute-start.11 = (s16[784,128]{1,0:T(8,128)(2,1)S(1)}, s16[784,128]{1,0:T(8,128)(2,1)S(1)}, u32[]{:S(2)}, u32[]{:S(2)}) collective-permute-start(s16[784,128]{1,0:T(8,128)(2,1)S(1)} %get-tuple-element.88), channel_id=1, source_target_pairs={{1,0},{0,1},{3,2},{2,3},{5,4},{4,5},{7,6},{6,7},{9,8},{8,9},{11,10... | collective-permute-start | bytes 602120 | tf_op jit(solution)/shard_map/ppermute | solution.py:24
  40.3 12.2 %collective-permute-start.12 = (s16[400,128]{1,0:T(8,128)(2,1)S(1)}, s16[400,128]{1,0:T(8,128)(2,1)S(1)}, u32[]{:S(2)}, u32[]{:S(2)}) collective-permute-start(s16[400,128]{1,0:T(8,128)(2,1)S(1)} %get-tuple-element.93), channel_id=1, source_target_pairs={{2,0},{3,1},{0,2},{1,3},{6,4},{7,5},{4,6},{5,7},{10,8},{11,9},{8,1... | collective-permute-start | bytes 307208 | tf_op jit(solution)/shard_map/ppermute | solution.py:24
  47.9 10.4 %collective-permute-start.13 = (s16[400,128]{1,0:T(8,128)(2,1)S(1)}, s16[400,128]{1,0:T(8,128)(2,1)S(1)}, u32[]{:S(2)}, u32[]{:S(2)}) collective-permute-start(s16[400,128]{1,0:T(8,128)(2,1)S(1)} %get-tuple-element.95), channel_id=1, source_target_pairs={{2,0},{3,1},{0,2},{1,3},{6,4},{7,5},{4,6},{5,7},{10,8},{11,9},{8,1... | collective-permute-start | bytes 307208 | tf_op jit(solution)/shard_map/ppermute | solution.py:24
  51.1 8.4 %collective-permute-start.14 = (s16[400,128]{1,0:T(8,128)(2,1)S(1)}, s16[400,128]{1,0:T(8,128)(2,1)S(1)}, u32[]{:S(2)}, u32[]{:S(2)}) collective-permute-start(s16[400,128]{1,0:T(8,128)(2,1)S(1)} %get-tuple-element.97), channel_id=1, source_target_pairs={{2,0},{3,1},{0,2},{1,3},{6,4},{7,5},{4,6},{5,7},{10,8},{11,9},{8,1... | collective-permute-start | bytes 307208 | tf_op jit(solution)/shard_map/ppermute | solution.py:24
  59.6 5.7 %collective-permute-start.17 = (f32[8,512]{1,0:T(8,128)S(1)}, f32[8,512]{1,0:T(8,128)S(1)}, u32[]{:S(2)}, u32[]{:S(2)}) collective-permute-start(f32[8,512]{1,0:T(8,128)S(1)} %get-tuple-element.108.refs_4_), channel_id=1, source_target_pairs={{3,0},{2,1},{1,2},{0,3},{7,4},{6,5},{5,6},{4,7},{11,8},{10,9},{9,1... | collective-permute-start | bytes 49160 | tf_op jit(solution)/shard_map/ppermute | solution.py:24
  61.4 4.6 %collective-permute-start.16 = (f32[8,512]{1,0:T(8,128)S(1)}, f32[8,512]{1,0:T(8,128)S(1)}, u32[]{:S(2)}, u32[]{:S(2)}) collective-permute-start(f32[8,512]{1,0:T(8,128)S(1)} %get-tuple-element.108.refs_4_), channel_id=1, source_target_pairs={{2,0},{3,1},{0,2},{1,3},{6,4},{7,5},{4,6},{5,7},{10,8},{11,9},{8,1... | collective-permute-start | bytes 49160 | tf_op jit(solution)/shard_map/ppermute | solution.py:24
  61.4 4.6 %collective-permute-start.15 = (f32[8,512]{1,0:T(8,128)S(1)}, f32[8,512]{1,0:T(8,128)S(1)}, u32[]{:S(2)}, u32[]{:S(2)}) collective-permute-start(f32[8,512]{1,0:T(8,128)S(1)} %get-tuple-element.108.refs_4_), channel_id=1, source_target_pairs={{1,0},{0,1},{3,2},{2,3},{5,4},{4,5},{7,6},{6,7},{9,8},{8,9},{11,10... | collective-permute-start | bytes 49160 | tf_op jit(solution)/shard_map/ppermute | solution.py:24

commit v7 on v6

--- a/solution.py
+++ b/solution.py
@@ -81,8 +81,8 @@
     return ref.at[0, :, pl.ds(pl.multiple_of(start * BS, BS), count * BS)]
 
 
-def rows_at(block, first=0):
-    return pl.ds(pl.multiple_of(first + block * BS, HEAD), BS)
+def blocks_at(block, count=1):
+    return pl.ds(pl.multiple_of(block * BS, BS), count * BS)
 
 
 class Sides:
@@ -91,14 +91,19 @@
         self.panel = panel
         self.first = lax.axis_index("layer") * (inner // BS)
         self.ext_side, self.int_side = odd * (2 * panel), (1 - odd) * (2 * panel)
-        self.columns = {"ext": self.ext_side, "own": panel, "int": self.int_side}
-        self.starts = {"ext": odd * panel, "own": 0, "int": (1 - odd) * panel}
+        self.ext_rows = odd * panel
+        self.rest = (1 - odd) * panel
+        self.own, self.int = odd * panel, (1 - odd) * panel
 
 
 class Coded:
     def __init__(self, refs):
         self.refs = refs
         self.heads = [jnp.zeros((HEAD, ref.shape[1]), jnp.float32) for ref in refs]
+
+    def write_all(self, product, place):
+        for i in range(product.shape[0] // BS):
+            self.write(product[i * BS : (i + 1) * BS], place + i)
 
     def write(self, product, place):
         column = 0
@@ -106,7 +111,7 @@
             chunk = product[:, column : column + ref.shape[1]]
             column += ref.shape[1]
             power = powers(chunk)
-            ref[rows_at(place, HEAD), :] = code(chunk, power)
+            ref[HEAD + place * BS : HEAD + (place + 1) * BS, :] = code(chunk, power)
             line = lax.broadcasted_iota(jnp.int32, self.heads[c].shape, 0)
             self.heads[c] = jnp.where(line == place, power, self.heads[c])
 
@@ -116,24 +121,18 @@
 
 
 def first_kernel(depth, a_hbm, b_hbm, flow_hbm, graph_hbm, *rest):
-    out_ref, rows_ref, graph_ref, flow_ref, flow_buf, total, a_ref, b_ref, sems = rest
-    inner, panel = flow_ref.shape[0], flow_ref.shape[1] // BS
+    out_refs, (rows_ref, graph_ref, flow_buf, total, a_ref, b_ref, sems) = rest[:-7], rest[-7:]
+    inner, panel = graph_ref.shape[0], graph_ref.shape[1] // BS
     at = Sides(inner, panel)
     steps = inner // depth
     small = [pltpu.make_async_copy(a_hbm, a_ref, sems.at[0]), pltpu.make_async_copy(b_hbm, b_ref, sems.at[1])]
-    side = pl.ds(pl.multiple_of(at.ext_side * BS, BS), panel * BS)
-    others = pl.ds(pl.multiple_of((panel * BS) - at.ext_side // 2 * BS, BS), 2 * panel * BS)
-    early = pltpu.make_async_copy(graph_hbm.at[0, :, side], graph_ref.at[:, side], sems.at[2])
-    late = [
-        pltpu.make_async_copy(columns_of(flow_hbm, at.int_side, panel), flow_ref, sems.at[3]),
-        pltpu.make_async_copy(graph_hbm.at[0, :, others], graph_ref.at[:, others], sems.at[4]),
-    ]
-    source = columns_of(flow_hbm, at.starts["ext"], 2 * panel)
+    graph_copy = pltpu.make_async_copy(columns_of(graph_hbm, at.ext_side, panel), graph_ref, sems.at[2])
+    source = columns_of(flow_hbm, at.ext_rows, 2 * panel)
     flows = []
     for t in range(steps):
         rows = slice(t * depth, (t + 1) * depth)
-        flows.append(pltpu.make_async_copy(source.at[rows], flow_buf.at[rows], sems.at[5 + t]))
-    for copy in small + [early] + flows + late:
+        flows.append(pltpu.make_async_copy(source.at[rows], flow_buf.at[rows], sems.at[3 + t]))
+    for copy in small + flows[:1] + [graph_copy] + flows[1:]:
         copy.start()
     for copy in small:
         copy.wait()
@@ -141,118 +140,121 @@
         rows = slice(t * depth, (t + 1) * depth)
         first = at.first + t * (depth // BS)
         flows[t].wait()
-        turned = masked(flow_buf[rows, :], a_ref, at.starts["ext"], first).T
+        turned = masked(flow_buf[rows, :], a_ref, at.ext_rows, first).T
         rows_ref[:, rows] = turned
         if t == 0:
-            early.wait()
-        right = masked(graph_ref[rows, rows_at(at.ext_side)], b_ref, at.ext_side, first)
-        product = dot(turned, right[:, : out_ref.shape[1]])
+            graph_copy.wait()
+        product = dot(turned, masked(graph_ref[rows, :BS], b_ref, at.ext_side, first))
         if t < steps - 1:
             total[...] = product if t == 0 else total[...] + product
-    coded = Coded([out_ref])
+    coded = Coded(out_refs)
     for i in range(2 * panel):
         rows = slice(i * BS, (i + 1) * BS)
         coded.write(product[rows] if steps == 1 else total[rows, :] + product[rows], i)
     coded.finish()
-    for copy in late:
-        copy.wait()
-
-
-def first_products(flow_t, graph, a_lines, b_lines):
+
+
+def in_hbm(*operands):
+    return [pltpu.with_memory_space_constraint(x, pltpu.HBM) for x in operands]
+
+
+def first_products(flow_t, graph, a_lines, b_lines, widths):
     inner, width = flow_t.shape[1:]
     panel = width // 3
     depth = min(512, inner)
-    operands = [pltpu.with_memory_space_constraint(x, pltpu.HBM) for x in (a_lines, b_lines, flow_t, graph)]
     return call(
         functools.partial(first_kernel, depth),
         "first_products",
-        operands,
+        in_hbm(a_lines, b_lines, flow_t, graph),
         [IN_HBM] * 4,
-        [
-            jax.ShapeDtypeStruct((HEAD + 2 * panel, LANES), jnp.int16),
-            pltpu.VMEM((2 * panel, inner), flow_t.dtype),
-            pltpu.VMEM((inner, width), graph.dtype),
-            pltpu.VMEM((inner, panel), flow_t.dtype),
-        ],
+        [jax.ShapeDtypeStruct((HEAD + 2 * panel, w), jnp.int16) for w in widths]
+        + [pltpu.VMEM((2 * panel, inner), flow_t.dtype), pltpu.VMEM((inner, panel), graph.dtype)],
         [
             pltpu.VMEM((inner, 2 * panel), flow_t.dtype),
-            pltpu.VMEM((2 * panel, LANES), jnp.float32),
+            pltpu.VMEM((2 * panel, BS), jnp.float32),
             pltpu.SMEM(a_lines.shape, a_lines.dtype),
             pltpu.SMEM(b_lines.shape, b_lines.dtype),
-            pltpu.SemaphoreType.DMA((5 + inner // depth,)),
+            pltpu.SemaphoreType.DMA((3 + inner // depth,)),
         ],
         limit=PRODUCT_LIMIT,
     )
 
 
-def right_side(at, parts, half, b_ref, graph_ref):
-    right = []
-    for part in parts:
-        column = at.columns[part] + half
-        right.append(masked(graph_ref[:, rows_at(column)], b_ref, column, at.first))
-    return jnp.concatenate(right, axis=1) if len(right) > 1 else right[0]
-
-
-def ext_kernel(b_ref, graph_ref, ext_rows_ref, *out_refs):
-    inner, panel = graph_ref.shape[0], graph_ref.shape[1] // BS // 3
+def own_half(at, half, b_ref, rest_ref, ext_rows_ref, int_rows_ref, own_ref, int_refs):
+    panel = at.panel
+    right = [
+        masked(rest_ref[:, blocks_at(column + half)], b_ref, at.rest + column + half, at.first)
+        for column in (at.own, at.int)
+    ]
+    both = jnp.concatenate(right, axis=1)
+    coded = Coded(int_refs)
+    mid = dot(ext_rows_ref[blocks_at(panel - at.ext_rows, panel), :], both)
+    own_ref[panel * BS : 2 * panel * BS, :] = mid[:, :BS]
+    coded.write_all(mid[:, BS:], 0)
+    own_ref[blocks_at(at.ext_side, panel), :] = dot(
+        ext_rows_ref[blocks_at(at.ext_side - at.ext_rows, panel), :], right[0]
+    )
+    side = dot(int_rows_ref[...], both)
+    own_ref[blocks_at(at.int_side, panel), :] = side[:, :BS]
+    coded.write_all(side[:, BS:], panel)
+    coded.finish()
+
+
+def second_kernel(ext_count, a_ref, b_ref, graph_ref, ext_rows_ref, flow_hbm, graph_hbm, *rest):
+    out_refs, (int_rows_ref, rest_ref, flow_buf, sems) = rest[:-4], rest[-4:]
+    ext_refs, (own_ref, *int_refs) = out_refs[:ext_count], out_refs[ext_count:]
+    inner, panel = graph_ref.shape[0], graph_ref.shape[1] // BS
     at = Sides(inner, panel)
-    side = pl.ds(pl.multiple_of(at.ext_side * BS, BS), panel * BS)
-    right = masked(graph_ref[:, side], b_ref, at.ext_side, at.first)[:, LANES:]
-    coded = Coded(out_refs)
-    for i in range(2 * panel):
-        coded.write(dot(ext_rows_ref[i * BS : (i + 1) * BS, :], right), i)
+    copies = [
+        pltpu.make_async_copy(columns_of(graph_hbm, at.rest, 2 * panel), rest_ref, sems.at[0]),
+        pltpu.make_async_copy(columns_of(flow_hbm, at.int_side, panel), flow_buf, sems.at[1]),
+    ]
+    for copy in copies:
+        copy.start()
+    right = masked(graph_ref[:, BS:], b_ref, at.ext_side + 1, at.first)
+    product = dot(ext_rows_ref[...], right)
+    coded = Coded(ext_refs)
+    coded.write_all(product, 0)
     coded.finish()
-
-
-def ext_products(b_lines, graph, ext_rows, widths):
-    rows = HEAD + 2 * (graph.shape[1] // 3)
-    return call(
-        ext_kernel,
-        "ext_products",
-        (b_lines, graph, ext_rows),
-        [IN_SMEM] + [IN_VMEM] * 2,
-        [jax.ShapeDtypeStruct((rows, w), jnp.int16) for w in widths],
+    for copy in copies:
+        copy.wait()
+    int_rows_ref[...] = masked(flow_buf[...], a_ref, at.int_side, at.first).T
+    own_half(at, 0, b_ref, rest_ref, ext_rows_ref, int_rows_ref, own_ref, int_refs)
+
+
+def second_products(a_lines, b_lines, graph_ext, ext_rows, flow_t, graph, ext_widths, int_widths):
+    inner, width = flow_t.shape[1:]
+    panel = width // 3
+    coded = [jax.ShapeDtypeStruct((HEAD + 2 * panel, w), jnp.int16) for w in ext_widths + int_widths]
+    own = jax.ShapeDtypeStruct((width, BS), jnp.float32)
+    return call(
+        functools.partial(second_kernel, len(ext_widths)),
+        "second_products",
+        (a_lines, b_lines, graph_ext, ext_rows, *in_hbm(flow_t, graph)),
+        [IN_SMEM, IN_SMEM, IN_VMEM, IN_VMEM, IN_HBM, IN_HBM],
+        coded[: len(ext_widths)]
+        + [own]
+        + coded[len(ext_widths) :]
+        + [pltpu.VMEM((panel, inner), flow_t.dtype), pltpu.VMEM((inner, 2 * panel), graph.dtype)],
+        [pltpu.VMEM((inner, panel), flow_t.dtype), pltpu.SemaphoreType.DMA((2,))],
         limit=PRODUCT_LIMIT,
     )
 
 
-def own_kernel(half, turns, a_ref, b_ref, graph_ref, ext_rows_ref, side_ref, own_ref, *rest):
-    refs = list(rest)
-    inner, panel = graph_ref.shape[0], graph_ref.shape[1] // BS // 3
-    at = Sides(inner, panel)
-    int_rows_ref = refs.pop() if turns else side_ref
-    coded = Coded(refs)
-    if turns:
-        int_rows_ref[...] = masked(side_ref[...], a_ref, at.int_side, at.first).T
-    right = right_side(at, ("own", "int"), half, b_ref, graph_ref)
-    for i in range(panel):
-        block = panel + i
-        product = dot(ext_rows_ref[rows_at(block - at.starts["ext"]), :], right)
-        own_ref[rows_at(block), :] = product[:, :BS]
-        coded.write(product[:, BS:], i)
-    for i in range(panel):
-        block = at.ext_side + i
-        own_ref[rows_at(block), :] = dot(ext_rows_ref[rows_at(block - at.starts["ext"]), :], right[:, :BS])
-    for i in range(panel):
-        product = dot(int_rows_ref[i * BS : (i + 1) * BS, :], right)
-        own_ref[rows_at(at.int_side + i), :] = product[:, :BS]
-        coded.write(product[:, BS:], panel + i)
-    coded.finish()
-
-
-def own_products(a_lines, b_lines, graph, ext_rows, side_rows, half, widths, turns=False):
-    inner, width = graph.shape
-    panel = width // 3
-    outs = [jax.ShapeDtypeStruct((width, BS), jnp.float32)]
-    outs += [jax.ShapeDtypeStruct((HEAD + 2 * panel, w), jnp.int16) for w in widths]
-    if turns:
-        outs.append(pltpu.VMEM((panel, inner), graph.dtype))
-    return call(
-        functools.partial(own_kernel, half, turns),
+def own_kernel(half, b_ref, rest_ref, ext_rows_ref, int_rows_ref, own_ref, *int_refs):
+    at = Sides(rest_ref.shape[0], rest_ref.shape[1] // BS // 2)
+    own_half(at, half, b_ref, rest_ref, ext_rows_ref, int_rows_ref, own_ref, int_refs)
+
+
+def own_products(b_lines, graph_rest, ext_rows, int_rows, half, widths):
+    panel = graph_rest.shape[1] // 2
+    return call(
+        functools.partial(own_kernel, half),
         f"own_products_{half}",
-        (a_lines, b_lines, graph, ext_rows, side_rows),
-        [IN_SMEM, IN_SMEM] + [IN_VMEM] * 3,
-        outs,
+        (b_lines, graph_rest, ext_rows, int_rows),
+        [IN_SMEM] + [IN_VMEM] * 3,
+        [jax.ShapeDtypeStruct((3 * panel, BS), jnp.float32)]
+        + [jax.ShapeDtypeStruct((HEAD + 2 * panel, w), jnp.int16) for w in widths],
         limit=PRODUCT_LIMIT,
     )
 
@@ -269,12 +271,11 @@
     send_ref[0:HEAD, :] = jnp.broadcast_to(power, (HEAD, power.shape[1])).astype(jnp.int32).astype(jnp.int16)
 
 
-def join_kernel(rows, half, lane, ext_lane, c_ref, own_ref, ext_ref, int_ref, keep_ref, send_ref, total):
+def join_kernel(rows, half, lane, c_ref, own_ref, ext_ref, int_ref, keep_ref, send_ref, total):
     odd = lax.rem(lax.axis_index("blk"), 2)
     panel = own_ref.shape[0] // BS // 3
-    width = send_ref.shape[1]
-    lanes = slice(lane, lane + width)
-    refs = (ext_ref.at[:, ext_lane : ext_lane + width], int_ref)
+    lanes = slice(lane, lane + ext_ref.shape[1])
+    refs = (ext_ref, int_ref)
     ext, int_ = ([(r, i) for i in range(2 * panel)] for r in range(2))
     odd_parts = [[part] for part in int_] + [[] for _ in range(panel)]
     even_parts = [[] for _ in range(panel)] + [[part] for part in int_[panel:] + int_[:panel]]
@@ -310,12 +311,12 @@
     ]
 
 
-def join(own, ext_part, ext_lane, int_part, c_lines, half, lane, layers):
+def join(own, ext_part, int_part, c_lines, half, lane, layers):
     height = own.shape[0]
     width = int_part.shape[1]
     rows = height // layers
     return call(
-        functools.partial(join_kernel, rows, half, lane, ext_lane),
+        functools.partial(join_kernel, rows, half, lane),
         f"join_{half}_{lane}",
         (c_lines, own, ext_part, int_part),
         [IN_SMEM] + [IN_VMEM] * 3,
@@ -416,29 +417,28 @@
 
     def send_ext(parts):
         for part in parts:
-            got = swap(part, "blk", other_chip)
-            ext.extend((got, lane) for lane in range(0, part.shape[1], LANES))
+            ext.append(swap(part, "blk", other_chip))
         latest.append(parts[0])
 
-    first_part, ext_rows, graph, side_rows = first_products(flow_t, graph, a_lines, b_lines)
-    send_ext([first_part])
-
-    def own_half(half, side_rows, turns):
-        own, *parts = own_products(a_lines, ordered(b_lines), graph, ext_rows, side_rows, half, fine, turns)
-        if turns:
-            side_rows = parts.pop()
+    *parts, ext_rows, graph_ext = first_products(flow_t, graph, a_lines, b_lines, fine)
+    send_ext(parts)
+    ext_widths = fine * (halves - 1)
+    *parts, int_rows, graph_rest = second_products(
+        a_lines, b_lines, graph_ext, ext_rows, flow_t, graph, ext_widths, fine
+    )
+    send_ext(parts[: len(ext_widths)])
+
+    def send_int(own, *parts):
         ints.extend(swap(part, "blk", same_chip) for part in parts)
         owns.append(own)
         latest.append(own)
-        return side_rows
-
-    side_rows = own_half(0, side_rows, True)
-    send_ext(ext_products(ordered(b_lines), graph, ext_rows, (panel - 2 * LANES, LANES)))
+
+    send_int(*parts[len(ext_widths) :])
     strips, squares, sums = [], [], []
 
     def add_up(chunk):
         half, lane = divmod(chunk, per_half)
-        kept, send = join(owns[half], *ext[chunk], ints[chunk], ordered(c_lines), half, lane * LANES, layers)
+        kept, send = join(owns[half], ext[chunk], ints[chunk], ordered(c_lines), half, lane * LANES, layers)
         latest.append(send)
         strips.append((kept, swap(send, "layer", lambda i: i ^ 1)))
 
@@ -461,9 +461,10 @@
 
     add_up(0)
     for half in range(1, halves):
-        own_half(half, side_rows, False)
+        send_int(*own_products(ordered(b_lines), graph_rest, ext_rows, int_rows, half, fine))
+    add_up(1)
     scatter(0)
-    for chunk in range(1, chunks):
+    for chunk in range(2, chunks):
         if chunk == chunks - 1:
             finish(0)
         add_up(chunk)

time: 67.2 us -> 68 us (1.012)
  Pallas kernels: 21.9 us -> 22.7 us
    pallas_call x17 -> x16, Pallas kernels: 21.9 us -> 22.7 us  [call(): pl.pallas_call(kernel, out_shape=out_shape, in_specs=in_specs, out_specs=...]
    ppermute x18 -> x19, starting transfers between devices: 23.6 us -> 23.7 us  [swap(): lax.ppermute(block, axis, [(partner(i), i) for i in range(lax.axis_size(a...]
    ppermute x18 -> x19, waiting for transfers between devices: 21.4 us -> 21.4 us  [swap(): lax.ppermute(block, axis, [(partner(i), i) for i in range(lax.axis_size(a...]
  transfers between devices with their start and end apart: 18 -> 19, of which waited for: 9 -> 12; matrix products, arithmetic and copies ran while one was open for 0% -> 0% of each run, Pallas kernels for 23% -> 25%
where the time goes in v7:
time: 68 us; the launch traced here: 67.9 us
  starting transfers between devices  23.7 us (35%)
  Pallas kernels  22.7 us (33%)
  waiting for transfers between devices  21.4 us (31%)
    ppermute x19, starting transfers between devices, swap(): lax.ppermute(block, axis, [(partner(i), i) for i in range(lax.axis_size(a...  23.7 us
    pallas_call x16, Pallas kernels, call(): pl.pallas_call(kernel, out_shape=out_shape, in_specs=in_specs, out_specs=...  22.7 us
    ppermute x19, waiting for transfers between devices, swap(): lax.ppermute(block, axis, [(partner(i), i) for i in range(lax.axis_size(a...  21.4 us
  transfers between devices with their start and end apart: 19, of which 12 were waited for; matrix products, arithmetic and copies ran while one was open for 0% of the time, Pallas kernels for 25%

profile of v7, /device:TPU:0, one launch (start us, length us, event | category | flops | bytes accessed | tf_op | source)
XLA Modules:
  0.0 67.9 jit_solution(15294293169328847489)
XLA Ops:
  0.0 4.8 %first_products.1 = (s16[1040,128]{1,0:T(8,128)(2,1)S(1)}, s16[1040,128]{1,0:T(8,128)(2,1)S(1)}, bf16[1024,2048]{1,0:T(8,128)(2,1)S(1)}, bf16[2048,512]{1,0:T(8,128)(2,1)S(1)}) custom-call(s32[6,1,32]{2,1,0:T(1,128)} %bitcast.10, s32[6,1,32]{2,1,0:T(1,128)} %bitcast.3, bf16[1,2048,1536]{2,1,0:T(8,128)(2,1)} %flow_hbm.3, bf16[1,2048,1536]{2,1,0:T(8,128)(2,1)} %graph_hbm.3), custom_call_target="tpu_custom_call" | custom-call | flops 1 | bytes 1 | tf_op jit(solution)/shard_map/first_products/pallas_call | solution.py:32
  4.8 3.4 %collective-permute-start = (s16[1040,128]{1,0:T(8,128)(2,1)S(1)}, s16[1040,128]{1,0:T(8,128)(2,1)S(1)}, u32[]{:S(2)}, u32[]{:S(2)}) collective-permute-start(s16[1040,128]{1,0:T(8,128)(2,1)S(1)} %get-tuple-element.60), channel_id=1, source_target_pairs={{28,0},{8,4},{4,8},{16,12},{12,16},{24,20},{20,24},{0,28},{29,1},{... | collective-permute-start | bytes 798728 | tf_op jit(solution)/shard_map/ppermute | solution.py:24
  8.2 8.3 %second_products.1 = (s16[1040,128]{1,0:T(8,128)(2,1)S(1)}, s16[1040,128]{1,0:T(8,128)(2,1)S(1)}, f32[1536,256]{1,0:T(8,128)S(1)}, s16[1040,128]{1,0:T(8,128)(2,...) custom-call(s32[6,1,32]{2,1,0:T(1,128)S(1)} %bitcast.11, ...), custom_call_target="tpu_custom_call" | custom-call | flops 1 | bytes 1 | tf_op jit(solution)/shard_map/second_products/pallas_call | solution.py:32
  16.6 0.7 %collective-permute-start.2 = (s16[1040,128]{1,0:T(8,128)(2,1)S(1)}, s16[1040,128]{1,0:T(8,128)(2,1)S(1)}, u32[]{:S(2)}, u32[]{:S(2)}) collective-permute-start(s16[1040,128]{1,0:T(8,128)(2,1)S(1)} %get-tuple-element.69), channel_id=1, source_target_pairs={{28,0},{8,4},{4,8},{16,12},{12,16},{24,20},{20,24},{0,28},{29,1},{... | collective-permute-start | bytes 798728 | tf_op jit(solution)/shard_map/ppermute | solution.py:24
  17.3 0.6 collective-permute-start.3
  18.1 1.0 %join_0_0.1 = (f32[2,384,128]{2,1,0:T(8,128)S(1)}, s16[784,128]{1,0:T(8,128)(2,1)S(1)}) custom-call(s32[1,2,6]{2,1,0:T(2,128)S(1)} %bitcast.6, f32[1536,256]{1,0:T(8,128)S(1)} %get-tuple-element.58.own_ref, s16[1040,128]{1,0:T(8,128)(2,1)S(1)} %collective-permute-done.ext_ref, s16[1040,128]{1,0:T(8,128)(2,1)S(1)} %collective-permute-done.1.int_ref), custom_call_target="tpu_custom_call" | custom-call | flops 1 | bytes 1 | tf_op jit(solution)/shard_map/join_0_0/pallas_call | solution.py:32
  19.1 1.6 %collective-permute-start.4 = (s16[784,128]{1,0:T(8,128)(2,1)S(1)}, s16[784,128]{1,0:T(8,128)(2,1)S(1)}, u32[]{:S(2)}, u32[]{:S(2)}) collective-permute-start(s16[784,128]{1,0:T(8,128)(2,1)S(1)} %get-tuple-element.63), channel_id=1, source_target_pairs={{1,0},{0,1},{3,2},{2,3},{5,4},{4,5},{7,6},{6,7},{9,8},{8,9},{11,10... | collective-permute-start | bytes 602120 | tf_op jit(solution)/shard_map/ppermute | solution.py:24
  20.8 0.9 %collective-permute-start.5 = (s16[1040,128]{1,0:T(8,128)(2,1)S(1)}, s16[1040,128]{1,0:T(8,128)(2,1)S(1)}, u32[]{:S(2)}, u32[]{:S(2)}) collective-permute-start(s16[1040,128]{1,0:T(8,128)(2,1)S(1)} %get-tuple-element.76), channel_id=1, source_target_pairs={{28,0},{8,4},{4,8},{16,12},{12,16},{24,20},{20,24},{0,28},{29,1},{... | collective-permute-start | bytes 798728 | tf_op jit(solution)/shard_map/ppermute | solution.py:24
  21.7 3.7 %own_products_1.1 = (f32[1536,256]{1,0:T(8,128)S(1)}, s16[1040,128]{1,0:T(8,128)(2,1)S(1)}, s16[1040,128]{1,0:T(8,128)(2,1)S(1)}) custom-call(s32[6,1,32]{2,1,0:T(1,128)S(1)} %bitcast.5, bf16[2048,1024]{1,0:T(8,128)(2,1)S(1)} %get-tuple-element.65.rest_ref, bf16[1024,2048]{1,0:T(8,128)(2,1)S(1)} %get-tuple-element.57.ext_rows_ref, ...), custom_call_target="tpu_custom_call" | custom-call | flops 1 | bytes 1 | tf_op jit(solution)/shard_map/own_products_1/pallas_call | solution.py:32
  25.4 0.6 collective-permute-start.6
  26.3 1.0 %collective-permute-start.8 = (s16[1040,128]{1,0:T(8,128)(2,1)S(1)}, s16[1040,128]{1,0:T(8,128)(2,1)S(1)}, u32[]{:S(2)}, u32[]{:S(2)}) collective-permute-start(s16[1040,128]{1,0:T(8,128)(2,1)S(1)} %get-tuple-element.84), channel_id=1, source_target_pairs={{28,0},{8,4},{4,8},{16,12},{12,16},{24,20},{20,24},{0,28},{29,1},{... | collective-permute-start | bytes 798728 | tf_op jit(solution)/shard_map/ppermute | solution.py:24
  27.3 1.0 %join_0_128.1 = (f32[2,384,128]{2,1,0:T(8,128)S(1)}, s16[784,128]{1,0:T(8,128)(2,1)S(1)}) custom-call(s32[1,2,6]{2,1,0:T(2,128)S(1)} %bitcast.7, f32[1536,256]{1,0:T(8,128)S(1)} %get-tuple-element.58.own_ref, s16[1040,128]{1,0:T(8,128)(2,1)S(1)} %collective-permute-done.2.ext_ref, s16[1040,128]{1,0:T(8,128)(2,1)S(1)} %collective-permute-done.3.int_ref), custom_call_target="tpu_custom_call" | custom-call | flops 1 | bytes 1 | tf_op jit(solution)/shard_map/join_0_128/pallas_call | solution.py:32
  28.4 2.6 %collective-permute-start.7 = (s16[400,128]{1,0:T(8,128)(2,1)S(1)}, s16[400,128]{1,0:T(8,128)(2,1)S(1)}, u32[]{:S(2)}, u32[]{:S(2)}) collective-permute-start(s16[400,128]{1,0:T(8,128)(2,1)S(1)} %get-tuple-element.74), channel_id=1, source_target_pairs={{2,0},{3,1},{0,2},{1,3},{6,4},{7,5},{4,6},{5,7},{10,8},{11,9},{8,1... | collective-permute-start | bytes 307208 | tf_op jit(solution)/shard_map/ppermute | solution.py:24
  31.1 0.9 %collective-permute-done.5.ext_ref = s16[1040,128]{1,0:T(8,128)(2,1)S(1)} collective-permute-done((s16[1040,128]{1,0:T(8,128)(2,1)S(1)}, s16[1040,128]{1,0:T(8,128)(2,1)S(1)}, u32[]{:S(2)}, u32[]{:S(2)}) %collective-permute-start.5) | collective-permute-done | bytes 266272 | tf_op jit(solution)/shard_map/ppermute | solution.py:24
  32.0 1.6 %collective-permute-start.10 = (s16[784,128]{1,0:T(8,128)(2,1)S(1)}, s16[784,128]{1,0:T(8,128)(2,1)S(1)}, u32[]{:S(2)}, u32[]{:S(2)}) collective-permute-start(s16[784,128]{1,0:T(8,128)(2,1)S(1)} %get-tuple-element.71), channel_id=1, source_target_pairs={{1,0},{0,1},{3,2},{2,3},{5,4},{4,5},{7,6},{6,7},{9,8},{8,9},{11,10... | collective-permute-start | bytes 602120 | tf_op jit(solution)/shard_map/ppermute | solution.py:24
  33.6 1.0 %join_1_0.1 = (f32[2,384,128]{2,1,0:T(8,128)S(1)}, s16[784,128]{1,0:T(8,128)(2,1)S(1)}) custom-call(s32[1,2,6]{2,1,0:T(2,128)S(1)} %bitcast.8, f32[1536,256]{1,0:T(8,128)S(1)} %get-tuple-element.67.own_ref, s16[1040,128]{1,0:T(8,128)(2,1)S(1)} %collective-permute-done.5.ext_ref, s16[1040,128]{1,0:T(8,128)(2,1)S(1)} %collective-permute-done.6.int_ref), custom_call_target="tpu_custom_call" | custom-call | flops 1 | bytes 1 | tf_op jit(solution)/shard_map/join_1_0/pallas_call | solution.py:32
  35.0 2.0 %collective-permute-done.7.got_ref = s16[400,128]{1,0:T(8,128)(2,1)S(1)} collective-permute-done((s16[400,128]{1,0:T(8,128)(2,1)S(1)}, s16[400,128]{1,0:T(8,128)(2,1)S(1)}, u32[]{:S(2)}, u32[]{:S(2)}) %collective-permute-start.7) | collective-permute-done | bytes 102432 | tf_op jit(solution)/shard_map/ppermute | solution.py:24
  37.1 0.6 collective-permute-done.8.ext_ref
  37.7 1.0 %join_1_128.1 = (f32[2,384,128]{2,1,0:T(8,128)S(1)}, s16[784,128]{1,0:T(8,128)(2,1)S(1)}) custom-call(s32[1,2,6]{2,1,0:T(2,128)S(1)} %bitcast.9, f32[1536,256]{1,0:T(8,128)S(1)} %get-tuple-element.67.own_ref, s16[1040,128]{1,0:T(8,128)(2,1)S(1)} %collective-permute-done.8.ext_ref, s16[1040,128]{1,0:T(8,128)(2,1)S(1)} %collective-permute-done.9.int_ref), custom_call_target="tpu_custom_call" | custom-call | flops 1 | bytes 1 | tf_op jit(solution)/shard_map/join_1_128/pallas_call | solution.py:32
  38.6 1.6 %collective-permute-start.12 = (s16[784,128]{1,0:T(8,128)(2,1)S(1)}, s16[784,128]{1,0:T(8,128)(2,1)S(1)}, u32[]{:S(2)}, u32[]{:S(2)}) collective-permute-start(s16[784,128]{1,0:T(8,128)(2,1)S(1)} %get-tuple-element.86), channel_id=1, source_target_pairs={{1,0},{0,1},{3,2},{2,3},{5,4},{4,5},{7,6},{6,7},{9,8},{8,9},{11,10... | collective-permute-start | bytes 602120 | tf_op jit(solution)/shard_map/ppermute | solution.py:24
  40.3 0.9 %collective-permute-done.10.got_ref = s16[784,128]{1,0:T(8,128)(2,1)S(1)} collective-permute-done((s16[784,128]{1,0:T(8,128)(2,1)S(1)}, s16[784,128]{1,0:T(8,128)(2,1)S(1)}, u32[]{:S(2)}, u32[]{:S(2)}) %collective-permute-start.10) | collective-permute-done | bytes 200736 | tf_op jit(solution)/shard_map/ppermute | solution.py:24
  41.3 1.8 %collective-permute-start.13 = (s16[400,128]{1,0:T(8,128)(2,1)S(1)}, s16[400,128]{1,0:T(8,128)(2,1)S(1)}, u32[]{:S(2)}, u32[]{:S(2)}) collective-permute-start(s16[400,128]{1,0:T(8,128)(2,1)S(1)} %get-tuple-element.91), channel_id=1, source_target_pairs={{2,0},{3,1},{0,2},{1,3},{6,4},{7,5},{4,6},{5,7},{10,8},{11,9},{8,1... | collective-permute-start | bytes 307208 | tf_op jit(solution)/shard_map/ppermute | solution.py:24
  43.1 5.6 %collective-permute-done.11.got_ref = s16[784,128]{1,0:T(8,128)(2,1)S(1)} collective-permute-done((s16[784,128]{1,0:T(8,128)(2,1)S(1)}, s16[784,128]{1,0:T(8,128)(2,1)S(1)}, u32[]{:S(2)}, u32[]{:S(2)}) %collective-permute-start.11) | collective-permute-done | bytes 200736 | tf_op jit(solution)/shard_map/ppermute | solution.py:24
  49.4 2.5 %collective-permute-done.12.got_ref = s16[784,128]{1,0:T(8,128)(2,1)S(1)} collective-permute-done((s16[784,128]{1,0:T(8,128)(2,1)S(1)}, s16[784,128]{1,0:T(8,128)(2,1)S(1)}, u32[]{:S(2)}, u32[]{:S(2)}) %collective-permute-start.12) | collective-permute-done | bytes 200736 | tf_op jit(solution)/shard_map/ppermute | solution.py:24
  52.1 1.7 %collective-permute-start.15 = (s16[400,128]{1,0:T(8,128)(2,1)S(1)}, s16[400,128]{1,0:T(8,128)(2,1)S(1)}, u32[]{:S(2)}, u32[]{:S(2)}) collective-permute-start(s16[400,128]{1,0:T(8,128)(2,1)S(1)} %get-tuple-element.95), channel_id=1, source_target_pairs={{2,0},{3,1},{0,2},{1,3},{6,4},{7,5},{4,6},{5,7},{10,8},{11,9},{8,1... | collective-permute-start | bytes 307208 | tf_op jit(solution)/shard_map/ppermute | solution.py:24
  53.8 2.0 %collective-permute-done.14.got_ref = s16[400,128]{1,0:T(8,128)(2,1)S(1)} collective-permute-done((s16[400,128]{1,0:T(8,128)(2,1)S(1)}, s16[400,128]{1,0:T(8,128)(2,1)S(1)}, u32[]{:S(2)}, u32[]{:S(2)}) %collective-permute-start.14) | collective-permute-done | bytes 102432 | tf_op jit(solution)/shard_map/ppermute | solution.py:24
  55.9 3.7 %collective-permute-done.15.got_ref = s16[400,128]{1,0:T(8,128)(2,1)S(1)} collective-permute-done((s16[400,128]{1,0:T(8,128)(2,1)S(1)}, s16[400,128]{1,0:T(8,128)(2,1)S(1)}, u32[]{:S(2)}, u32[]{:S(2)}) %collective-permute-start.15) | collective-permute-done | bytes 102432 | tf_op jit(solution)/shard_map/ppermute | solution.py:24
  59.6 2.6 %collective-permute-start.18 = (f32[8,512]{1,0:T(8,128)S(1)}, f32[8,512]{1,0:T(8,128)S(1)}, u32[]{:S(2)}, u32[]{:S(2)}) collective-permute-start(f32[8,512]{1,0:T(8,128)S(1)} %get-tuple-element.106.refs_4_), channel_id=1, source_target_pairs={{3,0},{2,1},{1,2},{0,3},{7,4},{6,5},{5,6},{4,7},{11,8},{10,9},{9,1... | collective-permute-start | bytes 49160 | tf_op jit(solution)/shard_map/ppermute | solution.py:24
  62.3 1.8 %collective-permute-start.16 = (f32[8,512]{1,0:T(8,128)S(1)}, f32[8,512]{1,0:T(8,128)S(1)}, u32[]{:S(2)}, u32[]{:S(2)}) collective-permute-start(f32[8,512]{1,0:T(8,128)S(1)} %get-tuple-element.106.refs_4_), channel_id=1, source_target_pairs={{1,0},{0,1},{3,2},{2,3},{5,4},{4,5},{7,6},{6,7},{9,8},{8,9},{11,10... | collective-permute-start | bytes 49160 | tf_op jit(solution)/shard_map/ppermute | solution.py:24
  64.1 1.2 %collective-permute-done.18.refs_7_ = f32[8,512]{1,0:T(8,128)S(1)} collective-permute-done((f32[8,512]{1,0:T(8,128)S(1)}, f32[8,512]{1,0:T(8,128)S(1)}, u32[]{:S(2)}, u32[]{:S(2)}) %collective-permute-start.18) | collective-permute-done | bytes 16416 | tf_op jit(solution)/shard_map/ppermute | solution.py:24
  65.3 1.6 %collective-permute-done.17.refs_6_ = f32[8,512]{1,0:T(8,128)S(1)} collective-permute-done((f32[8,512]{1,0:T(8,128)S(1)}, f32[8,512]{1,0:T(8,128)S(1)}, u32[]{:S(2)}, u32[]{:S(2)}) %collective-permute-start.17) | collective-permute-done | bytes 16416 | tf_op jit(solution)/shard_map/ppermute | solution.py:24
  66.9 1.0 %rescale.1 = f32[1,384,512]{2,1,0:T(8,128)} custom-call(f32[384,128]{1,0:T(8,128)S(1)} %get-tuple-element.80.refs_0_, f32[384,128]{1,0:T(8,128)S(1)} %get-tuple-element.97.refs_1_, f32[384,128]{1,0:T(8,128)S(1)} %get-tuple-element.101.refs_2_, f32[384,128]{1,0:T(8,128)S(1)} %get-tuple-element.105.refs_3_, f32[8,512]{1,0:T(8,128)S(1)} %get-tuple-element.106.refs_4_, ...), custom_call_target="tpu_custom_call" | custom-call | flops 1 | bytes 1 | tf_op jit(solution)/shard_map/rescale/pallas_call | solution.py:32
  (28 shorter events, 2.6 us)
Async XLA Ops:
  0.0 8.2 %copy-start = (s32[1,32,6]{1,0,2:T(1,128)S(1)}, s32[1,32,6]{1,0,2:T(1,128)}, u32[]{:S(2)}) copy-start(s32[1,32,6]{1,0,2:T(1,128)} %param.8) | copy-start | bytes 2308
  0.0 8.2 %copy-start.2 = (s32[1,32,6]{1,0,2:T(1,128)S(1)}, s32[1,32,6]{1,0,2:T(1,128)}, u32[]{:S(2)}) copy-start(s32[1,32,6]{1,0,2:T(1,128)} %param.7) | copy-start | bytes 2308
  4.8 13.1 %collective-permute-start = (s16[1040,128]{1,0:T(8,128)(2,1)S(1)}, s16[1040,128]{1,0:T(8,128)(2,1)S(1)}, u32[]{:S(2)}, u32[]{:S(2)}) collective-permute-start(s16[1040,128]{1,0:T(8,128)(2,1)S(1)} %get-tuple-element.60), channel_id=1, source_target_pairs={{28,0},{8,4},{4,8},{16,12},{12,16},{24,20},{20,24},{0,28},{29,1},{... | collective-permute-start | bytes 798728 | tf_op jit(solution)/shard_map/ppermute | solution.py:24
  8.2 9.9 %copy-start.1 = (s32[1,6,2]{1,2,0:T(2,128)S(1)}, s32[1,6,2]{1,2,0:T(2,128)}, u32[]{:S(2)}) copy-start(s32[1,6,2]{1,2,0:T(2,128)} %param.9) | copy-start | bytes 148
  16.5 1.6 %collective-permute-start.1 = (s16[1040,128]{1,0:T(8,128)(2,1)S(1)}, s16[1040,128]{1,0:T(8,128)(2,1)S(1)}, u32[]{:S(2)}, u32[]{:S(2)}) collective-permute-start(s16[1040,128]{1,0:T(8,128)(2,1)S(1)} %get-tuple-element.61), channel_id=1, source_target_pairs={{4,0},{0,4},{12,8},{8,12},{20,16},{16,20},{28,24},{24,28},{5,1},{1... | collective-permute-start | bytes 798728 | tf_op jit(solution)/shard_map/ppermute | solution.py:24
  16.6 9.7 %collective-permute-start.2 = (s16[1040,128]{1,0:T(8,128)(2,1)S(1)}, s16[1040,128]{1,0:T(8,128)(2,1)S(1)}, u32[]{:S(2)}, u32[]{:S(2)}) collective-permute-start(s16[1040,128]{1,0:T(8,128)(2,1)S(1)} %get-tuple-element.69), channel_id=1, source_target_pairs={{28,0},{8,4},{4,8},{16,12},{12,16},{24,20},{20,24},{0,28},{29,1},{... | collective-permute-start | bytes 798728 | tf_op jit(solution)/shard_map/ppermute | solution.py:24
  17.3 9.9 %collective-permute-start.3 = (s16[1040,128]{1,0:T(8,128)(2,1)S(1)}, s16[1040,128]{1,0:T(8,128)(2,1)S(1)}, u32[]{:S(2)}, u32[]{:S(2)}) collective-permute-start(s16[1040,128]{1,0:T(8,128)(2,1)S(1)} %get-tuple-element.70), channel_id=1, source_target_pairs={{4,0},{0,4},{12,8},{8,12},{20,16},{16,20},{28,24},{24,28},{5,1},{1... | collective-permute-start | bytes 798728 | tf_op jit(solution)/shard_map/ppermute | solution.py:24
  19.1 9.1 %collective-permute-start.4 = (s16[784,128]{1,0:T(8,128)(2,1)S(1)}, s16[784,128]{1,0:T(8,128)(2,1)S(1)}, u32[]{:S(2)}, u32[]{:S(2)}) collective-permute-start(s16[784,128]{1,0:T(8,128)(2,1)S(1)} %get-tuple-element.63), channel_id=1, source_target_pairs={{1,0},{0,1},{3,2},{2,3},{5,4},{4,5},{7,6},{6,7},{9,8},{8,9},{11,10... | collective-permute-start | bytes 602120 | tf_op jit(solution)/shard_map/ppermute | solution.py:24
  20.8 11.2 %collective-permute-start.5 = (s16[1040,128]{1,0:T(8,128)(2,1)S(1)}, s16[1040,128]{1,0:T(8,128)(2,1)S(1)}, u32[]{:S(2)}, u32[]{:S(2)}) collective-permute-start(s16[1040,128]{1,0:T(8,128)(2,1)S(1)} %get-tuple-element.76), channel_id=1, source_target_pairs={{28,0},{8,4},{4,8},{16,12},{12,16},{24,20},{20,24},{0,28},{29,1},{... | collective-permute-start | bytes 798728 | tf_op jit(solution)/shard_map/ppermute | solution.py:24
  25.4 8.2 %collective-permute-start.6 = (s16[1040,128]{1,0:T(8,128)(2,1)S(1)}, s16[1040,128]{1,0:T(8,128)(2,1)S(1)}, u32[]{:S(2)}, u32[]{:S(2)}) collective-permute-start(s16[1040,128]{1,0:T(8,128)(2,1)S(1)} %get-tuple-element.77), channel_id=1, source_target_pairs={{4,0},{0,4},{12,8},{8,12},{20,16},{16,20},{28,24},{24,28},{5,1},{1... | collective-permute-start | bytes 798728 | tf_op jit(solution)/shard_map/ppermute | solution.py:24
  26.3 11.4 %collective-permute-start.8 = (s16[1040,128]{1,0:T(8,128)(2,1)S(1)}, s16[1040,128]{1,0:T(8,128)(2,1)S(1)}, u32[]{:S(2)}, u32[]{:S(2)}) collective-permute-start(s16[1040,128]{1,0:T(8,128)(2,1)S(1)} %get-tuple-element.84), channel_id=1, source_target_pairs={{28,0},{8,4},{4,8},{16,12},{12,16},{24,20},{20,24},{0,28},{29,1},{... | collective-permute-start | bytes 798728 | tf_op jit(solution)/shard_map/ppermute | solution.py:24
  27.3 10.4 %collective-permute-start.9 = (s16[1040,128]{1,0:T(8,128)(2,1)S(1)}, s16[1040,128]{1,0:T(8,128)(2,1)S(1)}, u32[]{:S(2)}, u32[]{:S(2)}) collective-permute-start(s16[1040,128]{1,0:T(8,128)(2,1)S(1)} %get-tuple-element.85), channel_id=1, source_target_pairs={{4,0},{0,4},{12,8},{8,12},{20,16},{16,20},{28,24},{24,28},{5,1},{1... | collective-permute-start | bytes 798728 | tf_op jit(solution)/shard_map/ppermute | solution.py:24
  28.4 8.6 %collective-permute-start.7 = (s16[400,128]{1,0:T(8,128)(2,1)S(1)}, s16[400,128]{1,0:T(8,128)(2,1)S(1)}, u32[]{:S(2)}, u32[]{:S(2)}) collective-permute-start(s16[400,128]{1,0:T(8,128)(2,1)S(1)} %get-tuple-element.74), channel_id=1, source_target_pairs={{2,0},{3,1},{0,2},{1,3},{6,4},{7,5},{4,6},{5,7},{10,8},{11,9},{8,1... | collective-permute-start | bytes 307208 | tf_op jit(solution)/shard_map/ppermute | solution.py:24
  32.0 9.2 %collective-permute-start.10 = (s16[784,128]{1,0:T(8,128)(2,1)S(1)}, s16[784,128]{1,0:T(8,128)(2,1)S(1)}, u32[]{:S(2)}, u32[]{:S(2)}) collective-permute-start(s16[784,128]{1,0:T(8,128)(2,1)S(1)} %get-tuple-element.71), channel_id=1, source_target_pairs={{1,0},{0,1},{3,2},{2,3},{5,4},{4,5},{7,6},{6,7},{9,8},{8,9},{11,10... | collective-permute-start | bytes 602120 | tf_op jit(solution)/shard_map/ppermute | solution.py:24
  34.5 14.2 %collective-permute-start.11 = (s16[784,128]{1,0:T(8,128)(2,1)S(1)}, s16[784,128]{1,0:T(8,128)(2,1)S(1)}, u32[]{:S(2)}, u32[]{:S(2)}) collective-permute-start(s16[784,128]{1,0:T(8,128)(2,1)S(1)} %get-tuple-element.78), channel_id=1, source_target_pairs={{1,0},{0,1},{3,2},{2,3},{5,4},{4,5},{7,6},{6,7},{9,8},{8,9},{11,10... | collective-permute-start | bytes 602120 | tf_op jit(solution)/shard_map/ppermute | solution.py:24
  38.6 13.2 %collective-permute-start.12 = (s16[784,128]{1,0:T(8,128)(2,1)S(1)}, s16[784,128]{1,0:T(8,128)(2,1)S(1)}, u32[]{:S(2)}, u32[]{:S(2)}) collective-permute-start(s16[784,128]{1,0:T(8,128)(2,1)S(1)} %get-tuple-element.86), channel_id=1, source_target_pairs={{1,0},{0,1},{3,2},{2,3},{5,4},{4,5},{7,6},{6,7},{9,8},{8,9},{11,10... | collective-permute-start | bytes 602120 | tf_op jit(solution)/shard_map/ppermute | solution.py:24
  41.3 12.4 %collective-permute-start.13 = (s16[400,128]{1,0:T(8,128)(2,1)S(1)}, s16[400,128]{1,0:T(8,128)(2,1)S(1)}, u32[]{:S(2)}, u32[]{:S(2)}) collective-permute-start(s16[400,128]{1,0:T(8,128)(2,1)S(1)} %get-tuple-element.91), channel_id=1, source_target_pairs={{2,0},{3,1},{0,2},{1,3},{6,4},{7,5},{4,6},{5,7},{10,8},{11,9},{8,1... | collective-permute-start | bytes 307208 | tf_op jit(solution)/shard_map/ppermute | solution.py:24
  48.9 6.9 %collective-permute-start.14 = (s16[400,128]{1,0:T(8,128)(2,1)S(1)}, s16[400,128]{1,0:T(8,128)(2,1)S(1)}, u32[]{:S(2)}, u32[]{:S(2)}) collective-permute-start(s16[400,128]{1,0:T(8,128)(2,1)S(1)} %get-tuple-element.93), channel_id=1, source_target_pairs={{2,0},{3,1},{0,2},{1,3},{6,4},{7,5},{4,6},{5,7},{10,8},{11,9},{8,1... | collective-permute-start | bytes 307208 | tf_op jit(solution)/shard_map/ppermute | solution.py:24
  52.1 7.5 %collective-permute-start.15 = (s16[400,128]{1,0:T(8,128)(2,1)S(1)}, s16[400,128]{1,0:T(8,128)(2,1)S(1)}, u32[]{:S(2)}, u32[]{:S(2)}) collective-permute-start(s16[400,128]{1,0:T(8,128)(2,1)S(1)} %get-tuple-element.95), channel_id=1, source_target_pairs={{2,0},{3,1},{0,2},{1,3},{6,4},{7,5},{4,6},{5,7},{10,8},{11,9},{8,1... | collective-permute-start | bytes 307208 | tf_op jit(solution)/shard_map/ppermute | solution.py:24
  59.6 5.6 %collective-permute-start.18 = (f32[8,512]{1,0:T(8,128)S(1)}, f32[8,512]{1,0:T(8,128)S(1)}, u32[]{:S(2)}, u32[]{:S(2)}) collective-permute-start(f32[8,512]{1,0:T(8,128)S(1)} %get-tuple-element.106.refs_4_), channel_id=1, source_target_pairs={{3,0},{2,1},{1,2},{0,3},{7,4},{6,5},{5,6},{4,7},{11,8},{10,9},{9,1... | collective-permute-start | bytes 49160 | tf_op jit(solution)/shard_map/ppermute | solution.py:24
  62.2 4.6 %collective-permute-start.17 = (f32[8,512]{1,0:T(8,128)S(1)}, f32[8,512]{1,0:T(8,128)S(1)}, u32[]{:S(2)}, u32[]{:S(2)}) collective-permute-start(f32[8,512]{1,0:T(8,128)S(1)} %get-tuple-element.106.refs_4_), channel_id=1, source_target_pairs={{2,0},{3,1},{0,2},{1,3},{6,4},{7,5},{4,6},{5,7},{10,8},{11,9},{8,1... | collective-permute-start | bytes 49160 | tf_op jit(solution)/shard_map/ppermute | solution.py:24
  62.3 4.6 %collective-permute-start.16 = (f32[8,512]{1,0:T(8,128)S(1)}, f32[8,512]{1,0:T(8,128)S(1)}, u32[]{:S(2)}, u32[]{:S(2)}) collective-permute-start(f32[8,512]{1,0:T(8,128)S(1)} %get-tuple-element.106.refs_4_), channel_id=1, source_target_pairs={{1,0},{0,1},{3,2},{2,3},{5,4},{4,5},{7,6},{6,7},{9,8},{8,9},{11,10... | collective-permute-start | bytes 49160 | tf_op jit(solution)/shard_map/ppermute | solution.py:24

commit v8 on v3

v8 whole, which is shorter than its diff:
```python
import functools

import jax
import jax.numpy as jnp
from jax import lax
from jax.experimental import pallas as pl
from jax.experimental.pallas import tpu as pltpu
from jax.sharding import PartitionSpec as P

BS = 256
LANES = 128
HEAD = 16
STEPS = 256.0
TOP = 65534.0
LN2 = 0.6931471805599453
DIRECT = 0
PRODUCT_LIMIT = 24000000
SMALL_LIMIT = 8 * 1024 * 1024
IN_SMEM = pl.BlockSpec(memory_space=pltpu.SMEM)
IN_VMEM = pl.BlockSpec(memory_space=pltpu.VMEM)
IN_HBM = pl.BlockSpec(memory_space=pltpu.HBM)


def swap(block, axis, partner):
    return lax.ppermute(block, axis, [(partner(i), i) for i in range(lax.axis_size(axis))])


def after(value, *others):
    return lax.optimization_barrier((value, *others))[0]


def call(kernel, name, operands, in_specs, out_shape, scratch_shapes=(), limit=SMALL_LIMIT):
    return pl.pallas_call(
        kernel,
        out_shape=out_shape,
        in_specs=in_specs,
        out_specs=jax.tree.map(lambda _: IN_VMEM, out_shape),
        scratch_shapes=list(scratch_shapes),
        compiler_params=pltpu.CompilerParams(vmem_limit_bytes=limit),
        cost_estimate=pl.CostEstimate(flops=1, bytes_accessed=1, transcendentals=0),
        name=name,
    )(*operands)


def powers(values):
    largest = jnp.maximum(jnp.max(values, axis=0, keepdims=True), 1e-3)
    return jnp.floor(jnp.log(largest) * (STEPS / LN2)) + 2.0


def code(values, power):
    scaled = values * (TOP * jnp.exp(power * (-LN2 / STEPS)))
    return ((scaled + 0.5).astype(jnp.int32) - 32767).astype(jnp.int16)


def scales(head):
    return jnp.exp(head.astype(jnp.int32).astype(jnp.float32) * (LN2 / STEPS)) * (1.0 / TOP)


def decode(codes, scale):
    return (codes.astype(jnp.int32) + 32767).astype(jnp.float32) * scale


def masked(values, pattern, column, first):
    depth, width = values.shape
    place = lax.broadcasted_iota(jnp.int32, (1, width), 1) // BS
    parts = []
    for u in range(depth // BS):
        factor = jnp.zeros((1, width), jnp.float32)
        for v in range(width // BS):
            factor = jnp.where(place == v, pattern[column + v, 0, first + u].astype(jnp.float32), factor)
        parts.append(values[u * BS : (u + 1) * BS] * factor.astype(values.dtype))
    return jnp.concatenate(parts, axis=0) if len(parts) > 1 else parts[0]


def dot(left_side, right_side):
    return lax.dot_general(
        left_side, right_side, (((1,), (0,)), ((), ())), preferred_element_type=jnp.float32
    )


def columns_of(ref, start, count):
    return ref.at[0, :, pl.ds(pl.multiple_of(start * BS, BS), count * BS)]


def blocks_at(block, count=1):
    return pl.ds(pl.multiple_of(block * BS, BS), count * BS)


class Sides:
    def __init__(self, inner, panel):
        odd = lax.rem(lax.axis_index("blk"), 2)
        self.panel = panel
        self.first = lax.axis_index("layer") * (inner // BS)
        self.ext_side, self.int_side = odd * (2 * panel), (1 - odd) * (2 * panel)
        self.ext_rows = odd * panel
        self.columns = {"ext": self.ext_side, "own": panel, "int": self.int_side}


class Coded:
    def __init__(self, refs):
        self.refs = refs
        self.heads = [jnp.zeros((HEAD, ref.shape[1]), jnp.float32) for ref in refs]

    def write_all(self, product, place):
        for i in range(product.shape[0] // BS):
            self.write(product[i * BS : (i + 1) * BS], place + i)

    def write(self, product, place):
        column = 0
        for c, ref in enumerate(self.refs):
            chunk = product[:, column : column + ref.shape[1]]
            column += ref.shape[1]
            power = powers(chunk)
            ref[HEAD + place * BS : HEAD + (place + 1) * BS, :] = code(chunk, power)
            line = lax.broadcasted_iota(jnp.int32, self.heads[c].shape, 0)
            self.heads[c] = jnp.where(line == place, power, self.heads[c])

    def finish(self):
        for ref, head in zip(self.refs, self.heads):
            ref[0:HEAD, :] = head.astype(jnp.int32).astype(jnp.int16)


def first_kernel(a_hbm, b_hbm, flow_hbm, graph_hbm, *rest):
    out_refs, (rows_ref, graph_buf, flow_buf, total, a_ref, b_ref, sems) = rest[:-7], rest[-7:]
    inner, panel = flow_buf.shape[0], flow_buf.shape[1] // BS // 2
    at = Sides(inner, panel)
    steps = inner // BS
    small = [pltpu.make_async_copy(a_hbm, a_ref, sems.at[0]), pltpu.make_async_copy(b_hbm, b_ref, sems.at[1])]
    flows, graphs = [], []
    for t in range(steps):
        rows = slice(t * BS, (t + 1) * BS)
        flow = columns_of(flow_hbm, at.ext_rows, 2 * panel).at[rows]
        graph = columns_of(graph_hbm, at.ext_side, 1).at[rows]
        flows.append(pltpu.make_async_copy(flow, flow_buf.at[rows], sems.at[2 + 2 * t]))
        graphs.append(pltpu.make_async_copy(graph, graph_buf.at[rows], sems.at[3 + 2 * t]))
    for copy in small:
        copy.start()
    for t in range(steps):
        flows[t].start()
        graphs[t].start()
    for copy in small:
        copy.wait()
    per_dot = min(2, steps)
    for t in range(0, steps, per_dot):
        rows = slice(t * BS, (t + per_dot) * BS)
        for copy in flows[t : t + per_dot] + graphs[t : t + per_dot]:
            copy.wait()
        turned = masked(flow_buf[rows, :], a_ref, at.ext_rows, at.first + t).T
        rows_ref[:, rows] = turned
        product = dot(turned, masked(graph_buf[rows, :], b_ref, at.ext_side, at.first + t))
        if t + per_dot < steps:
            total[...] = product if t == 0 else total[...] + product
    if steps > per_dot:
        total[...] += product
    else:
        total[...] = product
    coded = Coded(out_refs)
    for place, first in ((0, panel), (panel, at.ext_side)):
        for i in range(panel):
            coded.write(total[blocks_at(first - at.ext_rows + i), :], place + i)
    coded.finish()


def first_products(flow_t, graph, a_lines, b_lines, widths):
    inner, width = flow_t.shape[1:]
    panel = width // 3
    return call(
        first_kernel,
        "first_products",
        [pltpu.with_memory_space_constraint(x, pltpu.HBM) for x in (a_lines, b_lines, flow_t, graph)],
        [IN_HBM] * 4,
        [jax.ShapeDtypeStruct((HEAD + 2 * panel, w), jnp.int16) for w in widths]
        + [pltpu.VMEM((2 * panel, inner), flow_t.dtype)],
        [
            pltpu.VMEM((inner, BS), graph.dtype),
            pltpu.VMEM((inner, 2 * panel), flow_t.dtype),
            pltpu.VMEM((2 * panel, BS), jnp.float32),
            pltpu.SMEM(a_lines.shape, a_lines.dtype),
            pltpu.SMEM(b_lines.shape, b_lines.dtype),
            pltpu.SemaphoreType.DMA((2 + 2 * (inner // BS),)),
        ],
        limit=PRODUCT_LIMIT,
    )


def product_kernel(half, wanted, turns, a_ref, b_ref, graph_ref, ext_rows_ref, side_ref, *rest):
    refs = list(rest)
    inner, panel = graph_ref.shape[1], graph_ref.shape[2] // BS // 3
    at = Sides(inner, panel)
    parts = [part for part in ("ext", "own", "int") if part in wanted]
    outs = {part: [refs.pop(0) for _ in wanted[part]] for part in parts}
    int_rows_ref = side_ref
    if turns:
        int_rows_ref = refs.pop(0)
        int_rows_ref[...] = masked(side_ref[0, :, blocks_at(at.int_side, panel)], a_ref, at.int_side, at.first).T
    coded = {part: Coded(outs[part]) for part in parts if part != "own"}
    right = []
    for part in parts:
        column = at.columns[part] + half
        right.append(masked(graph_ref[0, :, blocks_at(column)], b_ref, column, at.first))
    right = jnp.concatenate(right, axis=1) if len(right) > 1 else right[0]
    panels = (
        (panel, ext_rows_ref.at[blocks_at(panel - at.ext_rows, panel)], {"ext": 0, "own": 0, "int": 0}),
        (at.ext_side, ext_rows_ref.at[blocks_at(at.ext_side - at.ext_rows, panel)], {"ext": panel, "own": 0}),
        (at.int_side, int_rows_ref, {"own": 0, "int": panel}),
    )
    for first, source, takers in panels:
        used = [part for part in parts if part in takers]
        if not used:
            continue
        low = parts.index(used[0]) * BS
        for i in range(panel):
            product = dot(source[i * BS : (i + 1) * BS, :], right[:, low : low + len(used) * BS])
            for j, part in enumerate(used):
                piece = product[:, j * BS : (j + 1) * BS]
                if part == "own":
                    outs[part][0][blocks_at(first + i), :] = piece
                else:
                    coded[part].write(piece, takers[part] + i)
    for part in coded:
        coded[part].finish()


def products(a_lines, b_lines, graph, ext_rows, side, half, wanted, turns=False):
    inner, width = graph.shape[1:]
    panel = width // 3
    outs = []
    for part in ("ext", "own", "int"):
        for w in wanted.get(part, ()):
            if part == "own":
                outs.append(jax.ShapeDtypeStruct((width, w), jnp.float32))
            else:
                outs.append(jax.ShapeDtypeStruct((HEAD + 2 * panel, w), jnp.int16))
    if turns:
        outs.append(pltpu.VMEM((panel, inner), graph.dtype))
    return call(
        functools.partial(product_kernel, half, wanted, turns),
        "_".join(wanted) + f"_products_{half}",
        (a_lines, b_lines, graph, ext_rows, side),
        [IN_SMEM, IN_SMEM] + [IN_VMEM] * 3,
        outs,
        limit=PRODUCT_LIMIT,
    )


def send_strip(send_ref, strips, power):
    rows = strips[0].shape[0]
    for j, strip in enumerate(strips):
        send_ref[HEAD + j * rows : HEAD + (j + 1) * rows, :] = code(strip, power)
    send_ref[0:HEAD, :] = jnp.broadcast_to(power, (HEAD, power.shape[1])).astype(jnp.int32).astype(jnp.int16)


def split_strips(total, rows, position, keep_ref, send_refs):
    layer = lax.axis_index("layer")
    if len(send_refs) > 1:
        keep_ref[0] = total[pl.ds(layer * rows, rows), :]
        for other, send_ref in enumerate(send_refs, 1):
            strip = total[pl.ds((layer ^ other) * rows, rows), :]
            send_strip(send_ref, [strip], powers(strip))
        return
    bit = lax.rem(layer // position, 2)
    pairs = keep_ref.shape[0]
    for j in range(pairs):
        keep_ref[j] = total[pl.ds((2 * j + bit) * rows, rows), :]
    away = [total[pl.ds((2 * j + 1 - bit) * rows, rows), :] for j in range(pairs)]
    send_strip(send_refs[0], away, functools.reduce(jnp.maximum, [powers(strip) for strip in away]))


def join_kernel(rows, half, lane, c_ref, own_ref, ext_ref, int_ref, keep_ref, *rest):
    *send_refs, total = rest
    odd = lax.rem(lax.axis_index("blk"), 2)
    panel = own_ref.shape[0] // BS // 3
    lanes = slice(lane, lane + ext_ref.shape[1])
    refs = (ext_ref, int_ref)
    from_mid, from_side = ([[(r, start + i) for i in range(panel)] for r in range(2)] for start in (0, panel))
    middle = [list(both) for both in zip(from_side[0], from_side[1])]
    ext_only, int_only = ([[part] for part in from_mid[r]] for r in range(2))
    odd_parts = int_only + middle + ext_only
    even_parts = ext_only + middle + int_only

    def add(parts):
        scale = [scales(ref[0:HEAD, :]) for ref in refs]
        for v in range(3 * panel):
            kept = c_ref[0, half, v].astype(jnp.float32)
            block = own_ref[v * BS : (v + 1) * BS, lanes] * kept
            for r, i in parts[v]:
                codes = refs[r][HEAD + i * BS : HEAD + (i + 1) * BS, :]
                block += decode(codes, scale[r][i : i + 1] * kept)
            total[v * BS : (v + 1) * BS, :] = block

    @pl.when(odd == 1)
    def _():
        add(odd_parts)

    @pl.when(odd == 0)
    def _():
        add(even_parts)

    split_strips(total, rows, 1, keep_ref, send_refs)


def strips_shapes(pairs, rows, width, messages=1):
    return [
        jax.ShapeDtypeStruct((pairs, rows, width), jnp.float32),
        *[jax.ShapeDtypeStruct((HEAD + pairs * rows, width), jnp.int16)] * messages,
    ]


def join(own, ext_part, int_part, c_lines, half, lane, layers, direct):
    height = own.shape[0]
    width = int_part.shape[1]
    rows = height // layers
    return call(
        functools.partial(join_kernel, rows, half, lane),
        f"join_{half}_{lane}",
        (c_lines, own, ext_part, int_part),
        [IN_SMEM] + [IN_VMEM] * 3,
        strips_shapes(1, rows, width, layers - 1) if direct else strips_shapes(layers // 2, rows, width),
        [pltpu.VMEM((height, width), jnp.float32)],
    )


def halve_kernel(rows, position, kept_ref, got_ref, keep_ref, send_ref, total):
    scale = scales(got_ref[0:HEAD, :])[0:1]
    for j in range(kept_ref.shape[0]):
        codes = got_ref[HEAD + j * rows : HEAD + (j + 1) * rows, :]
        total[j * rows : (j + 1) * rows, :] = kept_ref[j] + decode(codes, scale)
    split_strips(total, rows, position, keep_ref, [send_ref])


def halve(kept, got, position, chunk):
    strips, rows, width = kept.shape
    return call(
        functools.partial(halve_kernel, rows, position),
        f"halve_{position}_{chunk}",
        (kept, got),
        [IN_VMEM] * 2,
        strips_shapes(strips // 2, rows, width),
        [pltpu.VMEM((strips * rows, width), jnp.float32)],
    )


def square_kernel(messages, kept_ref, *rest):
    got_refs, earlier, (square_ref, sums_ref) = rest[:messages], rest[messages:-2], rest[-2:]
    value = kept_ref[0]
    for ref in got_refs:
        value += decode(ref[HEAD:, :], scales(ref[0:HEAD, :])[0:1])
    square = value * value
    square_ref[...] = square
    sums = jnp.broadcast_to(jnp.sum(square, axis=0, keepdims=True), (8, square.shape[1]))
    sums_ref[...] = jnp.concatenate([ref[...] for ref in earlier] + [sums], axis=1)


def square(kept, got, earlier, chunk):
    _, rows, width = kept.shape
    return call(
        functools.partial(square_kernel, len(got)),
        f"square_{chunk}",
        (kept, *got, *earlier),
        [IN_VMEM] * (1 + len(got) + len(earlier)),
        [
            jax.ShapeDtypeStruct((rows, width), jnp.float32),
            jax.ShapeDtypeStruct((8, width + sum(sums.shape[1] for sums in earlier)), jnp.float32),
        ],
    )


def rescale_kernel(height, count, *refs):
    squares, sums, out_ref = refs[:count], refs[count:-1], refs[-1]
    total = functools.reduce(jnp.add, [ref[0:1, :] for ref in sums])
    divisor = total / height + 1e-6
    column = 0
    for ref in squares:
        columns = slice(column, column + ref.shape[1])
        column += ref.shape[1]
        out_ref[0, :, columns] = ref[...] / divisor[:, columns]


def rescale(squares, sums, height):
    rows = squares[0].shape[0]
    width = sums[0].shape[1]
    return call(
        functools.partial(rescale_kernel, float(height), len(squares)),
        "rescale",
        (*squares, *sums),
        [IN_VMEM] * (len(squares) + len(sums)),
        jax.ShapeDtypeStruct((1, rows, width), jnp.float32),
    )


def shards(flow_t, graph, a_pattern, b_pattern, c_pattern):
    layers = lax.axis_size("layer")
    blks = lax.axis_size("blk")
    width = flow_t.shape[2]
    panel = width // 3
    a_lines = a_pattern.transpose(2, 0, 1)
    b_lines = b_pattern.transpose(2, 0, 1)
    c_lines = c_pattern.transpose(0, 2, 1)

    def other_chip(i):
        return (i + 1 if i % 2 else i - 1) % blks

    def same_chip(i):
        return i ^ 1

    halves = panel // BS
    chunks = panel // LANES
    fine = (LANES,) * (BS // LANES)
    per_half = len(fine)
    ext, ints, owns, latest = [], [], [], []

    def ordered(value):
        return after(value, latest[-1])

    def send_ext(parts):
        ext.extend(swap(part, "blk", other_chip) for part in parts)
        latest.append(parts[0])

    def send_int(parts):
        ints.extend(swap(part, "blk", same_chip) for part in parts)
        latest.append(parts[0])

    *parts, ext_rows = first_products(flow_t, graph, a_lines, b_lines, fine)
    send_ext(parts)
    wanted = {"own": (BS,), "int": fine}
    own, *parts, int_rows = products(a_lines, ordered(b_lines), graph, ext_rows, flow_t, 0, wanted, turns=True)
    owns.append(own)
    send_int(parts)

    def more_products(half):
        wanted = {"ext": fine, "int": fine}
        parts = products(a_lines, ordered(b_lines), graph, ext_rows, int_rows, half, wanted)
        send_ext(parts[:per_half])
        send_int(parts[per_half:])
        owns.extend(products(a_lines, ordered(b_lines), graph, ext_rows, int_rows, half, {"own": (BS,)}))
        latest.append(owns[-1])

    strips, squares, sums = [], [], []

    def add_up(chunk):
        half, lane = divmod(chunk, per_half)
        direct = chunk >= chunks - DIRECT and layers <= 4
        kept, *sends = join(
            owns[half], ext[chunk], ints[chunk], ordered(c_lines), half, lane * LANES, layers, direct
        )
        latest.append(kept)
        strips.append((kept, [swap(send, "layer", lambda i: i ^ other) for other, send in enumerate(sends, 1)]))

    def scatter(chunk):
        kept, got = strips[chunk]
        position = 1
        while kept.shape[0] > 1:
            position *= 2
            kept, send = halve(ordered(kept), got[0], position, chunk)
            latest.append(kept)
            got = [swap(send, "layer", lambda i: i ^ position)]
        strips[chunk] = kept, got

    def finish(chunk):
        kept, got = strips[chunk]
        squared, summed = square(ordered(kept), got, sums if chunk == chunks - 1 else [], chunk)
        latest.append(summed)
        squares.append(squared)
        sums.append(summed)

    for chunk in range(chunks + 1):
        if chunk < chunks:
            add_up(chunk)
        if chunk >= 1:
            scatter(chunk - 1)
        if chunk == 2:
            finish(0)
        if chunk % per_half == 0 and chunk // per_half + 1 < halves:
            more_products(chunk // per_half + 1)
    for chunk in range(1, chunks):
        finish(chunk)

    mine = sums[-1]
    others = [swap(mine, "layer", lambda i: i ^ other) for other in range(1, layers)]
    return rescale(squares, [mine, *others], width)


def solution(mesh):
    placed = (
        P("blk", "layer", None),
        P("blk", "layer", None),
        P("blk", None, None),
        P("blk", None, None),
        P("blk", None, None),
    )
    return jax.shard_map(
        shards, mesh=mesh, in_specs=placed, out_specs=P("blk", "layer", None), check_vma=False
    )
```

time: 66.3 us -> 67.6 us (1.020)
  waiting for transfers between devices: 17.8 us -> 23.7 us
  starting transfers between devices: 27.6 us -> 23.1 us
    ppermute x19, waiting for transfers between devices: 17.8 us -> 23.7 us  [swap(): lax.ppermute(block, axis, [(partner(i), i) for i in range(lax.axis_size(a...]
    ppermute x19, starting transfers between devices: 27.6 us -> 23.1 us  [swap(): lax.ppermute(block, axis, [(partner(i), i) for i in range(lax.axis_size(a...]
where the time goes in v8:
time: 67.6 us; the launch traced here: 67.4 us
  waiting for transfers between devices  23.7 us (35%)
  starting transfers between devices  23.1 us (34%)
  Pallas kernels  20.4 us (30%)
    ppermute x19, waiting for transfers between devices, swap(): lax.ppermute(block, axis, [(partner(i), i) for i in range(lax.axis_size(a...  23.7 us
    ppermute x19, starting transfers between devices, swap(): lax.ppermute(block, axis, [(partner(i), i) for i in range(lax.axis_size(a...  23.1 us
    pallas_call x17, Pallas kernels, call(): pl.pallas_call(kernel, out_shape=out_shape, in_specs=in_specs, out_specs=...  20.4 us
  transfers between devices with their start and end apart: 19, of which 9 were waited for; matrix products, arithmetic and copies ran while one was open for 0% of the time, Pallas kernels for 22%

profile of v8, /device:TPU:0, one launch (start us, length us, event | category | flops | bytes accessed | tf_op | source)
XLA Modules:
  0.0 67.4 jit_solution(9256376971965791356)
XLA Ops:
  0.0 4.6 %first_products.1 = (s16[1040,128]{1,0:T(8,128)(2,1)S(1)}, s16[1040,128]{1,0:T(8,128)(2,1)S(1)}, bf16[1024,2048]{1,0:T(8,128)(2,1)S(1)}) custom-call(s32[6,1,32]{2,1,0:T(1,128)} %bitcast.5, s32[6,1,32]{2,1,0:T(1,128)} %bitcast.9, bf16[1,2048,1536]{2,1,0:T(8,128)(2,1)} %side_ref.1, bf16[1,2048,1536]{2,1,0:T(8,128)(2,1)} %graph_ref.5), custom_call_target="tpu_custom_call" | custom-call | flops 1 | bytes 1 | tf_op jit(solution)/shard_map/first_products/pallas_call | solution.py:33
  4.6 3.4 %collective-permute-start = (s16[1040,128]{1,0:T(8,128)(2,1)S(1)}, s16[1040,128]{1,0:T(8,128)(2,1)S(1)}, u32[]{:S(2)}, u32[]{:S(2)}) collective-permute-start(s16[1040,128]{1,0:T(8,128)(2,1)S(1)} %get-tuple-element.55), channel_id=1, source_target_pairs={{28,0},{8,4},{4,8},{16,12},{12,16},{24,20},{20,24},{0,28},{29,1},{... | collective-permute-start | bytes 798728 | tf_op jit(solution)/shard_map/ppermute | solution.py:25
  8.1 3.7 %own_int_products_0.1 = (f32[1536,256]{1,0:T(8,128)S(1)}, s16[1040,128]{1,0:T(8,128)(2,1)S(1)}, s16[1040,128]{1,0:T(8,128)(2,1)S(1)}, bf16[512,2048]{1,0:T(8,128)(2,1)S(1)}) custom-call(s32[6,1,32]{2,1,0:T(1,128)S(1)} %bitcast.6, s32[6,1,32]{2,1,0:T(1,128)S(1)} %bitcast.10, bf16[1,2048,1536]{2,1,0:T(8,128)(2,1)S(1)} %bitcast.4, ...), custom_call_target="tpu_custom_call" | custom-call | flops 1 | bytes 1 | tf_op jit(solution)/shard_map/own_int_products_0/pallas_call | solution.py:33
  11.9 2.2 %collective-permute-start.2 = (s16[1040,128]{1,0:T(8,128)(2,1)S(1)}, s16[1040,128]{1,0:T(8,128)(2,1)S(1)}, u32[]{:S(2)}, u32[]{:S(2)}) collective-permute-start(s16[1040,128]{1,0:T(8,128)(2,1)S(1)} %get-tuple-element.67), channel_id=1, source_target_pairs={{28,0},{8,4},{4,8},{16,12},{12,16},{24,20},{20,24},{0,28},{29,1},{... | collective-permute-start | bytes 798728 | tf_op jit(solution)/shard_map/ppermute | solution.py:25
  14.1 1.0 %join_0_0.1 = (f32[2,384,128]{2,1,0:T(8,128)S(1)}, s16[784,128]{1,0:T(8,128)(2,1)S(1)}) custom-call(s32[1,2,6]{2,1,0:T(2,128)S(1)} %bitcast.13, f32[1536,256]{1,0:T(8,128)S(1)} %get-tuple-element.60.own_ref, s16[1040,128]{1,0:T(8,128)(2,1)S(1)} %collective-permute-done.ext_ref, s16[1040,128]{1,0:T(8,128)(2,1)S(1)} %collective-permute-done.1.int_ref), custom_call_target="tpu_custom_call" | custom-call | flops 1 | bytes 1 | tf_op jit(solution)/shard_map/join_0_0/pallas_call | solution.py:33
  15.1 3.1 %collective-permute-start.4 = (s16[784,128]{1,0:T(8,128)(2,1)S(1)}, s16[784,128]{1,0:T(8,128)(2,1)S(1)}, u32[]{:S(2)}, u32[]{:S(2)}) collective-permute-start(s16[784,128]{1,0:T(8,128)(2,1)S(1)} %get-tuple-element.71), channel_id=1, source_target_pairs={{1,0},{0,1},{3,2},{2,3},{5,4},{4,5},{7,6},{6,7},{9,8},{8,9},{11,10... | collective-permute-start | bytes 602120 | tf_op jit(solution)/shard_map/ppermute | solution.py:25
  18.2 3.6 %ext_int_products_1.1 = (s16[1040,128]{1,0:T(8,128)(2,1)S(1)}, s16[1040,128]{1,0:T(8,128)(2,1)S(1)}, s16[1040,128]{1,0:T(8,128)(2,1)S(1)}, s16[1040,128]{1,0:T(8,128)(2,1)S(1)}) custom-call(s32[6,1,32]{2,1,0:T(1,128)S(1)} %bitcast.7, s32[6,1,32]{2,1,0:T(1,128)S(1)} %bitcast.11, bf16[1,2048,1536]{2,1,0:T(8,128)(2,1)S(1)} %bitcast.4, ...), custom_call_target="tpu_custom_call" | custom-call | flops 1 | bytes 1 | tf_op jit(solution)/shard_map/ext_int_products_1/pallas_call | solution.py:33
  21.9 1.0 %collective-permute-start.5 = (s16[1040,128]{1,0:T(8,128)(2,1)S(1)}, s16[1040,128]{1,0:T(8,128)(2,1)S(1)}, u32[]{:S(2)}, u32[]{:S(2)}) collective-permute-start(s16[1040,128]{1,0:T(8,128)(2,1)S(1)} %get-tuple-element.74), channel_id=1, source_target_pairs={{28,0},{8,4},{4,8},{16,12},{12,16},{24,20},{20,24},{0,28},{29,1},{... | collective-permute-start | bytes 798728 | tf_op jit(solution)/shard_map/ppermute | solution.py:25
  22.9 1.7 %collective-permute-start.9 = (s16[1040,128]{1,0:T(8,128)(2,1)S(1)}, s16[1040,128]{1,0:T(8,128)(2,1)S(1)}, u32[]{:S(2)}, u32[]{:S(2)}) collective-permute-start(s16[1040,128]{1,0:T(8,128)(2,1)S(1)} %get-tuple-element.84), channel_id=1, source_target_pairs={{28,0},{8,4},{4,8},{16,12},{12,16},{24,20},{20,24},{0,28},{29,1},{... | collective-permute-start | bytes 798728 | tf_op jit(solution)/shard_map/ppermute | solution.py:25
  24.6 2.4 %own_products_1.1.own_ref = f32[1536,256]{1,0:T(8,128)S(1)} custom-call(s32[6,1,32]{2,1,0:T(1,128)S(1)} %bitcast.8, s32[6,1,32]{2,1,0:T(1,128)S(1)} %bitcast.12, bf16[1,2048,1536]{2,1,0:T(8,128)(2,1)S(1)} %bitcast.4, bf16[1024,2048]{1,0:T(8,128)(2,1)S(1)} %get-tuple-element.57.ext_rows_ref, bf16[512,2048]{1,0:T(8,128)(2,1)S(1)} %get-tuple-element.63.side_ref), custom_call_target="tpu_custom_call" | custom-call | flops 1 | bytes 1 | tf_op jit(solution)/shard_map/own_products_1/pallas_call | solution.py:33
  27.0 1.0 %join_0_128.1 = (f32[2,384,128]{2,1,0:T(8,128)S(1)}, s16[784,128]{1,0:T(8,128)(2,1)S(1)}) custom-call(s32[1,2,6]{2,1,0:T(2,128)S(1)} %bitcast.14, f32[1536,256]{1,0:T(8,128)S(1)} %get-tuple-element.60.own_ref, s16[1040,128]{1,0:T(8,128)(2,1)S(1)} %collective-permute-done.2.ext_ref, s16[1040,128]{1,0:T(8,128)(2,1)S(1)} %collective-permute-done.3.int_ref), custom_call_target="tpu_custom_call" | custom-call | flops 1 | bytes 1 | tf_op jit(solution)/shard_map/join_0_128/pallas_call | solution.py:33
  28.0 0.3 collective-permute-start.7
  28.3 0.2 halve_2_0.1
  28.4 3.0 %collective-permute-done.5.ext_ref = s16[1040,128]{1,0:T(8,128)(2,1)S(1)} collective-permute-done((s16[1040,128]{1,0:T(8,128)(2,1)S(1)}, s16[1040,128]{1,0:T(8,128)(2,1)S(1)}, u32[]{:S(2)}, u32[]{:S(2)}) %collective-permute-start.5) | collective-permute-done | bytes 266272 | tf_op jit(solution)/shard_map/ppermute | solution.py:25
  31.5 2.6 %collective-permute-start.8 = (s16[400,128]{1,0:T(8,128)(2,1)S(1)}, s16[400,128]{1,0:T(8,128)(2,1)S(1)}, u32[]{:S(2)}, u32[]{:S(2)}) collective-permute-start(s16[400,128]{1,0:T(8,128)(2,1)S(1)} %get-tuple-element.80), channel_id=1, source_target_pairs={{2,0},{3,1},{0,2},{1,3},{6,4},{7,5},{4,6},{5,7},{10,8},{11,9},{8,1... | collective-permute-start | bytes 307208 | tf_op jit(solution)/shard_map/ppermute | solution.py:25
  34.1 1.1 %join_1_0.1 = (f32[2,384,128]{2,1,0:T(8,128)S(1)}, s16[784,128]{1,0:T(8,128)(2,1)S(1)}) custom-call(s32[1,2,6]{2,1,0:T(2,128)S(1)} %bitcast.15, f32[1536,256]{1,0:T(8,128)S(1)} %own_products_1.1.own_ref, s16[1040,128]{1,0:T(8,128)(2,1)S(1)} %collective-permute-done.5.ext_ref, s16[1040,128]{1,0:T(8,128)(2,1)S(1)} %collective-permute-done.6.int_ref), custom_call_target="tpu_custom_call" | custom-call | flops 1 | bytes 1 | tf_op jit(solution)/shard_map/join_1_0/pallas_call | solution.py:33
  35.2 2.4 %collective-permute-done.7.got_ref = s16[784,128]{1,0:T(8,128)(2,1)S(1)} collective-permute-done((s16[784,128]{1,0:T(8,128)(2,1)S(1)}, s16[784,128]{1,0:T(8,128)(2,1)S(1)}, u32[]{:S(2)}, u32[]{:S(2)}) %collective-permute-start.7) | collective-permute-done | bytes 200736 | tf_op jit(solution)/shard_map/ppermute | solution.py:25
  37.7 0.2 halve_2_1.1
  38.0 1.0 %join_1_128.1 = (f32[2,384,128]{2,1,0:T(8,128)S(1)}, s16[784,128]{1,0:T(8,128)(2,1)S(1)}) custom-call(s32[1,2,6]{2,1,0:T(2,128)S(1)} %bitcast.16, f32[1536,256]{1,0:T(8,128)S(1)} %own_products_1.1.own_ref, s16[1040,128]{1,0:T(8,128)(2,1)S(1)} %collective-permute-done.9.ext_ref, s16[1040,128]{1,0:T(8,128)(2,1)S(1)} %collective-permute-done.10.int_ref), custom_call_target="tpu_custom_call" | custom-call | flops 1 | bytes 1 | tf_op jit(solution)/shard_map/join_1_128/pallas_call | solution.py:33
  39.0 2.4 %collective-permute-start.12 = (s16[784,128]{1,0:T(8,128)(2,1)S(1)}, s16[784,128]{1,0:T(8,128)(2,1)S(1)}, u32[]{:S(2)}, u32[]{:S(2)}) collective-permute-start(s16[784,128]{1,0:T(8,128)(2,1)S(1)} %get-tuple-element.91), channel_id=1, source_target_pairs={{1,0},{0,1},{3,2},{2,3},{5,4},{4,5},{7,6},{6,7},{9,8},{8,9},{11,10... | collective-permute-start | bytes 602120 | tf_op jit(solution)/shard_map/ppermute | solution.py:25
  41.4 1.1 %collective-permute-start.13 = (s16[400,128]{1,0:T(8,128)(2,1)S(1)}, s16[400,128]{1,0:T(8,128)(2,1)S(1)}, u32[]{:S(2)}, u32[]{:S(2)}) collective-permute-start(s16[400,128]{1,0:T(8,128)(2,1)S(1)} %get-tuple-element.94), channel_id=1, source_target_pairs={{2,0},{3,1},{0,2},{1,3},{6,4},{7,5},{4,6},{5,7},{10,8},{11,9},{8,1... | collective-permute-start | bytes 307208 | tf_op jit(solution)/shard_map/ppermute | solution.py:25
  42.5 6.4 %collective-permute-done.11.got_ref = s16[784,128]{1,0:T(8,128)(2,1)S(1)} collective-permute-done((s16[784,128]{1,0:T(8,128)(2,1)S(1)}, s16[784,128]{1,0:T(8,128)(2,1)S(1)}, u32[]{:S(2)}, u32[]{:S(2)}) %collective-permute-start.11) | collective-permute-done | bytes 200736 | tf_op jit(solution)/shard_map/ppermute | solution.py:25
  48.9 0.2 halve_2_2.1
  49.1 0.6 collective-permute-start.14
  49.7 2.4 %collective-permute-done.12.got_ref = s16[784,128]{1,0:T(8,128)(2,1)S(1)} collective-permute-done((s16[784,128]{1,0:T(8,128)(2,1)S(1)}, s16[784,128]{1,0:T(8,128)(2,1)S(1)}, u32[]{:S(2)}, u32[]{:S(2)}) %collective-permute-start.12) | collective-permute-done | bytes 200736 | tf_op jit(solution)/shard_map/ppermute | solution.py:25
  52.5 6.1 %collective-permute-done.14.rest_0_ = s16[400,128]{1,0:T(8,128)(2,1)S(1)} collective-permute-done((s16[400,128]{1,0:T(8,128)(2,1)S(1)}, s16[400,128]{1,0:T(8,128)(2,1)S(1)}, u32[]{:S(2)}, u32[]{:S(2)}) %collective-permute-start.14) | collective-permute-done | bytes 102432 | tf_op jit(solution)/shard_map/ppermute | solution.py:25
  58.6 1.1 %collective-permute-done.15.rest_0_ = s16[400,128]{1,0:T(8,128)(2,1)S(1)} collective-permute-done((s16[400,128]{1,0:T(8,128)(2,1)S(1)}, s16[400,128]{1,0:T(8,128)(2,1)S(1)}, u32[]{:S(2)}, u32[]{:S(2)}) %collective-permute-start.15) | collective-permute-done | bytes 102432 | tf_op jit(solution)/shard_map/ppermute | solution.py:25
  59.8 2.0 %collective-permute-start.18 = (f32[8,512]{1,0:T(8,128)S(1)}, f32[8,512]{1,0:T(8,128)S(1)}, u32[]{:S(2)}, u32[]{:S(2)}) collective-permute-start(f32[8,512]{1,0:T(8,128)S(1)} %get-tuple-element.104.refs_4_), channel_id=1, source_target_pairs={{3,0},{2,1},{1,2},{0,3},{7,4},{6,5},{5,6},{4,7},{11,8},{10,9},{9,1... | collective-permute-start | bytes 49160 | tf_op jit(solution)/shard_map/ppermute | solution.py:25
  61.8 2.5 %collective-permute-start.16 = (f32[8,512]{1,0:T(8,128)S(1)}, f32[8,512]{1,0:T(8,128)S(1)}, u32[]{:S(2)}, u32[]{:S(2)}) collective-permute-start(f32[8,512]{1,0:T(8,128)S(1)} %get-tuple-element.104.refs_4_), channel_id=1, source_target_pairs={{1,0},{0,1},{3,2},{2,3},{5,4},{4,5},{7,6},{6,7},{9,8},{8,9},{11,10... | collective-permute-start | bytes 49160 | tf_op jit(solution)/shard_map/ppermute | solution.py:25
  64.3 1.2 %collective-permute-done.18.refs_7_ = f32[8,512]{1,0:T(8,128)S(1)} collective-permute-done((f32[8,512]{1,0:T(8,128)S(1)}, f32[8,512]{1,0:T(8,128)S(1)}, u32[]{:S(2)}, u32[]{:S(2)}) %collective-permute-start.18) | collective-permute-done | bytes 16416 | tf_op jit(solution)/shard_map/ppermute | solution.py:25
  65.5 1.0 %collective-permute-done.17.refs_6_ = f32[8,512]{1,0:T(8,128)S(1)} collective-permute-done((f32[8,512]{1,0:T(8,128)S(1)}, f32[8,512]{1,0:T(8,128)S(1)}, u32[]{:S(2)}, u32[]{:S(2)}) %collective-permute-start.17) | collective-permute-done | bytes 16416 | tf_op jit(solution)/shard_map/ppermute | solution.py:25
  66.4 1.0 %rescale.1 = f32[1,384,512]{2,1,0:T(8,128)} custom-call(f32[384,128]{1,0:T(8,128)S(1)} %get-tuple-element.81.refs_0_, f32[384,128]{1,0:T(8,128)S(1)} %get-tuple-element.95.refs_1_, f32[384,128]{1,0:T(8,128)S(1)} %get-tuple-element.99.refs_2_, f32[384,128]{1,0:T(8,128)S(1)} %get-tuple-element.103.refs_3_, f32[8,512]{1,0:T(8,128)S(1)} %get-tuple-element.104.refs_4_, ...), custom_call_target="tpu_custom_call" | custom-call | flops 1 | bytes 1 | tf_op jit(solution)/shard_map/rescale/pallas_call | solution.py:33
  (36 shorter events, 0.8 us)
Async XLA Ops:
  0.0 8.0 %slice-start = ((s8[6291456]{0:T(1024)(128)(4,1)}), s8[4194304]{0:T(1024)(128)(4,1)S(1)}, s32[]{:S(2)}) async-start(s8[6291456]{0:T(1024)(128)(4,1)} %bitcast.3), calls=%async_computation | async-start | bytes 8388608
  0.0 8.0 %slice-start.1 = ((s8[6291456]{0:T(1024)(128)(4,1)}), s8[2097152]{0:T(1024)(128)(4,1)S(1)}, s32[]{:S(2)}) async-start(s8[6291456]{0:T(1024)(128)(4,1)} %bitcast.3), calls=%async_computation.1 | async-start | bytes 4194304
  0.0 8.0 %copy-start = (bf16[1,2048,1536]{2,1,0:T(8,128)(2,1)S(1)}, bf16[1,2048,1536]{2,1,0:T(8,128)(2,1)}, u32[]{:S(2)}) copy-start(bf16[1,2048,1536]{2,1,0:T(8,128)(2,1)} %side_ref.1) | copy-start | bytes 18874372
  0.0 8.0 %copy-start.1 = (s32[1,32,6]{1,0,2:T(1,128)S(1)}, s32[1,32,6]{1,0,2:T(1,128)}, u32[]{:S(2)}) copy-start(s32[1,32,6]{1,0,2:T(1,128)} %param.7) | copy-start | bytes 2308
  0.0 8.0 %copy-start.2 = (s32[1,32,6]{1,0,2:T(1,128)S(1)}, s32[1,32,6]{1,0,2:T(1,128)}, u32[]{:S(2)}) copy-start(s32[1,32,6]{1,0,2:T(1,128)} %param.8) | copy-start | bytes 2308
  4.6 9.5 %collective-permute-start = (s16[1040,128]{1,0:T(8,128)(2,1)S(1)}, s16[1040,128]{1,0:T(8,128)(2,1)S(1)}, u32[]{:S(2)}, u32[]{:S(2)}) collective-permute-start(s16[1040,128]{1,0:T(8,128)(2,1)S(1)} %get-tuple-element.55), channel_id=1, source_target_pairs={{28,0},{8,4},{4,8},{16,12},{12,16},{24,20},{20,24},{0,28},{29,1},{... | collective-permute-start | bytes 798728 | tf_op jit(solution)/shard_map/ppermute | solution.py:25
  8.1 6.1 %copy-start.3 = (s32[1,6,2]{1,2,0:T(2,128)S(1)}, s32[1,6,2]{1,2,0:T(2,128)}, u32[]{:S(2)}) copy-start(s32[1,6,2]{1,2,0:T(2,128)} %param.9) | copy-start | bytes 148
  11.8 2.4 %collective-permute-start.1 = (s16[1040,128]{1,0:T(8,128)(2,1)S(1)}, s16[1040,128]{1,0:T(8,128)(2,1)S(1)}, u32[]{:S(2)}, u32[]{:S(2)}) collective-permute-start(s16[1040,128]{1,0:T(8,128)(2,1)S(1)} %get-tuple-element.58), channel_id=1, source_target_pairs={{4,0},{0,4},{12,8},{8,12},{20,16},{16,20},{28,24},{24,28},{5,1},{1... | collective-permute-start | bytes 798728 | tf_op jit(solution)/shard_map/ppermute | solution.py:25
  11.9 11.0 %collective-permute-start.2 = (s16[1040,128]{1,0:T(8,128)(2,1)S(1)}, s16[1040,128]{1,0:T(8,128)(2,1)S(1)}, u32[]{:S(2)}, u32[]{:S(2)}) collective-permute-start(s16[1040,128]{1,0:T(8,128)(2,1)S(1)} %get-tuple-element.67), channel_id=1, source_target_pairs={{28,0},{8,4},{4,8},{16,12},{12,16},{24,20},{20,24},{0,28},{29,1},{... | collective-permute-start | bytes 798728 | tf_op jit(solution)/shard_map/ppermute | solution.py:25
  14.1 10.5 %collective-permute-start.3 = (s16[1040,128]{1,0:T(8,128)(2,1)S(1)}, s16[1040,128]{1,0:T(8,128)(2,1)S(1)}, u32[]{:S(2)}, u32[]{:S(2)}) collective-permute-start(s16[1040,128]{1,0:T(8,128)(2,1)S(1)} %get-tuple-element.68), channel_id=1, source_target_pairs={{4,0},{0,4},{12,8},{8,12},{20,16},{16,20},{28,24},{24,28},{5,1},{1... | collective-permute-start | bytes 798728 | tf_op jit(solution)/shard_map/ppermute | solution.py:25
  15.1 12.9 %collective-permute-start.4 = (s16[784,128]{1,0:T(8,128)(2,1)S(1)}, s16[784,128]{1,0:T(8,128)(2,1)S(1)}, u32[]{:S(2)}, u32[]{:S(2)}) collective-permute-start(s16[784,128]{1,0:T(8,128)(2,1)S(1)} %get-tuple-element.71), channel_id=1, source_target_pairs={{1,0},{0,1},{3,2},{2,3},{5,4},{4,5},{7,6},{6,7},{9,8},{8,9},{11,10... | collective-permute-start | bytes 602120 | tf_op jit(solution)/shard_map/ppermute | solution.py:25
  21.9 9.6 %collective-permute-start.5 = (s16[1040,128]{1,0:T(8,128)(2,1)S(1)}, s16[1040,128]{1,0:T(8,128)(2,1)S(1)}, u32[]{:S(2)}, u32[]{:S(2)}) collective-permute-start(s16[1040,128]{1,0:T(8,128)(2,1)S(1)} %get-tuple-element.74), channel_id=1, source_target_pairs={{28,0},{8,4},{4,8},{16,12},{12,16},{24,20},{20,24},{0,28},{29,1},{... | collective-permute-start | bytes 798728 | tf_op jit(solution)/shard_map/ppermute | solution.py:25
  22.9 11.2 %collective-permute-start.6 = (s16[1040,128]{1,0:T(8,128)(2,1)S(1)}, s16[1040,128]{1,0:T(8,128)(2,1)S(1)}, u32[]{:S(2)}, u32[]{:S(2)}) collective-permute-start(s16[1040,128]{1,0:T(8,128)(2,1)S(1)} %get-tuple-element.64), channel_id=1, source_target_pairs={{4,0},{0,4},{12,8},{8,12},{20,16},{16,20},{28,24},{24,28},{5,1},{1... | collective-permute-start | bytes 798728 | tf_op jit(solution)/shard_map/ppermute | solution.py:25
  22.9 15.1 %collective-permute-start.9 = (s16[1040,128]{1,0:T(8,128)(2,1)S(1)}, s16[1040,128]{1,0:T(8,128)(2,1)S(1)}, u32[]{:S(2)}, u32[]{:S(2)}) collective-permute-start(s16[1040,128]{1,0:T(8,128)(2,1)S(1)} %get-tuple-element.84), channel_id=1, source_target_pairs={{28,0},{8,4},{4,8},{16,12},{12,16},{24,20},{20,24},{0,28},{29,1},{... | collective-permute-start | bytes 798728 | tf_op jit(solution)/shard_map/ppermute | solution.py:25
  24.6 13.4 %collective-permute-start.10 = (s16[1040,128]{1,0:T(8,128)(2,1)S(1)}, s16[1040,128]{1,0:T(8,128)(2,1)S(1)}, u32[]{:S(2)}, u32[]{:S(2)}) collective-permute-start(s16[1040,128]{1,0:T(8,128)(2,1)S(1)} %get-tuple-element.85), channel_id=1, source_target_pairs={{4,0},{0,4},{12,8},{8,12},{20,16},{16,20},{28,24},{24,28},{5,1},{1... | collective-permute-start | bytes 798728 | tf_op jit(solution)/shard_map/ppermute | solution.py:25
  28.0 9.6 %collective-permute-start.7 = (s16[784,128]{1,0:T(8,128)(2,1)S(1)}, s16[784,128]{1,0:T(8,128)(2,1)S(1)}, u32[]{:S(2)}, u32[]{:S(2)}) collective-permute-start(s16[784,128]{1,0:T(8,128)(2,1)S(1)} %get-tuple-element.77), channel_id=1, source_target_pairs={{1,0},{0,1},{3,2},{2,3},{5,4},{4,5},{7,6},{6,7},{9,8},{8,9},{11,10... | collective-permute-start | bytes 602120 | tf_op jit(solution)/shard_map/ppermute | solution.py:25
  31.5 6.5 %collective-permute-start.8 = (s16[400,128]{1,0:T(8,128)(2,1)S(1)}, s16[400,128]{1,0:T(8,128)(2,1)S(1)}, u32[]{:S(2)}, u32[]{:S(2)}) collective-permute-start(s16[400,128]{1,0:T(8,128)(2,1)S(1)} %get-tuple-element.80), channel_id=1, source_target_pairs={{2,0},{3,1},{0,2},{1,3},{6,4},{7,5},{4,6},{5,7},{10,8},{11,9},{8,1... | collective-permute-start | bytes 307208 | tf_op jit(solution)/shard_map/ppermute | solution.py:25
  37.8 11.1 %collective-permute-start.11 = (s16[784,128]{1,0:T(8,128)(2,1)S(1)}, s16[784,128]{1,0:T(8,128)(2,1)S(1)}, u32[]{:S(2)}, u32[]{:S(2)}) collective-permute-start(s16[784,128]{1,0:T(8,128)(2,1)S(1)} %get-tuple-element.88), channel_id=1, source_target_pairs={{1,0},{0,1},{3,2},{2,3},{5,4},{4,5},{7,6},{6,7},{9,8},{8,9},{11,10... | collective-permute-start | bytes 602120 | tf_op jit(solution)/shard_map/ppermute | solution.py:25
  39.0 13.1 %collective-permute-start.12 = (s16[784,128]{1,0:T(8,128)(2,1)S(1)}, s16[784,128]{1,0:T(8,128)(2,1)S(1)}, u32[]{:S(2)}, u32[]{:S(2)}) collective-permute-start(s16[784,128]{1,0:T(8,128)(2,1)S(1)} %get-tuple-element.91), channel_id=1, source_target_pairs={{1,0},{0,1},{3,2},{2,3},{5,4},{4,5},{7,6},{6,7},{9,8},{8,9},{11,10... | collective-permute-start | bytes 602120 | tf_op jit(solution)/shard_map/ppermute | solution.py:25
  41.4 11.0 %collective-permute-start.13 = (s16[400,128]{1,0:T(8,128)(2,1)S(1)}, s16[400,128]{1,0:T(8,128)(2,1)S(1)}, u32[]{:S(2)}, u32[]{:S(2)}) collective-permute-start(s16[400,128]{1,0:T(8,128)(2,1)S(1)} %get-tuple-element.94), channel_id=1, source_target_pairs={{2,0},{3,1},{0,2},{1,3},{6,4},{7,5},{4,6},{5,7},{10,8},{11,9},{8,1... | collective-permute-start | bytes 307208 | tf_op jit(solution)/shard_map/ppermute | solution.py:25
  49.1 9.5 %collective-permute-start.14 = (s16[400,128]{1,0:T(8,128)(2,1)S(1)}, s16[400,128]{1,0:T(8,128)(2,1)S(1)}, u32[]{:S(2)}, u32[]{:S(2)}) collective-permute-start(s16[400,128]{1,0:T(8,128)(2,1)S(1)} %get-tuple-element.98), channel_id=1, source_target_pairs={{2,0},{3,1},{0,2},{1,3},{6,4},{7,5},{4,6},{5,7},{10,8},{11,9},{8,1... | collective-permute-start | bytes 307208 | tf_op jit(solution)/shard_map/ppermute | solution.py:25
  52.3 7.4 %collective-permute-start.15 = (s16[400,128]{1,0:T(8,128)(2,1)S(1)}, s16[400,128]{1,0:T(8,128)(2,1)S(1)}, u32[]{:S(2)}, u32[]{:S(2)}) collective-permute-start(s16[400,128]{1,0:T(8,128)(2,1)S(1)} %get-tuple-element.102), channel_id=1, source_target_pairs={{2,0},{3,1},{0,2},{1,3},{6,4},{7,5},{4,6},{5,7},{10,8},{11,9},{8,1... | collective-permute-start | bytes 307208 | tf_op jit(solution)/shard_map/ppermute | solution.py:25
  59.8 5.7 %collective-permute-start.18 = (f32[8,512]{1,0:T(8,128)S(1)}, f32[8,512]{1,0:T(8,128)S(1)}, u32[]{:S(2)}, u32[]{:S(2)}) collective-permute-start(f32[8,512]{1,0:T(8,128)S(1)} %get-tuple-element.104.refs_4_), channel_id=1, source_target_pairs={{3,0},{2,1},{1,2},{0,3},{7,4},{6,5},{5,6},{4,7},{11,8},{10,9},{9,1... | collective-permute-start | bytes 49160 | tf_op jit(solution)/shard_map/ppermute | solution.py:25
  61.8 4.6 %collective-permute-start.17 = (f32[8,512]{1,0:T(8,128)S(1)}, f32[8,512]{1,0:T(8,128)S(1)}, u32[]{:S(2)}, u32[]{:S(2)}) collective-permute-start(f32[8,512]{1,0:T(8,128)S(1)} %get-tuple-element.104.refs_4_), channel_id=1, source_target_pairs={{2,0},{3,1},{0,2},{1,3},{6,4},{7,5},{4,6},{5,7},{10,8},{11,9},{8,1... | collective-permute-start | bytes 49160 | tf_op jit(solution)/shard_map/ppermute | solution.py:25
  61.8 4.6 %collective-permute-start.16 = (f32[8,512]{1,0:T(8,128)S(1)}, f32[8,512]{1,0:T(8,128)S(1)}, u32[]{:S(2)}, u32[]{:S(2)}) collective-permute-start(f32[8,512]{1,0:T(8,128)S(1)} %get-tuple-element.104.refs_4_), channel_id=1, source_target_pairs={{1,0},{0,1},{3,2},{2,3},{5,4},{4,5},{7,6},{6,7},{9,8},{8,9},{11,10... | collective-permute-start | bytes 49160 | tf_op jit(solution)/shard_map/ppermute | solution.py:25

commit v9 on v8

--- a/solution.py
+++ b/solution.py
@@ -16,7 +16,6 @@
 DIRECT = 0
 PRODUCT_LIMIT = 24000000
 SMALL_LIMIT = 8 * 1024 * 1024
-IN_SMEM = pl.BlockSpec(memory_space=pltpu.SMEM)
 IN_VMEM = pl.BlockSpec(memory_space=pltpu.VMEM)
 IN_HBM = pl.BlockSpec(memory_space=pltpu.HBM)
 
@@ -60,15 +59,19 @@
     return (codes.astype(jnp.int32) + 32767).astype(jnp.float32) * scale
 
 
-def masked(values, pattern, column, first):
-    depth, width = values.shape
-    place = lax.broadcasted_iota(jnp.int32, (1, width), 1) // BS
-    parts = []
-    for u in range(depth // BS):
-        factor = jnp.zeros((1, width), jnp.float32)
-        for v in range(width // BS):
-            factor = jnp.where(place == v, pattern[column + v, 0, first + u].astype(jnp.float32), factor)
-        parts.append(values[u * BS : (u + 1) * BS] * factor.astype(values.dtype))
+def factor_rows(pattern, column, first, ref):
+    place = lax.broadcasted_iota(jnp.int32, (1, ref.shape[1]), 1) // BS
+    for u in range(ref.shape[0]):
+        row = jnp.zeros((1, ref.shape[1]), jnp.float32)
+        for v in range(ref.shape[1] // BS):
+            row = jnp.where(place == v, pattern(column + v, first + u).astype(jnp.float32), row)
+        ref[u : u + 1, :] = row
+
+
+def masked(values, factors):
+    parts = [
+        values[u * BS : (u + 1) * BS] * factors[u : u + 1].astype(values.dtype) for u in range(values.shape[0] // BS)
+    ]
     return jnp.concatenate(parts, axis=0) if len(parts) > 1 else parts[0]
 
 
@@ -120,19 +123,23 @@
             ref[0:HEAD, :] = head.astype(jnp.int32).astype(jnp.int16)
 
 
-def first_kernel(a_hbm, b_hbm, flow_hbm, graph_hbm, *rest):
-    out_refs, (rows_ref, graph_buf, flow_buf, total, a_ref, b_ref, sems) = rest[:-7], rest[-7:]
+def first_kernel(a_hbm, b_hbm, c_hbm, flow_hbm, graph_hbm, *rest):
+    out_refs, rest = rest[:-12], rest[-12:]
+    rows_ref, a_rows_ref, b_rows_ref, c_rows_ref, graph_buf, flow_buf, total, ext_factors, a_ref, b_ref, c_ref, sems = rest
     inner, panel = flow_buf.shape[0], flow_buf.shape[1] // BS // 2
     at = Sides(inner, panel)
     steps = inner // BS
-    small = [pltpu.make_async_copy(a_hbm, a_ref, sems.at[0]), pltpu.make_async_copy(b_hbm, b_ref, sems.at[1])]
+    small = [
+        pltpu.make_async_copy(pattern, ref, sems.at[i])
+        for i, (pattern, ref) in enumerate(((a_hbm, a_ref), (b_hbm, b_ref), (c_hbm, c_ref)))
+    ]
     flows, graphs = [], []
     for t in range(steps):
         rows = slice(t * BS, (t + 1) * BS)
         flow = columns_of(flow_hbm, at.ext_rows, 2 * panel).at[rows]
         graph = columns_of(graph_hbm, at.ext_side, 1).at[rows]
-        flows.append(pltpu.make_async_copy(flow, flow_buf.at[rows], sems.at[2 + 2 * t]))
-        graphs.append(pltpu.make_async_copy(graph, graph_buf.at[rows], sems.at[3 + 2 * t]))
+        flows.append(pltpu.make_async_copy(flow, flow_buf.at[rows], sems.at[3 + 2 * t]))
+        graphs.append(pltpu.make_async_copy(graph, graph_buf.at[rows], sems.at[4 + 2 * t]))
     for copy in small:
         copy.start()
     for t in range(steps):
@@ -140,14 +147,19 @@
         graphs[t].start()
     for copy in small:
         copy.wait()
+    factor_rows(lambda column, inner: a_ref[column, 0, inner], 0, at.first, a_rows_ref)
+    factor_rows(lambda column, inner: b_ref[column, 0, inner], 0, at.first, b_rows_ref)
+    factor_rows(lambda column, row: c_ref[0, column, row], 0, 0, c_rows_ref)
+    ext_factors[...] = a_rows_ref[:, blocks_at(at.ext_rows, 2 * panel)]
+    right_factors = b_rows_ref[:, blocks_at(at.ext_side)]
     per_dot = min(2, steps)
     for t in range(0, steps, per_dot):
         rows = slice(t * BS, (t + per_dot) * BS)
         for copy in flows[t : t + per_dot] + graphs[t : t + per_dot]:
             copy.wait()
-        turned = masked(flow_buf[rows, :], a_ref, at.ext_rows, at.first + t).T
+        turned = masked(flow_buf[rows, :], ext_factors[t : t + per_dot]).T
         rows_ref[:, rows] = turned
-        product = dot(turned, masked(graph_buf[rows, :], b_ref, at.ext_side, at.first + t))
+        product = dot(turned, masked(graph_buf[rows, :], right_factors[t : t + per_dot]))
         if t + per_dot < steps:
             total[...] = product if t == 0 else total[...] + product
     if steps > per_dot:
@@ -161,29 +173,36 @@
     coded.finish()
 
 
-def first_products(flow_t, graph, a_lines, b_lines, widths):
+def first_products(flow_t, graph, a_lines, b_lines, c_lines, widths):
     inner, width = flow_t.shape[1:]
     panel = width // 3
     return call(
         first_kernel,
         "first_products",
-        [pltpu.with_memory_space_constraint(x, pltpu.HBM) for x in (a_lines, b_lines, flow_t, graph)],
-        [IN_HBM] * 4,
+        [pltpu.with_memory_space_constraint(x, pltpu.HBM) for x in (a_lines, b_lines, c_lines, flow_t, graph)],
+        [IN_HBM] * 5,
         [jax.ShapeDtypeStruct((HEAD + 2 * panel, w), jnp.int16) for w in widths]
-        + [pltpu.VMEM((2 * panel, inner), flow_t.dtype)],
+        + [
+            pltpu.VMEM((2 * panel, inner), flow_t.dtype),
+            pltpu.VMEM((inner // BS, width), jnp.float32),
+            pltpu.VMEM((inner // BS, width), jnp.float32),
+            pltpu.VMEM((width // BS, panel), jnp.float32),
+        ],
         [
             pltpu.VMEM((inner, BS), graph.dtype),
             pltpu.VMEM((inner, 2 * panel), flow_t.dtype),
             pltpu.VMEM((2 * panel, BS), jnp.float32),
+            pltpu.VMEM((inner // BS, 2 * panel), jnp.float32),
             pltpu.SMEM(a_lines.shape, a_lines.dtype),
             pltpu.SMEM(b_lines.shape, b_lines.dtype),
-            pltpu.SemaphoreType.DMA((2 + 2 * (inner // BS),)),
+            pltpu.SMEM(c_lines.shape, c_lines.dtype),
+            pltpu.SemaphoreType.DMA((3 + 2 * (inner // BS),)),
         ],
         limit=PRODUCT_LIMIT,
     )
 
 
-def product_kernel(half, wanted, turns, a_ref, b_ref, graph_ref, ext_rows_ref, side_ref, *rest):
+def product_kernel(half, wanted, turns, a_rows_ref, b_rows_ref, graph_ref, ext_rows_ref, side_ref, *rest):
     refs = list(rest)
     inner, panel = graph_ref.shape[1], graph_ref.shape[2] // BS // 3
     at = Sides(inner, panel)
@@ -192,12 +211,13 @@
     int_rows_ref = side_ref
     if turns:
         int_rows_ref = refs.pop(0)
-        int_rows_ref[...] = masked(side_ref[0, :, blocks_at(at.int_side, panel)], a_ref, at.int_side, at.first).T
+        place = blocks_at(at.int_side, panel)
+        int_rows_ref[...] = masked(side_ref[0, :, place], a_rows_ref[:, place]).T
     coded = {part: Coded(outs[part]) for part in parts if part != "own"}
     right = []
     for part in parts:
-        column = at.columns[part] + half
-        right.append(masked(graph_ref[0, :, blocks_at(column)], b_ref, column, at.first))
+        place = blocks_at(at.columns[part] + half)
+        right.append(masked(graph_ref[0, :, place], b_rows_ref[:, place]))
     right = jnp.concatenate(right, axis=1) if len(right) > 1 else right[0]
     panels = (
         (panel, ext_rows_ref.at[blocks_at(panel - at.ext_rows, panel)], {"ext": 0, "own": 0, "int": 0}),
@@ -221,7 +241,7 @@
         coded[part].finish()
 
 
-def products(a_lines, b_lines, graph, ext_rows, side, half, wanted, turns=False):
+def products(a_rows, b_rows, graph, ext_rows, side, half, wanted, turns=False):
     inner, width = graph.shape[1:]
     panel = width // 3
     outs = []
@@ -236,8 +256,8 @@
     return call(
         functools.partial(product_kernel, half, wanted, turns),
         "_".join(wanted) + f"_products_{half}",
-        (a_lines, b_lines, graph, ext_rows, side),
-        [IN_SMEM, IN_SMEM] + [IN_VMEM] * 3,
+        (a_rows, b_rows, graph, ext_rows, side),
+        [IN_VMEM] * 5,
         outs,
         limit=PRODUCT_LIMIT,
     )
@@ -281,7 +301,7 @@
     def add(parts):
         scale = [scales(ref[0:HEAD, :]) for ref in refs]
         for v in range(3 * panel):
-            kept = c_ref[0, half, v].astype(jnp.float32)
+            kept = c_ref[v : v + 1, half * BS + lane : half * BS + lane + ext_ref.shape[1]]
             block = own_ref[v * BS : (v + 1) * BS, lanes] * kept
             for r, i in parts[v]:
                 codes = refs[r][HEAD + i * BS : HEAD + (i + 1) * BS, :]
@@ -306,15 +326,15 @@
     ]
 
 
-def join(own, ext_part, int_part, c_lines, half, lane, layers, direct):
+def join(own, ext_part, int_part, c_rows, half, lane, layers, direct):
     height = own.shape[0]
     width = int_part.shape[1]
     rows = height // layers
     return call(
         functools.partial(join_kernel, rows, half, lane),
         f"join_{half}_{lane}",
-        (c_lines, own, ext_part, int_part),
-        [IN_SMEM] + [IN_VMEM] * 3,
+        (c_rows, own, ext_part, int_part),
+        [IN_VMEM] * 4,
         strips_shapes(1, rows, width, layers - 1) if direct else strips_shapes(layers // 2, rows, width),
         [pltpu.VMEM((height, width), jnp.float32)],
     )
@@ -420,19 +440,21 @@
         ints.extend(swap(part, "blk", same_chip) for part in parts)
         latest.append(parts[0])
 
-    *parts, ext_rows = first_products(flow_t, graph, a_lines, b_lines, fine)
+    *parts, ext_rows, a_rows, b_rows, c_rows = first_products(flow_t, graph, a_lines, b_lines, c_lines, fine)
     send_ext(parts)
     wanted = {"own": (BS,), "int": fine}
-    own, *parts, int_rows = products(a_lines, ordered(b_lines), graph, ext_rows, flow_t, 0, wanted, turns=True)
+    own, *parts, int_rows = products(a_rows, ordered(b_rows), graph, ext_rows, flow_t, 0, wanted, turns=True)
     owns.append(own)
     send_int(parts)
 
     def more_products(half):
         wanted = {"ext": fine, "int": fine}
-        parts = products(a_lines, ordered(b_lines), graph, ext_rows, int_rows, half, wanted)
+        parts = products(a_rows, ordered(b_rows), graph, ext_rows, int_rows, half, wanted)
         send_ext(parts[:per_half])
         send_int(parts[per_half:])
-        owns.extend(products(a_lines, ordered(b_lines), graph, ext_rows, int_rows, half, {"own": (BS,)}))
+
+    def more_own(half):
+        owns.extend(products(a_rows, ordered(b_rows), graph, ext_rows, int_rows, half, {"own": (BS,)}))
         latest.append(owns[-1])
 
     strips, squares, sums = [], [], []
@@ -441,7 +463,7 @@
         half, lane = divmod(chunk, per_half)
         direct = chunk >= chunks - DIRECT and layers <= 4
         kept, *sends = join(
-            owns[half], ext[chunk], ints[chunk], ordered(c_lines), half, lane * LANES, layers, direct
+            owns[half], ext[chunk], ints[chunk], ordered(c_rows), half, lane * LANES, layers, direct
         )
         latest.append(kept)
         strips.append((kept, [swap(send, "layer", lambda i: i ^ other) for other, send in enumerate(sends, 1)]))
@@ -466,6 +488,8 @@
     for chunk in range(chunks + 1):
         if chunk < chunks:
             add_up(chunk)
+        if (chunk + 1) % per_half == 0 and len(owns) < halves:
+            more_own(len(owns))
         if chunk >= 1:
             scatter(chunk - 1)
         if chunk == 2:

time: 67.6 us -> 63.3 us (0.936)
  Pallas kernels: 20.4 us -> 16 us
  waiting for transfers between devices: 23.7 us -> 24.6 us
  starting transfers between devices: 23.1 us -> 22.3 us
    pallas_call x17, Pallas kernels: 20.4 us -> 16 us  [call(): pl.pallas_call(kernel, out_shape=out_shape, in_specs=in_specs, out_specs=...]
    ppermute x19, waiting for transfers between devices: 23.7 us -> 24.6 us  [swap(): lax.ppermute(block, axis, [(partner(i), i) for i in range(lax.axis_size(a...]
    ppermute x19, starting transfers between devices: 23.1 us -> 22.3 us  [swap(): lax.ppermute(block, axis, [(partner(i), i) for i in range(lax.axis_size(a...]
  transfers between devices with their start and end apart: 19 -> 19, of which waited for: 9 -> 9; matrix products, arithmetic and copies ran while one was open for 0% -> 0% of each run, Pallas kernels for 22% -> 16%
where the time goes in v9:
time: 63.3 us; the launch traced here: 63.1 us
  waiting for transfers between devices  24.6 us (39%)
  starting transfers between devices  22.3 us (35%)
  Pallas kernels  16 us (25%)
    ppermute x19, waiting for transfers between devices, swap(): lax.ppermute(block, axis, [(partner(i), i) for i in range(lax.axis_size(a...  24.6 us
    ppermute x19, starting transfers between devices, swap(): lax.ppermute(block, axis, [(partner(i), i) for i in range(lax.axis_size(a...  22.3 us
    pallas_call x17, Pallas kernels, call(): pl.pallas_call(kernel, out_shape=out_shape, in_specs=in_specs, out_specs=...  16 us
  transfers between devices with their start and end apart: 19, of which 9 were waited for; matrix products, arithmetic and copies ran while one was open for 0% of the time, Pallas kernels for 16%

profile of v9, /device:TPU:0, one launch (start us, length us, event | category | flops | bytes accessed | tf_op | source)
XLA Modules:
  0.0 63.1 jit_solution(7210289305643650280)
XLA Ops:
  0.0 4.5 %first_products.1 = (s16[1040,128]{1,0:T(8,128)(2,1)S(1)}, s16[1040,128]{1,0:T(8,128)(2,1)S(1)}, bf16[1024,2048]{1,0:T(8,128)(2,1)S(1)}, f32[8,1536]{1,0:T(8,128...) custom-call(s32[6,1,32]{2,1,0:T(1,128)} %bitcast.5, s32[6,1,32]{2,1,0:T(1,128)} %bitcast.6, s32[1,2,6]{2,1,0:T(2,128)} %bitcast.7, ...), custom_call_target="tpu_custom_call" | custom-call | flops 1 | bytes 1 | tf_op jit(solution)/shard_map/first_products/pallas_call | solution.py:32
  4.6 3.4 %collective-permute-start = (s16[1040,128]{1,0:T(8,128)(2,1)S(1)}, s16[1040,128]{1,0:T(8,128)(2,1)S(1)}, u32[]{:S(2)}, u32[]{:S(2)}) collective-permute-start(s16[1040,128]{1,0:T(8,128)(2,1)S(1)} %get-tuple-element.61), channel_id=1, source_target_pairs={{28,0},{8,4},{4,8},{16,12},{12,16},{24,20},{20,24},{0,28},{29,1},{... | collective-permute-start | bytes 798728 | tf_op jit(solution)/shard_map/ppermute | solution.py:24
  8.0 3.1 %own_int_products_0.1 = (f32[1536,256]{1,0:T(8,128)S(1)}, s16[1040,128]{1,0:T(8,128)(2,1)S(1)}, s16[1040,128]{1,0:T(8,128)(2,1)S(1)}, bf16[512,2048]{1,0:T(8,128)(2,1)S(1)}) custom-call(f32[8,1536]{1,0:T(8,128)S(1)} %get-tuple-element.59.a_rows_ref, f32[8,1536]{1,0:T(8,128)S(1)} %get-tuple-element.75.b_rows_ref, bf16[1,2048,1536]{2,1,0:T(8,128)(2,1)S(1)} %bitcast.4, ...), custom_call_target="tpu_custom_call" | custom-call | flops 1 | bytes 1 | tf_op jit(solution)/shard_map/own_int_products_0/pallas_call | solution.py:32
  11.1 2.3 %collective-permute-start.2 = (s16[1040,128]{1,0:T(8,128)(2,1)S(1)}, s16[1040,128]{1,0:T(8,128)(2,1)S(1)}, u32[]{:S(2)}, u32[]{:S(2)}) collective-permute-start(s16[1040,128]{1,0:T(8,128)(2,1)S(1)} %get-tuple-element.72), channel_id=1, source_target_pairs={{28,0},{8,4},{4,8},{16,12},{12,16},{24,20},{20,24},{0,28},{29,1},{... | collective-permute-start | bytes 798728 | tf_op jit(solution)/shard_map/ppermute | solution.py:24
  13.4 1.2 %collective-permute-done.ext_ref = s16[1040,128]{1,0:T(8,128)(2,1)S(1)} collective-permute-done((s16[1040,128]{1,0:T(8,128)(2,1)S(1)}, s16[1040,128]{1,0:T(8,128)(2,1)S(1)}, u32[]{:S(2)}, u32[]{:S(2)}) %collective-permute-start) | collective-permute-done | bytes 266272 | tf_op jit(solution)/shard_map/ppermute | solution.py:24
  14.6 0.4 join_0_0.1
  15.0 2.6 %collective-permute-start.4 = (s16[784,128]{1,0:T(8,128)(2,1)S(1)}, s16[784,128]{1,0:T(8,128)(2,1)S(1)}, u32[]{:S(2)}, u32[]{:S(2)}) collective-permute-start(s16[784,128]{1,0:T(8,128)(2,1)S(1)} %get-tuple-element.77), channel_id=1, source_target_pairs={{1,0},{0,1},{3,2},{2,3},{5,4},{4,5},{7,6},{6,7},{9,8},{8,9},{11,10... | collective-permute-start | bytes 602120 | tf_op jit(solution)/shard_map/ppermute | solution.py:24
  17.6 3.0 %ext_int_products_1.1 = (s16[1040,128]{1,0:T(8,128)(2,1)S(1)}, s16[1040,128]{1,0:T(8,128)(2,1)S(1)}, s16[1040,128]{1,0:T(8,128)(2,1)S(1)}, s16[1040,128]{1,0:T(8,128)(2,1)S(1)}) custom-call(f32[8,1536]{1,0:T(8,128)S(1)} %get-tuple-element.59.a_rows_ref, f32[8,1536]{1,0:T(8,128)S(1)} %get-tuple-element.75.b_rows_ref, bf16[1,2048,1536]{2,1,0:T(8,128)(2,1)S(1)} %bitcast.4, ...), custom_call_target="tpu_custom_call" | custom-call | flops 1 | bytes 1 | tf_op jit(solution)/shard_map/ext_int_products_1/pallas_call | solution.py:32
  20.6 1.6 %collective-permute-start.5 = (s16[1040,128]{1,0:T(8,128)(2,1)S(1)}, s16[1040,128]{1,0:T(8,128)(2,1)S(1)}, u32[]{:S(2)}, u32[]{:S(2)}) collective-permute-start(s16[1040,128]{1,0:T(8,128)(2,1)S(1)} %get-tuple-element.80), channel_id=1, source_target_pairs={{28,0},{8,4},{4,8},{16,12},{12,16},{24,20},{20,24},{0,28},{29,1},{... | collective-permute-start | bytes 798728 | tf_op jit(solution)/shard_map/ppermute | solution.py:24
  22.3 1.1 %collective-permute-start.9 = (s16[1040,128]{1,0:T(8,128)(2,1)S(1)}, s16[1040,128]{1,0:T(8,128)(2,1)S(1)}, u32[]{:S(2)}, u32[]{:S(2)}) collective-permute-start(s16[1040,128]{1,0:T(8,128)(2,1)S(1)} %get-tuple-element.90), channel_id=1, source_target_pairs={{28,0},{8,4},{4,8},{16,12},{12,16},{24,20},{20,24},{0,28},{29,1},{... | collective-permute-start | bytes 798728 | tf_op jit(solution)/shard_map/ppermute | solution.py:24
  23.4 0.4 join_0_128.1
  23.8 0.6 collective-permute-start.7
  24.4 1.8 %own_products_1.1.own_ref = f32[1536,256]{1,0:T(8,128)S(1)} custom-call(f32[8,1536]{1,0:T(8,128)S(1)} %get-tuple-element.59.a_rows_ref, f32[8,1536]{1,0:T(8,128)S(1)} %get-tuple-element.75.b_rows_ref, bf16[1,2048,1536]{2,1,0:T(8,128)(2,1)S(1)} %bitcast.4, bf16[1024,2048]{1,0:T(8,128)(2,1)S(1)} %get-tuple-element.63.ext_rows_ref, ...), custom_call_target="tpu_custom_call" | custom-call | flops 1 | bytes 1 | tf_op jit(solution)/shard_map/own_products_1/pallas_call | solution.py:32
  26.2 0.2 halve_2_0.1
  26.4 3.9 %collective-permute-done.5.ext_ref = s16[1040,128]{1,0:T(8,128)(2,1)S(1)} collective-permute-done((s16[1040,128]{1,0:T(8,128)(2,1)S(1)}, s16[1040,128]{1,0:T(8,128)(2,1)S(1)}, u32[]{:S(2)}, u32[]{:S(2)}) %collective-permute-start.5) | collective-permute-done | bytes 266272 | tf_op jit(solution)/shard_map/ppermute | solution.py:24
  30.2 2.6 %collective-permute-start.8 = (s16[400,128]{1,0:T(8,128)(2,1)S(1)}, s16[400,128]{1,0:T(8,128)(2,1)S(1)}, u32[]{:S(2)}, u32[]{:S(2)}) collective-permute-start(s16[400,128]{1,0:T(8,128)(2,1)S(1)} %get-tuple-element.86), channel_id=1, source_target_pairs={{2,0},{3,1},{0,2},{1,3},{6,4},{7,5},{4,6},{5,7},{10,8},{11,9},{8,1... | collective-permute-start | bytes 307208 | tf_op jit(solution)/shard_map/ppermute | solution.py:24
  32.8 0.4 join_1_0.1
  33.2 0.2 halve_2_1.1
  33.4 0.5 collective-permute-start.11
  33.9 2.7 %collective-permute-done.8.rest_0_ = s16[400,128]{1,0:T(8,128)(2,1)S(1)} collective-permute-done((s16[400,128]{1,0:T(8,128)(2,1)S(1)}, s16[400,128]{1,0:T(8,128)(2,1)S(1)}, u32[]{:S(2)}, u32[]{:S(2)}) %collective-permute-start.8) | collective-permute-done | bytes 102432 | tf_op jit(solution)/shard_map/ppermute | solution.py:24
  36.8 0.4 join_1_128.1
  37.2 2.9 %collective-permute-start.13 = (s16[400,128]{1,0:T(8,128)(2,1)S(1)}, s16[400,128]{1,0:T(8,128)(2,1)S(1)}, u32[]{:S(2)}, u32[]{:S(2)}) collective-permute-start(s16[400,128]{1,0:T(8,128)(2,1)S(1)} %get-tuple-element.100), channel_id=1, source_target_pairs={{2,0},{3,1},{0,2},{1,3},{6,4},{7,5},{4,6},{5,7},{10,8},{11,9},{8,1... | collective-permute-start | bytes 307208 | tf_op jit(solution)/shard_map/ppermute | solution.py:24
  40.2 3.0 %collective-permute-done.11.got_ref = s16[784,128]{1,0:T(8,128)(2,1)S(1)} collective-permute-done((s16[784,128]{1,0:T(8,128)(2,1)S(1)}, s16[784,128]{1,0:T(8,128)(2,1)S(1)}, u32[]{:S(2)}, u32[]{:S(2)}) %collective-permute-start.11) | collective-permute-done | bytes 200736 | tf_op jit(solution)/shard_map/ppermute | solution.py:24
  43.4 4.5 %collective-permute-done.12.got_ref = s16[784,128]{1,0:T(8,128)(2,1)S(1)} collective-permute-done((s16[784,128]{1,0:T(8,128)(2,1)S(1)}, s16[784,128]{1,0:T(8,128)(2,1)S(1)}, u32[]{:S(2)}, u32[]{:S(2)}) %collective-permute-start.12) | collective-permute-done | bytes 200736 | tf_op jit(solution)/shard_map/ppermute | solution.py:24
  47.9 0.2 halve_2_3.1
  48.2 3.1 %collective-permute-done.14.rest_0_ = s16[400,128]{1,0:T(8,128)(2,1)S(1)} collective-permute-done((s16[400,128]{1,0:T(8,128)(2,1)S(1)}, s16[400,128]{1,0:T(8,128)(2,1)S(1)}, u32[]{:S(2)}, u32[]{:S(2)}) %collective-permute-start.14) | collective-permute-done | bytes 102432 | tf_op jit(solution)/shard_map/ppermute | solution.py:24
  51.4 2.9 %collective-permute-done.15.rest_0_ = s16[400,128]{1,0:T(8,128)(2,1)S(1)} collective-permute-done((s16[400,128]{1,0:T(8,128)(2,1)S(1)}, s16[400,128]{1,0:T(8,128)(2,1)S(1)}, u32[]{:S(2)}, u32[]{:S(2)}) %collective-permute-start.15) | collective-permute-done | bytes 102432 | tf_op jit(solution)/shard_map/ppermute | solution.py:24
  54.4 3.1 %collective-permute-start.18 = (f32[8,512]{1,0:T(8,128)S(1)}, f32[8,512]{1,0:T(8,128)S(1)}, u32[]{:S(2)}, u32[]{:S(2)}) collective-permute-start(f32[8,512]{1,0:T(8,128)S(1)} %get-tuple-element.110.refs_4_), channel_id=1, source_target_pairs={{3,0},{2,1},{1,2},{0,3},{7,4},{6,5},{5,6},{4,7},{11,8},{10,9},{9,1... | collective-permute-start | bytes 49160 | tf_op jit(solution)/shard_map/ppermute | solution.py:24
  57.5 1.4 %collective-permute-start.16 = (f32[8,512]{1,0:T(8,128)S(1)}, f32[8,512]{1,0:T(8,128)S(1)}, u32[]{:S(2)}, u32[]{:S(2)}) collective-permute-start(f32[8,512]{1,0:T(8,128)S(1)} %get-tuple-element.110.refs_4_), channel_id=1, source_target_pairs={{1,0},{0,1},{3,2},{2,3},{5,4},{4,5},{7,6},{6,7},{9,8},{8,9},{11,10... | collective-permute-start | bytes 49160 | tf_op jit(solution)/shard_map/ppermute | solution.py:24
  58.8 1.1 %collective-permute-done.18.refs_7_ = f32[8,512]{1,0:T(8,128)S(1)} collective-permute-done((f32[8,512]{1,0:T(8,128)S(1)}, f32[8,512]{1,0:T(8,128)S(1)}, u32[]{:S(2)}, u32[]{:S(2)}) %collective-permute-start.18) | collective-permute-done | bytes 16416 | tf_op jit(solution)/shard_map/ppermute | solution.py:24
  60.0 2.1 %collective-permute-done.17.refs_6_ = f32[8,512]{1,0:T(8,128)S(1)} collective-permute-done((f32[8,512]{1,0:T(8,128)S(1)}, f32[8,512]{1,0:T(8,128)S(1)}, u32[]{:S(2)}, u32[]{:S(2)}) %collective-permute-start.17) | collective-permute-done | bytes 16416 | tf_op jit(solution)/shard_map/ppermute | solution.py:24
  62.1 1.0 %rescale.1 = f32[1,384,512]{2,1,0:T(8,128)} custom-call(f32[384,128]{1,0:T(8,128)S(1)} %get-tuple-element.87.refs_0_, f32[384,128]{1,0:T(8,128)S(1)} %get-tuple-element.101.refs_1_, f32[384,128]{1,0:T(8,128)S(1)} %get-tuple-element.105.refs_2_, f32[384,128]{1,0:T(8,128)S(1)} %get-tuple-element.109.refs_3_, f32[8,512]{1,0:T(8,128)S(1)} %get-tuple-element.110.refs_4_, ...), custom_call_target="tpu_custom_call" | custom-call | flops 1 | bytes 1 | tf_op jit(solution)/shard_map/rescale/pallas_call | solution.py:32
  (30 shorter events, 0.8 us)
Async XLA Ops:
  0.0 8.0 %slice-start = ((s8[6291456]{0:T(1024)(128)(4,1)}), s8[4194304]{0:T(1024)(128)(4,1)S(1)}, s32[]{:S(2)}) async-start(s8[6291456]{0:T(1024)(128)(4,1)} %bitcast.3), calls=%async_computation | async-start | bytes 8388608
  0.0 8.0 %slice-start.1 = ((s8[6291456]{0:T(1024)(128)(4,1)}), s8[2097152]{0:T(1024)(128)(4,1)S(1)}, s32[]{:S(2)}) async-start(s8[6291456]{0:T(1024)(128)(4,1)} %bitcast.3), calls=%async_computation.1 | async-start | bytes 4194304
  0.0 8.0 %copy-start = (bf16[1,2048,1536]{2,1,0:T(8,128)(2,1)S(1)}, bf16[1,2048,1536]{2,1,0:T(8,128)(2,1)}, u32[]{:S(2)}) copy-start(bf16[1,2048,1536]{2,1,0:T(8,128)(2,1)} %side_ref.1) | copy-start | bytes 18874372
  4.6 10.1 %collective-permute-start = (s16[1040,128]{1,0:T(8,128)(2,1)S(1)}, s16[1040,128]{1,0:T(8,128)(2,1)S(1)}, u32[]{:S(2)}, u32[]{:S(2)}) collective-permute-start(s16[1040,128]{1,0:T(8,128)(2,1)S(1)} %get-tuple-element.61), channel_id=1, source_target_pairs={{28,0},{8,4},{4,8},{16,12},{12,16},{24,20},{20,24},{0,28},{29,1},{... | collective-permute-start | bytes 798728 | tf_op jit(solution)/shard_map/ppermute | solution.py:24
  11.1 3.6 %collective-permute-start.1 = (s16[1040,128]{1,0:T(8,128)(2,1)S(1)}, s16[1040,128]{1,0:T(8,128)(2,1)S(1)}, u32[]{:S(2)}, u32[]{:S(2)}) collective-permute-start(s16[1040,128]{1,0:T(8,128)(2,1)S(1)} %get-tuple-element.64), channel_id=1, source_target_pairs={{4,0},{0,4},{12,8},{8,12},{20,16},{16,20},{28,24},{24,28},{5,1},{1... | collective-permute-start | bytes 798728 | tf_op jit(solution)/shard_map/ppermute | solution.py:24
  11.1 11.1 %collective-permute-start.2 = (s16[1040,128]{1,0:T(8,128)(2,1)S(1)}, s16[1040,128]{1,0:T(8,128)(2,1)S(1)}, u32[]{:S(2)}, u32[]{:S(2)}) collective-permute-start(s16[1040,128]{1,0:T(8,128)(2,1)S(1)} %get-tuple-element.72), channel_id=1, source_target_pairs={{28,0},{8,4},{4,8},{16,12},{12,16},{24,20},{20,24},{0,28},{29,1},{... | collective-permute-start | bytes 798728 | tf_op jit(solution)/shard_map/ppermute | solution.py:24
  13.4 10.0 %collective-permute-start.3 = (s16[1040,128]{1,0:T(8,128)(2,1)S(1)}, s16[1040,128]{1,0:T(8,128)(2,1)S(1)}, u32[]{:S(2)}, u32[]{:S(2)}) collective-permute-start(s16[1040,128]{1,0:T(8,128)(2,1)S(1)} %get-tuple-element.73), channel_id=1, source_target_pairs={{4,0},{0,4},{12,8},{8,12},{20,16},{16,20},{28,24},{24,28},{5,1},{1... | collective-permute-start | bytes 798728 | tf_op jit(solution)/shard_map/ppermute | solution.py:24
  15.0 8.7 %collective-permute-start.4 = (s16[784,128]{1,0:T(8,128)(2,1)S(1)}, s16[784,128]{1,0:T(8,128)(2,1)S(1)}, u32[]{:S(2)}, u32[]{:S(2)}) collective-permute-start(s16[784,128]{1,0:T(8,128)(2,1)S(1)} %get-tuple-element.77), channel_id=1, source_target_pairs={{1,0},{0,1},{3,2},{2,3},{5,4},{4,5},{7,6},{6,7},{9,8},{8,9},{11,10... | collective-permute-start | bytes 602120 | tf_op jit(solution)/shard_map/ppermute | solution.py:24
  20.6 9.6 %collective-permute-start.5 = (s16[1040,128]{1,0:T(8,128)(2,1)S(1)}, s16[1040,128]{1,0:T(8,128)(2,1)S(1)}, u32[]{:S(2)}, u32[]{:S(2)}) collective-permute-start(s16[1040,128]{1,0:T(8,128)(2,1)S(1)} %get-tuple-element.80), channel_id=1, source_target_pairs={{28,0},{8,4},{4,8},{16,12},{12,16},{24,20},{20,24},{0,28},{29,1},{... | collective-permute-start | bytes 798728 | tf_op jit(solution)/shard_map/ppermute | solution.py:24
  22.3 10.6 %collective-permute-start.6 = (s16[1040,128]{1,0:T(8,128)(2,1)S(1)}, s16[1040,128]{1,0:T(8,128)(2,1)S(1)}, u32[]{:S(2)}, u32[]{:S(2)}) collective-permute-start(s16[1040,128]{1,0:T(8,128)(2,1)S(1)} %get-tuple-element.70), channel_id=1, source_target_pairs={{4,0},{0,4},{12,8},{8,12},{20,16},{16,20},{28,24},{24,28},{5,1},{1... | collective-permute-start | bytes 798728 | tf_op jit(solution)/shard_map/ppermute | solution.py:24
  22.3 14.5 %collective-permute-start.9 = (s16[1040,128]{1,0:T(8,128)(2,1)S(1)}, s16[1040,128]{1,0:T(8,128)(2,1)S(1)}, u32[]{:S(2)}, u32[]{:S(2)}) collective-permute-start(s16[1040,128]{1,0:T(8,128)(2,1)S(1)} %get-tuple-element.90), channel_id=1, source_target_pairs={{28,0},{8,4},{4,8},{16,12},{12,16},{24,20},{20,24},{0,28},{29,1},{... | collective-permute-start | bytes 798728 | tf_op jit(solution)/shard_map/ppermute | solution.py:24
  23.4 13.4 %collective-permute-start.10 = (s16[1040,128]{1,0:T(8,128)(2,1)S(1)}, s16[1040,128]{1,0:T(8,128)(2,1)S(1)}, u32[]{:S(2)}, u32[]{:S(2)}) collective-permute-start(s16[1040,128]{1,0:T(8,128)(2,1)S(1)} %get-tuple-element.91), channel_id=1, source_target_pairs={{4,0},{0,4},{12,8},{8,12},{20,16},{16,20},{28,24},{24,28},{5,1},{1... | collective-permute-start | bytes 798728 | tf_op jit(solution)/shard_map/ppermute | solution.py:24
  23.8 9.5 %collective-permute-start.7 = (s16[784,128]{1,0:T(8,128)(2,1)S(1)}, s16[784,128]{1,0:T(8,128)(2,1)S(1)}, u32[]{:S(2)}, u32[]{:S(2)}) collective-permute-start(s16[784,128]{1,0:T(8,128)(2,1)S(1)} %get-tuple-element.83), channel_id=1, source_target_pairs={{1,0},{0,1},{3,2},{2,3},{5,4},{4,5},{7,6},{6,7},{9,8},{8,9},{11,10... | collective-permute-start | bytes 602120 | tf_op jit(solution)/shard_map/ppermute | solution.py:24
  30.2 6.4 %collective-permute-start.8 = (s16[400,128]{1,0:T(8,128)(2,1)S(1)}, s16[400,128]{1,0:T(8,128)(2,1)S(1)}, u32[]{:S(2)}, u32[]{:S(2)}) collective-permute-start(s16[400,128]{1,0:T(8,128)(2,1)S(1)} %get-tuple-element.86), channel_id=1, source_target_pairs={{2,0},{3,1},{0,2},{1,3},{6,4},{7,5},{4,6},{5,7},{10,8},{11,9},{8,1... | collective-permute-start | bytes 307208 | tf_op jit(solution)/shard_map/ppermute | solution.py:24
  33.4 9.7 %collective-permute-start.11 = (s16[784,128]{1,0:T(8,128)(2,1)S(1)}, s16[784,128]{1,0:T(8,128)(2,1)S(1)}, u32[]{:S(2)}, u32[]{:S(2)}) collective-permute-start(s16[784,128]{1,0:T(8,128)(2,1)S(1)} %get-tuple-element.94), channel_id=1, source_target_pairs={{1,0},{0,1},{3,2},{2,3},{5,4},{4,5},{7,6},{6,7},{9,8},{8,9},{11,10... | collective-permute-start | bytes 602120 | tf_op jit(solution)/shard_map/ppermute | solution.py:24
  37.2 10.7 %collective-permute-start.12 = (s16[784,128]{1,0:T(8,128)(2,1)S(1)}, s16[784,128]{1,0:T(8,128)(2,1)S(1)}, u32[]{:S(2)}, u32[]{:S(2)}) collective-permute-start(s16[784,128]{1,0:T(8,128)(2,1)S(1)} %get-tuple-element.97), channel_id=1, source_target_pairs={{1,0},{0,1},{3,2},{2,3},{5,4},{4,5},{7,6},{6,7},{9,8},{8,9},{11,10... | collective-permute-start | bytes 602120 | tf_op jit(solution)/shard_map/ppermute | solution.py:24
  37.2 10.9 %collective-permute-start.13 = (s16[400,128]{1,0:T(8,128)(2,1)S(1)}, s16[400,128]{1,0:T(8,128)(2,1)S(1)}, u32[]{:S(2)}, u32[]{:S(2)}) collective-permute-start(s16[400,128]{1,0:T(8,128)(2,1)S(1)} %get-tuple-element.100), channel_id=1, source_target_pairs={{2,0},{3,1},{0,2},{1,3},{6,4},{7,5},{4,6},{5,7},{10,8},{11,9},{8,1... | collective-permute-start | bytes 307208 | tf_op jit(solution)/shard_map/ppermute | solution.py:24
  43.3 8.0 %collective-permute-start.14 = (s16[400,128]{1,0:T(8,128)(2,1)S(1)}, s16[400,128]{1,0:T(8,128)(2,1)S(1)}, u32[]{:S(2)}, u32[]{:S(2)}) collective-permute-start(s16[400,128]{1,0:T(8,128)(2,1)S(1)} %get-tuple-element.104), channel_id=1, source_target_pairs={{2,0},{3,1},{0,2},{1,3},{6,4},{7,5},{4,6},{5,7},{10,8},{11,9},{8,1... | collective-permute-start | bytes 307208 | tf_op jit(solution)/shard_map/ppermute | solution.py:24
  48.1 6.2 %collective-permute-start.15 = (s16[400,128]{1,0:T(8,128)(2,1)S(1)}, s16[400,128]{1,0:T(8,128)(2,1)S(1)}, u32[]{:S(2)}, u32[]{:S(2)}) collective-permute-start(s16[400,128]{1,0:T(8,128)(2,1)S(1)} %get-tuple-element.108), channel_id=1, source_target_pairs={{2,0},{3,1},{0,2},{1,3},{6,4},{7,5},{4,6},{5,7},{10,8},{11,9},{8,1... | collective-permute-start | bytes 307208 | tf_op jit(solution)/shard_map/ppermute | solution.py:24
  54.4 5.6 %collective-permute-start.18 = (f32[8,512]{1,0:T(8,128)S(1)}, f32[8,512]{1,0:T(8,128)S(1)}, u32[]{:S(2)}, u32[]{:S(2)}) collective-permute-start(f32[8,512]{1,0:T(8,128)S(1)} %get-tuple-element.110.refs_4_), channel_id=1, source_target_pairs={{3,0},{2,1},{1,2},{0,3},{7,4},{6,5},{5,6},{4,7},{11,8},{10,9},{9,1... | collective-permute-start | bytes 49160 | tf_op jit(solution)/shard_map/ppermute | solution.py:24
  57.5 4.6 %collective-permute-start.17 = (f32[8,512]{1,0:T(8,128)S(1)}, f32[8,512]{1,0:T(8,128)S(1)}, u32[]{:S(2)}, u32[]{:S(2)}) collective-permute-start(f32[8,512]{1,0:T(8,128)S(1)} %get-tuple-element.110.refs_4_), channel_id=1, source_target_pairs={{2,0},{3,1},{0,2},{1,3},{6,4},{7,5},{4,6},{5,7},{10,8},{11,9},{8,1... | collective-permute-start | bytes 49160 | tf_op jit(solution)/shard_map/ppermute | solution.py:24
  57.5 4.6 %collective-permute-start.16 = (f32[8,512]{1,0:T(8,128)S(1)}, f32[8,512]{1,0:T(8,128)S(1)}, u32[]{:S(2)}, u32[]{:S(2)}) collective-permute-start(f32[8,512]{1,0:T(8,128)S(1)} %get-tuple-element.110.refs_4_), channel_id=1, source_target_pairs={{1,0},{0,1},{3,2},{2,3},{5,4},{4,5},{7,6},{6,7},{9,8},{8,9},{11,10... | collective-permute-start | bytes 49160 | tf_op jit(solution)/shard_map/ppermute | solution.py:24

commit v10 on v9

--- a/solution.py
+++ b/solution.py
@@ -434,24 +434,26 @@
 
     def send_ext(parts):
         ext.extend(swap(part, "blk", other_chip) for part in parts)
-        latest.append(parts[0])
 
     def send_int(parts):
         ints.extend(swap(part, "blk", same_chip) for part in parts)
-        latest.append(parts[0])
 
     *parts, ext_rows, a_rows, b_rows, c_rows = first_products(flow_t, graph, a_lines, b_lines, c_lines, fine)
     send_ext(parts)
+    latest.append(parts[0])
     wanted = {"own": (BS,), "int": fine}
     own, *parts, int_rows = products(a_rows, ordered(b_rows), graph, ext_rows, flow_t, 0, wanted, turns=True)
     owns.append(own)
     send_int(parts)
+    latest.append(own)
 
     def more_products(half):
         wanted = {"ext": fine, "int": fine}
         parts = products(a_rows, ordered(b_rows), graph, ext_rows, int_rows, half, wanted)
-        send_ext(parts[:per_half])
-        send_int(parts[per_half:])
+        send_ext(parts[:1])
+        send_int(parts[per_half : per_half + 1])
+        latest.append(parts[0])
+        return parts[1:per_half], parts[per_half + 1 :]
 
     def more_own(half):
         owns.extend(products(a_rows, ordered(b_rows), graph, ext_rows, int_rows, half, {"own": (BS,)}))
@@ -485,17 +487,24 @@
         squares.append(squared)
         sums.append(summed)
 
-    for chunk in range(chunks + 1):
-        if chunk < chunks:
+    for half in range(halves):
+        first = half * per_half
+        add_up(first)
+        if half > 0:
+            scatter(first - 1)
+        if half + 1 < halves:
+            ext_parts, int_parts = more_products(half + 1)
+        for chunk in range(first + 1, first + per_half):
+            if chunk == chunks - 1:
+                finish(0)
             add_up(chunk)
-        if (chunk + 1) % per_half == 0 and len(owns) < halves:
-            more_own(len(owns))
-        if chunk >= 1:
             scatter(chunk - 1)
-        if chunk == 2:
-            finish(0)
-        if chunk % per_half == 0 and chunk // per_half + 1 < halves:
-            more_products(chunk // per_half + 1)
+        if half + 1 < halves:
+            before = latest[-1]
+            send_ext(after(part, before) for part in ext_parts)
+            send_int(after(part, before) for part in int_parts)
+            more_own(half + 1)
+    scatter(chunks - 1)
     for chunk in range(1, chunks):
         finish(chunk)
 

time: 63.3 us -> 65.1 us (1.028)
  starting transfers between devices: 22.3 us -> 26.6 us
  waiting for transfers between devices: 24.6 us -> 21.9 us
    ppermute x19, starting transfers between devices: 22.3 us -> 26.6 us  [swap(): lax.ppermute(block, axis, [(partner(i), i) for i in range(lax.axis_size(a...]
    ppermute x19, waiting for transfers between devices: 24.6 us -> 21.9 us  [swap(): lax.ppermute(block, axis, [(partner(i), i) for i in range(lax.axis_size(a...]
where the time goes in v10:
time: 65.1 us; the launch traced here: 64.9 us
  starting transfers between devices  26.6 us (41%)
  waiting for transfers between devices  21.9 us (34%)
  Pallas kernels  16.2 us (25%)
    ppermute x19, starting transfers between devices, swap(): lax.ppermute(block, axis, [(partner(i), i) for i in range(lax.axis_size(a...  26.6 us
    ppermute x19, waiting for transfers between devices, swap(): lax.ppermute(block, axis, [(partner(i), i) for i in range(lax.axis_size(a...  21.9 us
    pallas_call x17, Pallas kernels, call(): pl.pallas_call(kernel, out_shape=out_shape, in_specs=in_specs, out_specs=...  16.2 us
  transfers between devices with their start and end apart: 19, of which 9 were waited for; matrix products, arithmetic and copies ran while one was open for 0% of the time, Pallas kernels for 16%

profile of v10, /device:TPU:0, one launch (start us, length us, event | category | flops | bytes accessed | tf_op | source)
XLA Modules:
  0.0 64.9 jit_solution(14510317542329909515)
XLA Ops:
  0.0 4.5 %first_products.1 = (s16[1040,128]{1,0:T(8,128)(2,1)S(1)}, s16[1040,128]{1,0:T(8,128)(2,1)S(1)}, bf16[1024,2048]{1,0:T(8,128)(2,1)S(1)}, f32[8,1536]{1,0:T(8,128...) custom-call(s32[6,1,32]{2,1,0:T(1,128)} %bitcast.5, s32[6,1,32]{2,1,0:T(1,128)} %bitcast.6, s32[1,2,6]{2,1,0:T(2,128)} %bitcast.7, ...), custom_call_target="tpu_custom_call" | custom-call | flops 1 | bytes 1 | tf_op jit(solution)/shard_map/first_products/pallas_call | solution.py:32
  4.6 3.4 %collective-permute-start = (s16[1040,128]{1,0:T(8,128)(2,1)S(1)}, s16[1040,128]{1,0:T(8,128)(2,1)S(1)}, u32[]{:S(2)}, u32[]{:S(2)}) collective-permute-start(s16[1040,128]{1,0:T(8,128)(2,1)S(1)} %get-tuple-element.63), channel_id=1, source_target_pairs={{28,0},{8,4},{4,8},{16,12},{12,16},{24,20},{20,24},{0,28},{29,1},{... | collective-permute-start | bytes 798728 | tf_op jit(solution)/shard_map/ppermute | solution.py:24
  8.0 3.1 %own_int_products_0.1 = (f32[1536,256]{1,0:T(8,128)S(1)}, s16[1040,128]{1,0:T(8,128)(2,1)S(1)}, s16[1040,128]{1,0:T(8,128)(2,1)S(1)}, bf16[512,2048]{1,0:T(8,128)(2,1)S(1)}) custom-call(f32[8,1536]{1,0:T(8,128)S(1)} %get-tuple-element.61.a_rows_ref, f32[8,1536]{1,0:T(8,128)S(1)} %get-tuple-element.80.b_rows_ref, bf16[1,2048,1536]{2,1,0:T(8,128)(2,1)S(1)} %bitcast.4, ...), custom_call_target="tpu_custom_call" | custom-call | flops 1 | bytes 1 | tf_op jit(solution)/shard_map/own_int_products_0/pallas_call | solution.py:32
  11.1 2.3 %collective-permute-start.2 = (s16[1040,128]{1,0:T(8,128)(2,1)S(1)}, s16[1040,128]{1,0:T(8,128)(2,1)S(1)}, u32[]{:S(2)}, u32[]{:S(2)}) collective-permute-start(s16[1040,128]{1,0:T(8,128)(2,1)S(1)} %get-tuple-element.74), channel_id=1, source_target_pairs={{28,0},{8,4},{4,8},{16,12},{12,16},{24,20},{20,24},{0,28},{29,1},{... | collective-permute-start | bytes 798728 | tf_op jit(solution)/shard_map/ppermute | solution.py:24
  13.4 1.2 %collective-permute-done.ext_ref = s16[1040,128]{1,0:T(8,128)(2,1)S(1)} collective-permute-done((s16[1040,128]{1,0:T(8,128)(2,1)S(1)}, s16[1040,128]{1,0:T(8,128)(2,1)S(1)}, u32[]{:S(2)}, u32[]{:S(2)}) %collective-permute-start) | collective-permute-done | bytes 266272 | tf_op jit(solution)/shard_map/ppermute | solution.py:24
  14.6 0.4 join_0_0.1
  15.0 2.6 %collective-permute-start.4 = (s16[784,128]{1,0:T(8,128)(2,1)S(1)}, s16[784,128]{1,0:T(8,128)(2,1)S(1)}, u32[]{:S(2)}, u32[]{:S(2)}) collective-permute-start(s16[784,128]{1,0:T(8,128)(2,1)S(1)} %get-tuple-element.78), channel_id=1, source_target_pairs={{1,0},{0,1},{3,2},{2,3},{5,4},{4,5},{7,6},{6,7},{9,8},{8,9},{11,10... | collective-permute-start | bytes 602120 | tf_op jit(solution)/shard_map/ppermute | solution.py:24
  17.6 3.0 %ext_int_products_1.1 = (s16[1040,128]{1,0:T(8,128)(2,1)S(1)}, s16[1040,128]{1,0:T(8,128)(2,1)S(1)}, s16[1040,128]{1,0:T(8,128)(2,1)S(1)}, s16[1040,128]{1,0:T(8,128)(2,1)S(1)}) custom-call(f32[8,1536]{1,0:T(8,128)S(1)} %get-tuple-element.61.a_rows_ref, f32[8,1536]{1,0:T(8,128)S(1)} %get-tuple-element.80.b_rows_ref, bf16[1,2048,1536]{2,1,0:T(8,128)(2,1)S(1)} %bitcast.4, ...), custom_call_target="tpu_custom_call" | custom-call | flops 1 | bytes 1 | tf_op jit(solution)/shard_map/ext_int_products_1/pallas_call | solution.py:32
  20.7 1.8 %collective-permute-start.5 = (s16[1040,128]{1,0:T(8,128)(2,1)S(1)}, s16[1040,128]{1,0:T(8,128)(2,1)S(1)}, u32[]{:S(2)}, u32[]{:S(2)}) collective-permute-start(s16[1040,128]{1,0:T(8,128)(2,1)S(1)} %get-tuple-element.72), channel_id=1, source_target_pairs={{28,0},{8,4},{4,8},{16,12},{12,16},{24,20},{20,24},{0,28},{29,1},{... | collective-permute-start | bytes 798728 | tf_op jit(solution)/shard_map/ppermute | solution.py:24
  22.5 0.4 join_0_128.1
  22.9 0.2 halve_2_0.1
  23.1 1.8 %collective-permute-start.9 = (s16[1040,128]{1,0:T(8,128)(2,1)S(1)}, s16[1040,128]{1,0:T(8,128)(2,1)S(1)}, u32[]{:S(2)}, u32[]{:S(2)}) collective-permute-start(s16[1040,128]{1,0:T(8,128)(2,1)S(1)} %get-tuple-element.93), channel_id=1, source_target_pairs={{28,0},{8,4},{4,8},{16,12},{12,16},{24,20},{20,24},{0,28},{29,1},{... | collective-permute-start | bytes 798728 | tf_op jit(solution)/shard_map/ppermute | solution.py:24
  24.9 1.6 %collective-permute-start.7 = (s16[784,128]{1,0:T(8,128)(2,1)S(1)}, s16[784,128]{1,0:T(8,128)(2,1)S(1)}, u32[]{:S(2)}, u32[]{:S(2)}) collective-permute-start(s16[784,128]{1,0:T(8,128)(2,1)S(1)} %get-tuple-element.85), channel_id=1, source_target_pairs={{1,0},{0,1},{3,2},{2,3},{5,4},{4,5},{7,6},{6,7},{9,8},{8,9},{11,10... | collective-permute-start | bytes 602120 | tf_op jit(solution)/shard_map/ppermute | solution.py:24
  26.4 2.6 %collective-permute-start.8 = (s16[400,128]{1,0:T(8,128)(2,1)S(1)}, s16[400,128]{1,0:T(8,128)(2,1)S(1)}, u32[]{:S(2)}, u32[]{:S(2)}) collective-permute-start(s16[400,128]{1,0:T(8,128)(2,1)S(1)} %get-tuple-element.88), channel_id=1, source_target_pairs={{2,0},{3,1},{0,2},{1,3},{6,4},{7,5},{4,6},{5,7},{10,8},{11,9},{8,1... | collective-permute-start | bytes 307208 | tf_op jit(solution)/shard_map/ppermute | solution.py:24
  29.1 1.8 %own_products_1.1.own_ref = f32[1536,256]{1,0:T(8,128)S(1)} custom-call(f32[8,1536]{1,0:T(8,128)S(1)} %get-tuple-element.61.a_rows_ref, f32[8,1536]{1,0:T(8,128)S(1)} %get-tuple-element.80.b_rows_ref, bf16[1,2048,1536]{2,1,0:T(8,128)(2,1)S(1)} %bitcast.4, bf16[1024,2048]{1,0:T(8,128)(2,1)S(1)} %get-tuple-element.65.ext_rows_ref, ...), custom_call_target="tpu_custom_call" | custom-call | flops 1 | bytes 1 | tf_op jit(solution)/shard_map/own_products_1/pallas_call | solution.py:32
  30.9 0.6 join_1_0.1
  31.5 3.0 %collective-permute-done.7.got_ref = s16[784,128]{1,0:T(8,128)(2,1)S(1)} collective-permute-done((s16[784,128]{1,0:T(8,128)(2,1)S(1)}, s16[784,128]{1,0:T(8,128)(2,1)S(1)}, u32[]{:S(2)}, u32[]{:S(2)}) %collective-permute-start.7) | collective-permute-done | bytes 200736 | tf_op jit(solution)/shard_map/ppermute | solution.py:24
  34.8 1.1 %collective-permute-done.9.ext_ref = s16[1040,128]{1,0:T(8,128)(2,1)S(1)} collective-permute-done((s16[1040,128]{1,0:T(8,128)(2,1)S(1)}, s16[1040,128]{1,0:T(8,128)(2,1)S(1)}, u32[]{:S(2)}, u32[]{:S(2)}) %collective-permute-start.9) | collective-permute-done | bytes 266272 | tf_op jit(solution)/shard_map/ppermute | solution.py:24
  35.9 0.4 join_1_128.1
  36.3 1.3 %collective-permute-start.12 = (s16[784,128]{1,0:T(8,128)(2,1)S(1)}, s16[784,128]{1,0:T(8,128)(2,1)S(1)}, u32[]{:S(2)}, u32[]{:S(2)}) collective-permute-start(s16[784,128]{1,0:T(8,128)(2,1)S(1)} %get-tuple-element.101), channel_id=1, source_target_pairs={{1,0},{0,1},{3,2},{2,3},{5,4},{4,5},{7,6},{6,7},{9,8},{8,9},{11,10... | collective-permute-start | bytes 602120 | tf_op jit(solution)/shard_map/ppermute | solution.py:24
  37.6 1.9 %collective-permute-start.13 = (s16[400,128]{1,0:T(8,128)(2,1)S(1)}, s16[400,128]{1,0:T(8,128)(2,1)S(1)}, u32[]{:S(2)}, u32[]{:S(2)}) collective-permute-start(s16[400,128]{1,0:T(8,128)(2,1)S(1)} %get-tuple-element.104), channel_id=1, source_target_pairs={{2,0},{3,1},{0,2},{1,3},{6,4},{7,5},{4,6},{5,7},{10,8},{11,9},{8,1... | collective-permute-start | bytes 307208 | tf_op jit(solution)/shard_map/ppermute | solution.py:24
  39.6 6.4 %collective-permute-done.11.got_ref = s16[784,128]{1,0:T(8,128)(2,1)S(1)} collective-permute-done((s16[784,128]{1,0:T(8,128)(2,1)S(1)}, s16[784,128]{1,0:T(8,128)(2,1)S(1)}, u32[]{:S(2)}, u32[]{:S(2)}) %collective-permute-start.11) | collective-permute-done | bytes 200736 | tf_op jit(solution)/shard_map/ppermute | solution.py:24
  46.1 1.0 %collective-permute-start.14 = (s16[400,128]{1,0:T(8,128)(2,1)S(1)}, s16[400,128]{1,0:T(8,128)(2,1)S(1)}, u32[]{:S(2)}, u32[]{:S(2)}) collective-permute-start(s16[400,128]{1,0:T(8,128)(2,1)S(1)} %get-tuple-element.108), channel_id=1, source_target_pairs={{2,0},{3,1},{0,2},{1,3},{6,4},{7,5},{4,6},{5,7},{10,8},{11,9},{8,1... | collective-permute-start | bytes 307208 | tf_op jit(solution)/shard_map/ppermute | solution.py:24
  47.1 1.8 %collective-permute-done.12.got_ref = s16[784,128]{1,0:T(8,128)(2,1)S(1)} collective-permute-done((s16[784,128]{1,0:T(8,128)(2,1)S(1)}, s16[784,128]{1,0:T(8,128)(2,1)S(1)}, u32[]{:S(2)}, u32[]{:S(2)}) %collective-permute-start.12) | collective-permute-done | bytes 200736 | tf_op jit(solution)/shard_map/ppermute | solution.py:24
  49.1 1.7 %collective-permute-start.15 = (s16[400,128]{1,0:T(8,128)(2,1)S(1)}, s16[400,128]{1,0:T(8,128)(2,1)S(1)}, u32[]{:S(2)}, u32[]{:S(2)}) collective-permute-start(s16[400,128]{1,0:T(8,128)(2,1)S(1)} %get-tuple-element.112), channel_id=1, source_target_pairs={{2,0},{3,1},{0,2},{1,3},{6,4},{7,5},{4,6},{5,7},{10,8},{11,9},{8,1... | collective-permute-start | bytes 307208 | tf_op jit(solution)/shard_map/ppermute | solution.py:24
  51.0 5.2 %collective-permute-done.14.rest_0_ = s16[400,128]{1,0:T(8,128)(2,1)S(1)} collective-permute-done((s16[400,128]{1,0:T(8,128)(2,1)S(1)}, s16[400,128]{1,0:T(8,128)(2,1)S(1)}, u32[]{:S(2)}, u32[]{:S(2)}) %collective-permute-start.14) | collective-permute-done | bytes 102432 | tf_op jit(solution)/shard_map/ppermute | solution.py:24
  56.3 1.1 %collective-permute-done.15.rest_0_ = s16[400,128]{1,0:T(8,128)(2,1)S(1)} collective-permute-done((s16[400,128]{1,0:T(8,128)(2,1)S(1)}, s16[400,128]{1,0:T(8,128)(2,1)S(1)}, u32[]{:S(2)}, u32[]{:S(2)}) %collective-permute-start.15) | collective-permute-done | bytes 102432 | tf_op jit(solution)/shard_map/ppermute | solution.py:24
  57.5 1.8 %collective-permute-start.18 = (f32[8,512]{1,0:T(8,128)S(1)}, f32[8,512]{1,0:T(8,128)S(1)}, u32[]{:S(2)}, u32[]{:S(2)}) collective-permute-start(f32[8,512]{1,0:T(8,128)S(1)} %get-tuple-element.114.refs_4_), channel_id=1, source_target_pairs={{3,0},{2,1},{1,2},{0,3},{7,4},{6,5},{5,6},{4,7},{11,8},{10,9},{9,1... | collective-permute-start | bytes 49160 | tf_op jit(solution)/shard_map/ppermute | solution.py:24
  59.3 2.6 %collective-permute-start.16 = (f32[8,512]{1,0:T(8,128)S(1)}, f32[8,512]{1,0:T(8,128)S(1)}, u32[]{:S(2)}, u32[]{:S(2)}) collective-permute-start(f32[8,512]{1,0:T(8,128)S(1)} %get-tuple-element.114.refs_4_), channel_id=1, source_target_pairs={{1,0},{0,1},{3,2},{2,3},{5,4},{4,5},{7,6},{6,7},{9,8},{8,9},{11,10... | collective-permute-start | bytes 49160 | tf_op jit(solution)/shard_map/ppermute | solution.py:24
  61.9 1.2 %collective-permute-done.18.refs_7_ = f32[8,512]{1,0:T(8,128)S(1)} collective-permute-done((f32[8,512]{1,0:T(8,128)S(1)}, f32[8,512]{1,0:T(8,128)S(1)}, u32[]{:S(2)}, u32[]{:S(2)}) %collective-permute-start.18) | collective-permute-done | bytes 16416 | tf_op jit(solution)/shard_map/ppermute | solution.py:24
  63.2 0.8 %collective-permute-done.17.refs_6_ = f32[8,512]{1,0:T(8,128)S(1)} collective-permute-done((f32[8,512]{1,0:T(8,128)S(1)}, f32[8,512]{1,0:T(8,128)S(1)}, u32[]{:S(2)}, u32[]{:S(2)}) %collective-permute-start.17) | collective-permute-done | bytes 16416 | tf_op jit(solution)/shard_map/ppermute | solution.py:24
  63.9 1.0 %rescale.1 = f32[1,384,512]{2,1,0:T(8,128)} custom-call(f32[384,128]{1,0:T(8,128)S(1)} %get-tuple-element.89.refs_0_, f32[384,128]{1,0:T(8,128)S(1)} %get-tuple-element.105.refs_1_, f32[384,128]{1,0:T(8,128)S(1)} %get-tuple-element.109.refs_2_, f32[384,128]{1,0:T(8,128)S(1)} %get-tuple-element.113.refs_3_, f32[8,512]{1,0:T(8,128)S(1)} %get-tuple-element.114.refs_4_, ...), custom_call_target="tpu_custom_call" | custom-call | flops 1 | bytes 1 | tf_op jit(solution)/shard_map/rescale/pallas_call | solution.py:32
  (30 shorter events, 1.1 us)
Async XLA Ops:
  0.0 8.0 %slice-start = ((s8[6291456]{0:T(1024)(128)(4,1)}), s8[4194304]{0:T(1024)(128)(4,1)S(1)}, s32[]{:S(2)}) async-start(s8[6291456]{0:T(1024)(128)(4,1)} %bitcast.3), calls=%async_computation | async-start | bytes 8388608
  0.0 8.0 %slice-start.1 = ((s8[6291456]{0:T(1024)(128)(4,1)}), s8[2097152]{0:T(1024)(128)(4,1)S(1)}, s32[]{:S(2)}) async-start(s8[6291456]{0:T(1024)(128)(4,1)} %bitcast.3), calls=%async_computation.1 | async-start | bytes 4194304
  0.0 8.0 %copy-start = (bf16[1,2048,1536]{2,1,0:T(8,128)(2,1)S(1)}, bf16[1,2048,1536]{2,1,0:T(8,128)(2,1)}, u32[]{:S(2)}) copy-start(bf16[1,2048,1536]{2,1,0:T(8,128)(2,1)} %side_ref.1) | copy-start | bytes 18874372
  4.6 10.1 %collective-permute-start = (s16[1040,128]{1,0:T(8,128)(2,1)S(1)}, s16[1040,128]{1,0:T(8,128)(2,1)S(1)}, u32[]{:S(2)}, u32[]{:S(2)}) collective-permute-start(s16[1040,128]{1,0:T(8,128)(2,1)S(1)} %get-tuple-element.63), channel_id=1, source_target_pairs={{28,0},{8,4},{4,8},{16,12},{12,16},{24,20},{20,24},{0,28},{29,1},{... | collective-permute-start | bytes 798728 | tf_op jit(solution)/shard_map/ppermute | solution.py:24
  11.1 3.6 %collective-permute-start.1 = (s16[1040,128]{1,0:T(8,128)(2,1)S(1)}, s16[1040,128]{1,0:T(8,128)(2,1)S(1)}, u32[]{:S(2)}, u32[]{:S(2)}) collective-permute-start(s16[1040,128]{1,0:T(8,128)(2,1)S(1)} %get-tuple-element.68), channel_id=1, source_target_pairs={{4,0},{0,4},{12,8},{8,12},{20,16},{16,20},{28,24},{24,28},{5,1},{1... | collective-permute-start | bytes 798728 | tf_op jit(solution)/shard_map/ppermute | solution.py:24
  11.1 11.3 %collective-permute-start.2 = (s16[1040,128]{1,0:T(8,128)(2,1)S(1)}, s16[1040,128]{1,0:T(8,128)(2,1)S(1)}, u32[]{:S(2)}, u32[]{:S(2)}) collective-permute-start(s16[1040,128]{1,0:T(8,128)(2,1)S(1)} %get-tuple-element.74), channel_id=1, source_target_pairs={{28,0},{8,4},{4,8},{16,12},{12,16},{24,20},{20,24},{0,28},{29,1},{... | collective-permute-start | bytes 798728 | tf_op jit(solution)/shard_map/ppermute | solution.py:24
  13.4 9.1 %collective-permute-start.3 = (s16[1040,128]{1,0:T(8,128)(2,1)S(1)}, s16[1040,128]{1,0:T(8,128)(2,1)S(1)}, u32[]{:S(2)}, u32[]{:S(2)}) collective-permute-start(s16[1040,128]{1,0:T(8,128)(2,1)S(1)} %get-tuple-element.75), channel_id=1, source_target_pairs={{4,0},{0,4},{12,8},{8,12},{20,16},{16,20},{28,24},{24,28},{5,1},{1... | collective-permute-start | bytes 798728 | tf_op jit(solution)/shard_map/ppermute | solution.py:24
  15.0 7.8 %collective-permute-start.4 = (s16[784,128]{1,0:T(8,128)(2,1)S(1)}, s16[784,128]{1,0:T(8,128)(2,1)S(1)}, u32[]{:S(2)}, u32[]{:S(2)}) collective-permute-start(s16[784,128]{1,0:T(8,128)(2,1)S(1)} %get-tuple-element.78), channel_id=1, source_target_pairs={{1,0},{0,1},{3,2},{2,3},{5,4},{4,5},{7,6},{6,7},{9,8},{8,9},{11,10... | collective-permute-start | bytes 602120 | tf_op jit(solution)/shard_map/ppermute | solution.py:24
  20.6 5.8 %collective-permute-start.6 = (s16[1040,128]{1,0:T(8,128)(2,1)S(1)}, s16[1040,128]{1,0:T(8,128)(2,1)S(1)}, u32[]{:S(2)}, u32[]{:S(2)}) collective-permute-start(s16[1040,128]{1,0:T(8,128)(2,1)S(1)} %get-tuple-element.82), channel_id=1, source_target_pairs={{4,0},{0,4},{12,8},{8,12},{20,16},{16,20},{28,24},{24,28},{5,1},{1... | collective-permute-start | bytes 798728 | tf_op jit(solution)/shard_map/ppermute | solution.py:24
  20.7 10.2 %collective-permute-start.5 = (s16[1040,128]{1,0:T(8,128)(2,1)S(1)}, s16[1040,128]{1,0:T(8,128)(2,1)S(1)}, u32[]{:S(2)}, u32[]{:S(2)}) collective-permute-start(s16[1040,128]{1,0:T(8,128)(2,1)S(1)} %get-tuple-element.72), channel_id=1, source_target_pairs={{28,0},{8,4},{4,8},{16,12},{12,16},{24,20},{20,24},{0,28},{29,1},{... | collective-permute-start | bytes 798728 | tf_op jit(solution)/shard_map/ppermute | solution.py:24
  23.1 12.9 %collective-permute-start.9 = (s16[1040,128]{1,0:T(8,128)(2,1)S(1)}, s16[1040,128]{1,0:T(8,128)(2,1)S(1)}, u32[]{:S(2)}, u32[]{:S(2)}) collective-permute-start(s16[1040,128]{1,0:T(8,128)(2,1)S(1)} %get-tuple-element.93), channel_id=1, source_target_pairs={{28,0},{8,4},{4,8},{16,12},{12,16},{24,20},{20,24},{0,28},{29,1},{... | collective-permute-start | bytes 798728 | tf_op jit(solution)/shard_map/ppermute | solution.py:24
  24.9 11.1 %collective-permute-start.10 = (s16[1040,128]{1,0:T(8,128)(2,1)S(1)}, s16[1040,128]{1,0:T(8,128)(2,1)S(1)}, u32[]{:S(2)}, u32[]{:S(2)}) collective-permute-start(s16[1040,128]{1,0:T(8,128)(2,1)S(1)} %get-tuple-element.95), channel_id=1, source_target_pairs={{4,0},{0,4},{12,8},{8,12},{20,16},{16,20},{28,24},{24,28},{5,1},{1... | collective-permute-start | bytes 798728 | tf_op jit(solution)/shard_map/ppermute | solution.py:24
  24.9 9.6 %collective-permute-start.7 = (s16[784,128]{1,0:T(8,128)(2,1)S(1)}, s16[784,128]{1,0:T(8,128)(2,1)S(1)}, u32[]{:S(2)}, u32[]{:S(2)}) collective-permute-start(s16[784,128]{1,0:T(8,128)(2,1)S(1)} %get-tuple-element.85), channel_id=1, source_target_pairs={{1,0},{0,1},{3,2},{2,3},{5,4},{4,5},{7,6},{6,7},{9,8},{8,9},{11,10... | collective-permute-start | bytes 602120 | tf_op jit(solution)/shard_map/ppermute | solution.py:24
  26.4 8.3 %collective-permute-start.8 = (s16[400,128]{1,0:T(8,128)(2,1)S(1)}, s16[400,128]{1,0:T(8,128)(2,1)S(1)}, u32[]{:S(2)}, u32[]{:S(2)}) collective-permute-start(s16[400,128]{1,0:T(8,128)(2,1)S(1)} %get-tuple-element.88), channel_id=1, source_target_pairs={{2,0},{3,1},{0,2},{1,3},{6,4},{7,5},{4,6},{5,7},{10,8},{11,9},{8,1... | collective-permute-start | bytes 307208 | tf_op jit(solution)/shard_map/ppermute | solution.py:24
  34.7 11.2 %collective-permute-start.11 = (s16[784,128]{1,0:T(8,128)(2,1)S(1)}, s16[784,128]{1,0:T(8,128)(2,1)S(1)}, u32[]{:S(2)}, u32[]{:S(2)}) collective-permute-start(s16[784,128]{1,0:T(8,128)(2,1)S(1)} %get-tuple-element.98), channel_id=1, source_target_pairs={{1,0},{0,1},{3,2},{2,3},{5,4},{4,5},{7,6},{6,7},{9,8},{8,9},{11,10... | collective-permute-start | bytes 602120 | tf_op jit(solution)/shard_map/ppermute | solution.py:24
  36.3 12.6 %collective-permute-start.12 = (s16[784,128]{1,0:T(8,128)(2,1)S(1)}, s16[784,128]{1,0:T(8,128)(2,1)S(1)}, u32[]{:S(2)}, u32[]{:S(2)}) collective-permute-start(s16[784,128]{1,0:T(8,128)(2,1)S(1)} %get-tuple-element.101), channel_id=1, source_target_pairs={{1,0},{0,1},{3,2},{2,3},{5,4},{4,5},{7,6},{6,7},{9,8},{8,9},{11,10... | collective-permute-start | bytes 602120 | tf_op jit(solution)/shard_map/ppermute | solution.py:24
  37.6 13.2 %collective-permute-start.13 = (s16[400,128]{1,0:T(8,128)(2,1)S(1)}, s16[400,128]{1,0:T(8,128)(2,1)S(1)}, u32[]{:S(2)}, u32[]{:S(2)}) collective-permute-start(s16[400,128]{1,0:T(8,128)(2,1)S(1)} %get-tuple-element.104), channel_id=1, source_target_pairs={{2,0},{3,1},{0,2},{1,3},{6,4},{7,5},{4,6},{5,7},{10,8},{11,9},{8,1... | collective-permute-start | bytes 307208 | tf_op jit(solution)/shard_map/ppermute | solution.py:24
  46.1 10.1 %collective-permute-start.14 = (s16[400,128]{1,0:T(8,128)(2,1)S(1)}, s16[400,128]{1,0:T(8,128)(2,1)S(1)}, u32[]{:S(2)}, u32[]{:S(2)}) collective-permute-start(s16[400,128]{1,0:T(8,128)(2,1)S(1)} %get-tuple-element.108), channel_id=1, source_target_pairs={{2,0},{3,1},{0,2},{1,3},{6,4},{7,5},{4,6},{5,7},{10,8},{11,9},{8,1... | collective-permute-start | bytes 307208 | tf_op jit(solution)/shard_map/ppermute | solution.py:24
  49.1 8.3 %collective-permute-start.15 = (s16[400,128]{1,0:T(8,128)(2,1)S(1)}, s16[400,128]{1,0:T(8,128)(2,1)S(1)}, u32[]{:S(2)}, u32[]{:S(2)}) collective-permute-start(s16[400,128]{1,0:T(8,128)(2,1)S(1)} %get-tuple-element.112), channel_id=1, source_target_pairs={{2,0},{3,1},{0,2},{1,3},{6,4},{7,5},{4,6},{5,7},{10,8},{11,9},{8,1... | collective-permute-start | bytes 307208 | tf_op jit(solution)/shard_map/ppermute | solution.py:24
  57.5 5.7 %collective-permute-start.18 = (f32[8,512]{1,0:T(8,128)S(1)}, f32[8,512]{1,0:T(8,128)S(1)}, u32[]{:S(2)}, u32[]{:S(2)}) collective-permute-start(f32[8,512]{1,0:T(8,128)S(1)} %get-tuple-element.114.refs_4_), channel_id=1, source_target_pairs={{3,0},{2,1},{1,2},{0,3},{7,4},{6,5},{5,6},{4,7},{11,8},{10,9},{9,1... | collective-permute-start | bytes 49160 | tf_op jit(solution)/shard_map/ppermute | solution.py:24
  59.3 4.6 %collective-permute-start.17 = (f32[8,512]{1,0:T(8,128)S(1)}, f32[8,512]{1,0:T(8,128)S(1)}, u32[]{:S(2)}, u32[]{:S(2)}) collective-permute-start(f32[8,512]{1,0:T(8,128)S(1)} %get-tuple-element.114.refs_4_), channel_id=1, source_target_pairs={{2,0},{3,1},{0,2},{1,3},{6,4},{7,5},{4,6},{5,7},{10,8},{11,9},{8,1... | collective-permute-start | bytes 49160 | tf_op jit(solution)/shard_map/ppermute | solution.py:24
  59.3 4.6 %collective-permute-start.16 = (f32[8,512]{1,0:T(8,128)S(1)}, f32[8,512]{1,0:T(8,128)S(1)}, u32[]{:S(2)}, u32[]{:S(2)}) collective-permute-start(f32[8,512]{1,0:T(8,128)S(1)} %get-tuple-element.114.refs_4_), channel_id=1, source_target_pairs={{1,0},{0,1},{3,2},{2,3},{5,4},{4,5},{7,6},{6,7},{9,8},{8,9},{11,10... | collective-permute-start | bytes 49160 | tf_op jit(solution)/shard_map/ppermute | solution.py:24

commit v11 on v9

--- a/solution.py
+++ b/solution.py
@@ -13,7 +13,6 @@
 STEPS = 256.0
 TOP = 65534.0
 LN2 = 0.6931471805599453
-DIRECT = 0
 PRODUCT_LIMIT = 24000000
 SMALL_LIMIT = 8 * 1024 * 1024
 IN_VMEM = pl.BlockSpec(memory_space=pltpu.VMEM)
@@ -173,7 +172,7 @@
     coded.finish()
 
 
-def first_products(flow_t, graph, a_lines, b_lines, c_lines, widths):
+def first_products(flow_t, graph, a_lines, b_lines, c_lines):
     inner, width = flow_t.shape[1:]
     panel = width // 3
     return call(
@@ -181,8 +180,8 @@
         "first_products",
         [pltpu.with_memory_space_constraint(x, pltpu.HBM) for x in (a_lines, b_lines, c_lines, flow_t, graph)],
         [IN_HBM] * 5,
-        [jax.ShapeDtypeStruct((HEAD + 2 * panel, w), jnp.int16) for w in widths]
-        + [
+        [
+            jax.ShapeDtypeStruct((HEAD + 2 * panel, BS), jnp.int16),
             pltpu.VMEM((2 * panel, inner), flow_t.dtype),
             pltpu.VMEM((inner // BS, width), jnp.float32),
             pltpu.VMEM((inner // BS, width), jnp.float32),
@@ -270,28 +269,23 @@
     send_ref[0:HEAD, :] = jnp.broadcast_to(power, (HEAD, power.shape[1])).astype(jnp.int32).astype(jnp.int16)
 
 
-def split_strips(total, rows, position, keep_ref, send_refs):
-    layer = lax.axis_index("layer")
-    if len(send_refs) > 1:
-        keep_ref[0] = total[pl.ds(layer * rows, rows), :]
-        for other, send_ref in enumerate(send_refs, 1):
-            strip = total[pl.ds((layer ^ other) * rows, rows), :]
-            send_strip(send_ref, [strip], powers(strip))
-        return
-    bit = lax.rem(layer // position, 2)
+def split_strips(total, rows, position, keep_ref, send_ref):
+    bit = lax.rem(lax.axis_index("layer") // position, 2)
     pairs = keep_ref.shape[0]
     for j in range(pairs):
         keep_ref[j] = total[pl.ds((2 * j + bit) * rows, rows), :]
     away = [total[pl.ds((2 * j + 1 - bit) * rows, rows), :] for j in range(pairs)]
-    send_strip(send_refs[0], away, functools.reduce(jnp.maximum, [powers(strip) for strip in away]))
-
-
-def join_kernel(rows, half, lane, c_ref, own_ref, ext_ref, int_ref, keep_ref, *rest):
-    *send_refs, total = rest
+    power = functools.reduce(jnp.maximum, [powers(strip) for strip in away])
+    for j, strip in enumerate(away):
+        send_ref[HEAD + j * rows : HEAD + (j + 1) * rows, :] = code(strip, power)
+    send_ref[0:HEAD, :] = jnp.broadcast_to(power, (HEAD, power.shape[1])).astype(jnp.int32).astype(jnp.int16)
+
+
+def join_kernel(rows, half, lanes, c_ref, own_ref, ext_ref, int_ref, keep_ref, send_ref, total):
     odd = lax.rem(lax.axis_index("blk"), 2)
     panel = own_ref.shape[0] // BS // 3
-    lanes = slice(lane, lane + ext_ref.shape[1])
-    refs = (ext_ref, int_ref)
+    refs = (ext_ref.at[:, lanes], int_ref.at[:, lanes])
+    c_lanes = slice(half * BS + lanes.start, half * BS + lanes.stop)
     from_mid, from_side = ([[(r, start + i) for i in range(panel)] for r in range(2)] for start in (0, panel))
     middle = [list(both) for both in zip(from_side[0], from_side[1])]
     ext_only, int_only = ([[part] for part in from_mid[r]] for r in range(2))
@@ -301,7 +295,7 @@
     def add(parts):
         scale = [scales(ref[0:HEAD, :]) for ref in refs]
         for v in range(3 * panel):
-            kept = c_ref[v : v + 1, half * BS + lane : half * BS + lane + ext_ref.shape[1]]
+            kept = c_ref[v : v + 1, c_lanes]
             block = own_ref[v * BS : (v + 1) * BS, lanes] * kept
             for r, i in parts[v]:
                 codes = refs[r][HEAD + i * BS : HEAD + (i + 1) * BS, :]
@@ -316,26 +310,25 @@
     def _():
         add(even_parts)
 
-    split_strips(total, rows, 1, keep_ref, send_refs)
-
-
-def strips_shapes(pairs, rows, width, messages=1):
+    split_strips(total, rows, 1, keep_ref, send_ref)
+
+
+def strips_shapes(pairs, rows, width):
     return [
         jax.ShapeDtypeStruct((pairs, rows, width), jnp.float32),
-        *[jax.ShapeDtypeStruct((HEAD + pairs * rows, width), jnp.int16)] * messages,
+        jax.ShapeDtypeStruct((HEAD + pairs * rows, width), jnp.int16),
     ]
 
 
-def join(own, ext_part, int_part, c_rows, half, lane, layers, direct):
+def join(own, ext_part, lane, int_part, c_rows, half, width, layers):
     height = own.shape[0]
-    width = int_part.shape[1]
     rows = height // layers
     return call(
-        functools.partial(join_kernel, rows, half, lane),
+        functools.partial(join_kernel, rows, half, slice(lane, lane + width)),
         f"join_{half}_{lane}",
         (c_rows, own, ext_part, int_part),
         [IN_VMEM] * 4,
-        strips_shapes(1, rows, width, layers - 1) if direct else strips_shapes(layers // 2, rows, width),
+        strips_shapes(layers // 2, rows, width),
         [pltpu.VMEM((height, width), jnp.float32)],
     )
 
@@ -345,7 +338,7 @@
     for j in range(kept_ref.shape[0]):
         codes = got_ref[HEAD + j * rows : HEAD + (j + 1) * rows, :]
         total[j * rows : (j + 1) * rows, :] = kept_ref[j] + decode(codes, scale)
-    split_strips(total, rows, position, keep_ref, [send_ref])
+    split_strips(total, rows, position, keep_ref, send_ref)
 
 
 def halve(kept, got, position, chunk):
@@ -360,11 +353,9 @@
     )
 
 
-def square_kernel(messages, kept_ref, *rest):
-    got_refs, earlier, (square_ref, sums_ref) = rest[:messages], rest[messages:-2], rest[-2:]
-    value = kept_ref[0]
-    for ref in got_refs:
-        value += decode(ref[HEAD:, :], scales(ref[0:HEAD, :])[0:1])
+def square_kernel(kept_ref, got_ref, *rest):
+    earlier, (square_ref, sums_ref) = rest[:-2], rest[-2:]
+    value = kept_ref[0] + decode(got_ref[HEAD:, :], scales(got_ref[0:HEAD, :])[0:1])
     square = value * value
     square_ref[...] = square
     sums = jnp.broadcast_to(jnp.sum(square, axis=0, keepdims=True), (8, square.shape[1]))
@@ -374,10 +365,10 @@
 def square(kept, got, earlier, chunk):
     _, rows, width = kept.shape
     return call(
-        functools.partial(square_kernel, len(got)),
+        square_kernel,
         f"square_{chunk}",
-        (kept, *got, *earlier),
-        [IN_VMEM] * (1 + len(got) + len(earlier)),
+        (kept, got, *earlier),
+        [IN_VMEM] * (2 + len(earlier)),
         [
             jax.ShapeDtypeStruct((rows, width), jnp.float32),
             jax.ShapeDtypeStruct((8, width + sum(sums.shape[1] for sums in earlier)), jnp.float32),
@@ -424,58 +415,57 @@
         return i ^ 1
 
     halves = panel // BS
-    chunks = panel // LANES
     fine = (LANES,) * (BS // LANES)
-    per_half = len(fine)
+    widths = [(BS,)] * (halves - 1) + [fine]
     ext, ints, owns, latest = [], [], [], []
 
     def ordered(value):
         return after(value, latest[-1])
 
-    def send_ext(parts):
-        ext.extend(swap(part, "blk", other_chip) for part in parts)
-        latest.append(parts[0])
-
-    def send_int(parts):
-        ints.extend(swap(part, "blk", same_chip) for part in parts)
-        latest.append(parts[0])
-
-    *parts, ext_rows, a_rows, b_rows, c_rows = first_products(flow_t, graph, a_lines, b_lines, c_lines, fine)
-    send_ext(parts)
-    wanted = {"own": (BS,), "int": fine}
-    own, *parts, int_rows = products(a_rows, ordered(b_rows), graph, ext_rows, flow_t, 0, wanted, turns=True)
+    def send(part, partner, got):
+        whole = swap(part, "blk", partner)
+        half_widths = widths[len(got)]
+        got.append([(whole, sum(half_widths[:i])) for i in range(len(half_widths))])
+
+    part, ext_rows, a_rows, b_rows, c_rows = first_products(flow_t, graph, a_lines, b_lines, c_lines)
+    send(part, other_chip, ext)
+    latest.append(part)
+    wanted = {"own": (BS,), "int": (BS,)}
+    own, part, int_rows = products(a_rows, ordered(b_rows), graph, ext_rows, flow_t, 0, wanted, turns=True)
     owns.append(own)
-    send_int(parts)
-
-    def more_products(half):
-        wanted = {"ext": fine, "int": fine}
-        parts = products(a_rows, ordered(b_rows), graph, ext_rows, int_rows, half, wanted)
-        send_ext(parts[:per_half])
-        send_int(parts[per_half:])
-
-    def more_own(half):
+    send(part, same_chip, ints)
+    latest.append(own)
+
+    def side_products(half):
+        wanted = {"ext": (BS,), "int": (BS,)}
+        ext_part, int_part = products(a_rows, ordered(b_rows), graph, ext_rows, int_rows, half, wanted)
+        send(ext_part, other_chip, ext)
+        send(int_part, same_chip, ints)
+        latest.append(ext_part)
+
+    def own_products(half):
         owns.extend(products(a_rows, ordered(b_rows), graph, ext_rows, int_rows, half, {"own": (BS,)}))
         latest.append(owns[-1])
 
     strips, squares, sums = [], [], []
+    places = [(half, i) for half, each in enumerate(widths) for i in range(len(each))]
+    chunks = len(places)
 
     def add_up(chunk):
-        half, lane = divmod(chunk, per_half)
-        direct = chunk >= chunks - DIRECT and layers <= 4
-        kept, *sends = join(
-            owns[half], ext[chunk], ints[chunk], ordered(c_rows), half, lane * LANES, layers, direct
-        )
+        half, i = places[chunk]
+        width = widths[half][i]
+        kept, send = join(owns[half], *ext[half][i], ints[half][i][0], ordered(c_rows), half, width, layers)
         latest.append(kept)
-        strips.append((kept, [swap(send, "layer", lambda i: i ^ other) for other, send in enumerate(sends, 1)]))
+        strips.append((kept, swap(send, "layer", lambda i: i ^ 1)))
 
     def scatter(chunk):
         kept, got = strips[chunk]
         position = 1
         while kept.shape[0] > 1:
             position *= 2
-            kept, send = halve(ordered(kept), got[0], position, chunk)
+            kept, send = halve(ordered(kept), got, position, chunk)
             latest.append(kept)
-            got = [swap(send, "layer", lambda i: i ^ position)]
+            got = swap(send, "layer", lambda i: i ^ position)
         strips[chunk] = kept, got
 
     def finish(chunk):
@@ -485,17 +475,17 @@
         squares.append(squared)
         sums.append(summed)
 
-    for chunk in range(chunks + 1):
-        if chunk < chunks:
-            add_up(chunk)
-        if (chunk + 1) % per_half == 0 and len(owns) < halves:
-            more_own(len(owns))
-        if chunk >= 1:
-            scatter(chunk - 1)
-        if chunk == 2:
-            finish(0)
-        if chunk % per_half == 0 and chunk // per_half + 1 < halves:
-            more_products(chunk // per_half + 1)
+    for half in range(1, halves):
+        side_products(half)
+        add_up(half - 1)
+        own_products(half)
+    scatter(0)
+    for chunk in range(halves - 1, chunks):
+        add_up(chunk)
+    scatter(1)
+    finish(0)
+    for chunk in range(2, chunks):
+        scatter(chunk)
     for chunk in range(1, chunks):
         finish(chunk)
 

time: 63.3 us -> 66.1 us (1.044)
  the two profiles are of different devices: /device:TPU:0 before, /device:TPU:14 now
where the time goes in v11:
time: 66.1 us; the launch traced here: 66 us
  waiting for transfers between devices  31.1 us (47%)
  starting transfers between devices  17.3 us (26%)
  Pallas kernels  15.9 us (24%)
  local copies, waits for them, and re-layouts  1.59 us (2%)
    ppermute x13, waiting for transfers between devices, swap(): lax.ppermute(block, axis, [(partner(i), i) for i in range(lax.axis_size(a...  31.1 us
    ppermute x13, starting transfers between devices, swap(): lax.ppermute(block, axis, [(partner(i), i) for i in range(lax.axis_size(a...  17.3 us
    pallas_call x14, Pallas kernels, call(): pl.pallas_call(kernel, out_shape=out_shape, in_specs=in_specs, out_specs=...  15.9 us
    unnamed x6, local copies, waits for them, and re-layouts  1.59 us
  transfers between devices with their start and end apart: 13, of which 8 were waited for; matrix products, arithmetic and copies ran while one was open for 0% of the time, Pallas kernels for 16%

profile of v11, /device:TPU:14, one launch (start us, length us, event | category | flops | bytes accessed | tf_op | source)
XLA Modules:
  0.0 66.0 jit_solution(604214824177786048)
XLA Ops:
  0.0 4.6 %first_products.1 = (s16[1040,256]{1,0:T(8,128)(2,1)S(1)}, bf16[1024,2048]{1,0:T(8,128)(2,1)S(1)}, f32[8,1536]{1,0:T(8,128)S(1)}, f32[8,1536]{1,0:T(8,128)S(1)}, f32[6,512]{1,0:T(8,128)S(1)}) custom-call(s32[6,1,32]{2,1,0:T(1,128)} %bitcast.5, s32[6,1,32]{2,1,0:T(1,128)} %bitcast.6, s32[1,2,6]{2,1,0:T(2,128)} %bitcast.7, bf16[1,2048,1536]{2,1,0:T(8,128)(2,1)} %side_ref.1, ...), custom_call_target="tpu_custom_call" | custom-call | flops 1 | bytes 1 | tf_op jit(solution)/shard_map/first_products/pallas_call | solution.py:31
  4.7 1.6 %copy-done = bf16[1,2048,1536]{2,1,0:T(8,128)(2,1)S(1)} copy-done((bf16[1,2048,1536]{2,1,0:T(8,128)(2,1)S(1)}, bf16[1,2048,1536]{2,1,0:T(8,128)(2,1)}, u32[]{:S(2)}) %copy-start) | copy-done | bytes 6291480
  6.3 3.1 %own_int_products_0.1 = (f32[1536,256]{1,0:T(8,128)S(1)}, s16[1040,256]{1,0:T(8,128)(2,1)S(1)}, bf16[512,2048]{1,0:T(8,128)(2,1)S(1)}) custom-call(f32[8,1536]{1,0:T(8,128)S(1)} %get-tuple-element.46.a_rows_ref, f32[8,1536]{1,0:T(8,128)S(1)} %get-tuple-element.58.b_rows_ref, bf16[1,2048,1536]{2,1,0:T(8,128)(2,1)S(1)} %bitcast.4, ...), custom_call_target="tpu_custom_call" | custom-call | flops 1 | bytes 1 | tf_op jit(solution)/shard_map/own_int_products_0/pallas_call | solution.py:31
  9.4 3.0 %ext_int_products_1.1 = (s16[1040,256]{1,0:T(8,128)(2,1)S(1)}, s16[1040,256]{1,0:T(8,128)(2,1)S(1)}) custom-call(f32[8,1536]{1,0:T(8,128)S(1)} %get-tuple-element.46.a_rows_ref, f32[8,1536]{1,0:T(8,128)S(1)} %get-tuple-element.58.b_rows_ref, bf16[1,2048,1536]{2,1,0:T(8,128)(2,1)S(1)} %bitcast.4, bf16[1024,2048]{1,0:T(8,128)(2,1)S(1)} %get-tuple-element.50.ext_rows_ref, ...), custom_call_target="tpu_custom_call" | custom-call | flops 1 | bytes 1 | tf_op jit(solution)/shard_map/ext_int_products_1/pallas_call | solution.py:31
  12.4 0.5 collective-permute-start.4
  12.9 0.2 collective-permute-start.3
  13.2 5.9 %collective-permute-done.ext_ref = s16[1040,256]{1,0:T(8,128)(2,1)S(1)} collective-permute-done((s16[1040,256]{1,0:T(8,128)(2,1)S(1)}, s16[1040,256]{1,0:T(8,128)(2,1)S(1)}, u32[]{:S(2)}, u32[]{:S(2)}) %collective-permute-start) | collective-permute-done | bytes 532512 | tf_op jit(solution)/shard_map/ppermute | solution.py:23
  19.0 0.7 %join_0_0.1 = (f32[2,384,256]{2,1,0:T(8,128)S(1)}, s16[784,256]{1,0:T(8,128)(2,1)S(1)}) custom-call(f32[6,512]{1,0:T(8,128)S(1)} %get-tuple-element.65.c_ref, f32[1536,256]{1,0:T(8,128)S(1)} %get-tuple-element.51.own_ref, s16[1040,256]{1,0:T(8,128)(2,1)S(1)} %collective-permute-done.ext_ref, s16[1040,256]{1,0:T(8,128)(2,1)S(1)} %collective-permute-done.1.int_ref), custom_call_target="tpu_custom_call" | custom-call | flops 1 | bytes 1 | tf_op jit(solution)/shard_map/join_0_0/pallas_call | solution.py:31
  19.7 0.5 collective-permute-start.2
  20.2 1.8 %own_products_1.1.own_ref = f32[1536,256]{1,0:T(8,128)S(1)} custom-call(f32[8,1536]{1,0:T(8,128)S(1)} %get-tuple-element.46.a_rows_ref, f32[8,1536]{1,0:T(8,128)S(1)} %get-tuple-element.58.b_rows_ref, bf16[1,2048,1536]{2,1,0:T(8,128)(2,1)S(1)} %bitcast.4, bf16[1024,2048]{1,0:T(8,128)(2,1)S(1)} %get-tuple-element.50.ext_rows_ref, ...), custom_call_target="tpu_custom_call" | custom-call | flops 1 | bytes 1 | tf_op jit(solution)/shard_map/own_products_1/pallas_call | solution.py:31
  22.1 9.7 %collective-permute-done.2.got_ref = s16[784,256]{1,0:T(8,128)(2,1)S(1)} collective-permute-done((s16[784,256]{1,0:T(8,128)(2,1)S(1)}, s16[784,256]{1,0:T(8,128)(2,1)S(1)}, u32[]{:S(2)}, u32[]{:S(2)}) %collective-permute-start.2) | collective-permute-done | bytes 401440 | tf_op jit(solution)/shard_map/ppermute | solution.py:23
  31.7 0.4 halve_2_0.1
  32.1 2.7 %collective-permute-start.6 = (s16[400,256]{1,0:T(8,128)(2,1)S(1)}, s16[400,256]{1,0:T(8,128)(2,1)S(1)}, u32[]{:S(2)}, u32[]{:S(2)}) collective-permute-start(s16[400,256]{1,0:T(8,128)(2,1)S(1)} %get-tuple-element.71), channel_id=1, source_target_pairs={{2,0},{3,1},{0,2},{1,3},{6,4},{7,5},{4,6},{5,7},{10,8},{11,9},{8,1... | collective-permute-start | bytes 614408 | tf_op jit(solution)/shard_map/ppermute | solution.py:23
  34.8 0.4 join_1_0.1
  35.2 0.5 collective-permute-start.5
  35.7 0.4 join_1_128.1
  36.1 1.6 %collective-permute-start.7 = (s16[784,128]{1,0:T(8,128)(2,1)S(1)}, s16[784,128]{1,0:T(8,128)(2,1)S(1)}, u32[]{:S(2)}, u32[]{:S(2)}) collective-permute-start(s16[784,128]{1,0:T(8,128)(2,1)S(1)} %get-tuple-element.75), channel_id=1, source_target_pairs={{1,0},{0,1},{3,2},{2,3},{5,4},{4,5},{7,6},{6,7},{9,8},{8,9},{11,10... | collective-permute-start | bytes 602120 | tf_op jit(solution)/shard_map/ppermute | solution.py:23
  37.8 7.8 %collective-permute-done.5.got_ref = s16[784,128]{1,0:T(8,128)(2,1)S(1)} collective-permute-done((s16[784,128]{1,0:T(8,128)(2,1)S(1)}, s16[784,128]{1,0:T(8,128)(2,1)S(1)}, u32[]{:S(2)}, u32[]{:S(2)}) %collective-permute-start.5) | collective-permute-done | bytes 200736 | tf_op jit(solution)/shard_map/ppermute | solution.py:23
  45.5 0.2 halve_2_1.1
  45.7 3.5 %collective-permute-start.8 = (s16[400,128]{1,0:T(8,128)(2,1)S(1)}, s16[400,128]{1,0:T(8,128)(2,1)S(1)}, u32[]{:S(2)}, u32[]{:S(2)}) collective-permute-start(s16[400,128]{1,0:T(8,128)(2,1)S(1)} %get-tuple-element.78), channel_id=1, source_target_pairs={{2,0},{3,1},{0,2},{1,3},{6,4},{7,5},{4,6},{5,7},{10,8},{11,9},{8,1... | collective-permute-start | bytes 307208 | tf_op jit(solution)/shard_map/ppermute | solution.py:23
  49.2 0.1 square_0.1
  49.3 0.5 collective-permute-done.7.got_ref
  49.8 0.2 halve_2_2.1
  50.0 2.1 %collective-permute-start.9 = (s16[400,128]{1,0:T(8,128)(2,1)S(1)}, s16[400,128]{1,0:T(8,128)(2,1)S(1)}, u32[]{:S(2)}, u32[]{:S(2)}) collective-permute-start(s16[400,128]{1,0:T(8,128)(2,1)S(1)} %get-tuple-element.82), channel_id=1, source_target_pairs={{2,0},{3,1},{0,2},{1,3},{6,4},{7,5},{4,6},{5,7},{10,8},{11,9},{8,1... | collective-permute-start | bytes 307208 | tf_op jit(solution)/shard_map/ppermute | solution.py:23
  52.1 2.1 %collective-permute-done.8.got_ref = s16[400,128]{1,0:T(8,128)(2,1)S(1)} collective-permute-done((s16[400,128]{1,0:T(8,128)(2,1)S(1)}, s16[400,128]{1,0:T(8,128)(2,1)S(1)}, u32[]{:S(2)}, u32[]{:S(2)}) %collective-permute-start.8) | collective-permute-done | bytes 102432 | tf_op jit(solution)/shard_map/ppermute | solution.py:23
  54.3 1.5 %collective-permute-done.9.got_ref = s16[400,128]{1,0:T(8,128)(2,1)S(1)} collective-permute-done((s16[400,128]{1,0:T(8,128)(2,1)S(1)}, s16[400,128]{1,0:T(8,128)(2,1)S(1)}, u32[]{:S(2)}, u32[]{:S(2)}) %collective-permute-start.9) | collective-permute-done | bytes 102432 | tf_op jit(solution)/shard_map/ppermute | solution.py:23
  55.7 0.1 square_2.1
  55.8 1.2 %collective-permute-start.12 = (f32[8,512]{1,0:T(8,128)S(1)}, f32[8,512]{1,0:T(8,128)S(1)}, u32[]{:S(2)}, u32[]{:S(2)}) collective-permute-start(f32[8,512]{1,0:T(8,128)S(1)} %get-tuple-element.84.refs_3_), channel_id=1, source_target_pairs={{3,0},{2,1},{1,2},{0,3},{7,4},{6,5},{5,6},{4,7},{11,8},{10,9},{9,1... | collective-permute-start | bytes 49160 | tf_op jit(solution)/shard_map/ppermute | solution.py:23
  57.0 4.3 %collective-permute-start.11 = (f32[8,512]{1,0:T(8,128)S(1)}, f32[8,512]{1,0:T(8,128)S(1)}, u32[]{:S(2)}, u32[]{:S(2)}) collective-permute-start(f32[8,512]{1,0:T(8,128)S(1)} %get-tuple-element.84.refs_3_), channel_id=1, source_target_pairs={{2,0},{3,1},{0,2},{1,3},{6,4},{7,5},{4,6},{5,7},{10,8},{11,9},{8,1... | collective-permute-start | bytes 49160 | tf_op jit(solution)/shard_map/ppermute | solution.py:23
  61.2 1.9 %collective-permute-done.11.refs_5_ = f32[8,512]{1,0:T(8,128)S(1)} collective-permute-done((f32[8,512]{1,0:T(8,128)S(1)}, f32[8,512]{1,0:T(8,128)S(1)}, u32[]{:S(2)}, u32[]{:S(2)}) %collective-permute-start.11) | collective-permute-done | bytes 16416 | tf_op jit(solution)/shard_map/ppermute | solution.py:23
  63.1 1.9 %collective-permute-done.10.refs_4_ = f32[8,512]{1,0:T(8,128)S(1)} collective-permute-done((f32[8,512]{1,0:T(8,128)S(1)}, f32[8,512]{1,0:T(8,128)S(1)}, u32[]{:S(2)}, u32[]{:S(2)}) %collective-permute-start.10) | collective-permute-done | bytes 16416 | tf_op jit(solution)/shard_map/ppermute | solution.py:23
  65.0 1.0 %rescale.1 = f32[1,384,512]{2,1,0:T(8,128)} custom-call(f32[384,256]{1,0:T(8,128)S(1)} %get-tuple-element.72.refs_0_, f32[384,128]{1,0:T(8,128)S(1)} %get-tuple-element.79.refs_1_, f32[384,128]{1,0:T(8,128)S(1)} %get-tuple-element.83.refs_2_, f32[8,512]{1,0:T(8,128)S(1)} %get-tuple-element.84.refs_3_, f32[8,512]{1,0:T(8,128)S(1)} %collective-permute-done.10.refs_4_, ...), custom_call_target="tpu_custom_call" | custom-call | flops 1 | bytes 1 | tf_op jit(solution)/shard_map/rescale/pallas_call | solution.py:31
  (15 shorter events, 0.2 us)
Async XLA Ops:
  0.0 4.7 %slice-start = ((s8[6291456]{0:T(1024)(128)(4,1)}), s8[4194304]{0:T(1024)(128)(4,1)S(1)}, s32[]{:S(2)}) async-start(s8[6291456]{0:T(1024)(128)(4,1)} %bitcast.3), calls=%async_computation | async-start | bytes 8388608
  0.0 4.7 %slice-start.1 = ((s8[6291456]{0:T(1024)(128)(4,1)}), s8[2097152]{0:T(1024)(128)(4,1)S(1)}, s32[]{:S(2)}) async-start(s8[6291456]{0:T(1024)(128)(4,1)} %bitcast.3), calls=%async_computation.1 | async-start | bytes 4194304
  0.0 6.2 %copy-start = (bf16[1,2048,1536]{2,1,0:T(8,128)(2,1)S(1)}, bf16[1,2048,1536]{2,1,0:T(8,128)(2,1)}, u32[]{:S(2)}) copy-start(bf16[1,2048,1536]{2,1,0:T(8,128)(2,1)} %side_ref.1) | copy-start | bytes 18874372
  4.6 14.5 %collective-permute-start = (s16[1040,256]{1,0:T(8,128)(2,1)S(1)}, s16[1040,256]{1,0:T(8,128)(2,1)S(1)}, u32[]{:S(2)}, u32[]{:S(2)}) collective-permute-start(s16[1040,256]{1,0:T(8,128)(2,1)S(1)} %get-tuple-element.48), channel_id=1, source_target_pairs={{28,0},{8,4},{4,8},{16,12},{12,16},{24,20},{20,24},{0,28},{29,1},{... | collective-permute-start | bytes 1597448 | tf_op jit(solution)/shard_map/ppermute | solution.py:23
  9.3 9.7 %collective-permute-start.1 = (s16[1040,256]{1,0:T(8,128)(2,1)S(1)}, s16[1040,256]{1,0:T(8,128)(2,1)S(1)}, u32[]{:S(2)}, u32[]{:S(2)}) collective-permute-start(s16[1040,256]{1,0:T(8,128)(2,1)S(1)} %get-tuple-element.56), channel_id=1, source_target_pairs={{4,0},{0,4},{12,8},{8,12},{20,16},{16,20},{28,24},{24,28},{5,1},{1... | collective-permute-start | bytes 1597448 | tf_op jit(solution)/shard_map/ppermute | solution.py:23
  12.4 22.4 %collective-permute-start.4 = (s16[1040,256]{1,0:T(8,128)(2,1)S(1)}, s16[1040,256]{1,0:T(8,128)(2,1)S(1)}, u32[]{:S(2)}, u32[]{:S(2)}) collective-permute-start(s16[1040,256]{1,0:T(8,128)(2,1)S(1)} %get-tuple-element.63), channel_id=1, source_target_pairs={{4,0},{0,4},{12,8},{8,12},{20,16},{16,20},{28,24},{24,28},{5,1},{1... | collective-permute-start | bytes 1597448 | tf_op jit(solution)/shard_map/ppermute | solution.py:23
  12.9 21.9 %collective-permute-start.3 = (s16[1040,256]{1,0:T(8,128)(2,1)S(1)}, s16[1040,256]{1,0:T(8,128)(2,1)S(1)}, u32[]{:S(2)}, u32[]{:S(2)}) collective-permute-start(s16[1040,256]{1,0:T(8,128)(2,1)S(1)} %get-tuple-element.54), channel_id=1, source_target_pairs={{28,0},{8,4},{4,8},{16,12},{12,16},{24,20},{20,24},{0,28},{29,1},{... | collective-permute-start | bytes 1597448 | tf_op jit(solution)/shard_map/ppermute | solution.py:23
  19.7 12.0 %collective-permute-start.2 = (s16[784,256]{1,0:T(8,128)(2,1)S(1)}, s16[784,256]{1,0:T(8,128)(2,1)S(1)}, u32[]{:S(2)}, u32[]{:S(2)}) collective-permute-start(s16[784,256]{1,0:T(8,128)(2,1)S(1)} %get-tuple-element.60), channel_id=1, source_target_pairs={{1,0},{0,1},{3,2},{2,3},{5,4},{4,5},{7,6},{6,7},{9,8},{8,9},{11,10... | collective-permute-start | bytes 1204232 | tf_op jit(solution)/shard_map/ppermute | solution.py:23
  32.1 17.0 %collective-permute-start.6 = (s16[400,256]{1,0:T(8,128)(2,1)S(1)}, s16[400,256]{1,0:T(8,128)(2,1)S(1)}, u32[]{:S(2)}, u32[]{:S(2)}) collective-permute-start(s16[400,256]{1,0:T(8,128)(2,1)S(1)} %get-tuple-element.71), channel_id=1, source_target_pairs={{2,0},{3,1},{0,2},{1,3},{6,4},{7,5},{4,6},{5,7},{10,8},{11,9},{8,1... | collective-permute-start | bytes 614408 | tf_op jit(solution)/shard_map/ppermute | solution.py:23
  35.2 10.3 %collective-permute-start.5 = (s16[784,128]{1,0:T(8,128)(2,1)S(1)}, s16[784,128]{1,0:T(8,128)(2,1)S(1)}, u32[]{:S(2)}, u32[]{:S(2)}) collective-permute-start(s16[784,128]{1,0:T(8,128)(2,1)S(1)} %get-tuple-element.68), channel_id=1, source_target_pairs={{1,0},{0,1},{3,2},{2,3},{5,4},{4,5},{7,6},{6,7},{9,8},{8,9},{11,10... | collective-permute-start | bytes 602120 | tf_op jit(solution)/shard_map/ppermute | solution.py:23
  36.1 13.7 %collective-permute-start.7 = (s16[784,128]{1,0:T(8,128)(2,1)S(1)}, s16[784,128]{1,0:T(8,128)(2,1)S(1)}, u32[]{:S(2)}, u32[]{:S(2)}) collective-permute-start(s16[784,128]{1,0:T(8,128)(2,1)S(1)} %get-tuple-element.75), channel_id=1, source_target_pairs={{1,0},{0,1},{3,2},{2,3},{5,4},{4,5},{7,6},{6,7},{9,8},{8,9},{11,10... | collective-permute-start | bytes 602120 | tf_op jit(solution)/shard_map/ppermute | solution.py:23
  45.7 8.5 %collective-permute-start.8 = (s16[400,128]{1,0:T(8,128)(2,1)S(1)}, s16[400,128]{1,0:T(8,128)(2,1)S(1)}, u32[]{:S(2)}, u32[]{:S(2)}) collective-permute-start(s16[400,128]{1,0:T(8,128)(2,1)S(1)} %get-tuple-element.78), channel_id=1, source_target_pairs={{2,0},{3,1},{0,2},{1,3},{6,4},{7,5},{4,6},{5,7},{10,8},{11,9},{8,1... | collective-permute-start | bytes 307208 | tf_op jit(solution)/shard_map/ppermute | solution.py:23
  50.0 5.7 %collective-permute-start.9 = (s16[400,128]{1,0:T(8,128)(2,1)S(1)}, s16[400,128]{1,0:T(8,128)(2,1)S(1)}, u32[]{:S(2)}, u32[]{:S(2)}) collective-permute-start(s16[400,128]{1,0:T(8,128)(2,1)S(1)} %get-tuple-element.82), channel_id=1, source_target_pairs={{2,0},{3,1},{0,2},{1,3},{6,4},{7,5},{4,6},{5,7},{10,8},{11,9},{8,1... | collective-permute-start | bytes 307208 | tf_op jit(solution)/shard_map/ppermute | solution.py:23
  55.8 5.5 %collective-permute-start.12 = (f32[8,512]{1,0:T(8,128)S(1)}, f32[8,512]{1,0:T(8,128)S(1)}, u32[]{:S(2)}, u32[]{:S(2)}) collective-permute-start(f32[8,512]{1,0:T(8,128)S(1)} %get-tuple-element.84.refs_3_), channel_id=1, source_target_pairs={{3,0},{2,1},{1,2},{0,3},{7,4},{6,5},{5,6},{4,7},{11,8},{10,9},{9,1... | collective-permute-start | bytes 49160 | tf_op jit(solution)/shard_map/ppermute | solution.py:23
  57.0 6.2 %collective-permute-start.11 = (f32[8,512]{1,0:T(8,128)S(1)}, f32[8,512]{1,0:T(8,128)S(1)}, u32[]{:S(2)}, u32[]{:S(2)}) collective-permute-start(f32[8,512]{1,0:T(8,128)S(1)} %get-tuple-element.84.refs_3_), channel_id=1, source_target_pairs={{2,0},{3,1},{0,2},{1,3},{6,4},{7,5},{4,6},{5,7},{10,8},{11,9},{8,1... | collective-permute-start | bytes 49160 | tf_op jit(solution)/shard_map/ppermute | solution.py:23
  61.2 3.7 %collective-permute-start.10 = (f32[8,512]{1,0:T(8,128)S(1)}, f32[8,512]{1,0:T(8,128)S(1)}, u32[]{:S(2)}, u32[]{:S(2)}) collective-permute-start(f32[8,512]{1,0:T(8,128)S(1)} %get-tuple-element.84.refs_3_), channel_id=1, source_target_pairs={{1,0},{0,1},{3,2},{2,3},{5,4},{4,5},{7,6},{6,7},{9,8},{8,9},{11,10... | collective-permute-start | bytes 49160 | tf_op jit(solution)/shard_map/ppermute | solution.py:23

commit v12 on v9

--- a/solution.py
+++ b/solution.py
@@ -13,7 +13,7 @@
 STEPS = 256.0
 TOP = 65534.0
 LN2 = 0.6931471805599453
-DIRECT = 0
+DIRECT = 1
 PRODUCT_LIMIT = 24000000
 SMALL_LIMIT = 8 * 1024 * 1024
 IN_VMEM = pl.BlockSpec(memory_space=pltpu.VMEM)
@@ -360,27 +360,28 @@
     )
 
 
-def square_kernel(messages, kept_ref, *rest):
-    got_refs, earlier, (square_ref, sums_ref) = rest[:messages], rest[messages:-2], rest[-2:]
+def square_kernel(messages, place, kept_ref, *rest):
+    got_refs, others, (square_ref, sums_ref) = rest[:messages], rest[messages:-2], rest[-2:]
     value = kept_ref[0]
     for ref in got_refs:
         value += decode(ref[HEAD:, :], scales(ref[0:HEAD, :])[0:1])
     square = value * value
     square_ref[...] = square
     sums = jnp.broadcast_to(jnp.sum(square, axis=0, keepdims=True), (8, square.shape[1]))
-    sums_ref[...] = jnp.concatenate([ref[...] for ref in earlier] + [sums], axis=1)
-
-
-def square(kept, got, earlier, chunk):
+    every = [ref[...] for ref in others]
+    sums_ref[...] = jnp.concatenate(every[:place] + [sums] + every[place:], axis=1)
+
+
+def square(kept, got, others, place, chunk):
     _, rows, width = kept.shape
     return call(
-        functools.partial(square_kernel, len(got)),
+        functools.partial(square_kernel, len(got), place),
         f"square_{chunk}",
-        (kept, *got, *earlier),
-        [IN_VMEM] * (1 + len(got) + len(earlier)),
+        (kept, *got, *others),
+        [IN_VMEM] * (1 + len(got) + len(others)),
         [
             jax.ShapeDtypeStruct((rows, width), jnp.float32),
-            jax.ShapeDtypeStruct((8, width + sum(sums.shape[1] for sums in earlier)), jnp.float32),
+            jax.ShapeDtypeStruct((8, width + sum(sums.shape[1] for sums in others)), jnp.float32),
         ],
     )
 
@@ -457,7 +458,7 @@
         owns.extend(products(a_rows, ordered(b_rows), graph, ext_rows, int_rows, half, {"own": (BS,)}))
         latest.append(owns[-1])
 
-    strips, squares, sums = [], [], []
+    strips, squares, sums = [], {}, {}
 
     def add_up(chunk):
         half, lane = divmod(chunk, per_half)
@@ -480,26 +481,29 @@
 
     def finish(chunk):
         kept, got = strips[chunk]
-        squared, summed = square(ordered(kept), got, sums if chunk == chunks - 1 else [], chunk)
-        latest.append(summed)
-        squares.append(squared)
-        sums.append(summed)
-
-    for chunk in range(chunks + 1):
-        if chunk < chunks:
-            add_up(chunk)
+        others, place = ([], 0)
+        if len(squares) == chunks - 1:
+            others, place = [sums[i] for i in sorted(sums)], chunk
+        squares[chunk], sums[chunk] = square(ordered(kept), got, others, place, chunk)
+        latest.append(sums[chunk])
+
+    for chunk in range(chunks):
+        add_up(chunk)
         if (chunk + 1) % per_half == 0 and len(owns) < halves:
             more_own(len(owns))
-        if chunk >= 1:
+        if 1 <= chunk < chunks - 1:
             scatter(chunk - 1)
-        if chunk == 2:
-            finish(0)
         if chunk % per_half == 0 and chunk // per_half + 1 < halves:
             more_products(chunk // per_half + 1)
-    for chunk in range(1, chunks):
-        finish(chunk)
-
-    mine = sums[-1]
+    finish(0)
+    finish(1)
+    for chunk in range(chunks - 2, chunks):
+        scatter(chunk)
+    finish(chunks - 1)
+    finish(chunks - 2)
+
+    squares = [squares[i] for i in sorted(squares)]
+    mine = sums[chunks - 2]
     others = [swap(mine, "layer", lambda i: i ^ other) for other in range(1, layers)]
     return rescale(squares, [mine, *others], width)
 

time: 63.3 us -> 63.4 us (level)
  waiting for transfers between devices: 24.6 us -> 21.7 us
  starting transfers between devices: 22.3 us -> 25 us
    ppermute x19 -> x20, waiting for transfers between devices: 24.6 us -> 21.7 us  [swap(): lax.ppermute(block, axis, [(partner(i), i) for i in range(lax.axis_size(a...]
    ppermute x19 -> x20, starting transfers between devices: 22.3 us -> 25 us  [swap(): lax.ppermute(block, axis, [(partner(i), i) for i in range(lax.axis_size(a...]
    pallas_call x17 -> x16, Pallas kernels: 16 us -> 15.9 us  [call(): pl.pallas_call(kernel, out_shape=out_shape, in_specs=in_specs, out_specs=...]
  transfers between devices with their start and end apart: 19 -> 20, of which waited for: 9 -> 9; matrix products, arithmetic and copies ran while one was open for 0% -> 0% of each run, Pallas kernels for 16% -> 16%
where the time goes in v12:
time: 63.4 us; the launch traced here: 62.7 us
  starting transfers between devices  25 us (39%)
  waiting for transfers between devices  21.7 us (34%)
  Pallas kernels  15.9 us (25%)
    ppermute x20, starting transfers between devices, swap(): lax.ppermute(block, axis, [(partner(i), i) for i in range(lax.axis_size(a...  25 us
    ppermute x20, waiting for transfers between devices, swap(): lax.ppermute(block, axis, [(partner(i), i) for i in range(lax.axis_size(a...  21.7 us
    pallas_call x16, Pallas kernels, call(): pl.pallas_call(kernel, out_shape=out_shape, in_specs=in_specs, out_specs=...  15.9 us
  transfers between devices with their start and end apart: 20, of which 9 were waited for; matrix products, arithmetic and copies ran while one was open for 0% of the time, Pallas kernels for 16%

profile of v12, /device:TPU:0, one launch (start us, length us, event | category | flops | bytes accessed | tf_op | source)
XLA Modules:
  0.0 62.7 jit_solution(4837770446264539966)
XLA Ops:
  0.0 4.5 %first_products.1 = (s16[1040,128]{1,0:T(8,128)(2,1)S(1)}, s16[1040,128]{1,0:T(8,128)(2,1)S(1)}, bf16[1024,2048]{1,0:T(8,128)(2,1)S(1)}, f32[8,1536]{1,0:T(8,128...) custom-call(s32[6,1,32]{2,1,0:T(1,128)} %bitcast.5, s32[6,1,32]{2,1,0:T(1,128)} %bitcast.6, s32[1,2,6]{2,1,0:T(2,128)} %bitcast.7, ...), custom_call_target="tpu_custom_call" | custom-call | flops 1 | bytes 1 | tf_op jit(solution)/shard_map/first_products/pallas_call | solution.py:32
  4.6 3.4 %collective-permute-start = (s16[1040,128]{1,0:T(8,128)(2,1)S(1)}, s16[1040,128]{1,0:T(8,128)(2,1)S(1)}, u32[]{:S(2)}, u32[]{:S(2)}) collective-permute-start(s16[1040,128]{1,0:T(8,128)(2,1)S(1)} %get-tuple-element.60), channel_id=1, source_target_pairs={{28,0},{8,4},{4,8},{16,12},{12,16},{24,20},{20,24},{0,28},{29,1},{... | collective-permute-start | bytes 798728 | tf_op jit(solution)/shard_map/ppermute | solution.py:24
  8.0 3.1 %own_int_products_0.1 = (f32[1536,256]{1,0:T(8,128)S(1)}, s16[1040,128]{1,0:T(8,128)(2,1)S(1)}, s16[1040,128]{1,0:T(8,128)(2,1)S(1)}, bf16[512,2048]{1,0:T(8,128)(2,1)S(1)}) custom-call(f32[8,1536]{1,0:T(8,128)S(1)} %get-tuple-element.58.a_rows_ref, f32[8,1536]{1,0:T(8,128)S(1)} %get-tuple-element.74.b_rows_ref, bf16[1,2048,1536]{2,1,0:T(8,128)(2,1)S(1)} %bitcast.4, ...), custom_call_target="tpu_custom_call" | custom-call | flops 1 | bytes 1 | tf_op jit(solution)/shard_map/own_int_products_0/pallas_call | solution.py:32
  11.1 2.3 %collective-permute-start.2 = (s16[1040,128]{1,0:T(8,128)(2,1)S(1)}, s16[1040,128]{1,0:T(8,128)(2,1)S(1)}, u32[]{:S(2)}, u32[]{:S(2)}) collective-permute-start(s16[1040,128]{1,0:T(8,128)(2,1)S(1)} %get-tuple-element.71), channel_id=1, source_target_pairs={{28,0},{8,4},{4,8},{16,12},{12,16},{24,20},{20,24},{0,28},{29,1},{... | collective-permute-start | bytes 798728 | tf_op jit(solution)/shard_map/ppermute | solution.py:24
  13.4 1.2 %collective-permute-done.ext_ref = s16[1040,128]{1,0:T(8,128)(2,1)S(1)} collective-permute-done((s16[1040,128]{1,0:T(8,128)(2,1)S(1)}, s16[1040,128]{1,0:T(8,128)(2,1)S(1)}, u32[]{:S(2)}, u32[]{:S(2)}) %collective-permute-start) | collective-permute-done | bytes 266272 | tf_op jit(solution)/shard_map/ppermute | solution.py:24
  14.6 0.4 join_0_0.1
  15.0 2.6 %collective-permute-start.4 = (s16[784,128]{1,0:T(8,128)(2,1)S(1)}, s16[784,128]{1,0:T(8,128)(2,1)S(1)}, u32[]{:S(2)}, u32[]{:S(2)}) collective-permute-start(s16[784,128]{1,0:T(8,128)(2,1)S(1)} %get-tuple-element.76), channel_id=1, source_target_pairs={{1,0},{0,1},{3,2},{2,3},{5,4},{4,5},{7,6},{6,7},{9,8},{8,9},{11,10... | collective-permute-start | bytes 602120 | tf_op jit(solution)/shard_map/ppermute | solution.py:24
  17.6 3.0 %ext_int_products_1.1 = (s16[1040,128]{1,0:T(8,128)(2,1)S(1)}, s16[1040,128]{1,0:T(8,128)(2,1)S(1)}, s16[1040,128]{1,0:T(8,128)(2,1)S(1)}, s16[1040,128]{1,0:T(8,128)(2,1)S(1)}) custom-call(f32[8,1536]{1,0:T(8,128)S(1)} %get-tuple-element.58.a_rows_ref, f32[8,1536]{1,0:T(8,128)S(1)} %get-tuple-element.74.b_rows_ref, bf16[1,2048,1536]{2,1,0:T(8,128)(2,1)S(1)} %bitcast.4, ...), custom_call_target="tpu_custom_call" | custom-call | flops 1 | bytes 1 | tf_op jit(solution)/shard_map/ext_int_products_1/pallas_call | solution.py:32
  20.6 1.6 %collective-permute-start.5 = (s16[1040,128]{1,0:T(8,128)(2,1)S(1)}, s16[1040,128]{1,0:T(8,128)(2,1)S(1)}, u32[]{:S(2)}, u32[]{:S(2)}) collective-permute-start(s16[1040,128]{1,0:T(8,128)(2,1)S(1)} %get-tuple-element.79), channel_id=1, source_target_pairs={{28,0},{8,4},{4,8},{16,12},{12,16},{24,20},{20,24},{0,28},{29,1},{... | collective-permute-start | bytes 798728 | tf_op jit(solution)/shard_map/ppermute | solution.py:24
  22.3 0.4 join_0_128.1
  22.7 0.6 %collective-permute-start.7 = (s16[784,128]{1,0:T(8,128)(2,1)S(1)}, s16[784,128]{1,0:T(8,128)(2,1)S(1)}, u32[]{:S(2)}, u32[]{:S(2)}) collective-permute-start(s16[784,128]{1,0:T(8,128)(2,1)S(1)} %get-tuple-element.82), channel_id=1, source_target_pairs={{1,0},{0,1},{3,2},{2,3},{5,4},{4,5},{7,6},{6,7},{9,8},{8,9},{11,10... | collective-permute-start | bytes 602120 | tf_op jit(solution)/shard_map/ppermute | solution.py:24
  23.3 0.7 %collective-permute-start.8 = (s16[1040,128]{1,0:T(8,128)(2,1)S(1)}, s16[1040,128]{1,0:T(8,128)(2,1)S(1)}, u32[]{:S(2)}, u32[]{:S(2)}) collective-permute-start(s16[1040,128]{1,0:T(8,128)(2,1)S(1)} %get-tuple-element.85), channel_id=1, source_target_pairs={{28,0},{8,4},{4,8},{16,12},{12,16},{24,20},{20,24},{0,28},{29,1},{... | collective-permute-start | bytes 798728 | tf_op jit(solution)/shard_map/ppermute | solution.py:24
  24.1 1.8 %own_products_1.1.own_ref = f32[1536,256]{1,0:T(8,128)S(1)} custom-call(f32[8,1536]{1,0:T(8,128)S(1)} %get-tuple-element.58.a_rows_ref, f32[8,1536]{1,0:T(8,128)S(1)} %get-tuple-element.74.b_rows_ref, bf16[1,2048,1536]{2,1,0:T(8,128)(2,1)S(1)} %bitcast.4, bf16[1024,2048]{1,0:T(8,128)(2,1)S(1)} %get-tuple-element.62.ext_rows_ref, ...), custom_call_target="tpu_custom_call" | custom-call | flops 1 | bytes 1 | tf_op jit(solution)/shard_map/own_products_1/pallas_call | solution.py:32
  25.9 0.2 halve_2_0.1
  26.1 4.1 %collective-permute-done.5.ext_ref = s16[1040,128]{1,0:T(8,128)(2,1)S(1)} collective-permute-done((s16[1040,128]{1,0:T(8,128)(2,1)S(1)}, s16[1040,128]{1,0:T(8,128)(2,1)S(1)}, u32[]{:S(2)}, u32[]{:S(2)}) %collective-permute-start.5) | collective-permute-done | bytes 266272 | tf_op jit(solution)/shard_map/ppermute | solution.py:24
  30.2 0.4 join_1_0.1
  30.8 3.0 %collective-permute-start.10 = (s16[400,128]{1,0:T(8,128)(2,1)S(1)}, s16[400,128]{1,0:T(8,128)(2,1)S(1)}, u32[]{:S(2)}, u32[]{:S(2)}) collective-permute-start(s16[400,128]{1,0:T(8,128)(2,1)S(1)} %get-tuple-element.89), channel_id=1, source_target_pairs={{2,0},{3,1},{0,2},{1,3},{6,4},{7,5},{4,6},{5,7},{10,8},{11,9},{8,1... | collective-permute-start | bytes 307208 | tf_op jit(solution)/shard_map/ppermute | solution.py:24
  33.7 0.2 halve_2_1.1
  34.0 1.3 %collective-permute-done.8.ext_ref = s16[1040,128]{1,0:T(8,128)(2,1)S(1)} collective-permute-done((s16[1040,128]{1,0:T(8,128)(2,1)S(1)}, s16[1040,128]{1,0:T(8,128)(2,1)S(1)}, u32[]{:S(2)}, u32[]{:S(2)}) %collective-permute-start.8) | collective-permute-done | bytes 266272 | tf_op jit(solution)/shard_map/ppermute | solution.py:24
  35.3 0.4 join_1_128.1
  35.7 0.7 %collective-permute-start.13 = (s16[400,128]{1,0:T(8,128)(2,1)S(1)}, s16[400,128]{1,0:T(8,128)(2,1)S(1)}, u32[]{:S(2)}, u32[]{:S(2)}) collective-permute-start(s16[400,128]{1,0:T(8,128)(2,1)S(1)} %get-tuple-element.100), channel_id=1, source_target_pairs={{1,0},{0,1},{3,2},{2,3},{5,4},{4,5},{7,6},{6,7},{9,8},{8,9},{11,10... | collective-permute-start | bytes 307208 | tf_op jit(solution)/shard_map/ppermute | solution.py:24
  36.4 2.6 %collective-permute-start.14 = (s16[400,128]{1,0:T(8,128)(2,1)S(1)}, s16[400,128]{1,0:T(8,128)(2,1)S(1)}, u32[]{:S(2)}, u32[]{:S(2)}) collective-permute-start(s16[400,128]{1,0:T(8,128)(2,1)S(1)} %get-tuple-element.101), channel_id=1, source_target_pairs={{2,0},{3,1},{0,2},{1,3},{6,4},{7,5},{4,6},{5,7},{10,8},{11,9},{8,1... | collective-permute-start | bytes 307208 | tf_op jit(solution)/shard_map/ppermute | solution.py:24
  39.0 2.6 %collective-permute-start.15 = (s16[400,128]{1,0:T(8,128)(2,1)S(1)}, s16[400,128]{1,0:T(8,128)(2,1)S(1)}, u32[]{:S(2)}, u32[]{:S(2)}) collective-permute-start(s16[400,128]{1,0:T(8,128)(2,1)S(1)} %get-tuple-element.102), channel_id=1, source_target_pairs={{3,0},{2,1},{1,2},{0,3},{7,4},{6,5},{5,6},{4,7},{11,8},{10,9},{9,1... | collective-permute-start | bytes 307208 | tf_op jit(solution)/shard_map/ppermute | solution.py:24
  41.7 7.0 %collective-permute-done.11.rest_0_ = s16[400,128]{1,0:T(8,128)(2,1)S(1)} collective-permute-done((s16[400,128]{1,0:T(8,128)(2,1)S(1)}, s16[400,128]{1,0:T(8,128)(2,1)S(1)}, u32[]{:S(2)}, u32[]{:S(2)}) %collective-permute-start.11) | collective-permute-done | bytes 102432 | tf_op jit(solution)/shard_map/ppermute | solution.py:24
  48.8 0.2 halve_2_2.1
  49.1 1.8 %collective-permute-done.14.rest_1_ = s16[400,128]{1,0:T(8,128)(2,1)S(1)} collective-permute-done((s16[400,128]{1,0:T(8,128)(2,1)S(1)}, s16[400,128]{1,0:T(8,128)(2,1)S(1)}, u32[]{:S(2)}, u32[]{:S(2)}) %collective-permute-start.14) | collective-permute-done | bytes 102432 | tf_op jit(solution)/shard_map/ppermute | solution.py:24
  51.0 4.4 %collective-permute-done.16.rest_0_ = s16[400,128]{1,0:T(8,128)(2,1)S(1)} collective-permute-done((s16[400,128]{1,0:T(8,128)(2,1)S(1)}, s16[400,128]{1,0:T(8,128)(2,1)S(1)}, u32[]{:S(2)}, u32[]{:S(2)}) %collective-permute-start.16) | collective-permute-done | bytes 102432 | tf_op jit(solution)/shard_map/ppermute | solution.py:24
  55.5 1.5 %collective-permute-start.19 = (f32[8,512]{1,0:T(8,128)S(1)}, f32[8,512]{1,0:T(8,128)S(1)}, u32[]{:S(2)}, u32[]{:S(2)}) collective-permute-start(f32[8,512]{1,0:T(8,128)S(1)} %get-tuple-element.108.refs_4_), channel_id=1, source_target_pairs={{3,0},{2,1},{1,2},{0,3},{7,4},{6,5},{5,6},{4,7},{11,8},{10,9},{9,1... | collective-permute-start | bytes 49160 | tf_op jit(solution)/shard_map/ppermute | solution.py:24
  56.9 3.0 %collective-permute-start.17 = (f32[8,512]{1,0:T(8,128)S(1)}, f32[8,512]{1,0:T(8,128)S(1)}, u32[]{:S(2)}, u32[]{:S(2)}) collective-permute-start(f32[8,512]{1,0:T(8,128)S(1)} %get-tuple-element.108.refs_4_), channel_id=1, source_target_pairs={{1,0},{0,1},{3,2},{2,3},{5,4},{4,5},{7,6},{6,7},{9,8},{8,9},{11,10... | collective-permute-start | bytes 49160 | tf_op jit(solution)/shard_map/ppermute | solution.py:24
  59.9 1.1 %collective-permute-done.19.refs_7_ = f32[8,512]{1,0:T(8,128)S(1)} collective-permute-done((f32[8,512]{1,0:T(8,128)S(1)}, f32[8,512]{1,0:T(8,128)S(1)}, u32[]{:S(2)}, u32[]{:S(2)}) %collective-permute-start.19) | collective-permute-done | bytes 16416 | tf_op jit(solution)/shard_map/ppermute | solution.py:24
  61.1 0.5 collective-permute-done.18.refs_6_
  61.7 1.0 %rescale.1 = f32[1,384,512]{2,1,0:T(8,128)} custom-call(f32[384,128]{1,0:T(8,128)S(1)} %get-tuple-element.90.refs_0_, f32[384,128]{1,0:T(8,128)S(1)} %get-tuple-element.94.refs_1_, f32[384,128]{1,0:T(8,128)S(1)} %get-tuple-element.106.refs_2_, f32[384,128]{1,0:T(8,128)S(1)} %get-tuple-element.107.refs_3_, f32[8,512]{1,0:T(8,128)S(1)} %get-tuple-element.108.refs_4_, ...), custom_call_target="tpu_custom_call" | custom-call | flops 1 | bytes 1 | tf_op jit(solution)/shard_map/rescale/pallas_call | solution.py:32
  (31 shorter events, 0.9 us)
Async XLA Ops:
  0.0 8.0 %slice-start = ((s8[6291456]{0:T(1024)(128)(4,1)}), s8[4194304]{0:T(1024)(128)(4,1)S(1)}, s32[]{:S(2)}) async-start(s8[6291456]{0:T(1024)(128)(4,1)} %bitcast.3), calls=%async_computation | async-start | bytes 8388608
  0.0 8.0 %slice-start.1 = ((s8[6291456]{0:T(1024)(128)(4,1)}), s8[2097152]{0:T(1024)(128)(4,1)S(1)}, s32[]{:S(2)}) async-start(s8[6291456]{0:T(1024)(128)(4,1)} %bitcast.3), calls=%async_computation.1 | async-start | bytes 4194304
  0.0 8.0 %copy-start = (bf16[1,2048,1536]{2,1,0:T(8,128)(2,1)S(1)}, bf16[1,2048,1536]{2,1,0:T(8,128)(2,1)}, u32[]{:S(2)}) copy-start(bf16[1,2048,1536]{2,1,0:T(8,128)(2,1)} %side_ref.1) | copy-start | bytes 18874372
  4.6 10.1 %collective-permute-start = (s16[1040,128]{1,0:T(8,128)(2,1)S(1)}, s16[1040,128]{1,0:T(8,128)(2,1)S(1)}, u32[]{:S(2)}, u32[]{:S(2)}) collective-permute-start(s16[1040,128]{1,0:T(8,128)(2,1)S(1)} %get-tuple-element.60), channel_id=1, source_target_pairs={{28,0},{8,4},{4,8},{16,12},{12,16},{24,20},{20,24},{0,28},{29,1},{... | collective-permute-start | bytes 798728 | tf_op jit(solution)/shard_map/ppermute | solution.py:24
  11.1 3.6 %collective-permute-start.1 = (s16[1040,128]{1,0:T(8,128)(2,1)S(1)}, s16[1040,128]{1,0:T(8,128)(2,1)S(1)}, u32[]{:S(2)}, u32[]{:S(2)}) collective-permute-start(s16[1040,128]{1,0:T(8,128)(2,1)S(1)} %get-tuple-element.63), channel_id=1, source_target_pairs={{4,0},{0,4},{12,8},{8,12},{20,16},{16,20},{28,24},{24,28},{5,1},{1... | collective-permute-start | bytes 798728 | tf_op jit(solution)/shard_map/ppermute | solution.py:24
  11.1 11.1 %collective-permute-start.2 = (s16[1040,128]{1,0:T(8,128)(2,1)S(1)}, s16[1040,128]{1,0:T(8,128)(2,1)S(1)}, u32[]{:S(2)}, u32[]{:S(2)}) collective-permute-start(s16[1040,128]{1,0:T(8,128)(2,1)S(1)} %get-tuple-element.71), channel_id=1, source_target_pairs={{28,0},{8,4},{4,8},{16,12},{12,16},{24,20},{20,24},{0,28},{29,1},{... | collective-permute-start | bytes 798728 | tf_op jit(solution)/shard_map/ppermute | solution.py:24
  13.4 8.9 %collective-permute-start.3 = (s16[1040,128]{1,0:T(8,128)(2,1)S(1)}, s16[1040,128]{1,0:T(8,128)(2,1)S(1)}, u32[]{:S(2)}, u32[]{:S(2)}) collective-permute-start(s16[1040,128]{1,0:T(8,128)(2,1)S(1)} %get-tuple-element.72), channel_id=1, source_target_pairs={{4,0},{0,4},{12,8},{8,12},{20,16},{16,20},{28,24},{24,28},{5,1},{1... | collective-permute-start | bytes 798728 | tf_op jit(solution)/shard_map/ppermute | solution.py:24
  15.0 9.1 %collective-permute-start.4 = (s16[784,128]{1,0:T(8,128)(2,1)S(1)}, s16[784,128]{1,0:T(8,128)(2,1)S(1)}, u32[]{:S(2)}, u32[]{:S(2)}) collective-permute-start(s16[784,128]{1,0:T(8,128)(2,1)S(1)} %get-tuple-element.76), channel_id=1, source_target_pairs={{1,0},{0,1},{3,2},{2,3},{5,4},{4,5},{7,6},{6,7},{9,8},{8,9},{11,10... | collective-permute-start | bytes 602120 | tf_op jit(solution)/shard_map/ppermute | solution.py:24
  20.6 9.6 %collective-permute-start.5 = (s16[1040,128]{1,0:T(8,128)(2,1)S(1)}, s16[1040,128]{1,0:T(8,128)(2,1)S(1)}, u32[]{:S(2)}, u32[]{:S(2)}) collective-permute-start(s16[1040,128]{1,0:T(8,128)(2,1)S(1)} %get-tuple-element.79), channel_id=1, source_target_pairs={{28,0},{8,4},{4,8},{16,12},{12,16},{24,20},{20,24},{0,28},{29,1},{... | collective-permute-start | bytes 798728 | tf_op jit(solution)/shard_map/ppermute | solution.py:24
  22.3 8.0 %collective-permute-start.6 = (s16[1040,128]{1,0:T(8,128)(2,1)S(1)}, s16[1040,128]{1,0:T(8,128)(2,1)S(1)}, u32[]{:S(2)}, u32[]{:S(2)}) collective-permute-start(s16[1040,128]{1,0:T(8,128)(2,1)S(1)} %get-tuple-element.69), channel_id=1, source_target_pairs={{4,0},{0,4},{12,8},{8,12},{20,16},{16,20},{28,24},{24,28},{5,1},{1... | collective-permute-start | bytes 798728 | tf_op jit(solution)/shard_map/ppermute | solution.py:24
  22.7 11.0 %collective-permute-start.7 = (s16[784,128]{1,0:T(8,128)(2,1)S(1)}, s16[784,128]{1,0:T(8,128)(2,1)S(1)}, u32[]{:S(2)}, u32[]{:S(2)}) collective-permute-start(s16[784,128]{1,0:T(8,128)(2,1)S(1)} %get-tuple-element.82), channel_id=1, source_target_pairs={{1,0},{0,1},{3,2},{2,3},{5,4},{4,5},{7,6},{6,7},{9,8},{8,9},{11,10... | collective-permute-start | bytes 602120 | tf_op jit(solution)/shard_map/ppermute | solution.py:24
  23.3 12.0 %collective-permute-start.8 = (s16[1040,128]{1,0:T(8,128)(2,1)S(1)}, s16[1040,128]{1,0:T(8,128)(2,1)S(1)}, u32[]{:S(2)}, u32[]{:S(2)}) collective-permute-start(s16[1040,128]{1,0:T(8,128)(2,1)S(1)} %get-tuple-element.85), channel_id=1, source_target_pairs={{28,0},{8,4},{4,8},{16,12},{12,16},{24,20},{20,24},{0,28},{29,1},{... | collective-permute-start | bytes 798728 | tf_op jit(solution)/shard_map/ppermute | solution.py:24
  24.1 11.2 %collective-permute-start.9 = (s16[1040,128]{1,0:T(8,128)(2,1)S(1)}, s16[1040,128]{1,0:T(8,128)(2,1)S(1)}, u32[]{:S(2)}, u32[]{:S(2)}) collective-permute-start(s16[1040,128]{1,0:T(8,128)(2,1)S(1)} %get-tuple-element.86), channel_id=1, source_target_pairs={{4,0},{0,4},{12,8},{8,12},{20,16},{16,20},{28,24},{24,28},{5,1},{1... | collective-permute-start | bytes 798728 | tf_op jit(solution)/shard_map/ppermute | solution.py:24
  30.6 18.2 %collective-permute-start.12 = (s16[784,128]{1,0:T(8,128)(2,1)S(1)}, s16[784,128]{1,0:T(8,128)(2,1)S(1)}, u32[]{:S(2)}, u32[]{:S(2)}) collective-permute-start(s16[784,128]{1,0:T(8,128)(2,1)S(1)} %get-tuple-element.97), channel_id=1, source_target_pairs={{1,0},{0,1},{3,2},{2,3},{5,4},{4,5},{7,6},{6,7},{9,8},{8,9},{11,10... | collective-permute-start | bytes 602120 | tf_op jit(solution)/shard_map/ppermute | solution.py:24
  30.8 8.2 %collective-permute-start.10 = (s16[400,128]{1,0:T(8,128)(2,1)S(1)}, s16[400,128]{1,0:T(8,128)(2,1)S(1)}, u32[]{:S(2)}, u32[]{:S(2)}) collective-permute-start(s16[400,128]{1,0:T(8,128)(2,1)S(1)} %get-tuple-element.89), channel_id=1, source_target_pairs={{2,0},{3,1},{0,2},{1,3},{6,4},{7,5},{4,6},{5,7},{10,8},{11,9},{8,1... | collective-permute-start | bytes 307208 | tf_op jit(solution)/shard_map/ppermute | solution.py:24
  33.9 14.8 %collective-permute-start.11 = (s16[400,128]{1,0:T(8,128)(2,1)S(1)}, s16[400,128]{1,0:T(8,128)(2,1)S(1)}, u32[]{:S(2)}, u32[]{:S(2)}) collective-permute-start(s16[400,128]{1,0:T(8,128)(2,1)S(1)} %get-tuple-element.93), channel_id=1, source_target_pairs={{2,0},{3,1},{0,2},{1,3},{6,4},{7,5},{4,6},{5,7},{10,8},{11,9},{8,1... | collective-permute-start | bytes 307208 | tf_op jit(solution)/shard_map/ppermute | solution.py:24
  35.7 13.3 %collective-permute-start.13 = (s16[400,128]{1,0:T(8,128)(2,1)S(1)}, s16[400,128]{1,0:T(8,128)(2,1)S(1)}, u32[]{:S(2)}, u32[]{:S(2)}) collective-permute-start(s16[400,128]{1,0:T(8,128)(2,1)S(1)} %get-tuple-element.100), channel_id=1, source_target_pairs={{1,0},{0,1},{3,2},{2,3},{5,4},{4,5},{7,6},{6,7},{9,8},{8,9},{11,10... | collective-permute-start | bytes 307208 | tf_op jit(solution)/shard_map/ppermute | solution.py:24
  36.4 14.5 %collective-permute-start.14 = (s16[400,128]{1,0:T(8,128)(2,1)S(1)}, s16[400,128]{1,0:T(8,128)(2,1)S(1)}, u32[]{:S(2)}, u32[]{:S(2)}) collective-permute-start(s16[400,128]{1,0:T(8,128)(2,1)S(1)} %get-tuple-element.101), channel_id=1, source_target_pairs={{2,0},{3,1},{0,2},{1,3},{6,4},{7,5},{4,6},{5,7},{10,8},{11,9},{8,1... | collective-permute-start | bytes 307208 | tf_op jit(solution)/shard_map/ppermute | solution.py:24
  39.0 11.9 %collective-permute-start.15 = (s16[400,128]{1,0:T(8,128)(2,1)S(1)}, s16[400,128]{1,0:T(8,128)(2,1)S(1)}, u32[]{:S(2)}, u32[]{:S(2)}) collective-permute-start(s16[400,128]{1,0:T(8,128)(2,1)S(1)} %get-tuple-element.102), channel_id=1, source_target_pairs={{3,0},{2,1},{1,2},{0,3},{7,4},{6,5},{5,6},{4,7},{11,8},{10,9},{9,1... | collective-permute-start | bytes 307208 | tf_op jit(solution)/shard_map/ppermute | solution.py:24
  49.0 6.4 %collective-permute-start.16 = (s16[400,128]{1,0:T(8,128)(2,1)S(1)}, s16[400,128]{1,0:T(8,128)(2,1)S(1)}, u32[]{:S(2)}, u32[]{:S(2)}) collective-permute-start(s16[400,128]{1,0:T(8,128)(2,1)S(1)} %get-tuple-element.105), channel_id=1, source_target_pairs={{2,0},{3,1},{0,2},{1,3},{6,4},{7,5},{4,6},{5,7},{10,8},{11,9},{8,1... | collective-permute-start | bytes 307208 | tf_op jit(solution)/shard_map/ppermute | solution.py:24
  55.5 5.6 %collective-permute-start.19 = (f32[8,512]{1,0:T(8,128)S(1)}, f32[8,512]{1,0:T(8,128)S(1)}, u32[]{:S(2)}, u32[]{:S(2)}) collective-permute-start(f32[8,512]{1,0:T(8,128)S(1)} %get-tuple-element.108.refs_4_), channel_id=1, source_target_pairs={{3,0},{2,1},{1,2},{0,3},{7,4},{6,5},{5,6},{4,7},{11,8},{10,9},{9,1... | collective-permute-start | bytes 49160 | tf_op jit(solution)/shard_map/ppermute | solution.py:24
  56.9 4.6 %collective-permute-start.18 = (f32[8,512]{1,0:T(8,128)S(1)}, f32[8,512]{1,0:T(8,128)S(1)}, u32[]{:S(2)}, u32[]{:S(2)}) collective-permute-start(f32[8,512]{1,0:T(8,128)S(1)} %get-tuple-element.108.refs_4_), channel_id=1, source_target_pairs={{2,0},{3,1},{0,2},{1,3},{6,4},{7,5},{4,6},{5,7},{10,8},{11,9},{8,1... | collective-permute-start | bytes 49160 | tf_op jit(solution)/shard_map/ppermute | solution.py:24
  56.9 4.8 %collective-permute-start.17 = (f32[8,512]{1,0:T(8,128)S(1)}, f32[8,512]{1,0:T(8,128)S(1)}, u32[]{:S(2)}, u32[]{:S(2)}) collective-permute-start(f32[8,512]{1,0:T(8,128)S(1)} %get-tuple-element.108.refs_4_), channel_id=1, source_target_pairs={{1,0},{0,1},{3,2},{2,3},{5,4},{4,5},{7,6},{6,7},{9,8},{8,9},{11,10... | collective-permute-start | bytes 49160 | tf_op jit(solution)/shard_map/ppermute | solution.py:24

commit v13 on v12

--- a/solution.py
+++ b/solution.py
@@ -487,23 +487,24 @@
         squares[chunk], sums[chunk] = square(ordered(kept), got, others, place, chunk)
         latest.append(sums[chunk])
 
-    for chunk in range(chunks):
-        add_up(chunk)
-        if (chunk + 1) % per_half == 0 and len(owns) < halves:
-            more_own(len(owns))
-        if 1 <= chunk < chunks - 1:
-            scatter(chunk - 1)
-        if chunk % per_half == 0 and chunk // per_half + 1 < halves:
-            more_products(chunk // per_half + 1)
+    add_up(0)
+    for half in range(1, halves):
+        more_products(half)
+    add_up(1)
+    more_own(1)
+    scatter(0)
+    add_up(2)
+    scatter(1)
+    add_up(3)
+    scatter(2)
+    scatter(3)
+    finish(1)
     finish(0)
-    finish(1)
-    for chunk in range(chunks - 2, chunks):
-        scatter(chunk)
-    finish(chunks - 1)
-    finish(chunks - 2)
+    finish(3)
+    finish(2)
 
     squares = [squares[i] for i in sorted(squares)]
-    mine = sums[chunks - 2]
+    mine = sums[2]
     others = [swap(mine, "layer", lambda i: i ^ other) for other in range(1, layers)]
     return rescale(squares, [mine, *others], width)
 

time: 63.4 us -> 63.9 us (level)
  waiting for transfers between devices: 21.7 us -> 24.5 us
  starting transfers between devices: 25 us -> 23.2 us
    ppermute x20, waiting for transfers between devices: 21.7 us -> 24.5 us  [swap(): lax.ppermute(block, axis, [(partner(i), i) for i in range(lax.axis_size(a...]
    ppermute x20, starting transfers between devices: 25 us -> 23.2 us  [swap(): lax.ppermute(block, axis, [(partner(i), i) for i in range(lax.axis_size(a...]
where the time goes in v13:
time: 63.9 us; the launch traced here: 63.8 us
  waiting for transfers between devices  24.5 us (38%)
  starting transfers between devices  23.2 us (36%)
  Pallas kernels  15.9 us (25%)
    ppermute x20, waiting for transfers between devices, swap(): lax.ppermute(block, axis, [(partner(i), i) for i in range(lax.axis_size(a...  24.5 us
    ppermute x20, starting transfers between devices, swap(): lax.ppermute(block, axis, [(partner(i), i) for i in range(lax.axis_size(a...  23.2 us
    pallas_call x16, Pallas kernels, call(): pl.pallas_call(kernel, out_shape=out_shape, in_specs=in_specs, out_specs=...  15.9 us
  transfers between devices with their start and end apart: 20, of which 9 were waited for; matrix products, arithmetic and copies ran while one was open for 0% of the time, Pallas kernels for 16%

profile of v13, /device:TPU:0, one launch (start us, length us, event | category | flops | bytes accessed | tf_op | source)
XLA Modules:
  0.0 63.8 jit_solution(13548205860558811244)
XLA Ops:
  0.0 4.5 %first_products.1 = (s16[1040,128]{1,0:T(8,128)(2,1)S(1)}, s16[1040,128]{1,0:T(8,128)(2,1)S(1)}, bf16[1024,2048]{1,0:T(8,128)(2,1)S(1)}, f32[8,1536]{1,0:T(8,128...) custom-call(s32[6,1,32]{2,1,0:T(1,128)} %bitcast.5, s32[6,1,32]{2,1,0:T(1,128)} %bitcast.6, s32[1,2,6]{2,1,0:T(2,128)} %bitcast.7, ...), custom_call_target="tpu_custom_call" | custom-call | flops 1 | bytes 1 | tf_op jit(solution)/shard_map/first_products/pallas_call | solution.py:32
  4.6 3.4 %collective-permute-start = (s16[1040,128]{1,0:T(8,128)(2,1)S(1)}, s16[1040,128]{1,0:T(8,128)(2,1)S(1)}, u32[]{:S(2)}, u32[]{:S(2)}) collective-permute-start(s16[1040,128]{1,0:T(8,128)(2,1)S(1)} %get-tuple-element.60), channel_id=1, source_target_pairs={{28,0},{8,4},{4,8},{16,12},{12,16},{24,20},{20,24},{0,28},{29,1},{... | collective-permute-start | bytes 798728 | tf_op jit(solution)/shard_map/ppermute | solution.py:24
  8.0 3.1 %own_int_products_0.1 = (f32[1536,256]{1,0:T(8,128)S(1)}, s16[1040,128]{1,0:T(8,128)(2,1)S(1)}, s16[1040,128]{1,0:T(8,128)(2,1)S(1)}, bf16[512,2048]{1,0:T(8,128)(2,1)S(1)}) custom-call(f32[8,1536]{1,0:T(8,128)S(1)} %get-tuple-element.58.a_rows_ref, f32[8,1536]{1,0:T(8,128)S(1)} %get-tuple-element.74.b_rows_ref, bf16[1,2048,1536]{2,1,0:T(8,128)(2,1)S(1)} %bitcast.4, ...), custom_call_target="tpu_custom_call" | custom-call | flops 1 | bytes 1 | tf_op jit(solution)/shard_map/own_int_products_0/pallas_call | solution.py:32
  11.1 2.3 %collective-permute-start.2 = (s16[1040,128]{1,0:T(8,128)(2,1)S(1)}, s16[1040,128]{1,0:T(8,128)(2,1)S(1)}, u32[]{:S(2)}, u32[]{:S(2)}) collective-permute-start(s16[1040,128]{1,0:T(8,128)(2,1)S(1)} %get-tuple-element.71), channel_id=1, source_target_pairs={{28,0},{8,4},{4,8},{16,12},{12,16},{24,20},{20,24},{0,28},{29,1},{... | collective-permute-start | bytes 798728 | tf_op jit(solution)/shard_map/ppermute | solution.py:24
  13.4 1.2 %collective-permute-done.ext_ref = s16[1040,128]{1,0:T(8,128)(2,1)S(1)} collective-permute-done((s16[1040,128]{1,0:T(8,128)(2,1)S(1)}, s16[1040,128]{1,0:T(8,128)(2,1)S(1)}, u32[]{:S(2)}, u32[]{:S(2)}) %collective-permute-start) | collective-permute-done | bytes 266272 | tf_op jit(solution)/shard_map/ppermute | solution.py:24
  14.6 0.4 join_0_0.1
  15.0 2.6 %collective-permute-start.4 = (s16[784,128]{1,0:T(8,128)(2,1)S(1)}, s16[784,128]{1,0:T(8,128)(2,1)S(1)}, u32[]{:S(2)}, u32[]{:S(2)}) collective-permute-start(s16[784,128]{1,0:T(8,128)(2,1)S(1)} %get-tuple-element.76), channel_id=1, source_target_pairs={{1,0},{0,1},{3,2},{2,3},{5,4},{4,5},{7,6},{6,7},{9,8},{8,9},{11,10... | collective-permute-start | bytes 602120 | tf_op jit(solution)/shard_map/ppermute | solution.py:24
  17.6 3.0 %ext_int_products_1.1 = (s16[1040,128]{1,0:T(8,128)(2,1)S(1)}, s16[1040,128]{1,0:T(8,128)(2,1)S(1)}, s16[1040,128]{1,0:T(8,128)(2,1)S(1)}, s16[1040,128]{1,0:T(8,128)(2,1)S(1)}) custom-call(f32[8,1536]{1,0:T(8,128)S(1)} %get-tuple-element.58.a_rows_ref, f32[8,1536]{1,0:T(8,128)S(1)} %get-tuple-element.74.b_rows_ref, bf16[1,2048,1536]{2,1,0:T(8,128)(2,1)S(1)} %bitcast.4, ...), custom_call_target="tpu_custom_call" | custom-call | flops 1 | bytes 1 | tf_op jit(solution)/shard_map/ext_int_products_1/pallas_call | solution.py:32
  20.6 1.6 %collective-permute-start.5 = (s16[1040,128]{1,0:T(8,128)(2,1)S(1)}, s16[1040,128]{1,0:T(8,128)(2,1)S(1)}, u32[]{:S(2)}, u32[]{:S(2)}) collective-permute-start(s16[1040,128]{1,0:T(8,128)(2,1)S(1)} %get-tuple-element.79), channel_id=1, source_target_pairs={{28,0},{8,4},{4,8},{16,12},{12,16},{24,20},{20,24},{0,28},{29,1},{... | collective-permute-start | bytes 798728 | tf_op jit(solution)/shard_map/ppermute | solution.py:24
  22.3 0.4 join_0_128.1
  22.7 0.6 collective-permute-start.7
  23.3 0.7 %collective-permute-start.8 = (s16[1040,128]{1,0:T(8,128)(2,1)S(1)}, s16[1040,128]{1,0:T(8,128)(2,1)S(1)}, u32[]{:S(2)}, u32[]{:S(2)}) collective-permute-start(s16[1040,128]{1,0:T(8,128)(2,1)S(1)} %get-tuple-element.85), channel_id=1, source_target_pairs={{28,0},{8,4},{4,8},{16,12},{12,16},{24,20},{20,24},{0,28},{29,1},{... | collective-permute-start | bytes 798728 | tf_op jit(solution)/shard_map/ppermute | solution.py:24
  24.1 1.8 %own_products_1.1.own_ref = f32[1536,256]{1,0:T(8,128)S(1)} custom-call(f32[8,1536]{1,0:T(8,128)S(1)} %get-tuple-element.58.a_rows_ref, f32[8,1536]{1,0:T(8,128)S(1)} %get-tuple-element.74.b_rows_ref, bf16[1,2048,1536]{2,1,0:T(8,128)(2,1)S(1)} %bitcast.4, bf16[1024,2048]{1,0:T(8,128)(2,1)S(1)} %get-tuple-element.62.ext_rows_ref, ...), custom_call_target="tpu_custom_call" | custom-call | flops 1 | bytes 1 | tf_op jit(solution)/shard_map/own_products_1/pallas_call | solution.py:32
  25.9 0.2 halve_2_0.1
  26.1 4.1 %collective-permute-done.5.ext_ref = s16[1040,128]{1,0:T(8,128)(2,1)S(1)} collective-permute-done((s16[1040,128]{1,0:T(8,128)(2,1)S(1)}, s16[1040,128]{1,0:T(8,128)(2,1)S(1)}, u32[]{:S(2)}, u32[]{:S(2)}) %collective-permute-start.5) | collective-permute-done | bytes 266272 | tf_op jit(solution)/shard_map/ppermute | solution.py:24
  30.2 0.4 join_1_0.1
  31.0 3.0 %collective-permute-start.11 = (s16[400,128]{1,0:T(8,128)(2,1)S(1)}, s16[400,128]{1,0:T(8,128)(2,1)S(1)}, u32[]{:S(2)}, u32[]{:S(2)}) collective-permute-start(s16[400,128]{1,0:T(8,128)(2,1)S(1)} %get-tuple-element.92), channel_id=1, source_target_pairs={{2,0},{3,1},{0,2},{1,3},{6,4},{7,5},{4,6},{5,7},{10,8},{11,9},{8,1... | collective-permute-start | bytes 307208 | tf_op jit(solution)/shard_map/ppermute | solution.py:24
  34.1 1.2 %collective-permute-done.8.ext_ref = s16[1040,128]{1,0:T(8,128)(2,1)S(1)} collective-permute-done((s16[1040,128]{1,0:T(8,128)(2,1)S(1)}, s16[1040,128]{1,0:T(8,128)(2,1)S(1)}, u32[]{:S(2)}, u32[]{:S(2)}) %collective-permute-start.8) | collective-permute-done | bytes 266272 | tf_op jit(solution)/shard_map/ppermute | solution.py:24
  35.3 0.4 join_1_128.1
  35.7 0.7 %collective-permute-start.13 = (s16[400,128]{1,0:T(8,128)(2,1)S(1)}, s16[400,128]{1,0:T(8,128)(2,1)S(1)}, u32[]{:S(2)}, u32[]{:S(2)}) collective-permute-start(s16[400,128]{1,0:T(8,128)(2,1)S(1)} %get-tuple-element.100), channel_id=1, source_target_pairs={{1,0},{0,1},{3,2},{2,3},{5,4},{4,5},{7,6},{6,7},{9,8},{8,9},{11,10... | collective-permute-start | bytes 307208 | tf_op jit(solution)/shard_map/ppermute | solution.py:24
  36.4 2.6 %collective-permute-start.14 = (s16[400,128]{1,0:T(8,128)(2,1)S(1)}, s16[400,128]{1,0:T(8,128)(2,1)S(1)}, u32[]{:S(2)}, u32[]{:S(2)}) collective-permute-start(s16[400,128]{1,0:T(8,128)(2,1)S(1)} %get-tuple-element.101), channel_id=1, source_target_pairs={{2,0},{3,1},{0,2},{1,3},{6,4},{7,5},{4,6},{5,7},{10,8},{11,9},{8,1... | collective-permute-start | bytes 307208 | tf_op jit(solution)/shard_map/ppermute | solution.py:24
  39.0 2.1 %collective-permute-done.10.got_ref = s16[784,128]{1,0:T(8,128)(2,1)S(1)} collective-permute-done((s16[784,128]{1,0:T(8,128)(2,1)S(1)}, s16[784,128]{1,0:T(8,128)(2,1)S(1)}, u32[]{:S(2)}, u32[]{:S(2)}) %collective-permute-start.10) | collective-permute-done | bytes 200736 | tf_op jit(solution)/shard_map/ppermute | solution.py:24
  41.0 0.3 collective-permute-start.15
  41.5 0.6 collective-permute-start.16
  42.2 4.3 %collective-permute-done.12.rest_0_ = s16[400,128]{1,0:T(8,128)(2,1)S(1)} collective-permute-done((s16[400,128]{1,0:T(8,128)(2,1)S(1)}, s16[400,128]{1,0:T(8,128)(2,1)S(1)}, u32[]{:S(2)}, u32[]{:S(2)}) %collective-permute-start.12) | collective-permute-done | bytes 102432 | tf_op jit(solution)/shard_map/ppermute | solution.py:24
  46.7 5.4 %collective-permute-done.14.rest_1_ = s16[400,128]{1,0:T(8,128)(2,1)S(1)} collective-permute-done((s16[400,128]{1,0:T(8,128)(2,1)S(1)}, s16[400,128]{1,0:T(8,128)(2,1)S(1)}, u32[]{:S(2)}, u32[]{:S(2)}) %collective-permute-start.14) | collective-permute-done | bytes 102432 | tf_op jit(solution)/shard_map/ppermute | solution.py:24
  52.2 3.4 %collective-permute-done.16.rest_0_ = s16[400,128]{1,0:T(8,128)(2,1)S(1)} collective-permute-done((s16[400,128]{1,0:T(8,128)(2,1)S(1)}, s16[400,128]{1,0:T(8,128)(2,1)S(1)}, u32[]{:S(2)}, u32[]{:S(2)}) %collective-permute-start.16) | collective-permute-done | bytes 102432 | tf_op jit(solution)/shard_map/ppermute | solution.py:24
  55.7 2.5 %collective-permute-start.19 = (f32[8,512]{1,0:T(8,128)S(1)}, f32[8,512]{1,0:T(8,128)S(1)}, u32[]{:S(2)}, u32[]{:S(2)}) collective-permute-start(f32[8,512]{1,0:T(8,128)S(1)} %get-tuple-element.108.refs_4_), channel_id=1, source_target_pairs={{3,0},{2,1},{1,2},{0,3},{7,4},{6,5},{5,6},{4,7},{11,8},{10,9},{9,1... | collective-permute-start | bytes 49160 | tf_op jit(solution)/shard_map/ppermute | solution.py:24
  58.2 2.0 %collective-permute-start.17 = (f32[8,512]{1,0:T(8,128)S(1)}, f32[8,512]{1,0:T(8,128)S(1)}, u32[]{:S(2)}, u32[]{:S(2)}) collective-permute-start(f32[8,512]{1,0:T(8,128)S(1)} %get-tuple-element.108.refs_4_), channel_id=1, source_target_pairs={{1,0},{0,1},{3,2},{2,3},{5,4},{4,5},{7,6},{6,7},{9,8},{8,9},{11,10... | collective-permute-start | bytes 49160 | tf_op jit(solution)/shard_map/ppermute | solution.py:24
  60.1 1.1 %collective-permute-done.19.refs_7_ = f32[8,512]{1,0:T(8,128)S(1)} collective-permute-done((f32[8,512]{1,0:T(8,128)S(1)}, f32[8,512]{1,0:T(8,128)S(1)}, u32[]{:S(2)}, u32[]{:S(2)}) %collective-permute-start.19) | collective-permute-done | bytes 16416 | tf_op jit(solution)/shard_map/ppermute | solution.py:24
  61.3 1.5 %collective-permute-done.18.refs_6_ = f32[8,512]{1,0:T(8,128)S(1)} collective-permute-done((f32[8,512]{1,0:T(8,128)S(1)}, f32[8,512]{1,0:T(8,128)S(1)}, u32[]{:S(2)}, u32[]{:S(2)}) %collective-permute-start.18) | collective-permute-done | bytes 16416 | tf_op jit(solution)/shard_map/ppermute | solution.py:24
  62.8 1.0 %rescale.1 = f32[1,384,512]{2,1,0:T(8,128)} custom-call(f32[384,128]{1,0:T(8,128)S(1)} %get-tuple-element.96.refs_0_, f32[384,128]{1,0:T(8,128)S(1)} %get-tuple-element.97.refs_1_, f32[384,128]{1,0:T(8,128)S(1)} %get-tuple-element.106.refs_2_, f32[384,128]{1,0:T(8,128)S(1)} %get-tuple-element.107.refs_3_, f32[8,512]{1,0:T(8,128)S(1)} %get-tuple-element.108.refs_4_, ...), custom_call_target="tpu_custom_call" | custom-call | flops 1 | bytes 1 | tf_op jit(solution)/shard_map/rescale/pallas_call | solution.py:32
  (31 shorter events, 1.0 us)
Async XLA Ops:
  0.0 8.0 %slice-start = ((s8[6291456]{0:T(1024)(128)(4,1)}), s8[4194304]{0:T(1024)(128)(4,1)S(1)}, s32[]{:S(2)}) async-start(s8[6291456]{0:T(1024)(128)(4,1)} %bitcast.3), calls=%async_computation | async-start | bytes 8388608
  0.0 8.0 %slice-start.1 = ((s8[6291456]{0:T(1024)(128)(4,1)}), s8[2097152]{0:T(1024)(128)(4,1)S(1)}, s32[]{:S(2)}) async-start(s8[6291456]{0:T(1024)(128)(4,1)} %bitcast.3), calls=%async_computation.1 | async-start | bytes 4194304
  0.0 8.0 %copy-start = (bf16[1,2048,1536]{2,1,0:T(8,128)(2,1)S(1)}, bf16[1,2048,1536]{2,1,0:T(8,128)(2,1)}, u32[]{:S(2)}) copy-start(bf16[1,2048,1536]{2,1,0:T(8,128)(2,1)} %side_ref.1) | copy-start | bytes 18874372
  4.6 10.1 %collective-permute-start = (s16[1040,128]{1,0:T(8,128)(2,1)S(1)}, s16[1040,128]{1,0:T(8,128)(2,1)S(1)}, u32[]{:S(2)}, u32[]{:S(2)}) collective-permute-start(s16[1040,128]{1,0:T(8,128)(2,1)S(1)} %get-tuple-element.60), channel_id=1, source_target_pairs={{28,0},{8,4},{4,8},{16,12},{12,16},{24,20},{20,24},{0,28},{29,1},{... | collective-permute-start | bytes 798728 | tf_op jit(solution)/shard_map/ppermute | solution.py:24
  11.1 3.6 %collective-permute-start.1 = (s16[1040,128]{1,0:T(8,128)(2,1)S(1)}, s16[1040,128]{1,0:T(8,128)(2,1)S(1)}, u32[]{:S(2)}, u32[]{:S(2)}) collective-permute-start(s16[1040,128]{1,0:T(8,128)(2,1)S(1)} %get-tuple-element.63), channel_id=1, source_target_pairs={{4,0},{0,4},{12,8},{8,12},{20,16},{16,20},{28,24},{24,28},{5,1},{1... | collective-permute-start | bytes 798728 | tf_op jit(solution)/shard_map/ppermute | solution.py:24
  11.1 11.1 %collective-permute-start.2 = (s16[1040,128]{1,0:T(8,128)(2,1)S(1)}, s16[1040,128]{1,0:T(8,128)(2,1)S(1)}, u32[]{:S(2)}, u32[]{:S(2)}) collective-permute-start(s16[1040,128]{1,0:T(8,128)(2,1)S(1)} %get-tuple-element.71), channel_id=1, source_target_pairs={{28,0},{8,4},{4,8},{16,12},{12,16},{24,20},{20,24},{0,28},{29,1},{... | collective-permute-start | bytes 798728 | tf_op jit(solution)/shard_map/ppermute | solution.py:24
  13.4 8.9 %collective-permute-start.3 = (s16[1040,128]{1,0:T(8,128)(2,1)S(1)}, s16[1040,128]{1,0:T(8,128)(2,1)S(1)}, u32[]{:S(2)}, u32[]{:S(2)}) collective-permute-start(s16[1040,128]{1,0:T(8,128)(2,1)S(1)} %get-tuple-element.72), channel_id=1, source_target_pairs={{4,0},{0,4},{12,8},{8,12},{20,16},{16,20},{28,24},{24,28},{5,1},{1... | collective-permute-start | bytes 798728 | tf_op jit(solution)/shard_map/ppermute | solution.py:24
  15.0 9.1 %collective-permute-start.4 = (s16[784,128]{1,0:T(8,128)(2,1)S(1)}, s16[784,128]{1,0:T(8,128)(2,1)S(1)}, u32[]{:S(2)}, u32[]{:S(2)}) collective-permute-start(s16[784,128]{1,0:T(8,128)(2,1)S(1)} %get-tuple-element.76), channel_id=1, source_target_pairs={{1,0},{0,1},{3,2},{2,3},{5,4},{4,5},{7,6},{6,7},{9,8},{8,9},{11,10... | collective-permute-start | bytes 602120 | tf_op jit(solution)/shard_map/ppermute | solution.py:24
  20.6 9.6 %collective-permute-start.5 = (s16[1040,128]{1,0:T(8,128)(2,1)S(1)}, s16[1040,128]{1,0:T(8,128)(2,1)S(1)}, u32[]{:S(2)}, u32[]{:S(2)}) collective-permute-start(s16[1040,128]{1,0:T(8,128)(2,1)S(1)} %get-tuple-element.79), channel_id=1, source_target_pairs={{28,0},{8,4},{4,8},{16,12},{12,16},{24,20},{20,24},{0,28},{29,1},{... | collective-permute-start | bytes 798728 | tf_op jit(solution)/shard_map/ppermute | solution.py:24
  22.3 8.0 %collective-permute-start.6 = (s16[1040,128]{1,0:T(8,128)(2,1)S(1)}, s16[1040,128]{1,0:T(8,128)(2,1)S(1)}, u32[]{:S(2)}, u32[]{:S(2)}) collective-permute-start(s16[1040,128]{1,0:T(8,128)(2,1)S(1)} %get-tuple-element.69), channel_id=1, source_target_pairs={{4,0},{0,4},{12,8},{8,12},{20,16},{16,20},{28,24},{24,28},{5,1},{1... | collective-permute-start | bytes 798728 | tf_op jit(solution)/shard_map/ppermute | solution.py:24
  22.7 8.1 %collective-permute-start.7 = (s16[784,128]{1,0:T(8,128)(2,1)S(1)}, s16[784,128]{1,0:T(8,128)(2,1)S(1)}, u32[]{:S(2)}, u32[]{:S(2)}) collective-permute-start(s16[784,128]{1,0:T(8,128)(2,1)S(1)} %get-tuple-element.82), channel_id=1, source_target_pairs={{1,0},{0,1},{3,2},{2,3},{5,4},{4,5},{7,6},{6,7},{9,8},{8,9},{11,10... | collective-permute-start | bytes 602120 | tf_op jit(solution)/shard_map/ppermute | solution.py:24
  23.3 12.0 %collective-permute-start.8 = (s16[1040,128]{1,0:T(8,128)(2,1)S(1)}, s16[1040,128]{1,0:T(8,128)(2,1)S(1)}, u32[]{:S(2)}, u32[]{:S(2)}) collective-permute-start(s16[1040,128]{1,0:T(8,128)(2,1)S(1)} %get-tuple-element.85), channel_id=1, source_target_pairs={{28,0},{8,4},{4,8},{16,12},{12,16},{24,20},{20,24},{0,28},{29,1},{... | collective-permute-start | bytes 798728 | tf_op jit(solution)/shard_map/ppermute | solution.py:24
  24.1 11.2 %collective-permute-start.9 = (s16[1040,128]{1,0:T(8,128)(2,1)S(1)}, s16[1040,128]{1,0:T(8,128)(2,1)S(1)}, u32[]{:S(2)}, u32[]{:S(2)}) collective-permute-start(s16[1040,128]{1,0:T(8,128)(2,1)S(1)} %get-tuple-element.86), channel_id=1, source_target_pairs={{4,0},{0,4},{12,8},{8,12},{20,16},{16,20},{28,24},{24,28},{5,1},{1... | collective-permute-start | bytes 798728 | tf_op jit(solution)/shard_map/ppermute | solution.py:24
  30.6 10.4 %collective-permute-start.10 = (s16[784,128]{1,0:T(8,128)(2,1)S(1)}, s16[784,128]{1,0:T(8,128)(2,1)S(1)}, u32[]{:S(2)}, u32[]{:S(2)}) collective-permute-start(s16[784,128]{1,0:T(8,128)(2,1)S(1)} %get-tuple-element.89), channel_id=1, source_target_pairs={{1,0},{0,1},{3,2},{2,3},{5,4},{4,5},{7,6},{6,7},{9,8},{8,9},{11,10... | collective-permute-start | bytes 602120 | tf_op jit(solution)/shard_map/ppermute | solution.py:24
  31.0 10.6 %collective-permute-start.11 = (s16[400,128]{1,0:T(8,128)(2,1)S(1)}, s16[400,128]{1,0:T(8,128)(2,1)S(1)}, u32[]{:S(2)}, u32[]{:S(2)}) collective-permute-start(s16[400,128]{1,0:T(8,128)(2,1)S(1)} %get-tuple-element.92), channel_id=1, source_target_pairs={{2,0},{3,1},{0,2},{1,3},{6,4},{7,5},{4,6},{5,7},{10,8},{11,9},{8,1... | collective-permute-start | bytes 307208 | tf_op jit(solution)/shard_map/ppermute | solution.py:24
  34.0 12.6 %collective-permute-start.12 = (s16[400,128]{1,0:T(8,128)(2,1)S(1)}, s16[400,128]{1,0:T(8,128)(2,1)S(1)}, u32[]{:S(2)}, u32[]{:S(2)}) collective-permute-start(s16[400,128]{1,0:T(8,128)(2,1)S(1)} %get-tuple-element.95), channel_id=1, source_target_pairs={{2,0},{3,1},{0,2},{1,3},{6,4},{7,5},{4,6},{5,7},{10,8},{11,9},{8,1... | collective-permute-start | bytes 307208 | tf_op jit(solution)/shard_map/ppermute | solution.py:24
  35.7 10.9 %collective-permute-start.13 = (s16[400,128]{1,0:T(8,128)(2,1)S(1)}, s16[400,128]{1,0:T(8,128)(2,1)S(1)}, u32[]{:S(2)}, u32[]{:S(2)}) collective-permute-start(s16[400,128]{1,0:T(8,128)(2,1)S(1)} %get-tuple-element.100), channel_id=1, source_target_pairs={{1,0},{0,1},{3,2},{2,3},{5,4},{4,5},{7,6},{6,7},{9,8},{8,9},{11,10... | collective-permute-start | bytes 307208 | tf_op jit(solution)/shard_map/ppermute | solution.py:24
  36.4 15.7 %collective-permute-start.14 = (s16[400,128]{1,0:T(8,128)(2,1)S(1)}, s16[400,128]{1,0:T(8,128)(2,1)S(1)}, u32[]{:S(2)}, u32[]{:S(2)}) collective-permute-start(s16[400,128]{1,0:T(8,128)(2,1)S(1)} %get-tuple-element.101), channel_id=1, source_target_pairs={{2,0},{3,1},{0,2},{1,3},{6,4},{7,5},{4,6},{5,7},{10,8},{11,9},{8,1... | collective-permute-start | bytes 307208 | tf_op jit(solution)/shard_map/ppermute | solution.py:24
  41.0 11.0 %collective-permute-start.15 = (s16[400,128]{1,0:T(8,128)(2,1)S(1)}, s16[400,128]{1,0:T(8,128)(2,1)S(1)}, u32[]{:S(2)}, u32[]{:S(2)}) collective-permute-start(s16[400,128]{1,0:T(8,128)(2,1)S(1)} %get-tuple-element.102), channel_id=1, source_target_pairs={{3,0},{2,1},{1,2},{0,3},{7,4},{6,5},{5,6},{4,7},{11,8},{10,9},{9,1... | collective-permute-start | bytes 307208 | tf_op jit(solution)/shard_map/ppermute | solution.py:24
  41.5 14.1 %collective-permute-start.16 = (s16[400,128]{1,0:T(8,128)(2,1)S(1)}, s16[400,128]{1,0:T(8,128)(2,1)S(1)}, u32[]{:S(2)}, u32[]{:S(2)}) collective-permute-start(s16[400,128]{1,0:T(8,128)(2,1)S(1)} %get-tuple-element.105), channel_id=1, source_target_pairs={{2,0},{3,1},{0,2},{1,3},{6,4},{7,5},{4,6},{5,7},{10,8},{11,9},{8,1... | collective-permute-start | bytes 307208 | tf_op jit(solution)/shard_map/ppermute | solution.py:24
  55.7 5.6 %collective-permute-start.19 = (f32[8,512]{1,0:T(8,128)S(1)}, f32[8,512]{1,0:T(8,128)S(1)}, u32[]{:S(2)}, u32[]{:S(2)}) collective-permute-start(f32[8,512]{1,0:T(8,128)S(1)} %get-tuple-element.108.refs_4_), channel_id=1, source_target_pairs={{3,0},{2,1},{1,2},{0,3},{7,4},{6,5},{5,6},{4,7},{11,8},{10,9},{9,1... | collective-permute-start | bytes 49160 | tf_op jit(solution)/shard_map/ppermute | solution.py:24
  58.2 4.6 %collective-permute-start.18 = (f32[8,512]{1,0:T(8,128)S(1)}, f32[8,512]{1,0:T(8,128)S(1)}, u32[]{:S(2)}, u32[]{:S(2)}) collective-permute-start(f32[8,512]{1,0:T(8,128)S(1)} %get-tuple-element.108.refs_4_), channel_id=1, source_target_pairs={{2,0},{3,1},{0,2},{1,3},{6,4},{7,5},{4,6},{5,7},{10,8},{11,9},{8,1... | collective-permute-start | bytes 49160 | tf_op jit(solution)/shard_map/ppermute | solution.py:24
  58.2 4.6 %collective-permute-start.17 = (f32[8,512]{1,0:T(8,128)S(1)}, f32[8,512]{1,0:T(8,128)S(1)}, u32[]{:S(2)}, u32[]{:S(2)}) collective-permute-start(f32[8,512]{1,0:T(8,128)S(1)} %get-tuple-element.108.refs_4_), channel_id=1, source_target_pairs={{1,0},{0,1},{3,2},{2,3},{5,4},{4,5},{7,6},{6,7},{9,8},{8,9},{11,10... | collective-permute-start | bytes 49160 | tf_op jit(solution)/shard_map/ppermute | solution.py:24

commit v14 on v13

--- a/solution.py
+++ b/solution.py
@@ -488,18 +488,17 @@
         latest.append(sums[chunk])
 
     add_up(0)
-    for half in range(1, halves):
-        more_products(half)
+    more_products(1)
+    scatter(0)
     add_up(1)
     more_own(1)
-    scatter(0)
+    finish(0)
     add_up(2)
     scatter(1)
     add_up(3)
+    finish(1)
     scatter(2)
     scatter(3)
-    finish(1)
-    finish(0)
     finish(3)
     finish(2)
 

time: 63.9 us -> 65.3 us (1.022)
  starting transfers between devices: 23.2 us -> 24.4 us
    ppermute x20, starting transfers between devices: 23.2 us -> 24.4 us  [swap(): lax.ppermute(block, axis, [(partner(i), i) for i in range(lax.axis_size(a...]
  transfers between devices with their start and end apart: 20 -> 20, of which waited for: 9 -> 10; matrix products, arithmetic and copies ran while one was open for 0% -> 0% of each run, Pallas kernels for 16% -> 15%
where the time goes in v14:
time: 65.3 us; the launch traced here: 65.2 us
  waiting for transfers between devices  24.6 us (38%)
  starting transfers between devices  24.4 us (37%)
  Pallas kernels  16.1 us (25%)
    ppermute x20, waiting for transfers between devices, swap(): lax.ppermute(block, axis, [(partner(i), i) for i in range(lax.axis_size(a...  24.6 us
    ppermute x20, starting transfers between devices, swap(): lax.ppermute(block, axis, [(partner(i), i) for i in range(lax.axis_size(a...  24.4 us
    pallas_call x16, Pallas kernels, call(): pl.pallas_call(kernel, out_shape=out_shape, in_specs=in_specs, out_specs=...  16.1 us
  transfers between devices with their start and end apart: 20, of which 10 were waited for; matrix products, arithmetic and copies ran while one was open for 0% of the time, Pallas kernels for 15%

profile of v14, /device:TPU:0, one launch (start us, length us, event | category | flops | bytes accessed | tf_op | source)
XLA Modules:
  0.0 65.2 jit_solution(16635581555058563304)
XLA Ops:
  0.0 4.5 %first_products.1 = (s16[1040,128]{1,0:T(8,128)(2,1)S(1)}, s16[1040,128]{1,0:T(8,128)(2,1)S(1)}, bf16[1024,2048]{1,0:T(8,128)(2,1)S(1)}, f32[8,1536]{1,0:T(8,128...) custom-call(s32[6,1,32]{2,1,0:T(1,128)} %bitcast.5, s32[6,1,32]{2,1,0:T(1,128)} %bitcast.6, s32[1,2,6]{2,1,0:T(2,128)} %bitcast.7, ...), custom_call_target="tpu_custom_call" | custom-call | flops 1 | bytes 1 | tf_op jit(solution)/shard_map/first_products/pallas_call | solution.py:32
  4.6 3.4 %collective-permute-start = (s16[1040,128]{1,0:T(8,128)(2,1)S(1)}, s16[1040,128]{1,0:T(8,128)(2,1)S(1)}, u32[]{:S(2)}, u32[]{:S(2)}) collective-permute-start(s16[1040,128]{1,0:T(8,128)(2,1)S(1)} %get-tuple-element.60), channel_id=1, source_target_pairs={{28,0},{8,4},{4,8},{16,12},{12,16},{24,20},{20,24},{0,28},{29,1},{... | collective-permute-start | bytes 798728 | tf_op jit(solution)/shard_map/ppermute | solution.py:24
  8.0 3.1 %own_int_products_0.1 = (f32[1536,256]{1,0:T(8,128)S(1)}, s16[1040,128]{1,0:T(8,128)(2,1)S(1)}, s16[1040,128]{1,0:T(8,128)(2,1)S(1)}, bf16[512,2048]{1,0:T(8,128)(2,1)S(1)}) custom-call(f32[8,1536]{1,0:T(8,128)S(1)} %get-tuple-element.58.a_rows_ref, f32[8,1536]{1,0:T(8,128)S(1)} %get-tuple-element.77.b_rows_ref, bf16[1,2048,1536]{2,1,0:T(8,128)(2,1)S(1)} %bitcast.4, ...), custom_call_target="tpu_custom_call" | custom-call | flops 1 | bytes 1 | tf_op jit(solution)/shard_map/own_int_products_0/pallas_call | solution.py:32
  11.1 3.0 %collective-permute-done.ext_ref = s16[1040,128]{1,0:T(8,128)(2,1)S(1)} collective-permute-done((s16[1040,128]{1,0:T(8,128)(2,1)S(1)}, s16[1040,128]{1,0:T(8,128)(2,1)S(1)}, u32[]{:S(2)}, u32[]{:S(2)}) %collective-permute-start) | collective-permute-done | bytes 266272 | tf_op jit(solution)/shard_map/ppermute | solution.py:24
  14.1 0.4 join_0_0.1
  14.5 3.1 %collective-permute-start.2 = (s16[784,128]{1,0:T(8,128)(2,1)S(1)}, s16[784,128]{1,0:T(8,128)(2,1)S(1)}, u32[]{:S(2)}, u32[]{:S(2)}) collective-permute-start(s16[784,128]{1,0:T(8,128)(2,1)S(1)} %get-tuple-element.71), channel_id=1, source_target_pairs={{1,0},{0,1},{3,2},{2,3},{5,4},{4,5},{7,6},{6,7},{9,8},{8,9},{11,10... | collective-permute-start | bytes 602120 | tf_op jit(solution)/shard_map/ppermute | solution.py:24
  17.6 0.7 %collective-permute-start.3 = (s16[1040,128]{1,0:T(8,128)(2,1)S(1)}, s16[1040,128]{1,0:T(8,128)(2,1)S(1)}, u32[]{:S(2)}, u32[]{:S(2)}) collective-permute-start(s16[1040,128]{1,0:T(8,128)(2,1)S(1)} %get-tuple-element.74), channel_id=1, source_target_pairs={{28,0},{8,4},{4,8},{16,12},{12,16},{24,20},{20,24},{0,28},{29,1},{... | collective-permute-start | bytes 798728 | tf_op jit(solution)/shard_map/ppermute | solution.py:24
  18.4 3.0 %ext_int_products_1.1 = (s16[1040,128]{1,0:T(8,128)(2,1)S(1)}, s16[1040,128]{1,0:T(8,128)(2,1)S(1)}, s16[1040,128]{1,0:T(8,128)(2,1)S(1)}, s16[1040,128]{1,0:T(8,128)(2,1)S(1)}) custom-call(f32[8,1536]{1,0:T(8,128)S(1)} %get-tuple-element.58.a_rows_ref, f32[8,1536]{1,0:T(8,128)S(1)} %get-tuple-element.77.b_rows_ref, bf16[1,2048,1536]{2,1,0:T(8,128)(2,1)S(1)} %bitcast.4, ...), custom_call_target="tpu_custom_call" | custom-call | flops 1 | bytes 1 | tf_op jit(solution)/shard_map/ext_int_products_1/pallas_call | solution.py:32
  21.4 2.0 %collective-permute-start.6 = (s16[1040,128]{1,0:T(8,128)(2,1)S(1)}, s16[1040,128]{1,0:T(8,128)(2,1)S(1)}, u32[]{:S(2)}, u32[]{:S(2)}) collective-permute-start(s16[1040,128]{1,0:T(8,128)(2,1)S(1)} %get-tuple-element.83), channel_id=1, source_target_pairs={{28,0},{8,4},{4,8},{16,12},{12,16},{24,20},{20,24},{0,28},{29,1},{... | collective-permute-start | bytes 798728 | tf_op jit(solution)/shard_map/ppermute | solution.py:24
  23.5 2.7 %collective-permute-start.5 = (s16[400,128]{1,0:T(8,128)(2,1)S(1)}, s16[400,128]{1,0:T(8,128)(2,1)S(1)}, u32[]{:S(2)}, u32[]{:S(2)}) collective-permute-start(s16[400,128]{1,0:T(8,128)(2,1)S(1)} %get-tuple-element.79), channel_id=1, source_target_pairs={{2,0},{3,1},{0,2},{1,3},{6,4},{7,5},{4,6},{5,7},{10,8},{11,9},{8,1... | collective-permute-start | bytes 307208 | tf_op jit(solution)/shard_map/ppermute | solution.py:24
  26.2 0.7 %collective-permute-done.3.ext_ref = s16[1040,128]{1,0:T(8,128)(2,1)S(1)} collective-permute-done((s16[1040,128]{1,0:T(8,128)(2,1)S(1)}, s16[1040,128]{1,0:T(8,128)(2,1)S(1)}, u32[]{:S(2)}, u32[]{:S(2)}) %collective-permute-start.3) | collective-permute-done | bytes 266272 | tf_op jit(solution)/shard_map/ppermute | solution.py:24
  26.9 0.4 join_0_128.1
  27.3 0.4 collective-permute-start.8
  27.8 4.2 %collective-permute-done.5.rest_0_ = s16[400,128]{1,0:T(8,128)(2,1)S(1)} collective-permute-done((s16[400,128]{1,0:T(8,128)(2,1)S(1)}, s16[400,128]{1,0:T(8,128)(2,1)S(1)}, u32[]{:S(2)}, u32[]{:S(2)}) %collective-permute-start.5) | collective-permute-done | bytes 102432 | tf_op jit(solution)/shard_map/ppermute | solution.py:24
  32.0 1.8 %own_products_1.1.own_ref = f32[1536,256]{1,0:T(8,128)S(1)} custom-call(f32[8,1536]{1,0:T(8,128)S(1)} %get-tuple-element.58.a_rows_ref, f32[8,1536]{1,0:T(8,128)S(1)} %get-tuple-element.77.b_rows_ref, bf16[1,2048,1536]{2,1,0:T(8,128)(2,1)S(1)} %bitcast.4, bf16[1024,2048]{1,0:T(8,128)(2,1)S(1)} %get-tuple-element.62.ext_rows_ref, ...), custom_call_target="tpu_custom_call" | custom-call | flops 1 | bytes 1 | tf_op jit(solution)/shard_map/own_products_1/pallas_call | solution.py:32
  33.9 0.6 join_1_0.1
  34.5 1.3 %collective-permute-done.8.got_ref = s16[784,128]{1,0:T(8,128)(2,1)S(1)} collective-permute-done((s16[784,128]{1,0:T(8,128)(2,1)S(1)}, s16[784,128]{1,0:T(8,128)(2,1)S(1)}, u32[]{:S(2)}, u32[]{:S(2)}) %collective-permute-start.8) | collective-permute-done | bytes 200736 | tf_op jit(solution)/shard_map/ppermute | solution.py:24
  36.1 2.0 %collective-permute-start.11 = (s16[400,128]{1,0:T(8,128)(2,1)S(1)}, s16[400,128]{1,0:T(8,128)(2,1)S(1)}, u32[]{:S(2)}, u32[]{:S(2)}) collective-permute-start(s16[400,128]{1,0:T(8,128)(2,1)S(1)} %get-tuple-element.93), channel_id=1, source_target_pairs={{2,0},{3,1},{0,2},{1,3},{6,4},{7,5},{4,6},{5,7},{10,8},{11,9},{8,1... | collective-permute-start | bytes 307208 | tf_op jit(solution)/shard_map/ppermute | solution.py:24
  38.0 0.4 join_1_128.1
  38.4 0.4 collective-permute-start.13
  38.8 2.6 %collective-permute-start.14 = (s16[400,128]{1,0:T(8,128)(2,1)S(1)}, s16[400,128]{1,0:T(8,128)(2,1)S(1)}, u32[]{:S(2)}, u32[]{:S(2)}) collective-permute-start(s16[400,128]{1,0:T(8,128)(2,1)S(1)} %get-tuple-element.101), channel_id=1, source_target_pairs={{2,0},{3,1},{0,2},{1,3},{6,4},{7,5},{4,6},{5,7},{10,8},{11,9},{8,1... | collective-permute-start | bytes 307208 | tf_op jit(solution)/shard_map/ppermute | solution.py:24
  41.4 1.5 %collective-permute-start.15 = (s16[400,128]{1,0:T(8,128)(2,1)S(1)}, s16[400,128]{1,0:T(8,128)(2,1)S(1)}, u32[]{:S(2)}, u32[]{:S(2)}) collective-permute-start(s16[400,128]{1,0:T(8,128)(2,1)S(1)} %get-tuple-element.102), channel_id=1, source_target_pairs={{3,0},{2,1},{1,2},{0,3},{7,4},{6,5},{5,6},{4,7},{11,8},{10,9},{9,1... | collective-permute-start | bytes 307208 | tf_op jit(solution)/shard_map/ppermute | solution.py:24
  43.0 3.1 %collective-permute-done.12.got_ref = s16[784,128]{1,0:T(8,128)(2,1)S(1)} collective-permute-done((s16[784,128]{1,0:T(8,128)(2,1)S(1)}, s16[784,128]{1,0:T(8,128)(2,1)S(1)}, u32[]{:S(2)}, u32[]{:S(2)}) %collective-permute-start.12) | collective-permute-done | bytes 200736 | tf_op jit(solution)/shard_map/ppermute | solution.py:24
  46.2 1.0 %collective-permute-start.16 = (s16[400,128]{1,0:T(8,128)(2,1)S(1)}, s16[400,128]{1,0:T(8,128)(2,1)S(1)}, u32[]{:S(2)}, u32[]{:S(2)}) collective-permute-start(s16[400,128]{1,0:T(8,128)(2,1)S(1)} %get-tuple-element.105), channel_id=1, source_target_pairs={{2,0},{3,1},{0,2},{1,3},{6,4},{7,5},{4,6},{5,7},{10,8},{11,9},{8,1... | collective-permute-start | bytes 307208 | tf_op jit(solution)/shard_map/ppermute | solution.py:24
  47.2 1.3 %collective-permute-done.13.rest_0_ = s16[400,128]{1,0:T(8,128)(2,1)S(1)} collective-permute-done((s16[400,128]{1,0:T(8,128)(2,1)S(1)}, s16[400,128]{1,0:T(8,128)(2,1)S(1)}, u32[]{:S(2)}, u32[]{:S(2)}) %collective-permute-start.13) | collective-permute-done | bytes 102432 | tf_op jit(solution)/shard_map/ppermute | solution.py:24
  48.5 3.5 %collective-permute-done.15.rest_2_ = s16[400,128]{1,0:T(8,128)(2,1)S(1)} collective-permute-done((s16[400,128]{1,0:T(8,128)(2,1)S(1)}, s16[400,128]{1,0:T(8,128)(2,1)S(1)}, u32[]{:S(2)}, u32[]{:S(2)}) %collective-permute-start.15) | collective-permute-done | bytes 102432 | tf_op jit(solution)/shard_map/ppermute | solution.py:24
  52.1 5.3 %collective-permute-done.16.rest_0_ = s16[400,128]{1,0:T(8,128)(2,1)S(1)} collective-permute-done((s16[400,128]{1,0:T(8,128)(2,1)S(1)}, s16[400,128]{1,0:T(8,128)(2,1)S(1)}, u32[]{:S(2)}, u32[]{:S(2)}) %collective-permute-start.16) | collective-permute-done | bytes 102432 | tf_op jit(solution)/shard_map/ppermute | solution.py:24
  57.5 2.1 %collective-permute-start.19 = (f32[8,512]{1,0:T(8,128)S(1)}, f32[8,512]{1,0:T(8,128)S(1)}, u32[]{:S(2)}, u32[]{:S(2)}) collective-permute-start(f32[8,512]{1,0:T(8,128)S(1)} %get-tuple-element.108.refs_4_), channel_id=1, source_target_pairs={{3,0},{2,1},{1,2},{0,3},{7,4},{6,5},{5,6},{4,7},{11,8},{10,9},{9,1... | collective-permute-start | bytes 49160 | tf_op jit(solution)/shard_map/ppermute | solution.py:24
  59.6 2.3 %collective-permute-start.17 = (f32[8,512]{1,0:T(8,128)S(1)}, f32[8,512]{1,0:T(8,128)S(1)}, u32[]{:S(2)}, u32[]{:S(2)}) collective-permute-start(f32[8,512]{1,0:T(8,128)S(1)} %get-tuple-element.108.refs_4_), channel_id=1, source_target_pairs={{1,0},{0,1},{3,2},{2,3},{5,4},{4,5},{7,6},{6,7},{9,8},{8,9},{11,10... | collective-permute-start | bytes 49160 | tf_op jit(solution)/shard_map/ppermute | solution.py:24
  61.9 1.1 %collective-permute-done.19.refs_7_ = f32[8,512]{1,0:T(8,128)S(1)} collective-permute-done((f32[8,512]{1,0:T(8,128)S(1)}, f32[8,512]{1,0:T(8,128)S(1)}, u32[]{:S(2)}, u32[]{:S(2)}) %collective-permute-start.19) | collective-permute-done | bytes 16416 | tf_op jit(solution)/shard_map/ppermute | solution.py:24
  63.0 1.1 %collective-permute-done.18.refs_6_ = f32[8,512]{1,0:T(8,128)S(1)} collective-permute-done((f32[8,512]{1,0:T(8,128)S(1)}, f32[8,512]{1,0:T(8,128)S(1)}, u32[]{:S(2)}, u32[]{:S(2)}) %collective-permute-start.18) | collective-permute-done | bytes 16416 | tf_op jit(solution)/shard_map/ppermute | solution.py:24
  64.2 1.0 %rescale.1 = f32[1,384,512]{2,1,0:T(8,128)} custom-call(f32[384,128]{1,0:T(8,128)S(1)} %get-tuple-element.80.refs_0_, f32[384,128]{1,0:T(8,128)S(1)} %get-tuple-element.94.refs_1_, f32[384,128]{1,0:T(8,128)S(1)} %get-tuple-element.106.refs_2_, f32[384,128]{1,0:T(8,128)S(1)} %get-tuple-element.107.refs_3_, f32[8,512]{1,0:T(8,128)S(1)} %get-tuple-element.108.refs_4_, ...), custom_call_target="tpu_custom_call" | custom-call | flops 1 | bytes 1 | tf_op jit(solution)/shard_map/rescale/pallas_call | solution.py:32
  (31 shorter events, 1.2 us)
Async XLA Ops:
  0.0 8.0 %slice-start = ((s8[6291456]{0:T(1024)(128)(4,1)}), s8[4194304]{0:T(1024)(128)(4,1)S(1)}, s32[]{:S(2)}) async-start(s8[6291456]{0:T(1024)(128)(4,1)} %bitcast.3), calls=%async_computation | async-start | bytes 8388608
  0.0 8.0 %slice-start.1 = ((s8[6291456]{0:T(1024)(128)(4,1)}), s8[2097152]{0:T(1024)(128)(4,1)S(1)}, s32[]{:S(2)}) async-start(s8[6291456]{0:T(1024)(128)(4,1)} %bitcast.3), calls=%async_computation.1 | async-start | bytes 4194304
  0.0 8.0 %copy-start = (bf16[1,2048,1536]{2,1,0:T(8,128)(2,1)S(1)}, bf16[1,2048,1536]{2,1,0:T(8,128)(2,1)}, u32[]{:S(2)}) copy-start(bf16[1,2048,1536]{2,1,0:T(8,128)(2,1)} %side_ref.1) | copy-start | bytes 18874372
  4.6 9.5 %collective-permute-start = (s16[1040,128]{1,0:T(8,128)(2,1)S(1)}, s16[1040,128]{1,0:T(8,128)(2,1)S(1)}, u32[]{:S(2)}, u32[]{:S(2)}) collective-permute-start(s16[1040,128]{1,0:T(8,128)(2,1)S(1)} %get-tuple-element.60), channel_id=1, source_target_pairs={{28,0},{8,4},{4,8},{16,12},{12,16},{24,20},{20,24},{0,28},{29,1},{... | collective-permute-start | bytes 798728 | tf_op jit(solution)/shard_map/ppermute | solution.py:24
  11.1 3.0 %collective-permute-start.1 = (s16[1040,128]{1,0:T(8,128)(2,1)S(1)}, s16[1040,128]{1,0:T(8,128)(2,1)S(1)}, u32[]{:S(2)}, u32[]{:S(2)}) collective-permute-start(s16[1040,128]{1,0:T(8,128)(2,1)S(1)} %get-tuple-element.63), channel_id=1, source_target_pairs={{4,0},{0,4},{12,8},{8,12},{20,16},{16,20},{28,24},{24,28},{5,1},{1... | collective-permute-start | bytes 798728 | tf_op jit(solution)/shard_map/ppermute | solution.py:24
  14.5 8.8 %collective-permute-start.2 = (s16[784,128]{1,0:T(8,128)(2,1)S(1)}, s16[784,128]{1,0:T(8,128)(2,1)S(1)}, u32[]{:S(2)}, u32[]{:S(2)}) collective-permute-start(s16[784,128]{1,0:T(8,128)(2,1)S(1)} %get-tuple-element.71), channel_id=1, source_target_pairs={{1,0},{0,1},{3,2},{2,3},{5,4},{4,5},{7,6},{6,7},{9,8},{8,9},{11,10... | collective-permute-start | bytes 602120 | tf_op jit(solution)/shard_map/ppermute | solution.py:24
  17.6 9.3 %collective-permute-start.3 = (s16[1040,128]{1,0:T(8,128)(2,1)S(1)}, s16[1040,128]{1,0:T(8,128)(2,1)S(1)}, u32[]{:S(2)}, u32[]{:S(2)}) collective-permute-start(s16[1040,128]{1,0:T(8,128)(2,1)S(1)} %get-tuple-element.74), channel_id=1, source_target_pairs={{28,0},{8,4},{4,8},{16,12},{12,16},{24,20},{20,24},{0,28},{29,1},{... | collective-permute-start | bytes 798728 | tf_op jit(solution)/shard_map/ppermute | solution.py:24
  18.4 8.5 %collective-permute-start.4 = (s16[1040,128]{1,0:T(8,128)(2,1)S(1)}, s16[1040,128]{1,0:T(8,128)(2,1)S(1)}, u32[]{:S(2)}, u32[]{:S(2)}) collective-permute-start(s16[1040,128]{1,0:T(8,128)(2,1)S(1)} %get-tuple-element.75), channel_id=1, source_target_pairs={{4,0},{0,4},{12,8},{8,12},{20,16},{16,20},{28,24},{24,28},{5,1},{1... | collective-permute-start | bytes 798728 | tf_op jit(solution)/shard_map/ppermute | solution.py:24
  21.4 12.5 %collective-permute-start.6 = (s16[1040,128]{1,0:T(8,128)(2,1)S(1)}, s16[1040,128]{1,0:T(8,128)(2,1)S(1)}, u32[]{:S(2)}, u32[]{:S(2)}) collective-permute-start(s16[1040,128]{1,0:T(8,128)(2,1)S(1)} %get-tuple-element.83), channel_id=1, source_target_pairs={{28,0},{8,4},{4,8},{16,12},{12,16},{24,20},{20,24},{0,28},{29,1},{... | collective-permute-start | bytes 798728 | tf_op jit(solution)/shard_map/ppermute | solution.py:24
  23.3 10.5 %collective-permute-start.7 = (s16[1040,128]{1,0:T(8,128)(2,1)S(1)}, s16[1040,128]{1,0:T(8,128)(2,1)S(1)}, u32[]{:S(2)}, u32[]{:S(2)}) collective-permute-start(s16[1040,128]{1,0:T(8,128)(2,1)S(1)} %get-tuple-element.69), channel_id=1, source_target_pairs={{4,0},{0,4},{12,8},{8,12},{20,16},{16,20},{28,24},{24,28},{5,1},{1... | collective-permute-start | bytes 798728 | tf_op jit(solution)/shard_map/ppermute | solution.py:24
  23.5 8.4 %collective-permute-start.5 = (s16[400,128]{1,0:T(8,128)(2,1)S(1)}, s16[400,128]{1,0:T(8,128)(2,1)S(1)}, u32[]{:S(2)}, u32[]{:S(2)}) collective-permute-start(s16[400,128]{1,0:T(8,128)(2,1)S(1)} %get-tuple-element.79), channel_id=1, source_target_pairs={{2,0},{3,1},{0,2},{1,3},{6,4},{7,5},{4,6},{5,7},{10,8},{11,9},{8,1... | collective-permute-start | bytes 307208 | tf_op jit(solution)/shard_map/ppermute | solution.py:24
  27.3 8.6 %collective-permute-start.8 = (s16[784,128]{1,0:T(8,128)(2,1)S(1)}, s16[784,128]{1,0:T(8,128)(2,1)S(1)}, u32[]{:S(2)}, u32[]{:S(2)}) collective-permute-start(s16[784,128]{1,0:T(8,128)(2,1)S(1)} %get-tuple-element.86), channel_id=1, source_target_pairs={{1,0},{0,1},{3,2},{2,3},{5,4},{4,5},{7,6},{6,7},{9,8},{8,9},{11,10... | collective-permute-start | bytes 602120 | tf_op jit(solution)/shard_map/ppermute | solution.py:24
  27.7 10.4 %collective-permute-start.9 = (s16[1040,128]{1,0:T(8,128)(2,1)S(1)}, s16[1040,128]{1,0:T(8,128)(2,1)S(1)}, u32[]{:S(2)}, u32[]{:S(2)}) collective-permute-start(s16[1040,128]{1,0:T(8,128)(2,1)S(1)} %get-tuple-element.89), channel_id=1, source_target_pairs={{28,0},{8,4},{4,8},{16,12},{12,16},{24,20},{20,24},{0,28},{29,1},{... | collective-permute-start | bytes 798728 | tf_op jit(solution)/shard_map/ppermute | solution.py:24
  31.9 6.1 %collective-permute-start.10 = (s16[1040,128]{1,0:T(8,128)(2,1)S(1)}, s16[1040,128]{1,0:T(8,128)(2,1)S(1)}, u32[]{:S(2)}, u32[]{:S(2)}) collective-permute-start(s16[1040,128]{1,0:T(8,128)(2,1)S(1)} %get-tuple-element.90), channel_id=1, source_target_pairs={{4,0},{0,4},{12,8},{8,12},{20,16},{16,20},{28,24},{24,28},{5,1},{1... | collective-permute-start | bytes 798728 | tf_op jit(solution)/shard_map/ppermute | solution.py:24
  34.5 11.6 %collective-permute-start.12 = (s16[784,128]{1,0:T(8,128)(2,1)S(1)}, s16[784,128]{1,0:T(8,128)(2,1)S(1)}, u32[]{:S(2)}, u32[]{:S(2)}) collective-permute-start(s16[784,128]{1,0:T(8,128)(2,1)S(1)} %get-tuple-element.97), channel_id=1, source_target_pairs={{1,0},{0,1},{3,2},{2,3},{5,4},{4,5},{7,6},{6,7},{9,8},{8,9},{11,10... | collective-permute-start | bytes 602120 | tf_op jit(solution)/shard_map/ppermute | solution.py:24
  36.1 6.8 %collective-permute-start.11 = (s16[400,128]{1,0:T(8,128)(2,1)S(1)}, s16[400,128]{1,0:T(8,128)(2,1)S(1)}, u32[]{:S(2)}, u32[]{:S(2)}) collective-permute-start(s16[400,128]{1,0:T(8,128)(2,1)S(1)} %get-tuple-element.93), channel_id=1, source_target_pairs={{2,0},{3,1},{0,2},{1,3},{6,4},{7,5},{4,6},{5,7},{10,8},{11,9},{8,1... | collective-permute-start | bytes 307208 | tf_op jit(solution)/shard_map/ppermute | solution.py:24
  38.4 10.1 %collective-permute-start.13 = (s16[400,128]{1,0:T(8,128)(2,1)S(1)}, s16[400,128]{1,0:T(8,128)(2,1)S(1)}, u32[]{:S(2)}, u32[]{:S(2)}) collective-permute-start(s16[400,128]{1,0:T(8,128)(2,1)S(1)} %get-tuple-element.100), channel_id=1, source_target_pairs={{1,0},{0,1},{3,2},{2,3},{5,4},{4,5},{7,6},{6,7},{9,8},{8,9},{11,10... | collective-permute-start | bytes 307208 | tf_op jit(solution)/shard_map/ppermute | solution.py:24
  38.8 9.7 %collective-permute-start.14 = (s16[400,128]{1,0:T(8,128)(2,1)S(1)}, s16[400,128]{1,0:T(8,128)(2,1)S(1)}, u32[]{:S(2)}, u32[]{:S(2)}) collective-permute-start(s16[400,128]{1,0:T(8,128)(2,1)S(1)} %get-tuple-element.101), channel_id=1, source_target_pairs={{2,0},{3,1},{0,2},{1,3},{6,4},{7,5},{4,6},{5,7},{10,8},{11,9},{8,1... | collective-permute-start | bytes 307208 | tf_op jit(solution)/shard_map/ppermute | solution.py:24
  41.4 10.6 %collective-permute-start.15 = (s16[400,128]{1,0:T(8,128)(2,1)S(1)}, s16[400,128]{1,0:T(8,128)(2,1)S(1)}, u32[]{:S(2)}, u32[]{:S(2)}) collective-permute-start(s16[400,128]{1,0:T(8,128)(2,1)S(1)} %get-tuple-element.102), channel_id=1, source_target_pairs={{3,0},{2,1},{1,2},{0,3},{7,4},{6,5},{5,6},{4,7},{11,8},{10,9},{9,1... | collective-permute-start | bytes 307208 | tf_op jit(solution)/shard_map/ppermute | solution.py:24
  46.2 11.2 %collective-permute-start.16 = (s16[400,128]{1,0:T(8,128)(2,1)S(1)}, s16[400,128]{1,0:T(8,128)(2,1)S(1)}, u32[]{:S(2)}, u32[]{:S(2)}) collective-permute-start(s16[400,128]{1,0:T(8,128)(2,1)S(1)} %get-tuple-element.105), channel_id=1, source_target_pairs={{2,0},{3,1},{0,2},{1,3},{6,4},{7,5},{4,6},{5,7},{10,8},{11,9},{8,1... | collective-permute-start | bytes 307208 | tf_op jit(solution)/shard_map/ppermute | solution.py:24
  57.5 5.6 %collective-permute-start.19 = (f32[8,512]{1,0:T(8,128)S(1)}, f32[8,512]{1,0:T(8,128)S(1)}, u32[]{:S(2)}, u32[]{:S(2)}) collective-permute-start(f32[8,512]{1,0:T(8,128)S(1)} %get-tuple-element.108.refs_4_), channel_id=1, source_target_pairs={{3,0},{2,1},{1,2},{0,3},{7,4},{6,5},{5,6},{4,7},{11,8},{10,9},{9,1... | collective-permute-start | bytes 49160 | tf_op jit(solution)/shard_map/ppermute | solution.py:24
  59.5 4.6 %collective-permute-start.18 = (f32[8,512]{1,0:T(8,128)S(1)}, f32[8,512]{1,0:T(8,128)S(1)}, u32[]{:S(2)}, u32[]{:S(2)}) collective-permute-start(f32[8,512]{1,0:T(8,128)S(1)} %get-tuple-element.108.refs_4_), channel_id=1, source_target_pairs={{2,0},{3,1},{0,2},{1,3},{6,4},{7,5},{4,6},{5,7},{10,8},{11,9},{8,1... | collective-permute-start | bytes 49160 | tf_op jit(solution)/shard_map/ppermute | solution.py:24
  59.6 4.6 %collective-permute-start.17 = (f32[8,512]{1,0:T(8,128)S(1)}, f32[8,512]{1,0:T(8,128)S(1)}, u32[]{:S(2)}, u32[]{:S(2)}) collective-permute-start(f32[8,512]{1,0:T(8,128)S(1)} %get-tuple-element.108.refs_4_), channel_id=1, source_target_pairs={{1,0},{0,1},{3,2},{2,3},{5,4},{4,5},{7,6},{6,7},{9,8},{8,9},{11,10... | collective-permute-start | bytes 49160 | tf_op jit(solution)/shard_map/ppermute | solution.py:24

commit v15 on v11

--- a/solution.py
+++ b/solution.py
@@ -353,25 +353,26 @@
     )
 
 
-def square_kernel(kept_ref, got_ref, *rest):
-    earlier, (square_ref, sums_ref) = rest[:-2], rest[-2:]
+def square_kernel(place, kept_ref, got_ref, *rest):
+    others, (square_ref, sums_ref) = rest[:-2], rest[-2:]
     value = kept_ref[0] + decode(got_ref[HEAD:, :], scales(got_ref[0:HEAD, :])[0:1])
     square = value * value
     square_ref[...] = square
     sums = jnp.broadcast_to(jnp.sum(square, axis=0, keepdims=True), (8, square.shape[1]))
-    sums_ref[...] = jnp.concatenate([ref[...] for ref in earlier] + [sums], axis=1)
-
-
-def square(kept, got, earlier, chunk):
+    every = [ref[...] for ref in others]
+    sums_ref[...] = jnp.concatenate(every[:place] + [sums] + every[place:], axis=1)
+
+
+def square(kept, got, others, place, chunk):
     _, rows, width = kept.shape
     return call(
-        square_kernel,
+        functools.partial(square_kernel, place),
         f"square_{chunk}",
-        (kept, got, *earlier),
-        [IN_VMEM] * (2 + len(earlier)),
+        (kept, got, *others),
+        [IN_VMEM] * (2 + len(others)),
         [
             jax.ShapeDtypeStruct((rows, width), jnp.float32),
-            jax.ShapeDtypeStruct((8, width + sum(sums.shape[1] for sums in earlier)), jnp.float32),
+            jax.ShapeDtypeStruct((8, width + sum(sums.shape[1] for sums in others)), jnp.float32),
         ],
     )
 
@@ -416,7 +417,7 @@
 
     halves = panel // BS
     fine = (LANES,) * (BS // LANES)
-    widths = [(BS,)] * (halves - 1) + [fine]
+    widths = [fine] * halves
     ext, ints, owns, latest = [], [], [], []
 
     def ordered(value):
@@ -447,7 +448,7 @@
         owns.extend(products(a_rows, ordered(b_rows), graph, ext_rows, int_rows, half, {"own": (BS,)}))
         latest.append(owns[-1])
 
-    strips, squares, sums = [], [], []
+    strips, squares, sums = [], {}, {}
     places = [(half, i) for half, each in enumerate(widths) for i in range(len(each))]
     chunks = len(places)
 
@@ -470,26 +471,29 @@
 
     def finish(chunk):
         kept, got = strips[chunk]
-        squared, summed = square(ordered(kept), got, sums if chunk == chunks - 1 else [], chunk)
-        latest.append(summed)
-        squares.append(squared)
-        sums.append(summed)
-
-    for half in range(1, halves):
-        side_products(half)
-        add_up(half - 1)
-        own_products(half)
+        others, place = ([], 0)
+        if len(squares) == chunks - 1:
+            others, place = [sums[i] for i in sorted(sums)], chunk
+        squares[chunk], sums[chunk] = square(ordered(kept), got, others, place, chunk)
+        latest.append(sums[chunk])
+
+    side_products(1)
+    add_up(0)
+    add_up(1)
+    own_products(1)
     scatter(0)
-    for chunk in range(halves - 1, chunks):
-        add_up(chunk)
     scatter(1)
+    add_up(2)
     finish(0)
-    for chunk in range(2, chunks):
-        scatter(chunk)
-    for chunk in range(1, chunks):
-        finish(chunk)
-
-    mine = sums[-1]
+    add_up(3)
+    finish(1)
+    scatter(2)
+    scatter(3)
+    finish(2)
+    finish(3)
+
+    squares = [squares[i] for i in sorted(squares)]
+    mine = sums[3]
     others = [swap(mine, "layer", lambda i: i ^ other) for other in range(1, layers)]
     return rescale(squares, [mine, *others], width)
 

time: 66.1 us -> 66.2 us (level)
  the two profiles are of different devices: /device:TPU:14 before, /device:TPU:0 now
where the time goes in v15:
time: 66.2 us; the launch traced here: 65 us
  waiting for transfers between devices  25.2 us (38%)
  starting transfers between devices  23.7 us (36%)
  Pallas kernels  16 us (24%)
    ppermute x15, waiting for transfers between devices, swap(): lax.ppermute(block, axis, [(partner(i), i) for i in range(lax.axis_size(a...  25.2 us
    ppermute x15, starting transfers between devices, swap(): lax.ppermute(block, axis, [(partner(i), i) for i in range(lax.axis_size(a...  23.7 us
    pallas_call x17, Pallas kernels, call(): pl.pallas_call(kernel, out_shape=out_shape, in_specs=in_specs, out_specs=...  16 us
  transfers between devices with their start and end apart: 15, of which 8 were waited for; matrix products, arithmetic and copies ran while one was open for 0% of the time, Pallas kernels for 16%

profile of v15, /device:TPU:0, one launch (start us, length us, event | category | flops | bytes accessed | tf_op | source)
XLA Modules:
  0.0 65.0 jit_solution(17253898018082972304)
XLA Ops:
  0.0 4.5 %first_products.1 = (s16[1040,256]{1,0:T(8,128)(2,1)S(1)}, bf16[1024,2048]{1,0:T(8,128)(2,1)S(1)}, f32[8,1536]{1,0:T(8,128)S(1)}, f32[8,1536]{1,0:T(8,128)S(1)}, f32[6,512]{1,0:T(8,128)S(1)}) custom-call(s32[6,1,32]{2,1,0:T(1,128)} %bitcast.5, s32[6,1,32]{2,1,0:T(1,128)} %bitcast.6, s32[1,2,6]{2,1,0:T(2,128)} %bitcast.7, bf16[1,2048,1536]{2,1,0:T(8,128)(2,1)} %side_ref.1, ...), custom_call_target="tpu_custom_call" | custom-call | flops 1 | bytes 1 | tf_op jit(solution)/shard_map/first_products/pallas_call | solution.py:31
  4.6 3.4 %collective-permute-start = (s16[1040,256]{1,0:T(8,128)(2,1)S(1)}, s16[1040,256]{1,0:T(8,128)(2,1)S(1)}, u32[]{:S(2)}, u32[]{:S(2)}) collective-permute-start(s16[1040,256]{1,0:T(8,128)(2,1)S(1)} %get-tuple-element.57), channel_id=1, source_target_pairs={{28,0},{8,4},{4,8},{16,12},{12,16},{24,20},{20,24},{0,28},{29,1},{... | collective-permute-start | bytes 1597448 | tf_op jit(solution)/shard_map/ppermute | solution.py:23
  8.0 3.1 %own_int_products_0.1 = (f32[1536,256]{1,0:T(8,128)S(1)}, s16[1040,256]{1,0:T(8,128)(2,1)S(1)}, bf16[512,2048]{1,0:T(8,128)(2,1)S(1)}) custom-call(f32[8,1536]{1,0:T(8,128)S(1)} %get-tuple-element.55.a_rows_ref, f32[8,1536]{1,0:T(8,128)S(1)} %get-tuple-element.69.b_rows_ref, bf16[1,2048,1536]{2,1,0:T(8,128)(2,1)S(1)} %bitcast.4, ...), custom_call_target="tpu_custom_call" | custom-call | flops 1 | bytes 1 | tf_op jit(solution)/shard_map/own_int_products_0/pallas_call | solution.py:31
  11.1 3.0 %ext_int_products_1.1 = (s16[1040,256]{1,0:T(8,128)(2,1)S(1)}, s16[1040,256]{1,0:T(8,128)(2,1)S(1)}) custom-call(f32[8,1536]{1,0:T(8,128)S(1)} %get-tuple-element.55.a_rows_ref, f32[8,1536]{1,0:T(8,128)S(1)} %get-tuple-element.69.b_rows_ref, bf16[1,2048,1536]{2,1,0:T(8,128)(2,1)S(1)} %bitcast.4, bf16[1024,2048]{1,0:T(8,128)(2,1)S(1)} %get-tuple-element.59.ext_rows_ref, ...), custom_call_target="tpu_custom_call" | custom-call | flops 1 | bytes 1 | tf_op jit(solution)/shard_map/ext_int_products_1/pallas_call | solution.py:31
  14.1 0.5 collective-permute-start.5
  14.7 1.8 %collective-permute-start.4 = (s16[1040,256]{1,0:T(8,128)(2,1)S(1)}, s16[1040,256]{1,0:T(8,128)(2,1)S(1)}, u32[]{:S(2)}, u32[]{:S(2)}) collective-permute-start(s16[1040,256]{1,0:T(8,128)(2,1)S(1)} %get-tuple-element.63), channel_id=1, source_target_pairs={{28,0},{8,4},{4,8},{16,12},{12,16},{24,20},{20,24},{0,28},{29,1},{... | collective-permute-start | bytes 1597448 | tf_op jit(solution)/shard_map/ppermute | solution.py:23
  16.5 3.9 %collective-permute-done.ext_ref = s16[1040,256]{1,0:T(8,128)(2,1)S(1)} collective-permute-done((s16[1040,256]{1,0:T(8,128)(2,1)S(1)}, s16[1040,256]{1,0:T(8,128)(2,1)S(1)}, u32[]{:S(2)}, u32[]{:S(2)}) %collective-permute-start) | collective-permute-done | bytes 532512 | tf_op jit(solution)/shard_map/ppermute | solution.py:23
  20.5 0.4 join_0_0.1
  20.9 2.5 %collective-permute-start.2 = (s16[784,128]{1,0:T(8,128)(2,1)S(1)}, s16[784,128]{1,0:T(8,128)(2,1)S(1)}, u32[]{:S(2)}, u32[]{:S(2)}) collective-permute-start(s16[784,128]{1,0:T(8,128)(2,1)S(1)} %get-tuple-element.71), channel_id=1, source_target_pairs={{1,0},{0,1},{3,2},{2,3},{5,4},{4,5},{7,6},{6,7},{9,8},{8,9},{11,10... | collective-permute-start | bytes 602120 | tf_op jit(solution)/shard_map/ppermute | solution.py:23
  23.3 0.4 join_0_128.1
  23.7 0.1 collective-permute-start.3
  23.8 1.8 %own_products_1.1.own_ref = f32[1536,256]{1,0:T(8,128)S(1)} custom-call(f32[8,1536]{1,0:T(8,128)S(1)} %get-tuple-element.55.a_rows_ref, f32[8,1536]{1,0:T(8,128)S(1)} %get-tuple-element.69.b_rows_ref, bf16[1,2048,1536]{2,1,0:T(8,128)(2,1)S(1)} %bitcast.4, bf16[1024,2048]{1,0:T(8,128)(2,1)S(1)} %get-tuple-element.59.ext_rows_ref, ...), custom_call_target="tpu_custom_call" | custom-call | flops 1 | bytes 1 | tf_op jit(solution)/shard_map/own_products_1/pallas_call | solution.py:31
  25.6 4.7 %collective-permute-done.2.got_ref = s16[784,128]{1,0:T(8,128)(2,1)S(1)} collective-permute-done((s16[784,128]{1,0:T(8,128)(2,1)S(1)}, s16[784,128]{1,0:T(8,128)(2,1)S(1)}, u32[]{:S(2)}, u32[]{:S(2)}) %collective-permute-start.2) | collective-permute-done | bytes 200736 | tf_op jit(solution)/shard_map/ppermute | solution.py:23
  30.3 0.2 halve_2_0.1
  30.5 2.0 %collective-permute-start.6 = (s16[400,128]{1,0:T(8,128)(2,1)S(1)}, s16[400,128]{1,0:T(8,128)(2,1)S(1)}, u32[]{:S(2)}, u32[]{:S(2)}) collective-permute-start(s16[400,128]{1,0:T(8,128)(2,1)S(1)} %get-tuple-element.80), channel_id=1, source_target_pairs={{2,0},{3,1},{0,2},{1,3},{6,4},{7,5},{4,6},{5,7},{10,8},{11,9},{8,1... | collective-permute-start | bytes 307208 | tf_op jit(solution)/shard_map/ppermute | solution.py:23
  32.5 0.2 halve_2_1.1
  32.7 0.4 join_1_0.1
  33.1 1.7 %collective-permute-start.8 = (s16[784,128]{1,0:T(8,128)(2,1)S(1)}, s16[784,128]{1,0:T(8,128)(2,1)S(1)}, u32[]{:S(2)}, u32[]{:S(2)}) collective-permute-start(s16[784,128]{1,0:T(8,128)(2,1)S(1)} %get-tuple-element.90), channel_id=1, source_target_pairs={{1,0},{0,1},{3,2},{2,3},{5,4},{4,5},{7,6},{6,7},{9,8},{8,9},{11,10... | collective-permute-start | bytes 602120 | tf_op jit(solution)/shard_map/ppermute | solution.py:23
  34.8 2.5 %collective-permute-done.6.got_ref = s16[400,128]{1,0:T(8,128)(2,1)S(1)} collective-permute-done((s16[400,128]{1,0:T(8,128)(2,1)S(1)}, s16[400,128]{1,0:T(8,128)(2,1)S(1)}, u32[]{:S(2)}, u32[]{:S(2)}) %collective-permute-start.6) | collective-permute-done | bytes 102432 | tf_op jit(solution)/shard_map/ppermute | solution.py:23
  37.4 0.4 join_1_128.1
  37.9 3.5 %collective-permute-start.7 = (s16[400,128]{1,0:T(8,128)(2,1)S(1)}, s16[400,128]{1,0:T(8,128)(2,1)S(1)}, u32[]{:S(2)}, u32[]{:S(2)}) collective-permute-start(s16[400,128]{1,0:T(8,128)(2,1)S(1)} %get-tuple-element.86), channel_id=1, source_target_pairs={{2,0},{3,1},{0,2},{1,3},{6,4},{7,5},{4,6},{5,7},{10,8},{11,9},{8,1... | collective-permute-start | bytes 307208 | tf_op jit(solution)/shard_map/ppermute | solution.py:23
  41.4 3.8 %collective-permute-done.7.got_ref = s16[400,128]{1,0:T(8,128)(2,1)S(1)} collective-permute-done((s16[400,128]{1,0:T(8,128)(2,1)S(1)}, s16[400,128]{1,0:T(8,128)(2,1)S(1)}, u32[]{:S(2)}, u32[]{:S(2)}) %collective-permute-start.7) | collective-permute-done | bytes 102432 | tf_op jit(solution)/shard_map/ppermute | solution.py:23
  45.3 0.2 halve_2_2.1
  45.5 3.5 %collective-permute-start.10 = (s16[400,128]{1,0:T(8,128)(2,1)S(1)}, s16[400,128]{1,0:T(8,128)(2,1)S(1)}, u32[]{:S(2)}, u32[]{:S(2)}) collective-permute-start(s16[400,128]{1,0:T(8,128)(2,1)S(1)} %get-tuple-element.96), channel_id=1, source_target_pairs={{2,0},{3,1},{0,2},{1,3},{6,4},{7,5},{4,6},{5,7},{10,8},{11,9},{8,1... | collective-permute-start | bytes 307208 | tf_op jit(solution)/shard_map/ppermute | solution.py:23
  49.0 0.2 halve_2_3.1
  49.3 5.8 %collective-permute-done.10.got_ref = s16[400,128]{1,0:T(8,128)(2,1)S(1)} collective-permute-done((s16[400,128]{1,0:T(8,128)(2,1)S(1)}, s16[400,128]{1,0:T(8,128)(2,1)S(1)}, u32[]{:S(2)}, u32[]{:S(2)}) %collective-permute-start.10) | collective-permute-done | bytes 102432 | tf_op jit(solution)/shard_map/ppermute | solution.py:23
  55.2 1.6 %collective-permute-done.11.got_ref = s16[400,128]{1,0:T(8,128)(2,1)S(1)} collective-permute-done((s16[400,128]{1,0:T(8,128)(2,1)S(1)}, s16[400,128]{1,0:T(8,128)(2,1)S(1)}, u32[]{:S(2)}, u32[]{:S(2)}) %collective-permute-start.11) | collective-permute-done | bytes 102432 | tf_op jit(solution)/shard_map/ppermute | solution.py:23
  56.9 2.5 %collective-permute-start.14 = (f32[8,512]{1,0:T(8,128)S(1)}, f32[8,512]{1,0:T(8,128)S(1)}, u32[]{:S(2)}, u32[]{:S(2)}) collective-permute-start(f32[8,512]{1,0:T(8,128)S(1)} %get-tuple-element.102.refs_4_), channel_id=1, source_target_pairs={{3,0},{2,1},{1,2},{0,3},{7,4},{6,5},{5,6},{4,7},{11,8},{10,9},{9,1... | collective-permute-start | bytes 49160 | tf_op jit(solution)/shard_map/ppermute | solution.py:23
  59.4 1.9 %collective-permute-start.12 = (f32[8,512]{1,0:T(8,128)S(1)}, f32[8,512]{1,0:T(8,128)S(1)}, u32[]{:S(2)}, u32[]{:S(2)}) collective-permute-start(f32[8,512]{1,0:T(8,128)S(1)} %get-tuple-element.102.refs_4_), channel_id=1, source_target_pairs={{1,0},{0,1},{3,2},{2,3},{5,4},{4,5},{7,6},{6,7},{9,8},{8,9},{11,10... | collective-permute-start | bytes 49160 | tf_op jit(solution)/shard_map/ppermute | solution.py:23
  61.4 1.1 %collective-permute-done.14.refs_7_ = f32[8,512]{1,0:T(8,128)S(1)} collective-permute-done((f32[8,512]{1,0:T(8,128)S(1)}, f32[8,512]{1,0:T(8,128)S(1)}, u32[]{:S(2)}, u32[]{:S(2)}) %collective-permute-start.14) | collective-permute-done | bytes 16416 | tf_op jit(solution)/shard_map/ppermute | solution.py:23
  62.5 1.5 %collective-permute-done.13.refs_6_ = f32[8,512]{1,0:T(8,128)S(1)} collective-permute-done((f32[8,512]{1,0:T(8,128)S(1)}, f32[8,512]{1,0:T(8,128)S(1)}, u32[]{:S(2)}, u32[]{:S(2)}) %collective-permute-start.13) | collective-permute-done | bytes 16416 | tf_op jit(solution)/shard_map/ppermute | solution.py:23
  64.0 1.0 %rescale.1 = f32[1,384,512]{2,1,0:T(8,128)} custom-call(f32[384,128]{1,0:T(8,128)S(1)} %get-tuple-element.81.refs_0_, f32[384,128]{1,0:T(8,128)S(1)} %get-tuple-element.87.refs_1_, f32[384,128]{1,0:T(8,128)S(1)} %get-tuple-element.97.refs_2_, f32[384,128]{1,0:T(8,128)S(1)} %get-tuple-element.101.refs_3_, f32[8,512]{1,0:T(8,128)S(1)} %get-tuple-element.102.refs_4_, ...), custom_call_target="tpu_custom_call" | custom-call | flops 1 | bytes 1 | tf_op jit(solution)/shard_map/rescale/pallas_call | solution.py:31
  (22 shorter events, 0.6 us)
Async XLA Ops:
  0.0 8.0 %slice-start = ((s8[6291456]{0:T(1024)(128)(4,1)}), s8[4194304]{0:T(1024)(128)(4,1)S(1)}, s32[]{:S(2)}) async-start(s8[6291456]{0:T(1024)(128)(4,1)} %bitcast.3), calls=%async_computation | async-start | bytes 8388608
  0.0 8.0 %slice-start.1 = ((s8[6291456]{0:T(1024)(128)(4,1)}), s8[2097152]{0:T(1024)(128)(4,1)S(1)}, s32[]{:S(2)}) async-start(s8[6291456]{0:T(1024)(128)(4,1)} %bitcast.3), calls=%async_computation.1 | async-start | bytes 4194304
  0.0 8.0 %copy-start = (bf16[1,2048,1536]{2,1,0:T(8,128)(2,1)S(1)}, bf16[1,2048,1536]{2,1,0:T(8,128)(2,1)}, u32[]{:S(2)}) copy-start(bf16[1,2048,1536]{2,1,0:T(8,128)(2,1)} %side_ref.1) | copy-start | bytes 18874372
  4.6 15.9 %collective-permute-start = (s16[1040,256]{1,0:T(8,128)(2,1)S(1)}, s16[1040,256]{1,0:T(8,128)(2,1)S(1)}, u32[]{:S(2)}, u32[]{:S(2)}) collective-permute-start(s16[1040,256]{1,0:T(8,128)(2,1)S(1)} %get-tuple-element.57), channel_id=1, source_target_pairs={{28,0},{8,4},{4,8},{16,12},{12,16},{24,20},{20,24},{0,28},{29,1},{... | collective-permute-start | bytes 1597448 | tf_op jit(solution)/shard_map/ppermute | solution.py:23
  11.1 9.4 %collective-permute-start.1 = (s16[1040,256]{1,0:T(8,128)(2,1)S(1)}, s16[1040,256]{1,0:T(8,128)(2,1)S(1)}, u32[]{:S(2)}, u32[]{:S(2)}) collective-permute-start(s16[1040,256]{1,0:T(8,128)(2,1)S(1)} %get-tuple-element.65), channel_id=1, source_target_pairs={{4,0},{0,4},{12,8},{8,12},{20,16},{16,20},{28,24},{24,28},{5,1},{1... | collective-permute-start | bytes 1597448 | tf_op jit(solution)/shard_map/ppermute | solution.py:23
  14.1 18.6 %collective-permute-start.5 = (s16[1040,256]{1,0:T(8,128)(2,1)S(1)}, s16[1040,256]{1,0:T(8,128)(2,1)S(1)}, u32[]{:S(2)}, u32[]{:S(2)}) collective-permute-start(s16[1040,256]{1,0:T(8,128)(2,1)S(1)} %get-tuple-element.77), channel_id=1, source_target_pairs={{4,0},{0,4},{12,8},{8,12},{20,16},{16,20},{28,24},{24,28},{5,1},{1... | collective-permute-start | bytes 1597448 | tf_op jit(solution)/shard_map/ppermute | solution.py:23
  14.7 18.1 %collective-permute-start.4 = (s16[1040,256]{1,0:T(8,128)(2,1)S(1)}, s16[1040,256]{1,0:T(8,128)(2,1)S(1)}, u32[]{:S(2)}, u32[]{:S(2)}) collective-permute-start(s16[1040,256]{1,0:T(8,128)(2,1)S(1)} %get-tuple-element.63), channel_id=1, source_target_pairs={{28,0},{8,4},{4,8},{16,12},{12,16},{24,20},{20,24},{0,28},{29,1},{... | collective-permute-start | bytes 1597448 | tf_op jit(solution)/shard_map/ppermute | solution.py:23
  20.9 9.5 %collective-permute-start.2 = (s16[784,128]{1,0:T(8,128)(2,1)S(1)}, s16[784,128]{1,0:T(8,128)(2,1)S(1)}, u32[]{:S(2)}, u32[]{:S(2)}) collective-permute-start(s16[784,128]{1,0:T(8,128)(2,1)S(1)} %get-tuple-element.71), channel_id=1, source_target_pairs={{1,0},{0,1},{3,2},{2,3},{5,4},{4,5},{7,6},{6,7},{9,8},{8,9},{11,10... | collective-permute-start | bytes 602120 | tf_op jit(solution)/shard_map/ppermute | solution.py:23
  23.7 8.8 %collective-permute-start.3 = (s16[784,128]{1,0:T(8,128)(2,1)S(1)}, s16[784,128]{1,0:T(8,128)(2,1)S(1)}, u32[]{:S(2)}, u32[]{:S(2)}) collective-permute-start(s16[784,128]{1,0:T(8,128)(2,1)S(1)} %get-tuple-element.74), channel_id=1, source_target_pairs={{1,0},{0,1},{3,2},{2,3},{5,4},{4,5},{7,6},{6,7},{9,8},{8,9},{11,10... | collective-permute-start | bytes 602120 | tf_op jit(solution)/shard_map/ppermute | solution.py:23
  30.5 6.8 %collective-permute-start.6 = (s16[400,128]{1,0:T(8,128)(2,1)S(1)}, s16[400,128]{1,0:T(8,128)(2,1)S(1)}, u32[]{:S(2)}, u32[]{:S(2)}) collective-permute-start(s16[400,128]{1,0:T(8,128)(2,1)S(1)} %get-tuple-element.80), channel_id=1, source_target_pairs={{2,0},{3,1},{0,2},{1,3},{6,4},{7,5},{4,6},{5,7},{10,8},{11,9},{8,1... | collective-permute-start | bytes 307208 | tf_op jit(solution)/shard_map/ppermute | solution.py:23
  33.1 12.1 %collective-permute-start.8 = (s16[784,128]{1,0:T(8,128)(2,1)S(1)}, s16[784,128]{1,0:T(8,128)(2,1)S(1)}, u32[]{:S(2)}, u32[]{:S(2)}) collective-permute-start(s16[784,128]{1,0:T(8,128)(2,1)S(1)} %get-tuple-element.90), channel_id=1, source_target_pairs={{1,0},{0,1},{3,2},{2,3},{5,4},{4,5},{7,6},{6,7},{9,8},{8,9},{11,10... | collective-permute-start | bytes 602120 | tf_op jit(solution)/shard_map/ppermute | solution.py:23
  37.8 11.2 %collective-permute-start.9 = (s16[784,128]{1,0:T(8,128)(2,1)S(1)}, s16[784,128]{1,0:T(8,128)(2,1)S(1)}, u32[]{:S(2)}, u32[]{:S(2)}) collective-permute-start(s16[784,128]{1,0:T(8,128)(2,1)S(1)} %get-tuple-element.93), channel_id=1, source_target_pairs={{1,0},{0,1},{3,2},{2,3},{5,4},{4,5},{7,6},{6,7},{9,8},{8,9},{11,10... | collective-permute-start | bytes 602120 | tf_op jit(solution)/shard_map/ppermute | solution.py:23
  37.9 7.3 %collective-permute-start.7 = (s16[400,128]{1,0:T(8,128)(2,1)S(1)}, s16[400,128]{1,0:T(8,128)(2,1)S(1)}, u32[]{:S(2)}, u32[]{:S(2)}) collective-permute-start(s16[400,128]{1,0:T(8,128)(2,1)S(1)} %get-tuple-element.86), channel_id=1, source_target_pairs={{2,0},{3,1},{0,2},{1,3},{6,4},{7,5},{4,6},{5,7},{10,8},{11,9},{8,1... | collective-permute-start | bytes 307208 | tf_op jit(solution)/shard_map/ppermute | solution.py:23
  45.5 9.6 %collective-permute-start.10 = (s16[400,128]{1,0:T(8,128)(2,1)S(1)}, s16[400,128]{1,0:T(8,128)(2,1)S(1)}, u32[]{:S(2)}, u32[]{:S(2)}) collective-permute-start(s16[400,128]{1,0:T(8,128)(2,1)S(1)} %get-tuple-element.96), channel_id=1, source_target_pairs={{2,0},{3,1},{0,2},{1,3},{6,4},{7,5},{4,6},{5,7},{10,8},{11,9},{8,1... | collective-permute-start | bytes 307208 | tf_op jit(solution)/shard_map/ppermute | solution.py:23
  49.2 7.6 %collective-permute-start.11 = (s16[400,128]{1,0:T(8,128)(2,1)S(1)}, s16[400,128]{1,0:T(8,128)(2,1)S(1)}, u32[]{:S(2)}, u32[]{:S(2)}) collective-permute-start(s16[400,128]{1,0:T(8,128)(2,1)S(1)} %get-tuple-element.100), channel_id=1, source_target_pairs={{2,0},{3,1},{0,2},{1,3},{6,4},{7,5},{4,6},{5,7},{10,8},{11,9},{8,1... | collective-permute-start | bytes 307208 | tf_op jit(solution)/shard_map/ppermute | solution.py:23
  56.9 5.6 %collective-permute-start.14 = (f32[8,512]{1,0:T(8,128)S(1)}, f32[8,512]{1,0:T(8,128)S(1)}, u32[]{:S(2)}, u32[]{:S(2)}) collective-permute-start(f32[8,512]{1,0:T(8,128)S(1)} %get-tuple-element.102.refs_4_), channel_id=1, source_target_pairs={{3,0},{2,1},{1,2},{0,3},{7,4},{6,5},{5,6},{4,7},{11,8},{10,9},{9,1... | collective-permute-start | bytes 49160 | tf_op jit(solution)/shard_map/ppermute | solution.py:23
  59.4 4.6 %collective-permute-start.13 = (f32[8,512]{1,0:T(8,128)S(1)}, f32[8,512]{1,0:T(8,128)S(1)}, u32[]{:S(2)}, u32[]{:S(2)}) collective-permute-start(f32[8,512]{1,0:T(8,128)S(1)} %get-tuple-element.102.refs_4_), channel_id=1, source_target_pairs={{2,0},{3,1},{0,2},{1,3},{6,4},{7,5},{4,6},{5,7},{10,8},{11,9},{8,1... | collective-permute-start | bytes 49160 | tf_op jit(solution)/shard_map/ppermute | solution.py:23
  59.4 4.6 %collective-permute-start.12 = (f32[8,512]{1,0:T(8,128)S(1)}, f32[8,512]{1,0:T(8,128)S(1)}, u32[]{:S(2)}, u32[]{:S(2)}) collective-permute-start(f32[8,512]{1,0:T(8,128)S(1)} %get-tuple-element.102.refs_4_), channel_id=1, source_target_pairs={{1,0},{0,1},{3,2},{2,3},{5,4},{4,5},{7,6},{6,7},{9,8},{8,9},{11,10... | collective-permute-start | bytes 49160 | tf_op jit(solution)/shard_map/ppermute | solution.py:23

commit v16 on v14

--- a/solution.py
+++ b/solution.py
@@ -462,7 +462,7 @@
 
     def add_up(chunk):
         half, lane = divmod(chunk, per_half)
-        direct = chunk >= chunks - DIRECT and layers <= 4
+        direct = chunk < DIRECT and layers <= 4
         kept, *sends = join(
             owns[half], ext[chunk], ints[chunk], ordered(c_rows), half, lane * LANES, layers, direct
         )
@@ -489,21 +489,21 @@
 
     add_up(0)
     more_products(1)
-    scatter(0)
     add_up(1)
     more_own(1)
+    scatter(0)
     finish(0)
     add_up(2)
     scatter(1)
     add_up(3)
-    finish(1)
     scatter(2)
     scatter(3)
+    finish(1)
+    finish(2)
     finish(3)
-    finish(2)
 
     squares = [squares[i] for i in sorted(squares)]
-    mine = sums[2]
+    mine = sums[3]
     others = [swap(mine, "layer", lambda i: i ^ other) for other in range(1, layers)]
     return rescale(squares, [mine, *others], width)
 

time: 65.3 us -> 62.9 us (0.963)
  waiting for transfers between devices: 24.6 us -> 18.2 us
  starting transfers between devices: 24.4 us -> 28.6 us
    ppermute x20, waiting for transfers between devices: 24.6 us -> 18.2 us  [swap(): lax.ppermute(block, axis, [(partner(i), i) for i in range(lax.axis_size(a...]
    ppermute x20, starting transfers between devices: 24.4 us -> 28.6 us  [swap(): lax.ppermute(block, axis, [(partner(i), i) for i in range(lax.axis_size(a...]
  transfers between devices with their start and end apart: 20 -> 20, of which waited for: 10 -> 10; matrix products, arithmetic and copies ran while one was open for 0% -> 0% of each run, Pallas kernels for 15% -> 16%
where the time goes in v16:
time: 62.9 us; the launch traced here: 62.8 us
  starting transfers between devices  28.6 us (45%)
  waiting for transfers between devices  18.2 us (29%)
  Pallas kernels  15.9 us (25%)
    ppermute x20, starting transfers between devices, swap(): lax.ppermute(block, axis, [(partner(i), i) for i in range(lax.axis_size(a...  28.6 us
    ppermute x20, waiting for transfers between devices, swap(): lax.ppermute(block, axis, [(partner(i), i) for i in range(lax.axis_size(a...  18.2 us
    pallas_call x16, Pallas kernels, call(): pl.pallas_call(kernel, out_shape=out_shape, in_specs=in_specs, out_specs=...  15.9 us
  transfers between devices with their start and end apart: 20, of which 10 were waited for; matrix products, arithmetic and copies ran while one was open for 0% of the time, Pallas kernels for 16%

profile of v16, /device:TPU:0, one launch (start us, length us, event | category | flops | bytes accessed | tf_op | source)
XLA Modules:
  0.0 62.8 jit_solution(13485342403341783035)
XLA Ops:
  0.0 4.5 %first_products.1 = (s16[1040,128]{1,0:T(8,128)(2,1)S(1)}, s16[1040,128]{1,0:T(8,128)(2,1)S(1)}, bf16[1024,2048]{1,0:T(8,128)(2,1)S(1)}, f32[8,1536]{1,0:T(8,128...) custom-call(s32[6,1,32]{2,1,0:T(1,128)} %bitcast.5, s32[6,1,32]{2,1,0:T(1,128)} %bitcast.6, s32[1,2,6]{2,1,0:T(2,128)} %bitcast.7, ...), custom_call_target="tpu_custom_call" | custom-call | flops 1 | bytes 1 | tf_op jit(solution)/shard_map/first_products/pallas_call | solution.py:32
  4.6 3.4 %collective-permute-start = (s16[1040,128]{1,0:T(8,128)(2,1)S(1)}, s16[1040,128]{1,0:T(8,128)(2,1)S(1)}, u32[]{:S(2)}, u32[]{:S(2)}) collective-permute-start(s16[1040,128]{1,0:T(8,128)(2,1)S(1)} %get-tuple-element.60), channel_id=1, source_target_pairs={{28,0},{8,4},{4,8},{16,12},{12,16},{24,20},{20,24},{0,28},{29,1},{... | collective-permute-start | bytes 798728 | tf_op jit(solution)/shard_map/ppermute | solution.py:24
  8.0 3.1 %own_int_products_0.1 = (f32[1536,256]{1,0:T(8,128)S(1)}, s16[1040,128]{1,0:T(8,128)(2,1)S(1)}, s16[1040,128]{1,0:T(8,128)(2,1)S(1)}, bf16[512,2048]{1,0:T(8,128)(2,1)S(1)}) custom-call(f32[8,1536]{1,0:T(8,128)S(1)} %get-tuple-element.58.a_rows_ref, f32[8,1536]{1,0:T(8,128)S(1)} %get-tuple-element.74.b_rows_ref, bf16[1,2048,1536]{2,1,0:T(8,128)(2,1)S(1)} %bitcast.4, ...), custom_call_target="tpu_custom_call" | custom-call | flops 1 | bytes 1 | tf_op jit(solution)/shard_map/own_int_products_0/pallas_call | solution.py:32
  11.1 2.3 %collective-permute-start.2 = (s16[1040,128]{1,0:T(8,128)(2,1)S(1)}, s16[1040,128]{1,0:T(8,128)(2,1)S(1)}, u32[]{:S(2)}, u32[]{:S(2)}) collective-permute-start(s16[1040,128]{1,0:T(8,128)(2,1)S(1)} %get-tuple-element.71), channel_id=1, source_target_pairs={{28,0},{8,4},{4,8},{16,12},{12,16},{24,20},{20,24},{0,28},{29,1},{... | collective-permute-start | bytes 798728 | tf_op jit(solution)/shard_map/ppermute | solution.py:24
  13.4 1.2 %collective-permute-done.ext_ref = s16[1040,128]{1,0:T(8,128)(2,1)S(1)} collective-permute-done((s16[1040,128]{1,0:T(8,128)(2,1)S(1)}, s16[1040,128]{1,0:T(8,128)(2,1)S(1)}, u32[]{:S(2)}, u32[]{:S(2)}) %collective-permute-start) | collective-permute-done | bytes 266272 | tf_op jit(solution)/shard_map/ppermute | solution.py:24
  14.6 0.4 join_0_0.1
  15.0 2.6 %collective-permute-start.4 = (s16[400,128]{1,0:T(8,128)(2,1)S(1)}, s16[400,128]{1,0:T(8,128)(2,1)S(1)}, u32[]{:S(2)}, u32[]{:S(2)}) collective-permute-start(s16[400,128]{1,0:T(8,128)(2,1)S(1)} %get-tuple-element.76), channel_id=1, source_target_pairs={{1,0},{0,1},{3,2},{2,3},{5,4},{4,5},{7,6},{6,7},{9,8},{8,9},{11,10... | collective-permute-start | bytes 307208 | tf_op jit(solution)/shard_map/ppermute | solution.py:24
  17.6 2.6 %collective-permute-start.5 = (s16[400,128]{1,0:T(8,128)(2,1)S(1)}, s16[400,128]{1,0:T(8,128)(2,1)S(1)}, u32[]{:S(2)}, u32[]{:S(2)}) collective-permute-start(s16[400,128]{1,0:T(8,128)(2,1)S(1)} %get-tuple-element.77), channel_id=1, source_target_pairs={{2,0},{3,1},{0,2},{1,3},{6,4},{7,5},{4,6},{5,7},{10,8},{11,9},{8,1... | collective-permute-start | bytes 307208 | tf_op jit(solution)/shard_map/ppermute | solution.py:24
  20.2 3.0 %ext_int_products_1.1 = (s16[1040,128]{1,0:T(8,128)(2,1)S(1)}, s16[1040,128]{1,0:T(8,128)(2,1)S(1)}, s16[1040,128]{1,0:T(8,128)(2,1)S(1)}, s16[1040,128]{1,0:T(8,128)(2,1)S(1)}) custom-call(f32[8,1536]{1,0:T(8,128)S(1)} %get-tuple-element.58.a_rows_ref, f32[8,1536]{1,0:T(8,128)S(1)} %get-tuple-element.74.b_rows_ref, bf16[1,2048,1536]{2,1,0:T(8,128)(2,1)S(1)} %bitcast.4, ...), custom_call_target="tpu_custom_call" | custom-call | flops 1 | bytes 1 | tf_op jit(solution)/shard_map/ext_int_products_1/pallas_call | solution.py:32
  23.2 1.4 %collective-permute-start.7 = (s16[1040,128]{1,0:T(8,128)(2,1)S(1)}, s16[1040,128]{1,0:T(8,128)(2,1)S(1)}, u32[]{:S(2)}, u32[]{:S(2)}) collective-permute-start(s16[1040,128]{1,0:T(8,128)(2,1)S(1)} %get-tuple-element.82), channel_id=1, source_target_pairs={{28,0},{8,4},{4,8},{16,12},{12,16},{24,20},{20,24},{0,28},{29,1},{... | collective-permute-start | bytes 798728 | tf_op jit(solution)/shard_map/ppermute | solution.py:24
  24.6 1.4 %collective-permute-start.10 = (s16[1040,128]{1,0:T(8,128)(2,1)S(1)}, s16[1040,128]{1,0:T(8,128)(2,1)S(1)}, u32[]{:S(2)}, u32[]{:S(2)}) collective-permute-start(s16[1040,128]{1,0:T(8,128)(2,1)S(1)} %get-tuple-element.88), channel_id=1, source_target_pairs={{28,0},{8,4},{4,8},{16,12},{12,16},{24,20},{20,24},{0,28},{29,1},{... | collective-permute-start | bytes 798728 | tf_op jit(solution)/shard_map/ppermute | solution.py:24
  26.0 1.0 %collective-permute-done.5.rest_1_ = s16[400,128]{1,0:T(8,128)(2,1)S(1)} collective-permute-done((s16[400,128]{1,0:T(8,128)(2,1)S(1)}, s16[400,128]{1,0:T(8,128)(2,1)S(1)}, u32[]{:S(2)}, u32[]{:S(2)}) %collective-permute-start.5) | collective-permute-done | bytes 102432 | tf_op jit(solution)/shard_map/ppermute | solution.py:24
  27.4 1.3 %collective-permute-start.9 = (s16[784,128]{1,0:T(8,128)(2,1)S(1)}, s16[784,128]{1,0:T(8,128)(2,1)S(1)}, u32[]{:S(2)}, u32[]{:S(2)}) collective-permute-start(s16[784,128]{1,0:T(8,128)(2,1)S(1)} %get-tuple-element.85), channel_id=1, source_target_pairs={{1,0},{0,1},{3,2},{2,3},{5,4},{4,5},{7,6},{6,7},{9,8},{8,9},{11,10... | collective-permute-start | bytes 602120 | tf_op jit(solution)/shard_map/ppermute | solution.py:24
  28.7 1.8 %own_products_1.1.own_ref = f32[1536,256]{1,0:T(8,128)S(1)} custom-call(f32[8,1536]{1,0:T(8,128)S(1)} %get-tuple-element.58.a_rows_ref, f32[8,1536]{1,0:T(8,128)S(1)} %get-tuple-element.74.b_rows_ref, bf16[1,2048,1536]{2,1,0:T(8,128)(2,1)S(1)} %bitcast.4, bf16[1024,2048]{1,0:T(8,128)(2,1)S(1)} %get-tuple-element.62.ext_rows_ref, ...), custom_call_target="tpu_custom_call" | custom-call | flops 1 | bytes 1 | tf_op jit(solution)/shard_map/own_products_1/pallas_call | solution.py:32
  30.6 2.2 %collective-permute-done.7.ext_ref = s16[1040,128]{1,0:T(8,128)(2,1)S(1)} collective-permute-done((s16[1040,128]{1,0:T(8,128)(2,1)S(1)}, s16[1040,128]{1,0:T(8,128)(2,1)S(1)}, u32[]{:S(2)}, u32[]{:S(2)}) %collective-permute-start.7) | collective-permute-done | bytes 266272 | tf_op jit(solution)/shard_map/ppermute | solution.py:24
  32.8 0.4 join_1_0.1
  33.2 1.0 %collective-permute-start.12 = (s16[784,128]{1,0:T(8,128)(2,1)S(1)}, s16[784,128]{1,0:T(8,128)(2,1)S(1)}, u32[]{:S(2)}, u32[]{:S(2)}) collective-permute-start(s16[784,128]{1,0:T(8,128)(2,1)S(1)} %get-tuple-element.92), channel_id=1, source_target_pairs={{1,0},{0,1},{3,2},{2,3},{5,4},{4,5},{7,6},{6,7},{9,8},{8,9},{11,10... | collective-permute-start | bytes 602120 | tf_op jit(solution)/shard_map/ppermute | solution.py:24
  34.2 1.0 %collective-permute-done.9.got_ref = s16[784,128]{1,0:T(8,128)(2,1)S(1)} collective-permute-done((s16[784,128]{1,0:T(8,128)(2,1)S(1)}, s16[784,128]{1,0:T(8,128)(2,1)S(1)}, u32[]{:S(2)}, u32[]{:S(2)}) %collective-permute-start.9) | collective-permute-done | bytes 200736 | tf_op jit(solution)/shard_map/ppermute | solution.py:24
  35.4 2.7 %collective-permute-done.10.ext_ref = s16[1040,128]{1,0:T(8,128)(2,1)S(1)} collective-permute-done((s16[1040,128]{1,0:T(8,128)(2,1)S(1)}, s16[1040,128]{1,0:T(8,128)(2,1)S(1)}, u32[]{:S(2)}, u32[]{:S(2)}) %collective-permute-start.10) | collective-permute-done | bytes 266272 | tf_op jit(solution)/shard_map/ppermute | solution.py:24
  38.1 0.4 join_1_128.1
  38.5 0.7 %collective-permute-start.13 = (s16[784,128]{1,0:T(8,128)(2,1)S(1)}, s16[784,128]{1,0:T(8,128)(2,1)S(1)}, u32[]{:S(2)}, u32[]{:S(2)}) collective-permute-start(s16[784,128]{1,0:T(8,128)(2,1)S(1)} %get-tuple-element.95), channel_id=1, source_target_pairs={{1,0},{0,1},{3,2},{2,3},{5,4},{4,5},{7,6},{6,7},{9,8},{8,9},{11,10... | collective-permute-start | bytes 602120 | tf_op jit(solution)/shard_map/ppermute | solution.py:24
  39.3 3.5 %collective-permute-start.14 = (s16[400,128]{1,0:T(8,128)(2,1)S(1)}, s16[400,128]{1,0:T(8,128)(2,1)S(1)}, u32[]{:S(2)}, u32[]{:S(2)}) collective-permute-start(s16[400,128]{1,0:T(8,128)(2,1)S(1)} %get-tuple-element.98), channel_id=1, source_target_pairs={{2,0},{3,1},{0,2},{1,3},{6,4},{7,5},{4,6},{5,7},{10,8},{11,9},{8,1... | collective-permute-start | bytes 307208 | tf_op jit(solution)/shard_map/ppermute | solution.py:24
  43.0 2.1 %collective-permute-start.15 = (s16[400,128]{1,0:T(8,128)(2,1)S(1)}, s16[400,128]{1,0:T(8,128)(2,1)S(1)}, u32[]{:S(2)}, u32[]{:S(2)}) collective-permute-start(s16[400,128]{1,0:T(8,128)(2,1)S(1)} %get-tuple-element.102), channel_id=1, source_target_pairs={{2,0},{3,1},{0,2},{1,3},{6,4},{7,5},{4,6},{5,7},{10,8},{11,9},{8,1... | collective-permute-start | bytes 307208 | tf_op jit(solution)/shard_map/ppermute | solution.py:24
  45.1 1.7 %collective-permute-done.13.got_ref = s16[784,128]{1,0:T(8,128)(2,1)S(1)} collective-permute-done((s16[784,128]{1,0:T(8,128)(2,1)S(1)}, s16[784,128]{1,0:T(8,128)(2,1)S(1)}, u32[]{:S(2)}, u32[]{:S(2)}) %collective-permute-start.13) | collective-permute-done | bytes 200736 | tf_op jit(solution)/shard_map/ppermute | solution.py:24
  46.9 1.8 %collective-permute-start.16 = (s16[400,128]{1,0:T(8,128)(2,1)S(1)}, s16[400,128]{1,0:T(8,128)(2,1)S(1)}, u32[]{:S(2)}, u32[]{:S(2)}) collective-permute-start(s16[400,128]{1,0:T(8,128)(2,1)S(1)} %get-tuple-element.106), channel_id=1, source_target_pairs={{2,0},{3,1},{0,2},{1,3},{6,4},{7,5},{4,6},{5,7},{10,8},{11,9},{8,1... | collective-permute-start | bytes 307208 | tf_op jit(solution)/shard_map/ppermute | solution.py:24
  48.9 5.1 %collective-permute-done.15.rest_0_ = s16[400,128]{1,0:T(8,128)(2,1)S(1)} collective-permute-done((s16[400,128]{1,0:T(8,128)(2,1)S(1)}, s16[400,128]{1,0:T(8,128)(2,1)S(1)}, u32[]{:S(2)}, u32[]{:S(2)}) %collective-permute-start.15) | collective-permute-done | bytes 102432 | tf_op jit(solution)/shard_map/ppermute | solution.py:24
  54.0 1.0 %collective-permute-done.16.rest_0_ = s16[400,128]{1,0:T(8,128)(2,1)S(1)} collective-permute-done((s16[400,128]{1,0:T(8,128)(2,1)S(1)}, s16[400,128]{1,0:T(8,128)(2,1)S(1)}, u32[]{:S(2)}, u32[]{:S(2)}) %collective-permute-start.16) | collective-permute-done | bytes 102432 | tf_op jit(solution)/shard_map/ppermute | solution.py:24
  55.1 2.1 %collective-permute-start.19 = (f32[8,512]{1,0:T(8,128)S(1)}, f32[8,512]{1,0:T(8,128)S(1)}, u32[]{:S(2)}, u32[]{:S(2)}) collective-permute-start(f32[8,512]{1,0:T(8,128)S(1)} %get-tuple-element.108.refs_4_), channel_id=1, source_target_pairs={{3,0},{2,1},{1,2},{0,3},{7,4},{6,5},{5,6},{4,7},{11,8},{10,9},{9,1... | collective-permute-start | bytes 49160 | tf_op jit(solution)/shard_map/ppermute | solution.py:24
  57.1 2.4 %collective-permute-start.17 = (f32[8,512]{1,0:T(8,128)S(1)}, f32[8,512]{1,0:T(8,128)S(1)}, u32[]{:S(2)}, u32[]{:S(2)}) collective-permute-start(f32[8,512]{1,0:T(8,128)S(1)} %get-tuple-element.108.refs_4_), channel_id=1, source_target_pairs={{1,0},{0,1},{3,2},{2,3},{5,4},{4,5},{7,6},{6,7},{9,8},{8,9},{11,10... | collective-permute-start | bytes 49160 | tf_op jit(solution)/shard_map/ppermute | solution.py:24
  59.5 1.2 %collective-permute-done.19.refs_7_ = f32[8,512]{1,0:T(8,128)S(1)} collective-permute-done((f32[8,512]{1,0:T(8,128)S(1)}, f32[8,512]{1,0:T(8,128)S(1)}, u32[]{:S(2)}, u32[]{:S(2)}) %collective-permute-start.19) | collective-permute-done | bytes 16416 | tf_op jit(solution)/shard_map/ppermute | solution.py:24
  60.7 1.0 %collective-permute-done.18.refs_6_ = f32[8,512]{1,0:T(8,128)S(1)} collective-permute-done((f32[8,512]{1,0:T(8,128)S(1)}, f32[8,512]{1,0:T(8,128)S(1)}, u32[]{:S(2)}, u32[]{:S(2)}) %collective-permute-start.18) | collective-permute-done | bytes 16416 | tf_op jit(solution)/shard_map/ppermute | solution.py:24
  61.8 1.0 %rescale.1 = f32[1,384,512]{2,1,0:T(8,128)} custom-call(f32[384,128]{1,0:T(8,128)S(1)} %get-tuple-element.79.refs_0_, f32[384,128]{1,0:T(8,128)S(1)} %get-tuple-element.99.refs_1_, f32[384,128]{1,0:T(8,128)S(1)} %get-tuple-element.103.refs_2_, f32[384,128]{1,0:T(8,128)S(1)} %get-tuple-element.107.refs_3_, f32[8,512]{1,0:T(8,128)S(1)} %get-tuple-element.108.refs_4_, ...), custom_call_target="tpu_custom_call" | custom-call | flops 1 | bytes 1 | tf_op jit(solution)/shard_map/rescale/pallas_call | solution.py:32
  (31 shorter events, 1.4 us)
Async XLA Ops:
  0.0 8.0 %slice-start = ((s8[6291456]{0:T(1024)(128)(4,1)}), s8[4194304]{0:T(1024)(128)(4,1)S(1)}, s32[]{:S(2)}) async-start(s8[6291456]{0:T(1024)(128)(4,1)} %bitcast.3), calls=%async_computation | async-start | bytes 8388608
  0.0 8.0 %slice-start.1 = ((s8[6291456]{0:T(1024)(128)(4,1)}), s8[2097152]{0:T(1024)(128)(4,1)S(1)}, s32[]{:S(2)}) async-start(s8[6291456]{0:T(1024)(128)(4,1)} %bitcast.3), calls=%async_computation.1 | async-start | bytes 4194304
  0.0 8.0 %copy-start = (bf16[1,2048,1536]{2,1,0:T(8,128)(2,1)S(1)}, bf16[1,2048,1536]{2,1,0:T(8,128)(2,1)}, u32[]{:S(2)}) copy-start(bf16[1,2048,1536]{2,1,0:T(8,128)(2,1)} %side_ref.1) | copy-start | bytes 18874372
  4.6 10.1 %collective-permute-start = (s16[1040,128]{1,0:T(8,128)(2,1)S(1)}, s16[1040,128]{1,0:T(8,128)(2,1)S(1)}, u32[]{:S(2)}, u32[]{:S(2)}) collective-permute-start(s16[1040,128]{1,0:T(8,128)(2,1)S(1)} %get-tuple-element.60), channel_id=1, source_target_pairs={{28,0},{8,4},{4,8},{16,12},{12,16},{24,20},{20,24},{0,28},{29,1},{... | collective-permute-start | bytes 798728 | tf_op jit(solution)/shard_map/ppermute | solution.py:24
  11.1 3.6 %collective-permute-start.1 = (s16[1040,128]{1,0:T(8,128)(2,1)S(1)}, s16[1040,128]{1,0:T(8,128)(2,1)S(1)}, u32[]{:S(2)}, u32[]{:S(2)}) collective-permute-start(s16[1040,128]{1,0:T(8,128)(2,1)S(1)} %get-tuple-element.63), channel_id=1, source_target_pairs={{4,0},{0,4},{12,8},{8,12},{20,16},{16,20},{28,24},{24,28},{5,1},{1... | collective-permute-start | bytes 798728 | tf_op jit(solution)/shard_map/ppermute | solution.py:24
  11.1 12.1 %collective-permute-start.2 = (s16[1040,128]{1,0:T(8,128)(2,1)S(1)}, s16[1040,128]{1,0:T(8,128)(2,1)S(1)}, u32[]{:S(2)}, u32[]{:S(2)}) collective-permute-start(s16[1040,128]{1,0:T(8,128)(2,1)S(1)} %get-tuple-element.71), channel_id=1, source_target_pairs={{28,0},{8,4},{4,8},{16,12},{12,16},{24,20},{20,24},{0,28},{29,1},{... | collective-permute-start | bytes 798728 | tf_op jit(solution)/shard_map/ppermute | solution.py:24
  13.4 11.2 %collective-permute-start.3 = (s16[1040,128]{1,0:T(8,128)(2,1)S(1)}, s16[1040,128]{1,0:T(8,128)(2,1)S(1)}, u32[]{:S(2)}, u32[]{:S(2)}) collective-permute-start(s16[1040,128]{1,0:T(8,128)(2,1)S(1)} %get-tuple-element.72), channel_id=1, source_target_pairs={{4,0},{0,4},{12,8},{8,12},{20,16},{16,20},{28,24},{24,28},{5,1},{1... | collective-permute-start | bytes 798728 | tf_op jit(solution)/shard_map/ppermute | solution.py:24
  15.0 9.6 %collective-permute-start.4 = (s16[400,128]{1,0:T(8,128)(2,1)S(1)}, s16[400,128]{1,0:T(8,128)(2,1)S(1)}, u32[]{:S(2)}, u32[]{:S(2)}) collective-permute-start(s16[400,128]{1,0:T(8,128)(2,1)S(1)} %get-tuple-element.76), channel_id=1, source_target_pairs={{1,0},{0,1},{3,2},{2,3},{5,4},{4,5},{7,6},{6,7},{9,8},{8,9},{11,10... | collective-permute-start | bytes 307208 | tf_op jit(solution)/shard_map/ppermute | solution.py:24
  17.6 9.4 %collective-permute-start.5 = (s16[400,128]{1,0:T(8,128)(2,1)S(1)}, s16[400,128]{1,0:T(8,128)(2,1)S(1)}, u32[]{:S(2)}, u32[]{:S(2)}) collective-permute-start(s16[400,128]{1,0:T(8,128)(2,1)S(1)} %get-tuple-element.77), channel_id=1, source_target_pairs={{2,0},{3,1},{0,2},{1,3},{6,4},{7,5},{4,6},{5,7},{10,8},{11,9},{8,1... | collective-permute-start | bytes 307208 | tf_op jit(solution)/shard_map/ppermute | solution.py:24
  20.2 7.2 %collective-permute-start.6 = (s16[400,128]{1,0:T(8,128)(2,1)S(1)}, s16[400,128]{1,0:T(8,128)(2,1)S(1)}, u32[]{:S(2)}, u32[]{:S(2)}) collective-permute-start(s16[400,128]{1,0:T(8,128)(2,1)S(1)} %get-tuple-element.78), channel_id=1, source_target_pairs={{3,0},{2,1},{1,2},{0,3},{7,4},{6,5},{5,6},{4,7},{11,8},{10,9},{9,1... | collective-permute-start | bytes 307208 | tf_op jit(solution)/shard_map/ppermute | solution.py:24
  23.2 9.6 %collective-permute-start.7 = (s16[1040,128]{1,0:T(8,128)(2,1)S(1)}, s16[1040,128]{1,0:T(8,128)(2,1)S(1)}, u32[]{:S(2)}, u32[]{:S(2)}) collective-permute-start(s16[1040,128]{1,0:T(8,128)(2,1)S(1)} %get-tuple-element.82), channel_id=1, source_target_pairs={{28,0},{8,4},{4,8},{16,12},{12,16},{24,20},{20,24},{0,28},{29,1},{... | collective-permute-start | bytes 798728 | tf_op jit(solution)/shard_map/ppermute | solution.py:24
  24.6 8.2 %collective-permute-start.8 = (s16[1040,128]{1,0:T(8,128)(2,1)S(1)}, s16[1040,128]{1,0:T(8,128)(2,1)S(1)}, u32[]{:S(2)}, u32[]{:S(2)}) collective-permute-start(s16[1040,128]{1,0:T(8,128)(2,1)S(1)} %get-tuple-element.69), channel_id=1, source_target_pairs={{4,0},{0,4},{12,8},{8,12},{20,16},{16,20},{28,24},{24,28},{5,1},{1... | collective-permute-start | bytes 798728 | tf_op jit(solution)/shard_map/ppermute | solution.py:24
  24.6 13.5 %collective-permute-start.10 = (s16[1040,128]{1,0:T(8,128)(2,1)S(1)}, s16[1040,128]{1,0:T(8,128)(2,1)S(1)}, u32[]{:S(2)}, u32[]{:S(2)}) collective-permute-start(s16[1040,128]{1,0:T(8,128)(2,1)S(1)} %get-tuple-element.88), channel_id=1, source_target_pairs={{28,0},{8,4},{4,8},{16,12},{12,16},{24,20},{20,24},{0,28},{29,1},{... | collective-permute-start | bytes 798728 | tf_op jit(solution)/shard_map/ppermute | solution.py:24
  27.0 11.1 %collective-permute-start.11 = (s16[1040,128]{1,0:T(8,128)(2,1)S(1)}, s16[1040,128]{1,0:T(8,128)(2,1)S(1)}, u32[]{:S(2)}, u32[]{:S(2)}) collective-permute-start(s16[1040,128]{1,0:T(8,128)(2,1)S(1)} %get-tuple-element.89), channel_id=1, source_target_pairs={{4,0},{0,4},{12,8},{8,12},{20,16},{16,20},{28,24},{24,28},{5,1},{1... | collective-permute-start | bytes 798728 | tf_op jit(solution)/shard_map/ppermute | solution.py:24
  27.4 7.8 %collective-permute-start.9 = (s16[784,128]{1,0:T(8,128)(2,1)S(1)}, s16[784,128]{1,0:T(8,128)(2,1)S(1)}, u32[]{:S(2)}, u32[]{:S(2)}) collective-permute-start(s16[784,128]{1,0:T(8,128)(2,1)S(1)} %get-tuple-element.85), channel_id=1, source_target_pairs={{1,0},{0,1},{3,2},{2,3},{5,4},{4,5},{7,6},{6,7},{9,8},{8,9},{11,10... | collective-permute-start | bytes 602120 | tf_op jit(solution)/shard_map/ppermute | solution.py:24
  33.2 9.6 %collective-permute-start.12 = (s16[784,128]{1,0:T(8,128)(2,1)S(1)}, s16[784,128]{1,0:T(8,128)(2,1)S(1)}, u32[]{:S(2)}, u32[]{:S(2)}) collective-permute-start(s16[784,128]{1,0:T(8,128)(2,1)S(1)} %get-tuple-element.92), channel_id=1, source_target_pairs={{1,0},{0,1},{3,2},{2,3},{5,4},{4,5},{7,6},{6,7},{9,8},{8,9},{11,10... | collective-permute-start | bytes 602120 | tf_op jit(solution)/shard_map/ppermute | solution.py:24
  38.5 8.2 %collective-permute-start.13 = (s16[784,128]{1,0:T(8,128)(2,1)S(1)}, s16[784,128]{1,0:T(8,128)(2,1)S(1)}, u32[]{:S(2)}, u32[]{:S(2)}) collective-permute-start(s16[784,128]{1,0:T(8,128)(2,1)S(1)} %get-tuple-element.95), channel_id=1, source_target_pairs={{1,0},{0,1},{3,2},{2,3},{5,4},{4,5},{7,6},{6,7},{9,8},{8,9},{11,10... | collective-permute-start | bytes 602120 | tf_op jit(solution)/shard_map/ppermute | solution.py:24
  39.3 9.5 %collective-permute-start.14 = (s16[400,128]{1,0:T(8,128)(2,1)S(1)}, s16[400,128]{1,0:T(8,128)(2,1)S(1)}, u32[]{:S(2)}, u32[]{:S(2)}) collective-permute-start(s16[400,128]{1,0:T(8,128)(2,1)S(1)} %get-tuple-element.98), channel_id=1, source_target_pairs={{2,0},{3,1},{0,2},{1,3},{6,4},{7,5},{4,6},{5,7},{10,8},{11,9},{8,1... | collective-permute-start | bytes 307208 | tf_op jit(solution)/shard_map/ppermute | solution.py:24
  43.0 10.9 %collective-permute-start.15 = (s16[400,128]{1,0:T(8,128)(2,1)S(1)}, s16[400,128]{1,0:T(8,128)(2,1)S(1)}, u32[]{:S(2)}, u32[]{:S(2)}) collective-permute-start(s16[400,128]{1,0:T(8,128)(2,1)S(1)} %get-tuple-element.102), channel_id=1, source_target_pairs={{2,0},{3,1},{0,2},{1,3},{6,4},{7,5},{4,6},{5,7},{10,8},{11,9},{8,1... | collective-permute-start | bytes 307208 | tf_op jit(solution)/shard_map/ppermute | solution.py:24
  46.9 8.1 %collective-permute-start.16 = (s16[400,128]{1,0:T(8,128)(2,1)S(1)}, s16[400,128]{1,0:T(8,128)(2,1)S(1)}, u32[]{:S(2)}, u32[]{:S(2)}) collective-permute-start(s16[400,128]{1,0:T(8,128)(2,1)S(1)} %get-tuple-element.106), channel_id=1, source_target_pairs={{2,0},{3,1},{0,2},{1,3},{6,4},{7,5},{4,6},{5,7},{10,8},{11,9},{8,1... | collective-permute-start | bytes 307208 | tf_op jit(solution)/shard_map/ppermute | solution.py:24
  55.1 5.7 %collective-permute-start.19 = (f32[8,512]{1,0:T(8,128)S(1)}, f32[8,512]{1,0:T(8,128)S(1)}, u32[]{:S(2)}, u32[]{:S(2)}) collective-permute-start(f32[8,512]{1,0:T(8,128)S(1)} %get-tuple-element.108.refs_4_), channel_id=1, source_target_pairs={{3,0},{2,1},{1,2},{0,3},{7,4},{6,5},{5,6},{4,7},{11,8},{10,9},{9,1... | collective-permute-start | bytes 49160 | tf_op jit(solution)/shard_map/ppermute | solution.py:24
  57.1 4.6 %collective-permute-start.18 = (f32[8,512]{1,0:T(8,128)S(1)}, f32[8,512]{1,0:T(8,128)S(1)}, u32[]{:S(2)}, u32[]{:S(2)}) collective-permute-start(f32[8,512]{1,0:T(8,128)S(1)} %get-tuple-element.108.refs_4_), channel_id=1, source_target_pairs={{2,0},{3,1},{0,2},{1,3},{6,4},{7,5},{4,6},{5,7},{10,8},{11,9},{8,1... | collective-permute-start | bytes 49160 | tf_op jit(solution)/shard_map/ppermute | solution.py:24
  57.1 4.6 %collective-permute-start.17 = (f32[8,512]{1,0:T(8,128)S(1)}, f32[8,512]{1,0:T(8,128)S(1)}, u32[]{:S(2)}, u32[]{:S(2)}) collective-permute-start(f32[8,512]{1,0:T(8,128)S(1)} %get-tuple-element.108.refs_4_), channel_id=1, source_target_pairs={{1,0},{0,1},{3,2},{2,3},{5,4},{4,5},{7,6},{6,7},{9,8},{8,9},{11,10... | collective-permute-start | bytes 49160 | tf_op jit(solution)/shard_map/ppermute | solution.py:24

commit v17 on v14

--- a/solution.py
+++ b/solution.py
@@ -13,7 +13,6 @@
 STEPS = 256.0
 TOP = 65534.0
 LN2 = 0.6931471805599453
-DIRECT = 1
 PRODUCT_LIMIT = 24000000
 SMALL_LIMIT = 8 * 1024 * 1024
 IN_VMEM = pl.BlockSpec(memory_space=pltpu.VMEM)
@@ -462,7 +461,7 @@
 
     def add_up(chunk):
         half, lane = divmod(chunk, per_half)
-        direct = chunk >= chunks - DIRECT and layers <= 4
+        direct = chunk in (0, chunks - 1) and layers <= 4
         kept, *sends = join(
             owns[half], ext[chunk], ints[chunk], ordered(c_rows), half, lane * LANES, layers, direct
         )
@@ -489,9 +488,9 @@
 
     add_up(0)
     more_products(1)
-    scatter(0)
     add_up(1)
     more_own(1)
+    scatter(0)
     finish(0)
     add_up(2)
     scatter(1)

time: 65.3 us -> 68.2 us (1.044)
  starting transfers between devices: 24.4 us -> 29.1 us
  waiting for transfers between devices: 24.6 us -> 22.9 us
    ppermute x20 -> x21, starting transfers between devices: 24.4 us -> 29.1 us  [swap(): lax.ppermute(block, axis, [(partner(i), i) for i in range(lax.axis_size(a...]
    ppermute x20 -> x21, waiting for transfers between devices: 24.6 us -> 22.9 us  [swap(): lax.ppermute(block, axis, [(partner(i), i) for i in range(lax.axis_size(a...]
    pallas_call x16 -> x15, Pallas kernels: 16.1 us -> 16 us  [call(): pl.pallas_call(kernel, out_shape=out_shape, in_specs=in_specs, out_specs=...]
  transfers between devices with their start and end apart: 20 -> 21, of which waited for: 10 -> 10; matrix products, arithmetic and copies ran while one was open for 0% -> 0% of each run, Pallas kernels for 15% -> 15%
where the time goes in v17:
time: 68.2 us; the launch traced here: 68.1 us
  starting transfers between devices  29.1 us (43%)
  waiting for transfers between devices  22.9 us (34%)
  Pallas kernels  16 us (23%)
    ppermute x21, starting transfers between devices, swap(): lax.ppermute(block, axis, [(partner(i), i) for i in range(lax.axis_size(a...  29.1 us
    ppermute x21, waiting for transfers between devices, swap(): lax.ppermute(block, axis, [(partner(i), i) for i in range(lax.axis_size(a...  22.9 us
    pallas_call x15, Pallas kernels, call(): pl.pallas_call(kernel, out_shape=out_shape, in_specs=in_specs, out_specs=...  16 us
  transfers between devices with their start and end apart: 21, of which 10 were waited for; matrix products, arithmetic and copies ran while one was open for 0% of the time, Pallas kernels for 15%

profile of v17, /device:TPU:0, one launch (start us, length us, event | category | flops | bytes accessed | tf_op | source)
XLA Modules:
  0.0 68.1 jit_solution(17468552939648072528)
XLA Ops:
  0.0 4.5 %first_products.1 = (s16[1040,128]{1,0:T(8,128)(2,1)S(1)}, s16[1040,128]{1,0:T(8,128)(2,1)S(1)}, bf16[1024,2048]{1,0:T(8,128)(2,1)S(1)}, f32[8,1536]{1,0:T(8,128...) custom-call(s32[6,1,32]{2,1,0:T(1,128)} %bitcast.5, s32[6,1,32]{2,1,0:T(1,128)} %bitcast.6, s32[1,2,6]{2,1,0:T(2,128)} %bitcast.7, ...), custom_call_target="tpu_custom_call" | custom-call | flops 1 | bytes 1 | tf_op jit(solution)/shard_map/first_products/pallas_call | solution.py:31
  4.6 3.4 %collective-permute-start = (s16[1040,128]{1,0:T(8,128)(2,1)S(1)}, s16[1040,128]{1,0:T(8,128)(2,1)S(1)}, u32[]{:S(2)}, u32[]{:S(2)}) collective-permute-start(s16[1040,128]{1,0:T(8,128)(2,1)S(1)} %get-tuple-element.59), channel_id=1, source_target_pairs={{28,0},{8,4},{4,8},{16,12},{12,16},{24,20},{20,24},{0,28},{29,1},{... | collective-permute-start | bytes 798728 | tf_op jit(solution)/shard_map/ppermute | solution.py:23
  8.0 3.1 %own_int_products_0.1 = (f32[1536,256]{1,0:T(8,128)S(1)}, s16[1040,128]{1,0:T(8,128)(2,1)S(1)}, s16[1040,128]{1,0:T(8,128)(2,1)S(1)}, bf16[512,2048]{1,0:T(8,128)(2,1)S(1)}) custom-call(f32[8,1536]{1,0:T(8,128)S(1)} %get-tuple-element.57.a_rows_ref, f32[8,1536]{1,0:T(8,128)S(1)} %get-tuple-element.73.b_rows_ref, bf16[1,2048,1536]{2,1,0:T(8,128)(2,1)S(1)} %bitcast.4, ...), custom_call_target="tpu_custom_call" | custom-call | flops 1 | bytes 1 | tf_op jit(solution)/shard_map/own_int_products_0/pallas_call | solution.py:31
  11.1 2.3 %collective-permute-start.2 = (s16[1040,128]{1,0:T(8,128)(2,1)S(1)}, s16[1040,128]{1,0:T(8,128)(2,1)S(1)}, u32[]{:S(2)}, u32[]{:S(2)}) collective-permute-start(s16[1040,128]{1,0:T(8,128)(2,1)S(1)} %get-tuple-element.70), channel_id=1, source_target_pairs={{28,0},{8,4},{4,8},{16,12},{12,16},{24,20},{20,24},{0,28},{29,1},{... | collective-permute-start | bytes 798728 | tf_op jit(solution)/shard_map/ppermute | solution.py:23
  13.4 1.2 %collective-permute-done.ext_ref = s16[1040,128]{1,0:T(8,128)(2,1)S(1)} collective-permute-done((s16[1040,128]{1,0:T(8,128)(2,1)S(1)}, s16[1040,128]{1,0:T(8,128)(2,1)S(1)}, u32[]{:S(2)}, u32[]{:S(2)}) %collective-permute-start) | collective-permute-done | bytes 266272 | tf_op jit(solution)/shard_map/ppermute | solution.py:23
  14.6 0.4 join_0_0.1
  15.0 3.0 %ext_int_products_1.1 = (s16[1040,128]{1,0:T(8,128)(2,1)S(1)}, s16[1040,128]{1,0:T(8,128)(2,1)S(1)}, s16[1040,128]{1,0:T(8,128)(2,1)S(1)}, s16[1040,128]{1,0:T(8,128)(2,1)S(1)}) custom-call(f32[8,1536]{1,0:T(8,128)S(1)} %get-tuple-element.57.a_rows_ref, f32[8,1536]{1,0:T(8,128)S(1)} %get-tuple-element.73.b_rows_ref, bf16[1,2048,1536]{2,1,0:T(8,128)(2,1)S(1)} %bitcast.4, ...), custom_call_target="tpu_custom_call" | custom-call | flops 1 | bytes 1 | tf_op jit(solution)/shard_map/ext_int_products_1/pallas_call | solution.py:31
  18.0 2.9 %collective-permute-start.7 = (s16[1040,128]{1,0:T(8,128)(2,1)S(1)}, s16[1040,128]{1,0:T(8,128)(2,1)S(1)}, u32[]{:S(2)}, u32[]{:S(2)}) collective-permute-start(s16[1040,128]{1,0:T(8,128)(2,1)S(1)} %get-tuple-element.81), channel_id=1, source_target_pairs={{28,0},{8,4},{4,8},{16,12},{12,16},{24,20},{20,24},{0,28},{29,1},{... | collective-permute-start | bytes 798728 | tf_op jit(solution)/shard_map/ppermute | solution.py:23
  20.9 1.6 %collective-permute-start.4 = (s16[400,128]{1,0:T(8,128)(2,1)S(1)}, s16[400,128]{1,0:T(8,128)(2,1)S(1)}, u32[]{:S(2)}, u32[]{:S(2)}) collective-permute-start(s16[400,128]{1,0:T(8,128)(2,1)S(1)} %get-tuple-element.75), channel_id=1, source_target_pairs={{1,0},{0,1},{3,2},{2,3},{5,4},{4,5},{7,6},{6,7},{9,8},{8,9},{11,10... | collective-permute-start | bytes 307208 | tf_op jit(solution)/shard_map/ppermute | solution.py:23
  22.5 2.6 %collective-permute-start.5 = (s16[400,128]{1,0:T(8,128)(2,1)S(1)}, s16[400,128]{1,0:T(8,128)(2,1)S(1)}, u32[]{:S(2)}, u32[]{:S(2)}) collective-permute-start(s16[400,128]{1,0:T(8,128)(2,1)S(1)} %get-tuple-element.76), channel_id=1, source_target_pairs={{2,0},{3,1},{0,2},{1,3},{6,4},{7,5},{4,6},{5,7},{10,8},{11,9},{8,1... | collective-permute-start | bytes 307208 | tf_op jit(solution)/shard_map/ppermute | solution.py:23
  25.3 0.4 join_0_128.1
  25.7 0.5 collective-permute-done.4.rest_0_
  26.2 1.6 %collective-permute-start.9 = (s16[784,128]{1,0:T(8,128)(2,1)S(1)}, s16[784,128]{1,0:T(8,128)(2,1)S(1)}, u32[]{:S(2)}, u32[]{:S(2)}) collective-permute-start(s16[784,128]{1,0:T(8,128)(2,1)S(1)} %get-tuple-element.84), channel_id=1, source_target_pairs={{1,0},{0,1},{3,2},{2,3},{5,4},{4,5},{7,6},{6,7},{9,8},{8,9},{11,10... | collective-permute-start | bytes 602120 | tf_op jit(solution)/shard_map/ppermute | solution.py:23
  27.8 5.8 %collective-permute-done.5.rest_1_ = s16[400,128]{1,0:T(8,128)(2,1)S(1)} collective-permute-done((s16[400,128]{1,0:T(8,128)(2,1)S(1)}, s16[400,128]{1,0:T(8,128)(2,1)S(1)}, u32[]{:S(2)}, u32[]{:S(2)}) %collective-permute-start.5) | collective-permute-done | bytes 102432 | tf_op jit(solution)/shard_map/ppermute | solution.py:23
  33.6 1.8 %own_products_1.1.own_ref = f32[1536,256]{1,0:T(8,128)S(1)} custom-call(f32[8,1536]{1,0:T(8,128)S(1)} %get-tuple-element.57.a_rows_ref, f32[8,1536]{1,0:T(8,128)S(1)} %get-tuple-element.73.b_rows_ref, bf16[1,2048,1536]{2,1,0:T(8,128)(2,1)S(1)} %bitcast.4, bf16[1024,2048]{1,0:T(8,128)(2,1)S(1)} %get-tuple-element.61.ext_rows_ref, ...), custom_call_target="tpu_custom_call" | custom-call | flops 1 | bytes 1 | tf_op jit(solution)/shard_map/own_products_1/pallas_call | solution.py:31
  35.5 0.6 join_1_0.1
  36.1 2.1 %collective-permute-start.13 = (s16[784,128]{1,0:T(8,128)(2,1)S(1)}, s16[784,128]{1,0:T(8,128)(2,1)S(1)}, u32[]{:S(2)}, u32[]{:S(2)}) collective-permute-start(s16[784,128]{1,0:T(8,128)(2,1)S(1)} %get-tuple-element.95), channel_id=1, source_target_pairs={{1,0},{0,1},{3,2},{2,3},{5,4},{4,5},{7,6},{6,7},{9,8},{8,9},{11,10... | collective-permute-start | bytes 602120 | tf_op jit(solution)/shard_map/ppermute | solution.py:23
  38.4 1.5 %collective-permute-start.12 = (s16[400,128]{1,0:T(8,128)(2,1)S(1)}, s16[400,128]{1,0:T(8,128)(2,1)S(1)}, u32[]{:S(2)}, u32[]{:S(2)}) collective-permute-start(s16[400,128]{1,0:T(8,128)(2,1)S(1)} %get-tuple-element.91), channel_id=1, source_target_pairs={{2,0},{3,1},{0,2},{1,3},{6,4},{7,5},{4,6},{5,7},{10,8},{11,9},{8,1... | collective-permute-start | bytes 307208 | tf_op jit(solution)/shard_map/ppermute | solution.py:23
  39.9 1.7 %collective-permute-done.10.ext_ref = s16[1040,128]{1,0:T(8,128)(2,1)S(1)} collective-permute-done((s16[1040,128]{1,0:T(8,128)(2,1)S(1)}, s16[1040,128]{1,0:T(8,128)(2,1)S(1)}, u32[]{:S(2)}, u32[]{:S(2)}) %collective-permute-start.10) | collective-permute-done | bytes 266272 | tf_op jit(solution)/shard_map/ppermute | solution.py:23
  41.6 0.4 join_1_128.1
  42.1 3.3 %collective-permute-start.15 = (s16[400,128]{1,0:T(8,128)(2,1)S(1)}, s16[400,128]{1,0:T(8,128)(2,1)S(1)}, u32[]{:S(2)}, u32[]{:S(2)}) collective-permute-start(s16[400,128]{1,0:T(8,128)(2,1)S(1)} %get-tuple-element.99), channel_id=1, source_target_pairs={{2,0},{3,1},{0,2},{1,3},{6,4},{7,5},{4,6},{5,7},{10,8},{11,9},{8,1... | collective-permute-start | bytes 307208 | tf_op jit(solution)/shard_map/ppermute | solution.py:23
  45.4 1.1 %collective-permute-start.16 = (s16[400,128]{1,0:T(8,128)(2,1)S(1)}, s16[400,128]{1,0:T(8,128)(2,1)S(1)}, u32[]{:S(2)}, u32[]{:S(2)}) collective-permute-start(s16[400,128]{1,0:T(8,128)(2,1)S(1)} %get-tuple-element.100), channel_id=1, source_target_pairs={{3,0},{2,1},{1,2},{0,3},{7,4},{6,5},{5,6},{4,7},{11,8},{10,9},{9,1... | collective-permute-start | bytes 307208 | tf_op jit(solution)/shard_map/ppermute | solution.py:23
  46.5 0.8 %collective-permute-done.13.got_ref = s16[784,128]{1,0:T(8,128)(2,1)S(1)} collective-permute-done((s16[784,128]{1,0:T(8,128)(2,1)S(1)}, s16[784,128]{1,0:T(8,128)(2,1)S(1)}, u32[]{:S(2)}, u32[]{:S(2)}) %collective-permute-start.13) | collective-permute-done | bytes 200736 | tf_op jit(solution)/shard_map/ppermute | solution.py:23
  47.5 2.0 %collective-permute-start.17 = (s16[400,128]{1,0:T(8,128)(2,1)S(1)}, s16[400,128]{1,0:T(8,128)(2,1)S(1)}, u32[]{:S(2)}, u32[]{:S(2)}) collective-permute-start(s16[400,128]{1,0:T(8,128)(2,1)S(1)} %get-tuple-element.103), channel_id=1, source_target_pairs={{2,0},{3,1},{0,2},{1,3},{6,4},{7,5},{4,6},{5,7},{10,8},{11,9},{8,1... | collective-permute-start | bytes 307208 | tf_op jit(solution)/shard_map/ppermute | solution.py:23
  49.5 0.8 %collective-permute-done.14.rest_0_ = s16[400,128]{1,0:T(8,128)(2,1)S(1)} collective-permute-done((s16[400,128]{1,0:T(8,128)(2,1)S(1)}, s16[400,128]{1,0:T(8,128)(2,1)S(1)}, u32[]{:S(2)}, u32[]{:S(2)}) %collective-permute-start.14) | collective-permute-done | bytes 102432 | tf_op jit(solution)/shard_map/ppermute | solution.py:23
  50.3 7.0 %collective-permute-done.15.rest_1_ = s16[400,128]{1,0:T(8,128)(2,1)S(1)} collective-permute-done((s16[400,128]{1,0:T(8,128)(2,1)S(1)}, s16[400,128]{1,0:T(8,128)(2,1)S(1)}, u32[]{:S(2)}, u32[]{:S(2)}) %collective-permute-start.15) | collective-permute-done | bytes 102432 | tf_op jit(solution)/shard_map/ppermute | solution.py:23
  57.4 3.2 %collective-permute-done.17.rest_0_ = s16[400,128]{1,0:T(8,128)(2,1)S(1)} collective-permute-done((s16[400,128]{1,0:T(8,128)(2,1)S(1)}, s16[400,128]{1,0:T(8,128)(2,1)S(1)}, u32[]{:S(2)}, u32[]{:S(2)}) %collective-permute-start.17) | collective-permute-done | bytes 102432 | tf_op jit(solution)/shard_map/ppermute | solution.py:23
  60.6 1.8 %collective-permute-start.20 = (f32[8,512]{1,0:T(8,128)S(1)}, f32[8,512]{1,0:T(8,128)S(1)}, u32[]{:S(2)}, u32[]{:S(2)}) collective-permute-start(f32[8,512]{1,0:T(8,128)S(1)} %get-tuple-element.106.refs_4_), channel_id=1, source_target_pairs={{3,0},{2,1},{1,2},{0,3},{7,4},{6,5},{5,6},{4,7},{11,8},{10,9},{9,1... | collective-permute-start | bytes 49160 | tf_op jit(solution)/shard_map/ppermute | solution.py:23
  62.4 2.6 %collective-permute-start.18 = (f32[8,512]{1,0:T(8,128)S(1)}, f32[8,512]{1,0:T(8,128)S(1)}, u32[]{:S(2)}, u32[]{:S(2)}) collective-permute-start(f32[8,512]{1,0:T(8,128)S(1)} %get-tuple-element.106.refs_4_), channel_id=1, source_target_pairs={{1,0},{0,1},{3,2},{2,3},{5,4},{4,5},{7,6},{6,7},{9,8},{8,9},{11,10... | collective-permute-start | bytes 49160 | tf_op jit(solution)/shard_map/ppermute | solution.py:23
  65.1 1.1 %collective-permute-done.20.refs_7_ = f32[8,512]{1,0:T(8,128)S(1)} collective-permute-done((f32[8,512]{1,0:T(8,128)S(1)}, f32[8,512]{1,0:T(8,128)S(1)}, u32[]{:S(2)}, u32[]{:S(2)}) %collective-permute-start.20) | collective-permute-done | bytes 16416 | tf_op jit(solution)/shard_map/ppermute | solution.py:23
  66.2 0.9 %collective-permute-done.19.refs_6_ = f32[8,512]{1,0:T(8,128)S(1)} collective-permute-done((f32[8,512]{1,0:T(8,128)S(1)}, f32[8,512]{1,0:T(8,128)S(1)}, u32[]{:S(2)}, u32[]{:S(2)}) %collective-permute-start.19) | collective-permute-done | bytes 16416 | tf_op jit(solution)/shard_map/ppermute | solution.py:23
  67.1 1.0 %rescale.1 = f32[1,384,512]{2,1,0:T(8,128)} custom-call(f32[384,128]{1,0:T(8,128)S(1)} %get-tuple-element.78.refs_0_, f32[384,128]{1,0:T(8,128)S(1)} %get-tuple-element.92.refs_1_, f32[384,128]{1,0:T(8,128)S(1)} %get-tuple-element.104.refs_2_, f32[384,128]{1,0:T(8,128)S(1)} %get-tuple-element.105.refs_3_, f32[8,512]{1,0:T(8,128)S(1)} %get-tuple-element.106.refs_4_, ...), custom_call_target="tpu_custom_call" | custom-call | flops 1 | bytes 1 | tf_op jit(solution)/shard_map/rescale/pallas_call | solution.py:31
  (32 shorter events, 1.2 us)
Async XLA Ops:
  0.0 8.0 %slice-start = ((s8[6291456]{0:T(1024)(128)(4,1)}), s8[4194304]{0:T(1024)(128)(4,1)S(1)}, s32[]{:S(2)}) async-start(s8[6291456]{0:T(1024)(128)(4,1)} %bitcast.3), calls=%async_computation | async-start | bytes 8388608
  0.0 8.0 %slice-start.1 = ((s8[6291456]{0:T(1024)(128)(4,1)}), s8[2097152]{0:T(1024)(128)(4,1)S(1)}, s32[]{:S(2)}) async-start(s8[6291456]{0:T(1024)(128)(4,1)} %bitcast.3), calls=%async_computation.1 | async-start | bytes 4194304
  0.0 8.0 %copy-start = (bf16[1,2048,1536]{2,1,0:T(8,128)(2,1)S(1)}, bf16[1,2048,1536]{2,1,0:T(8,128)(2,1)}, u32[]{:S(2)}) copy-start(bf16[1,2048,1536]{2,1,0:T(8,128)(2,1)} %side_ref.1) | copy-start | bytes 18874372
  4.6 10.1 %collective-permute-start = (s16[1040,128]{1,0:T(8,128)(2,1)S(1)}, s16[1040,128]{1,0:T(8,128)(2,1)S(1)}, u32[]{:S(2)}, u32[]{:S(2)}) collective-permute-start(s16[1040,128]{1,0:T(8,128)(2,1)S(1)} %get-tuple-element.59), channel_id=1, source_target_pairs={{28,0},{8,4},{4,8},{16,12},{12,16},{24,20},{20,24},{0,28},{29,1},{... | collective-permute-start | bytes 798728 | tf_op jit(solution)/shard_map/ppermute | solution.py:23
  11.1 3.6 %collective-permute-start.1 = (s16[1040,128]{1,0:T(8,128)(2,1)S(1)}, s16[1040,128]{1,0:T(8,128)(2,1)S(1)}, u32[]{:S(2)}, u32[]{:S(2)}) collective-permute-start(s16[1040,128]{1,0:T(8,128)(2,1)S(1)} %get-tuple-element.62), channel_id=1, source_target_pairs={{4,0},{0,4},{12,8},{8,12},{20,16},{16,20},{28,24},{24,28},{5,1},{1... | collective-permute-start | bytes 798728 | tf_op jit(solution)/shard_map/ppermute | solution.py:23
  11.1 11.3 %collective-permute-start.2 = (s16[1040,128]{1,0:T(8,128)(2,1)S(1)}, s16[1040,128]{1,0:T(8,128)(2,1)S(1)}, u32[]{:S(2)}, u32[]{:S(2)}) collective-permute-start(s16[1040,128]{1,0:T(8,128)(2,1)S(1)} %get-tuple-element.70), channel_id=1, source_target_pairs={{28,0},{8,4},{4,8},{16,12},{12,16},{24,20},{20,24},{0,28},{29,1},{... | collective-permute-start | bytes 798728 | tf_op jit(solution)/shard_map/ppermute | solution.py:23
  13.4 11.7 %collective-permute-start.3 = (s16[1040,128]{1,0:T(8,128)(2,1)S(1)}, s16[1040,128]{1,0:T(8,128)(2,1)S(1)}, u32[]{:S(2)}, u32[]{:S(2)}) collective-permute-start(s16[1040,128]{1,0:T(8,128)(2,1)S(1)} %get-tuple-element.71), channel_id=1, source_target_pairs={{4,0},{0,4},{12,8},{8,12},{20,16},{16,20},{28,24},{24,28},{5,1},{1... | collective-permute-start | bytes 798728 | tf_op jit(solution)/shard_map/ppermute | solution.py:23
  18.0 17.5 %collective-permute-start.7 = (s16[1040,128]{1,0:T(8,128)(2,1)S(1)}, s16[1040,128]{1,0:T(8,128)(2,1)S(1)}, u32[]{:S(2)}, u32[]{:S(2)}) collective-permute-start(s16[1040,128]{1,0:T(8,128)(2,1)S(1)} %get-tuple-element.81), channel_id=1, source_target_pairs={{28,0},{8,4},{4,8},{16,12},{12,16},{24,20},{20,24},{0,28},{29,1},{... | collective-permute-start | bytes 798728 | tf_op jit(solution)/shard_map/ppermute | solution.py:23
  20.9 14.6 %collective-permute-start.8 = (s16[1040,128]{1,0:T(8,128)(2,1)S(1)}, s16[1040,128]{1,0:T(8,128)(2,1)S(1)}, u32[]{:S(2)}, u32[]{:S(2)}) collective-permute-start(s16[1040,128]{1,0:T(8,128)(2,1)S(1)} %get-tuple-element.68), channel_id=1, source_target_pairs={{4,0},{0,4},{12,8},{8,12},{20,16},{16,20},{28,24},{24,28},{5,1},{1... | collective-permute-start | bytes 798728 | tf_op jit(solution)/shard_map/ppermute | solution.py:23
  20.9 5.3 %collective-permute-start.4 = (s16[400,128]{1,0:T(8,128)(2,1)S(1)}, s16[400,128]{1,0:T(8,128)(2,1)S(1)}, u32[]{:S(2)}, u32[]{:S(2)}) collective-permute-start(s16[400,128]{1,0:T(8,128)(2,1)S(1)} %get-tuple-element.75), channel_id=1, source_target_pairs={{1,0},{0,1},{3,2},{2,3},{5,4},{4,5},{7,6},{6,7},{9,8},{8,9},{11,10... | collective-permute-start | bytes 307208 | tf_op jit(solution)/shard_map/ppermute | solution.py:23
  22.5 11.1 %collective-permute-start.5 = (s16[400,128]{1,0:T(8,128)(2,1)S(1)}, s16[400,128]{1,0:T(8,128)(2,1)S(1)}, u32[]{:S(2)}, u32[]{:S(2)}) collective-permute-start(s16[400,128]{1,0:T(8,128)(2,1)S(1)} %get-tuple-element.76), channel_id=1, source_target_pairs={{2,0},{3,1},{0,2},{1,3},{6,4},{7,5},{4,6},{5,7},{10,8},{11,9},{8,1... | collective-permute-start | bytes 307208 | tf_op jit(solution)/shard_map/ppermute | solution.py:23
  25.1 8.5 %collective-permute-start.6 = (s16[400,128]{1,0:T(8,128)(2,1)S(1)}, s16[400,128]{1,0:T(8,128)(2,1)S(1)}, u32[]{:S(2)}, u32[]{:S(2)}) collective-permute-start(s16[400,128]{1,0:T(8,128)(2,1)S(1)} %get-tuple-element.77), channel_id=1, source_target_pairs={{3,0},{2,1},{1,2},{0,3},{7,4},{6,5},{5,6},{4,7},{11,8},{10,9},{9,1... | collective-permute-start | bytes 307208 | tf_op jit(solution)/shard_map/ppermute | solution.py:23
  26.2 12.0 %collective-permute-start.9 = (s16[784,128]{1,0:T(8,128)(2,1)S(1)}, s16[784,128]{1,0:T(8,128)(2,1)S(1)}, u32[]{:S(2)}, u32[]{:S(2)}) collective-permute-start(s16[784,128]{1,0:T(8,128)(2,1)S(1)} %get-tuple-element.84), channel_id=1, source_target_pairs={{1,0},{0,1},{3,2},{2,3},{5,4},{4,5},{7,6},{6,7},{9,8},{8,9},{11,10... | collective-permute-start | bytes 602120 | tf_op jit(solution)/shard_map/ppermute | solution.py:23
  33.6 8.0 %collective-permute-start.10 = (s16[1040,128]{1,0:T(8,128)(2,1)S(1)}, s16[1040,128]{1,0:T(8,128)(2,1)S(1)}, u32[]{:S(2)}, u32[]{:S(2)}) collective-permute-start(s16[1040,128]{1,0:T(8,128)(2,1)S(1)} %get-tuple-element.87), channel_id=1, source_target_pairs={{28,0},{8,4},{4,8},{16,12},{12,16},{24,20},{20,24},{0,28},{29,1},{... | collective-permute-start | bytes 798728 | tf_op jit(solution)/shard_map/ppermute | solution.py:23
  33.6 8.0 %collective-permute-start.11 = (s16[1040,128]{1,0:T(8,128)(2,1)S(1)}, s16[1040,128]{1,0:T(8,128)(2,1)S(1)}, u32[]{:S(2)}, u32[]{:S(2)}) collective-permute-start(s16[1040,128]{1,0:T(8,128)(2,1)S(1)} %get-tuple-element.88), channel_id=1, source_target_pairs={{4,0},{0,4},{12,8},{8,12},{20,16},{16,20},{28,24},{24,28},{5,1},{1... | collective-permute-start | bytes 798728 | tf_op jit(solution)/shard_map/ppermute | solution.py:23
  36.1 11.2 %collective-permute-start.13 = (s16[784,128]{1,0:T(8,128)(2,1)S(1)}, s16[784,128]{1,0:T(8,128)(2,1)S(1)}, u32[]{:S(2)}, u32[]{:S(2)}) collective-permute-start(s16[784,128]{1,0:T(8,128)(2,1)S(1)} %get-tuple-element.95), channel_id=1, source_target_pairs={{1,0},{0,1},{3,2},{2,3},{5,4},{4,5},{7,6},{6,7},{9,8},{8,9},{11,10... | collective-permute-start | bytes 602120 | tf_op jit(solution)/shard_map/ppermute | solution.py:23
  38.4 8.0 %collective-permute-start.12 = (s16[400,128]{1,0:T(8,128)(2,1)S(1)}, s16[400,128]{1,0:T(8,128)(2,1)S(1)}, u32[]{:S(2)}, u32[]{:S(2)}) collective-permute-start(s16[400,128]{1,0:T(8,128)(2,1)S(1)} %get-tuple-element.91), channel_id=1, source_target_pairs={{2,0},{3,1},{0,2},{1,3},{6,4},{7,5},{4,6},{5,7},{10,8},{11,9},{8,1... | collective-permute-start | bytes 307208 | tf_op jit(solution)/shard_map/ppermute | solution.py:23
  42.0 8.3 %collective-permute-start.14 = (s16[400,128]{1,0:T(8,128)(2,1)S(1)}, s16[400,128]{1,0:T(8,128)(2,1)S(1)}, u32[]{:S(2)}, u32[]{:S(2)}) collective-permute-start(s16[400,128]{1,0:T(8,128)(2,1)S(1)} %get-tuple-element.98), channel_id=1, source_target_pairs={{1,0},{0,1},{3,2},{2,3},{5,4},{4,5},{7,6},{6,7},{9,8},{8,9},{11,10... | collective-permute-start | bytes 307208 | tf_op jit(solution)/shard_map/ppermute | solution.py:23
  42.1 15.2 %collective-permute-start.15 = (s16[400,128]{1,0:T(8,128)(2,1)S(1)}, s16[400,128]{1,0:T(8,128)(2,1)S(1)}, u32[]{:S(2)}, u32[]{:S(2)}) collective-permute-start(s16[400,128]{1,0:T(8,128)(2,1)S(1)} %get-tuple-element.99), channel_id=1, source_target_pairs={{2,0},{3,1},{0,2},{1,3},{6,4},{7,5},{4,6},{5,7},{10,8},{11,9},{8,1... | collective-permute-start | bytes 307208 | tf_op jit(solution)/shard_map/ppermute | solution.py:23
  45.4 11.8 %collective-permute-start.16 = (s16[400,128]{1,0:T(8,128)(2,1)S(1)}, s16[400,128]{1,0:T(8,128)(2,1)S(1)}, u32[]{:S(2)}, u32[]{:S(2)}) collective-permute-start(s16[400,128]{1,0:T(8,128)(2,1)S(1)} %get-tuple-element.100), channel_id=1, source_target_pairs={{3,0},{2,1},{1,2},{0,3},{7,4},{6,5},{5,6},{4,7},{11,8},{10,9},{9,1... | collective-permute-start | bytes 307208 | tf_op jit(solution)/shard_map/ppermute | solution.py:23
  47.5 13.0 %collective-permute-start.17 = (s16[400,128]{1,0:T(8,128)(2,1)S(1)}, s16[400,128]{1,0:T(8,128)(2,1)S(1)}, u32[]{:S(2)}, u32[]{:S(2)}) collective-permute-start(s16[400,128]{1,0:T(8,128)(2,1)S(1)} %get-tuple-element.103), channel_id=1, source_target_pairs={{2,0},{3,1},{0,2},{1,3},{6,4},{7,5},{4,6},{5,7},{10,8},{11,9},{8,1... | collective-permute-start | bytes 307208 | tf_op jit(solution)/shard_map/ppermute | solution.py:23
  60.6 5.6 %collective-permute-start.20 = (f32[8,512]{1,0:T(8,128)S(1)}, f32[8,512]{1,0:T(8,128)S(1)}, u32[]{:S(2)}, u32[]{:S(2)}) collective-permute-start(f32[8,512]{1,0:T(8,128)S(1)} %get-tuple-element.106.refs_4_), channel_id=1, source_target_pairs={{3,0},{2,1},{1,2},{0,3},{7,4},{6,5},{5,6},{4,7},{11,8},{10,9},{9,1... | collective-permute-start | bytes 49160 | tf_op jit(solution)/shard_map/ppermute | solution.py:23
  62.4 4.6 %collective-permute-start.19 = (f32[8,512]{1,0:T(8,128)S(1)}, f32[8,512]{1,0:T(8,128)S(1)}, u32[]{:S(2)}, u32[]{:S(2)}) collective-permute-start(f32[8,512]{1,0:T(8,128)S(1)} %get-tuple-element.106.refs_4_), channel_id=1, source_target_pairs={{2,0},{3,1},{0,2},{1,3},{6,4},{7,5},{4,6},{5,7},{10,8},{11,9},{8,1... | collective-permute-start | bytes 49160 | tf_op jit(solution)/shard_map/ppermute | solution.py:23
  62.4 4.6 %collective-permute-start.18 = (f32[8,512]{1,0:T(8,128)S(1)}, f32[8,512]{1,0:T(8,128)S(1)}, u32[]{:S(2)}, u32[]{:S(2)}) collective-permute-start(f32[8,512]{1,0:T(8,128)S(1)} %get-tuple-element.106.refs_4_), channel_id=1, source_target_pairs={{1,0},{0,1},{3,2},{2,3},{5,4},{4,5},{7,6},{6,7},{9,8},{8,9},{11,10... | collective-permute-start | bytes 49160 | tf_op jit(solution)/shard_map/ppermute | solution.py:23

commit v18 on v16

--- a/solution.py
+++ b/solution.py
@@ -387,26 +387,39 @@
 
 
 def rescale_kernel(height, count, *refs):
-    squares, sums, out_ref = refs[:count], refs[count:-1], refs[-1]
+    squares, sums, (out_ref, buf, sems) = refs[:count], refs[count:-3], refs[-3:]
     total = functools.reduce(jnp.add, [ref[0:1, :] for ref in sums])
-    divisor = total / height + 1e-6
-    column = 0
-    for ref in squares:
-        columns = slice(column, column + ref.shape[1])
-        column += ref.shape[1]
-        out_ref[0, :, columns] = ref[...] / divisor[:, columns]
+    factor = 1.0 / (total / height + 1e-6)
+    groups = sems.shape[0]
+    depth = buf.shape[1] // groups
+    copies = []
+    for g in range(groups):
+        rows = slice(g * depth, (g + 1) * depth)
+        column = 0
+        for ref in squares:
+            columns = slice(column, column + ref.shape[1])
+            column += ref.shape[1]
+            buf[0, rows, columns] = ref[rows, :] * factor[:, columns]
+        copies.append(pltpu.make_async_copy(buf.at[0, rows], out_ref.at[0, rows], sems.at[g]))
+        copies[-1].start()
+    for copy in copies:
+        copy.wait()
 
 
 def rescale(squares, sums, height):
     rows = squares[0].shape[0]
-    width = sums[0].shape[1]
-    return call(
+    shape = (1, rows, sums[0].shape[1])
+    groups = 4 if rows % 32 == 0 else 1
+    return pl.pallas_call(
         functools.partial(rescale_kernel, float(height), len(squares)),
-        "rescale",
-        (*squares, *sums),
-        [IN_VMEM] * (len(squares) + len(sums)),
-        jax.ShapeDtypeStruct((1, rows, width), jnp.float32),
-    )
+        out_shape=jax.ShapeDtypeStruct(shape, jnp.float32),
+        in_specs=[IN_VMEM] * (len(squares) + len(sums)),
+        out_specs=IN_HBM,
+        scratch_shapes=[pltpu.VMEM(shape, jnp.float32), pltpu.SemaphoreType.DMA((groups,))],
+        compiler_params=pltpu.CompilerParams(vmem_limit_bytes=SMALL_LIMIT),
+        cost_estimate=pl.CostEstimate(flops=1, bytes_accessed=1, transcendentals=0),
+        name="rescale",
+    )(*squares, *sums)
 
 
 def shards(flow_t, graph, a_pattern, b_pattern, c_pattern):

time: 62.9 us -> 63 us (level)
    pallas_call x16 -> x15, Pallas kernels: 15.9 us -> 14.9 us  [call(): pl.pallas_call(kernel, out_shape=out_shape, in_specs=in_specs, out_specs=...]
    pallas_call x0 -> x1, Pallas kernels: none -> 0.94 us  [rescale(): pl.pallas_call(functools.partial(rescale_kernel, float(height), len(squar...]
where the time goes in v18:
time: 63 us; the launch traced here: 62.9 us
  starting transfers between devices  28.6 us (45%)
  waiting for transfers between devices  18.2 us (29%)
  Pallas kernels  15.8 us (25%)
    ppermute x20, starting transfers between devices, swap(): lax.ppermute(block, axis, [(partner(i), i) for i in range(lax.axis_size(a...  28.6 us
    ppermute x20, waiting for transfers between devices, swap(): lax.ppermute(block, axis, [(partner(i), i) for i in range(lax.axis_size(a...  18.2 us
    pallas_call x15, Pallas kernels, call(): pl.pallas_call(kernel, out_shape=out_shape, in_specs=in_specs, out_specs=...  14.9 us
  transfers between devices with their start and end apart: 20, of which 10 were waited for; matrix products, arithmetic and copies ran while one was open for 0% of the time, Pallas kernels for 16%

profile of v18, /device:TPU:0, one launch (start us, length us, event | category | flops | bytes accessed | tf_op | source)
XLA Modules:
  0.0 62.9 jit_solution(10265037117435440919)
XLA Ops:
  0.0 4.5 %first_products.1 = (s16[1040,128]{1,0:T(8,128)(2,1)S(1)}, s16[1040,128]{1,0:T(8,128)(2,1)S(1)}, bf16[1024,2048]{1,0:T(8,128)(2,1)S(1)}, f32[8,1536]{1,0:T(8,128...) custom-call(s32[6,1,32]{2,1,0:T(1,128)} %bitcast.5, s32[6,1,32]{2,1,0:T(1,128)} %bitcast.6, s32[1,2,6]{2,1,0:T(2,128)} %bitcast.7, ...), custom_call_target="tpu_custom_call" | custom-call | flops 1 | bytes 1 | tf_op jit(solution)/shard_map/first_products/pallas_call | solution.py:32
  4.6 3.4 %collective-permute-start = (s16[1040,128]{1,0:T(8,128)(2,1)S(1)}, s16[1040,128]{1,0:T(8,128)(2,1)S(1)}, u32[]{:S(2)}, u32[]{:S(2)}) collective-permute-start(s16[1040,128]{1,0:T(8,128)(2,1)S(1)} %get-tuple-element.60), channel_id=1, source_target_pairs={{28,0},{8,4},{4,8},{16,12},{12,16},{24,20},{20,24},{0,28},{29,1},{... | collective-permute-start | bytes 798728 | tf_op jit(solution)/shard_map/ppermute | solution.py:24
  8.0 3.1 %own_int_products_0.1 = (f32[1536,256]{1,0:T(8,128)S(1)}, s16[1040,128]{1,0:T(8,128)(2,1)S(1)}, s16[1040,128]{1,0:T(8,128)(2,1)S(1)}, bf16[512,2048]{1,0:T(8,128)(2,1)S(1)}) custom-call(f32[8,1536]{1,0:T(8,128)S(1)} %get-tuple-element.58.a_rows_ref, f32[8,1536]{1,0:T(8,128)S(1)} %get-tuple-element.74.b_rows_ref, bf16[1,2048,1536]{2,1,0:T(8,128)(2,1)S(1)} %bitcast.4, ...), custom_call_target="tpu_custom_call" | custom-call | flops 1 | bytes 1 | tf_op jit(solution)/shard_map/own_int_products_0/pallas_call | solution.py:32
  11.1 2.3 %collective-permute-start.2 = (s16[1040,128]{1,0:T(8,128)(2,1)S(1)}, s16[1040,128]{1,0:T(8,128)(2,1)S(1)}, u32[]{:S(2)}, u32[]{:S(2)}) collective-permute-start(s16[1040,128]{1,0:T(8,128)(2,1)S(1)} %get-tuple-element.71), channel_id=1, source_target_pairs={{28,0},{8,4},{4,8},{16,12},{12,16},{24,20},{20,24},{0,28},{29,1},{... | collective-permute-start | bytes 798728 | tf_op jit(solution)/shard_map/ppermute | solution.py:24
  13.4 1.2 %collective-permute-done.ext_ref = s16[1040,128]{1,0:T(8,128)(2,1)S(1)} collective-permute-done((s16[1040,128]{1,0:T(8,128)(2,1)S(1)}, s16[1040,128]{1,0:T(8,128)(2,1)S(1)}, u32[]{:S(2)}, u32[]{:S(2)}) %collective-permute-start) | collective-permute-done | bytes 266272 | tf_op jit(solution)/shard_map/ppermute | solution.py:24
  14.6 0.4 join_0_0.1
  15.0 2.6 %collective-permute-start.4 = (s16[400,128]{1,0:T(8,128)(2,1)S(1)}, s16[400,128]{1,0:T(8,128)(2,1)S(1)}, u32[]{:S(2)}, u32[]{:S(2)}) collective-permute-start(s16[400,128]{1,0:T(8,128)(2,1)S(1)} %get-tuple-element.76), channel_id=1, source_target_pairs={{1,0},{0,1},{3,2},{2,3},{5,4},{4,5},{7,6},{6,7},{9,8},{8,9},{11,10... | collective-permute-start | bytes 307208 | tf_op jit(solution)/shard_map/ppermute | solution.py:24
  17.6 2.6 %collective-permute-start.5 = (s16[400,128]{1,0:T(8,128)(2,1)S(1)}, s16[400,128]{1,0:T(8,128)(2,1)S(1)}, u32[]{:S(2)}, u32[]{:S(2)}) collective-permute-start(s16[400,128]{1,0:T(8,128)(2,1)S(1)} %get-tuple-element.77), channel_id=1, source_target_pairs={{2,0},{3,1},{0,2},{1,3},{6,4},{7,5},{4,6},{5,7},{10,8},{11,9},{8,1... | collective-permute-start | bytes 307208 | tf_op jit(solution)/shard_map/ppermute | solution.py:24
  20.2 3.0 %ext_int_products_1.1 = (s16[1040,128]{1,0:T(8,128)(2,1)S(1)}, s16[1040,128]{1,0:T(8,128)(2,1)S(1)}, s16[1040,128]{1,0:T(8,128)(2,1)S(1)}, s16[1040,128]{1,0:T(8,128)(2,1)S(1)}) custom-call(f32[8,1536]{1,0:T(8,128)S(1)} %get-tuple-element.58.a_rows_ref, f32[8,1536]{1,0:T(8,128)S(1)} %get-tuple-element.74.b_rows_ref, bf16[1,2048,1536]{2,1,0:T(8,128)(2,1)S(1)} %bitcast.4, ...), custom_call_target="tpu_custom_call" | custom-call | flops 1 | bytes 1 | tf_op jit(solution)/shard_map/ext_int_products_1/pallas_call | solution.py:32
  23.2 1.4 %collective-permute-start.7 = (s16[1040,128]{1,0:T(8,128)(2,1)S(1)}, s16[1040,128]{1,0:T(8,128)(2,1)S(1)}, u32[]{:S(2)}, u32[]{:S(2)}) collective-permute-start(s16[1040,128]{1,0:T(8,128)(2,1)S(1)} %get-tuple-element.82), channel_id=1, source_target_pairs={{28,0},{8,4},{4,8},{16,12},{12,16},{24,20},{20,24},{0,28},{29,1},{... | collective-permute-start | bytes 798728 | tf_op jit(solution)/shard_map/ppermute | solution.py:24
  24.6 1.4 %collective-permute-start.10 = (s16[1040,128]{1,0:T(8,128)(2,1)S(1)}, s16[1040,128]{1,0:T(8,128)(2,1)S(1)}, u32[]{:S(2)}, u32[]{:S(2)}) collective-permute-start(s16[1040,128]{1,0:T(8,128)(2,1)S(1)} %get-tuple-element.88), channel_id=1, source_target_pairs={{28,0},{8,4},{4,8},{16,12},{12,16},{24,20},{20,24},{0,28},{29,1},{... | collective-permute-start | bytes 798728 | tf_op jit(solution)/shard_map/ppermute | solution.py:24
  26.0 1.0 %collective-permute-done.5.rest_1_ = s16[400,128]{1,0:T(8,128)(2,1)S(1)} collective-permute-done((s16[400,128]{1,0:T(8,128)(2,1)S(1)}, s16[400,128]{1,0:T(8,128)(2,1)S(1)}, u32[]{:S(2)}, u32[]{:S(2)}) %collective-permute-start.5) | collective-permute-done | bytes 102432 | tf_op jit(solution)/shard_map/ppermute | solution.py:24
  27.4 1.3 %collective-permute-start.9 = (s16[784,128]{1,0:T(8,128)(2,1)S(1)}, s16[784,128]{1,0:T(8,128)(2,1)S(1)}, u32[]{:S(2)}, u32[]{:S(2)}) collective-permute-start(s16[784,128]{1,0:T(8,128)(2,1)S(1)} %get-tuple-element.85), channel_id=1, source_target_pairs={{1,0},{0,1},{3,2},{2,3},{5,4},{4,5},{7,6},{6,7},{9,8},{8,9},{11,10... | collective-permute-start | bytes 602120 | tf_op jit(solution)/shard_map/ppermute | solution.py:24
  28.7 1.8 %own_products_1.1.own_ref = f32[1536,256]{1,0:T(8,128)S(1)} custom-call(f32[8,1536]{1,0:T(8,128)S(1)} %get-tuple-element.58.a_rows_ref, f32[8,1536]{1,0:T(8,128)S(1)} %get-tuple-element.74.b_rows_ref, bf16[1,2048,1536]{2,1,0:T(8,128)(2,1)S(1)} %bitcast.4, bf16[1024,2048]{1,0:T(8,128)(2,1)S(1)} %get-tuple-element.62.ext_rows_ref, ...), custom_call_target="tpu_custom_call" | custom-call | flops 1 | bytes 1 | tf_op jit(solution)/shard_map/own_products_1/pallas_call | solution.py:32
  30.6 2.2 %collective-permute-done.7.ext_ref = s16[1040,128]{1,0:T(8,128)(2,1)S(1)} collective-permute-done((s16[1040,128]{1,0:T(8,128)(2,1)S(1)}, s16[1040,128]{1,0:T(8,128)(2,1)S(1)}, u32[]{:S(2)}, u32[]{:S(2)}) %collective-permute-start.7) | collective-permute-done | bytes 266272 | tf_op jit(solution)/shard_map/ppermute | solution.py:24
  32.8 0.4 join_1_0.1
  33.2 1.0 %collective-permute-start.12 = (s16[784,128]{1,0:T(8,128)(2,1)S(1)}, s16[784,128]{1,0:T(8,128)(2,1)S(1)}, u32[]{:S(2)}, u32[]{:S(2)}) collective-permute-start(s16[784,128]{1,0:T(8,128)(2,1)S(1)} %get-tuple-element.92), channel_id=1, source_target_pairs={{1,0},{0,1},{3,2},{2,3},{5,4},{4,5},{7,6},{6,7},{9,8},{8,9},{11,10... | collective-permute-start | bytes 602120 | tf_op jit(solution)/shard_map/ppermute | solution.py:24
  34.2 1.0 %collective-permute-done.9.got_ref = s16[784,128]{1,0:T(8,128)(2,1)S(1)} collective-permute-done((s16[784,128]{1,0:T(8,128)(2,1)S(1)}, s16[784,128]{1,0:T(8,128)(2,1)S(1)}, u32[]{:S(2)}, u32[]{:S(2)}) %collective-permute-start.9) | collective-permute-done | bytes 200736 | tf_op jit(solution)/shard_map/ppermute | solution.py:24
  35.4 2.7 %collective-permute-done.10.ext_ref = s16[1040,128]{1,0:T(8,128)(2,1)S(1)} collective-permute-done((s16[1040,128]{1,0:T(8,128)(2,1)S(1)}, s16[1040,128]{1,0:T(8,128)(2,1)S(1)}, u32[]{:S(2)}, u32[]{:S(2)}) %collective-permute-start.10) | collective-permute-done | bytes 266272 | tf_op jit(solution)/shard_map/ppermute | solution.py:24
  38.1 0.4 join_1_128.1
  38.5 0.7 %collective-permute-start.13 = (s16[784,128]{1,0:T(8,128)(2,1)S(1)}, s16[784,128]{1,0:T(8,128)(2,1)S(1)}, u32[]{:S(2)}, u32[]{:S(2)}) collective-permute-start(s16[784,128]{1,0:T(8,128)(2,1)S(1)} %get-tuple-element.95), channel_id=1, source_target_pairs={{1,0},{0,1},{3,2},{2,3},{5,4},{4,5},{7,6},{6,7},{9,8},{8,9},{11,10... | collective-permute-start | bytes 602120 | tf_op jit(solution)/shard_map/ppermute | solution.py:24
  39.3 3.5 %collective-permute-start.14 = (s16[400,128]{1,0:T(8,128)(2,1)S(1)}, s16[400,128]{1,0:T(8,128)(2,1)S(1)}, u32[]{:S(2)}, u32[]{:S(2)}) collective-permute-start(s16[400,128]{1,0:T(8,128)(2,1)S(1)} %get-tuple-element.98), channel_id=1, source_target_pairs={{2,0},{3,1},{0,2},{1,3},{6,4},{7,5},{4,6},{5,7},{10,8},{11,9},{8,1... | collective-permute-start | bytes 307208 | tf_op jit(solution)/shard_map/ppermute | solution.py:24
  43.0 2.1 %collective-permute-start.15 = (s16[400,128]{1,0:T(8,128)(2,1)S(1)}, s16[400,128]{1,0:T(8,128)(2,1)S(1)}, u32[]{:S(2)}, u32[]{:S(2)}) collective-permute-start(s16[400,128]{1,0:T(8,128)(2,1)S(1)} %get-tuple-element.102), channel_id=1, source_target_pairs={{2,0},{3,1},{0,2},{1,3},{6,4},{7,5},{4,6},{5,7},{10,8},{11,9},{8,1... | collective-permute-start | bytes 307208 | tf_op jit(solution)/shard_map/ppermute | solution.py:24
  45.1 1.7 %collective-permute-done.13.got_ref = s16[784,128]{1,0:T(8,128)(2,1)S(1)} collective-permute-done((s16[784,128]{1,0:T(8,128)(2,1)S(1)}, s16[784,128]{1,0:T(8,128)(2,1)S(1)}, u32[]{:S(2)}, u32[]{:S(2)}) %collective-permute-start.13) | collective-permute-done | bytes 200736 | tf_op jit(solution)/shard_map/ppermute | solution.py:24
  46.9 1.8 %collective-permute-start.16 = (s16[400,128]{1,0:T(8,128)(2,1)S(1)}, s16[400,128]{1,0:T(8,128)(2,1)S(1)}, u32[]{:S(2)}, u32[]{:S(2)}) collective-permute-start(s16[400,128]{1,0:T(8,128)(2,1)S(1)} %get-tuple-element.106), channel_id=1, source_target_pairs={{2,0},{3,1},{0,2},{1,3},{6,4},{7,5},{4,6},{5,7},{10,8},{11,9},{8,1... | collective-permute-start | bytes 307208 | tf_op jit(solution)/shard_map/ppermute | solution.py:24
  48.9 5.1 %collective-permute-done.15.rest_0_ = s16[400,128]{1,0:T(8,128)(2,1)S(1)} collective-permute-done((s16[400,128]{1,0:T(8,128)(2,1)S(1)}, s16[400,128]{1,0:T(8,128)(2,1)S(1)}, u32[]{:S(2)}, u32[]{:S(2)}) %collective-permute-start.15) | collective-permute-done | bytes 102432 | tf_op jit(solution)/shard_map/ppermute | solution.py:24
  54.0 1.0 %collective-permute-done.16.rest_0_ = s16[400,128]{1,0:T(8,128)(2,1)S(1)} collective-permute-done((s16[400,128]{1,0:T(8,128)(2,1)S(1)}, s16[400,128]{1,0:T(8,128)(2,1)S(1)}, u32[]{:S(2)}, u32[]{:S(2)}) %collective-permute-start.16) | collective-permute-done | bytes 102432 | tf_op jit(solution)/shard_map/ppermute | solution.py:24
  55.1 2.1 %collective-permute-start.19 = (f32[8,512]{1,0:T(8,128)S(1)}, f32[8,512]{1,0:T(8,128)S(1)}, u32[]{:S(2)}, u32[]{:S(2)}) collective-permute-start(f32[8,512]{1,0:T(8,128)S(1)} %get-tuple-element.108.refs_4_), channel_id=1, source_target_pairs={{3,0},{2,1},{1,2},{0,3},{7,4},{6,5},{5,6},{4,7},{11,8},{10,9},{9,1... | collective-permute-start | bytes 49160 | tf_op jit(solution)/shard_map/ppermute | solution.py:24
  57.1 2.4 %collective-permute-start.17 = (f32[8,512]{1,0:T(8,128)S(1)}, f32[8,512]{1,0:T(8,128)S(1)}, u32[]{:S(2)}, u32[]{:S(2)}) collective-permute-start(f32[8,512]{1,0:T(8,128)S(1)} %get-tuple-element.108.refs_4_), channel_id=1, source_target_pairs={{1,0},{0,1},{3,2},{2,3},{5,4},{4,5},{7,6},{6,7},{9,8},{8,9},{11,10... | collective-permute-start | bytes 49160 | tf_op jit(solution)/shard_map/ppermute | solution.py:24
  59.5 1.2 %collective-permute-done.19.refs_7_ = f32[8,512]{1,0:T(8,128)S(1)} collective-permute-done((f32[8,512]{1,0:T(8,128)S(1)}, f32[8,512]{1,0:T(8,128)S(1)}, u32[]{:S(2)}, u32[]{:S(2)}) %collective-permute-start.19) | collective-permute-done | bytes 16416 | tf_op jit(solution)/shard_map/ppermute | solution.py:24
  60.7 1.0 %collective-permute-done.18.refs_6_ = f32[8,512]{1,0:T(8,128)S(1)} collective-permute-done((f32[8,512]{1,0:T(8,128)S(1)}, f32[8,512]{1,0:T(8,128)S(1)}, u32[]{:S(2)}, u32[]{:S(2)}) %collective-permute-start.18) | collective-permute-done | bytes 16416 | tf_op jit(solution)/shard_map/ppermute | solution.py:24
  61.8 0.9 %rescale.1 = f32[1,384,512]{2,1,0:T(8,128)} custom-call(f32[384,128]{1,0:T(8,128)S(1)} %get-tuple-element.79.refs_0_, f32[384,128]{1,0:T(8,128)S(1)} %get-tuple-element.99.refs_1_, f32[384,128]{1,0:T(8,128)S(1)} %get-tuple-element.103.refs_2_, f32[384,128]{1,0:T(8,128)S(1)} %get-tuple-element.107.refs_3_, f32[8,512]{1,0:T(8,128)S(1)} %get-tuple-element.108.refs_4_, ...), custom_call_target="tpu_custom_call" | custom-call | flops 1 | bytes 1 | tf_op jit(solution)/shard_map/rescale/pallas_call | solution.py:413
  (31 shorter events, 1.4 us)
Async XLA Ops:
  0.0 8.0 %slice-start = ((s8[6291456]{0:T(1024)(128)(4,1)}), s8[4194304]{0:T(1024)(128)(4,1)S(1)}, s32[]{:S(2)}) async-start(s8[6291456]{0:T(1024)(128)(4,1)} %bitcast.3), calls=%async_computation | async-start | bytes 8388608
  0.0 8.0 %slice-start.1 = ((s8[6291456]{0:T(1024)(128)(4,1)}), s8[2097152]{0:T(1024)(128)(4,1)S(1)}, s32[]{:S(2)}) async-start(s8[6291456]{0:T(1024)(128)(4,1)} %bitcast.3), calls=%async_computation.1 | async-start | bytes 4194304
  0.0 8.0 %copy-start = (bf16[1,2048,1536]{2,1,0:T(8,128)(2,1)S(1)}, bf16[1,2048,1536]{2,1,0:T(8,128)(2,1)}, u32[]{:S(2)}) copy-start(bf16[1,2048,1536]{2,1,0:T(8,128)(2,1)} %side_ref.1) | copy-start | bytes 18874372
  4.6 10.1 %collective-permute-start = (s16[1040,128]{1,0:T(8,128)(2,1)S(1)}, s16[1040,128]{1,0:T(8,128)(2,1)S(1)}, u32[]{:S(2)}, u32[]{:S(2)}) collective-permute-start(s16[1040,128]{1,0:T(8,128)(2,1)S(1)} %get-tuple-element.60), channel_id=1, source_target_pairs={{28,0},{8,4},{4,8},{16,12},{12,16},{24,20},{20,24},{0,28},{29,1},{... | collective-permute-start | bytes 798728 | tf_op jit(solution)/shard_map/ppermute | solution.py:24
  11.1 3.6 %collective-permute-start.1 = (s16[1040,128]{1,0:T(8,128)(2,1)S(1)}, s16[1040,128]{1,0:T(8,128)(2,1)S(1)}, u32[]{:S(2)}, u32[]{:S(2)}) collective-permute-start(s16[1040,128]{1,0:T(8,128)(2,1)S(1)} %get-tuple-element.63), channel_id=1, source_target_pairs={{4,0},{0,4},{12,8},{8,12},{20,16},{16,20},{28,24},{24,28},{5,1},{1... | collective-permute-start | bytes 798728 | tf_op jit(solution)/shard_map/ppermute | solution.py:24
  11.1 12.1 %collective-permute-start.2 = (s16[1040,128]{1,0:T(8,128)(2,1)S(1)}, s16[1040,128]{1,0:T(8,128)(2,1)S(1)}, u32[]{:S(2)}, u32[]{:S(2)}) collective-permute-start(s16[1040,128]{1,0:T(8,128)(2,1)S(1)} %get-tuple-element.71), channel_id=1, source_target_pairs={{28,0},{8,4},{4,8},{16,12},{12,16},{24,20},{20,24},{0,28},{29,1},{... | collective-permute-start | bytes 798728 | tf_op jit(solution)/shard_map/ppermute | solution.py:24
  13.4 11.2 %collective-permute-start.3 = (s16[1040,128]{1,0:T(8,128)(2,1)S(1)}, s16[1040,128]{1,0:T(8,128)(2,1)S(1)}, u32[]{:S(2)}, u32[]{:S(2)}) collective-permute-start(s16[1040,128]{1,0:T(8,128)(2,1)S(1)} %get-tuple-element.72), channel_id=1, source_target_pairs={{4,0},{0,4},{12,8},{8,12},{20,16},{16,20},{28,24},{24,28},{5,1},{1... | collective-permute-start | bytes 798728 | tf_op jit(solution)/shard_map/ppermute | solution.py:24
  15.0 9.6 %collective-permute-start.4 = (s16[400,128]{1,0:T(8,128)(2,1)S(1)}, s16[400,128]{1,0:T(8,128)(2,1)S(1)}, u32[]{:S(2)}, u32[]{:S(2)}) collective-permute-start(s16[400,128]{1,0:T(8,128)(2,1)S(1)} %get-tuple-element.76), channel_id=1, source_target_pairs={{1,0},{0,1},{3,2},{2,3},{5,4},{4,5},{7,6},{6,7},{9,8},{8,9},{11,10... | collective-permute-start | bytes 307208 | tf_op jit(solution)/shard_map/ppermute | solution.py:24
  17.6 9.4 %collective-permute-start.5 = (s16[400,128]{1,0:T(8,128)(2,1)S(1)}, s16[400,128]{1,0:T(8,128)(2,1)S(1)}, u32[]{:S(2)}, u32[]{:S(2)}) collective-permute-start(s16[400,128]{1,0:T(8,128)(2,1)S(1)} %get-tuple-element.77), channel_id=1, source_target_pairs={{2,0},{3,1},{0,2},{1,3},{6,4},{7,5},{4,6},{5,7},{10,8},{11,9},{8,1... | collective-permute-start | bytes 307208 | tf_op jit(solution)/shard_map/ppermute | solution.py:24
  20.2 7.2 %collective-permute-start.6 = (s16[400,128]{1,0:T(8,128)(2,1)S(1)}, s16[400,128]{1,0:T(8,128)(2,1)S(1)}, u32[]{:S(2)}, u32[]{:S(2)}) collective-permute-start(s16[400,128]{1,0:T(8,128)(2,1)S(1)} %get-tuple-element.78), channel_id=1, source_target_pairs={{3,0},{2,1},{1,2},{0,3},{7,4},{6,5},{5,6},{4,7},{11,8},{10,9},{9,1... | collective-permute-start | bytes 307208 | tf_op jit(solution)/shard_map/ppermute | solution.py:24
  23.2 9.6 %collective-permute-start.7 = (s16[1040,128]{1,0:T(8,128)(2,1)S(1)}, s16[1040,128]{1,0:T(8,128)(2,1)S(1)}, u32[]{:S(2)}, u32[]{:S(2)}) collective-permute-start(s16[1040,128]{1,0:T(8,128)(2,1)S(1)} %get-tuple-element.82), channel_id=1, source_target_pairs={{28,0},{8,4},{4,8},{16,12},{12,16},{24,20},{20,24},{0,28},{29,1},{... | collective-permute-start | bytes 798728 | tf_op jit(solution)/shard_map/ppermute | solution.py:24
  24.6 8.2 %collective-permute-start.8 = (s16[1040,128]{1,0:T(8,128)(2,1)S(1)}, s16[1040,128]{1,0:T(8,128)(2,1)S(1)}, u32[]{:S(2)}, u32[]{:S(2)}) collective-permute-start(s16[1040,128]{1,0:T(8,128)(2,1)S(1)} %get-tuple-element.69), channel_id=1, source_target_pairs={{4,0},{0,4},{12,8},{8,12},{20,16},{16,20},{28,24},{24,28},{5,1},{1... | collective-permute-start | bytes 798728 | tf_op jit(solution)/shard_map/ppermute | solution.py:24
  24.6 13.5 %collective-permute-start.10 = (s16[1040,128]{1,0:T(8,128)(2,1)S(1)}, s16[1040,128]{1,0:T(8,128)(2,1)S(1)}, u32[]{:S(2)}, u32[]{:S(2)}) collective-permute-start(s16[1040,128]{1,0:T(8,128)(2,1)S(1)} %get-tuple-element.88), channel_id=1, source_target_pairs={{28,0},{8,4},{4,8},{16,12},{12,16},{24,20},{20,24},{0,28},{29,1},{... | collective-permute-start | bytes 798728 | tf_op jit(solution)/shard_map/ppermute | solution.py:24
  27.0 11.1 %collective-permute-start.11 = (s16[1040,128]{1,0:T(8,128)(2,1)S(1)}, s16[1040,128]{1,0:T(8,128)(2,1)S(1)}, u32[]{:S(2)}, u32[]{:S(2)}) collective-permute-start(s16[1040,128]{1,0:T(8,128)(2,1)S(1)} %get-tuple-element.89), channel_id=1, source_target_pairs={{4,0},{0,4},{12,8},{8,12},{20,16},{16,20},{28,24},{24,28},{5,1},{1... | collective-permute-start | bytes 798728 | tf_op jit(solution)/shard_map/ppermute | solution.py:24
  27.4 7.8 %collective-permute-start.9 = (s16[784,128]{1,0:T(8,128)(2,1)S(1)}, s16[784,128]{1,0:T(8,128)(2,1)S(1)}, u32[]{:S(2)}, u32[]{:S(2)}) collective-permute-start(s16[784,128]{1,0:T(8,128)(2,1)S(1)} %get-tuple-element.85), channel_id=1, source_target_pairs={{1,0},{0,1},{3,2},{2,3},{5,4},{4,5},{7,6},{6,7},{9,8},{8,9},{11,10... | collective-permute-start | bytes 602120 | tf_op jit(solution)/shard_map/ppermute | solution.py:24
  33.2 9.6 %collective-permute-start.12 = (s16[784,128]{1,0:T(8,128)(2,1)S(1)}, s16[784,128]{1,0:T(8,128)(2,1)S(1)}, u32[]{:S(2)}, u32[]{:S(2)}) collective-permute-start(s16[784,128]{1,0:T(8,128)(2,1)S(1)} %get-tuple-element.92), channel_id=1, source_target_pairs={{1,0},{0,1},{3,2},{2,3},{5,4},{4,5},{7,6},{6,7},{9,8},{8,9},{11,10... | collective-permute-start | bytes 602120 | tf_op jit(solution)/shard_map/ppermute | solution.py:24
  38.5 8.2 %collective-permute-start.13 = (s16[784,128]{1,0:T(8,128)(2,1)S(1)}, s16[784,128]{1,0:T(8,128)(2,1)S(1)}, u32[]{:S(2)}, u32[]{:S(2)}) collective-permute-start(s16[784,128]{1,0:T(8,128)(2,1)S(1)} %get-tuple-element.95), channel_id=1, source_target_pairs={{1,0},{0,1},{3,2},{2,3},{5,4},{4,5},{7,6},{6,7},{9,8},{8,9},{11,10... | collective-permute-start | bytes 602120 | tf_op jit(solution)/shard_map/ppermute | solution.py:24
  39.3 9.5 %collective-permute-start.14 = (s16[400,128]{1,0:T(8,128)(2,1)S(1)}, s16[400,128]{1,0:T(8,128)(2,1)S(1)}, u32[]{:S(2)}, u32[]{:S(2)}) collective-permute-start(s16[400,128]{1,0:T(8,128)(2,1)S(1)} %get-tuple-element.98), channel_id=1, source_target_pairs={{2,0},{3,1},{0,2},{1,3},{6,4},{7,5},{4,6},{5,7},{10,8},{11,9},{8,1... | collective-permute-start | bytes 307208 | tf_op jit(solution)/shard_map/ppermute | solution.py:24
  43.0 10.9 %collective-permute-start.15 = (s16[400,128]{1,0:T(8,128)(2,1)S(1)}, s16[400,128]{1,0:T(8,128)(2,1)S(1)}, u32[]{:S(2)}, u32[]{:S(2)}) collective-permute-start(s16[400,128]{1,0:T(8,128)(2,1)S(1)} %get-tuple-element.102), channel_id=1, source_target_pairs={{2,0},{3,1},{0,2},{1,3},{6,4},{7,5},{4,6},{5,7},{10,8},{11,9},{8,1... | collective-permute-start | bytes 307208 | tf_op jit(solution)/shard_map/ppermute | solution.py:24
  46.9 8.1 %collective-permute-start.16 = (s16[400,128]{1,0:T(8,128)(2,1)S(1)}, s16[400,128]{1,0:T(8,128)(2,1)S(1)}, u32[]{:S(2)}, u32[]{:S(2)}) collective-permute-start(s16[400,128]{1,0:T(8,128)(2,1)S(1)} %get-tuple-element.106), channel_id=1, source_target_pairs={{2,0},{3,1},{0,2},{1,3},{6,4},{7,5},{4,6},{5,7},{10,8},{11,9},{8,1... | collective-permute-start | bytes 307208 | tf_op jit(solution)/shard_map/ppermute | solution.py:24
  55.1 5.7 %collective-permute-start.19 = (f32[8,512]{1,0:T(8,128)S(1)}, f32[8,512]{1,0:T(8,128)S(1)}, u32[]{:S(2)}, u32[]{:S(2)}) collective-permute-start(f32[8,512]{1,0:T(8,128)S(1)} %get-tuple-element.108.refs_4_), channel_id=1, source_target_pairs={{3,0},{2,1},{1,2},{0,3},{7,4},{6,5},{5,6},{4,7},{11,8},{10,9},{9,1... | collective-permute-start | bytes 49160 | tf_op jit(solution)/shard_map/ppermute | solution.py:24
  57.1 4.6 %collective-permute-start.18 = (f32[8,512]{1,0:T(8,128)S(1)}, f32[8,512]{1,0:T(8,128)S(1)}, u32[]{:S(2)}, u32[]{:S(2)}) collective-permute-start(f32[8,512]{1,0:T(8,128)S(1)} %get-tuple-element.108.refs_4_), channel_id=1, source_target_pairs={{2,0},{3,1},{0,2},{1,3},{6,4},{7,5},{4,6},{5,7},{10,8},{11,9},{8,1... | collective-permute-start | bytes 49160 | tf_op jit(solution)/shard_map/ppermute | solution.py:24
  57.1 4.6 %collective-permute-start.17 = (f32[8,512]{1,0:T(8,128)S(1)}, f32[8,512]{1,0:T(8,128)S(1)}, u32[]{:S(2)}, u32[]{:S(2)}) collective-permute-start(f32[8,512]{1,0:T(8,128)S(1)} %get-tuple-element.108.refs_4_), channel_id=1, source_target_pairs={{1,0},{0,1},{3,2},{2,3},{5,4},{4,5},{7,6},{6,7},{9,8},{8,9},{11,10... | collective-permute-start | bytes 49160 | tf_op jit(solution)/shard_map/ppermute | solution.py:24
